TPU v7x, 32 devices: a whole 2x2x4 slice. The times are simulated.
32 devices in a mesh: ctx: 8 (over z, x), tp: 4 (over y, core).
Axes of the slice: x: 2, y: 2, z: 4, core: 2. Of those that a mesh axis runs over, the one named last changes fastest.
Arguments:
- clean: bfloat16 [8192, 128], P('ctx'), may hold values from -5 to 5
- noise: bfloat16 [8192, 128], P('ctx'), may hold values from -5 to 5
- levels: int32 [32], replicated, may hold values from 0 to 999
- lengths: int32 [4], replicated, may hold values from 1 to 16, as said below
- order: int32 [16], replicated, may hold values from 0 to 15, as said below
- step: int32 [1], replicated, may hold values from 1 to 20
- w_attn: float32 [4, 1024, 1024], P(None, 'ctx', 'tp'), may hold values from -0.46875 to 0.46875
- m_attn: float32 [4, 1024, 1024], P(None, 'ctx', 'tp'), may hold values from -1.4901161e-07 to 1.4901161e-07
- v_attn: float32 [4, 1024, 1024], P(None, 'ctx', 'tp'), may hold values from 5.2286e-17 to 2.09144e-16
- w_mlp: float32 [2, 1024, 4096], P(None, 'ctx', 'tp'), may hold values from -0.15625 to 0.15625
- m_mlp: float32 [2, 1024, 4096], P(None, 'ctx', 'tp'), may hold values from -1.4901161e-07 to 1.4901161e-07
- v_mlp: float32 [2, 1024, 4096], P(None, 'ctx', 'tp'), may hold values from 5.2286e-17 to 2.09144e-16
- w_mod: float32 [1024, 6144], P('ctx'), may hold values from -0.1875 to 0.1875
- m_mod: float32 [1024, 6144], P('ctx'), may hold values from -1.4901161e-07 to 1.4901161e-07
- v_mod: float32 [1024, 6144], P('ctx'), may hold values from 5.2286e-17 to 2.09144e-16
- w_io: float32 [2, 128, 1024], P(None, None, 'ctx'), may hold values from -0.44194174 to 0.44194174
- m_io: float32 [2, 128, 1024], P(None, None, 'ctx'), may hold values from -1.3810679e-06 to 1.3810679e-06
- v_io: float32 [2, 128, 1024], P(None, None, 'ctx'), may hold values from 6.0796738e-17 to 2.5177002e-14
- vectors: float32 [8, 1024], P(None, 'ctx'), may hold values from -1.5 to 1.5
- m_vec: float32 [8, 1024], P(None, 'ctx'), may hold values from -1.4901161e-07 to 1.4901161e-07
- v_vec: float32 [8, 1024], P(None, 'ctx'), may hold values from 5.2286e-17 to 2.09144e-16
Outputs:
- loss_value: float32 [], replicated
- grad_norm: float32 [], replicated
- new_w_attn: float32 [4, 1024, 1024], P(None, 'ctx', 'tp')
- new_m_attn: float32 [4, 1024, 1024], P(None, 'ctx', 'tp')
- new_v_attn: float32 [4, 1024, 1024], P(None, 'ctx', 'tp')
- copy_attn: bfloat16 [4, 1024, 1024], P(None, 'ctx', 'tp')
- new_w_mlp: float32 [2, 1024, 4096], P(None, 'ctx', 'tp')
- new_m_mlp: float32 [2, 1024, 4096], P(None, 'ctx', 'tp')
- new_v_mlp: float32 [2, 1024, 4096], P(None, 'ctx', 'tp')
- copy_mlp: bfloat16 [2, 1024, 4096], P(None, 'ctx', 'tp')
- new_w_mod: float32 [1024, 6144], P('ctx')
- new_m_mod: float32 [1024, 6144], P('ctx')
- new_v_mod: float32 [1024, 6144], P('ctx')
- copy_mod: bfloat16 [1024, 6144], P('ctx')
- new_w_io: float32 [2, 128, 1024], P(None, None, 'ctx')
- new_m_io: float32 [2, 128, 1024], P(None, None, 'ctx')
- new_v_embed: float32 [128, 1024], P(None, 'ctx')
- new_v_head: float32 [128, 1024], P(None, 'ctx')
- copy_io: bfloat16 [2, 128, 1024], P(None, None, 'ctx')
- new_vectors: float32 [8, 1024], P(None, 'ctx')
- new_m_vec: float32 [8, 1024], P(None, 'ctx')
- new_v_vec: float32 [8, 1024], P(None, 'ctx')
- copy_vec: bfloat16 [8, 1024], P(None, 'ctx')
Inputs may be any that keep to these rules, and one draw needn't show every extreme that they name: `lengths`: clips are runs of consecutive logical frames in the given order; the longest has exactly 16 frames. `order`: each logical stretch appears once; storage stretches 0, 8 and 15 hold frames of one clip of 16 frames.
All inputs are finite; a program needn't handle non-finite values.
Results may differ from a plain program's by a relative error of at most 0.017.
Values may be sent and summed in bfloat16 or wider, within the bound.
No kernel may reach another device: no remote copies, remote signals or barrier semaphores. Data moves between devices by JAX's collectives and lax.ppermute only.
A program may use at most 320 MiB of HBM per device.

v0:
```python
import math

import jax
import jax.numpy as jnp
from jax import lax
from jax.sharding import PartitionSpec as P

D = 1024
HD = 64
GRID = 16
PATCHES = 256
LEVELS = 1000


ln_eps = 1e-06
snr_limit = 5.0
clip_limit = 0.001
beta_one = 0.9
beta_two = 0.999
adam_eps = 1e-08
rate_matrix = 0.05
rate_vector = 0.3
decay_rate = 0.1
neg_large = -1e30


def clip_starts(frame_ids, lengths):
    clip_ends = jnp.cumsum(lengths)
    before = (clip_ends[None, :] <= frame_ids[:, None]).astype(jnp.int32)
    return jnp.sum(before * lengths[None, :], axis=1)


def plan(levels):
    fraction = (levels.astype(jnp.float32) + 1.0) / (LEVELS + 1.0)
    signal_scale = jnp.cos(0.5 * math.pi * fraction)
    noise_scale = jnp.sin(0.5 * math.pi * fraction)
    snr_value = signal_scale * signal_scale / (noise_scale * noise_scale)
    weight = jnp.minimum(snr_value, snr_limit) / (snr_value + 1.0)
    return (signal_scale, noise_scale, weight)


def condition(levels, width):
    half_dim = width // 2
    frequency = jnp.exp(-math.log(10000.0) * jnp.arange(half_dim, dtype=jnp.float32) / half_dim)
    angle_tab = levels.astype(jnp.float32)[:, None] * frequency[None, :]
    return jax.nn.silu(jnp.concatenate([jnp.cos(angle_tab), jnp.sin(angle_tab)], axis=1))


def rope_tables(time_pos, height_pos, width_pos, head_dim):
    pair_count = head_dim // 2
    time_pairs = head_dim // 8
    height_pairs = (pair_count - time_pairs) // 2
    width_pairs = pair_count - time_pairs - height_pairs

    def angles(position, count):
        frequency = 10000.0 ** (-jnp.arange(count, dtype=jnp.float32) / count)
        return position.astype(jnp.float32)[:, None] * frequency[None, :]

    angle_tab = jnp.concatenate(
        [
            angles(time_pos, time_pairs),
            angles(height_pos, height_pairs),
            angles(width_pos, width_pairs),
        ],
        axis=1,
    )
    return (jnp.cos(angle_tab), jnp.sin(angle_tab))


def rotate(values, cosine, sine):
    half_dim = values.shape[-1] // 2
    first_half = values[..., :half_dim]
    second_half = values[..., half_dim:]
    cosine = cosine[:, None, :]
    sine = sine[:, None, :]
    return jnp.concatenate(
        [first_half * cosine - second_half * sine, second_half * cosine + first_half * sine],
        axis=-1,
    )


def rotate_back(grads, cosine, sine):
    half_dim = grads.shape[-1] // 2
    first_half = grads[..., :half_dim]
    second_half = grads[..., half_dim:]
    cosine = cosine[:, None, :]
    sine = sine[:, None, :]
    return jnp.concatenate(
        [first_half * cosine + second_half * sine, second_half * cosine - first_half * sine],
        axis=-1,
    )


def layer_norm(values):
    centred = values - jnp.mean(values, axis=-1, keepdims=True)
    inv_std = lax.rsqrt(jnp.mean(centred * centred, axis=-1, keepdims=True) + ln_eps)
    return (centred * inv_std, inv_std)


def norm_back(grad_in, normed, inv_std):
    mean_grad = jnp.mean(grad_in, axis=-1, keepdims=True)
    mean_proj = jnp.mean(grad_in * normed, axis=-1, keepdims=True)
    return inv_std * (grad_in - mean_grad - normed * mean_proj)


def gelu_slope(values):
    return 0.5 * (1.0 + lax.erf(values / math.sqrt(2.0))) + values * jnp.exp(
        -0.5 * values * values
    ) / math.sqrt(2.0 * math.pi)


def stretch_mask(query_stretch, key_stretch, stretch_frames, lengths):
    offsets = jnp.arange(stretch_frames, dtype=jnp.int32)
    query_frames = query_stretch * stretch_frames + offsets
    key_frames = key_stretch * stretch_frames + offsets
    starts = clip_starts(query_frames, lengths)
    return (key_frames[None, :] <= query_frames[:, None]) & (key_frames[None, :] >= starts[:, None])


def expand_mask(allowed):
    return jnp.repeat(jnp.repeat(allowed, PATCHES, axis=0), PATCHES, axis=1)


def online_step(current, query_block, key_block, value_block, keep, scale):
    run_max, run_sum, run_acc = current
    scores = (
        jnp.einsum("qhe,khe->hqk", query_block, key_block, preferred_element_type=jnp.float32)
        * scale
    )
    scores = jnp.where(keep[None], scores, neg_large)
    new_max = jnp.maximum(run_max, jnp.max(scores, axis=-1))
    probs = jnp.where(keep[None], jnp.exp(scores - new_max[..., None]), 0.0)
    shrink = jnp.exp(run_max - new_max)
    run_sum = run_sum * shrink + jnp.sum(probs, axis=-1)
    added = jnp.einsum(
        "hqk,khe->qhe", probs.astype(jnp.bfloat16), value_block, preferred_element_type=jnp.float32
    )
    run_acc = run_acc * jnp.transpose(shrink)[:, :, None] + added
    return (new_max, run_sum, run_acc)


def pair_grads(
    query_block, grad_block, lse_block, delta_block, key_block, value_block, keep, scale
):
    scores = (
        jnp.einsum("qhe,khe->hqk", query_block, key_block, preferred_element_type=jnp.float32)
        * scale
    )
    probs = jnp.where(keep[None], jnp.exp(scores - lse_block[..., None]), 0.0)
    grad_probs = jnp.einsum(
        "qhe,khe->hqk", grad_block, value_block, preferred_element_type=jnp.float32
    )
    grad_scores = (probs * (grad_probs - delta_block[..., None])).astype(jnp.bfloat16)
    grad_query = (
        jnp.einsum("hqk,khe->qhe", grad_scores, key_block, preferred_element_type=jnp.float32)
        * scale
    )
    grad_key = (
        jnp.einsum("hqk,qhe->khe", grad_scores, query_block, preferred_element_type=jnp.float32)
        * scale
    )
    grad_value = jnp.einsum(
        "hqk,qhe->khe", probs.astype(jnp.bfloat16), grad_block, preferred_element_type=jnp.float32
    )
    return (grad_query, grad_key, grad_value)


def adam(weight_now, first_mom, second_mom, grad, factor, count, rate, decay):
    grad = grad * factor
    first_mom = beta_one * first_mom + (1.0 - beta_one) * grad
    second_mom = beta_two * second_mom + (1.0 - beta_two) * grad * grad
    first_hat = first_mom / (1.0 - beta_one**count)
    second_hat = second_mom / (1.0 - beta_two**count)
    updated = weight_now - rate * (
        first_hat / (jnp.sqrt(second_hat) + adam_eps) + decay * weight_now
    )
    return (updated, first_mom, second_mom, updated.astype(jnp.bfloat16))


def shards(
    clean,
    noise,
    levels,
    lengths,
    order,
    step,
    w_attn,
    m_attn,
    v_attn,
    w_mlp,
    m_mlp,
    v_mlp,
    w_mod,
    m_mod,
    v_mod,
    w_io,
    m_io,
    v_io,
    vectors,
    m_vec,
    v_vec,
):
    ctx_count = lax.axis_size("ctx")
    ctx_index = lax.axis_index("ctx")
    tp_index = lax.axis_index("tp")
    tok_rows = clean.shape[0]
    feat_dim = clean.shape[1]
    frames_dev = tok_rows // PATCHES
    stretch_frames = frames_dev // 2
    stretch_rows = stretch_frames * PATCHES
    scale = HD ** (-0.5)
    bfloat = jnp.bfloat16
    single = jnp.float32
    attn_w, mlp_w, mod_w, io_w, vec_low = (
        lax.all_gather(w_attn.astype(bfloat), "ctx", axis=1, tiled=True),
        lax.all_gather(w_mlp.astype(bfloat), "ctx", axis=1, tiled=True),
        lax.all_gather(w_mod.astype(bfloat), "ctx", axis=0, tiled=True),
        lax.all_gather(w_io.astype(bfloat), "ctx", axis=2, tiled=True),
        lax.all_gather(vectors.astype(bfloat), "ctx", axis=1, tiled=True),
    )
    vec_w = vec_low.astype(single)
    local_width = attn_w.shape[2]
    heads_dev = local_width // HD
    frame_count = levels.shape[0]
    local_stretches = lax.dynamic_slice_in_dim(order, 2 * ctx_index, 2, 0)
    frame_ids = (
        local_stretches[:, None] * stretch_frames
        + jnp.arange(stretch_frames, dtype=jnp.int32)[None, :]
    ).reshape(frames_dev)
    table_hit = frame_ids[:, None] == jnp.arange(frame_count, dtype=jnp.int32)[None, :]
    frame_levels = jnp.sum(jnp.where(table_hit, levels[None, :], 0), axis=1)
    starts = clip_starts(frame_ids, lengths)
    signal_scale, noise_scale, weight = plan(frame_levels)
    signal_col = signal_scale[:, None, None]
    noise_col = noise_scale[:, None, None]
    clean_full = clean.astype(single).reshape(frames_dev, PATCHES, feat_dim)
    noise_full = noise.astype(single).reshape(frames_dev, PATCHES, feat_dim)
    noisy = signal_col * clean_full + noise_col * noise_full
    target = signal_col * noise_full - noise_col * clean_full
    noisy_low = noisy.reshape(tok_rows, feat_dim).astype(bfloat)
    embedded = jnp.dot(noisy_low, io_w[0], preferred_element_type=single) + vec_w[6]
    cond_low = condition(frame_levels, D).astype(bfloat)
    modulate = (
        jnp.dot(cond_low, mod_w, preferred_element_type=single) + vec_w[:6].reshape(6 * D)
    ).reshape(frames_dev, 6, 1, D)
    patch_ids = jnp.arange(PATCHES, dtype=jnp.int32)
    time_pos = jnp.repeat(frame_ids - starts, PATCHES)
    height_pos = jnp.tile(patch_ids // GRID, frames_dev)
    width_pos = jnp.tile(patch_ids % GRID, frames_dev)
    cosine, sine = rope_tables(time_pos, height_pos, width_pos, HD)
    resid_in = embedded.reshape(frames_dev, PATCHES, D)
    normed_one, inv_one = layer_norm(resid_in)
    hidden_one = (
        (normed_one * (1.0 + modulate[:, 1]) + modulate[:, 0]).reshape(tok_rows, D).astype(bfloat)
    )
    query_pre = jnp.dot(hidden_one, attn_w[0], preferred_element_type=single).reshape(
        tok_rows, heads_dev, HD
    )
    key_pre = jnp.dot(hidden_one, attn_w[1], preferred_element_type=single).reshape(
        tok_rows, heads_dev, HD
    )
    query_low = rotate(query_pre, cosine, sine).astype(bfloat)
    key_low = rotate(key_pre, cosine, sine).astype(bfloat)
    value_low = (
        jnp.dot(hidden_one, attn_w[2], preferred_element_type=single)
        .astype(bfloat)
        .reshape(tok_rows, heads_dev, HD)
    )
    query_stretches = query_low.reshape(2, stretch_rows, heads_dev, HD)
    init_state = (
        jnp.full((2, heads_dev, stretch_rows), neg_large, single),
        jnp.zeros((2, heads_dev, stretch_rows), single),
        jnp.zeros((2, stretch_rows, heads_dev, HD), single),
    )
    key_flat = key_low.reshape(tok_rows, local_width)
    value_flat = value_low.reshape(tok_rows, local_width)
    carry_state = init_state
    key_piece = lax.all_gather(key_flat, "ctx", axis=0, tiled=True)
    value_piece = lax.all_gather(value_flat, "ctx", axis=0, tiled=True)

    def per_stretch(block_num, carry_state):
        key_block = lax.dynamic_slice_in_dim(
            key_piece, block_num * stretch_rows, stretch_rows, 0
        ).reshape(stretch_rows, heads_dev, HD)
        value_block = lax.dynamic_slice_in_dim(
            value_piece, block_num * stretch_rows, stretch_rows, 0
        ).reshape(stretch_rows, heads_dev, HD)
        key_stretch = lax.dynamic_index_in_dim(order, block_num, 0, keepdims=False)
        updated = []
        for half_num in range(2):
            allowed = stretch_mask(local_stretches[half_num], key_stretch, stretch_frames, lengths)
            current = (carry_state[0][half_num], carry_state[1][half_num], carry_state[2][half_num])
            current = lax.cond(
                jnp.any(allowed),
                lambda cur, keep_mask: online_step(
                    cur,
                    query_stretches[half_num],
                    key_block,
                    value_block,
                    expand_mask(keep_mask),
                    scale,
                ),
                lambda cur, keep_mask: cur,
                current,
                allowed,
            )
            updated.append(current)
        return tuple((jnp.stack([updated[0][member], updated[1][member]]) for member in range(3)))

    run_max, run_sum, run_acc = lax.fori_loop(
        0, key_piece.shape[0] // stretch_rows, per_stretch, carry_state
    )
    mix_rows = (run_acc / jnp.transpose(run_sum, (0, 2, 1))[..., None]).reshape(
        tok_rows, heads_dev, HD
    )
    lse_stretches = run_max + jnp.log(run_sum)
    mix_low = mix_rows.reshape(tok_rows, local_width).astype(bfloat)
    attn_out = lax.psum(
        jnp.einsum("rh,dh->rd", mix_low, attn_w[3], preferred_element_type=single).astype(
            jnp.bfloat16
        ),
        "tp",
    ).astype(jnp.float32)
    attn_full = attn_out.reshape(frames_dev, PATCHES, D)
    resid_mid = resid_in + modulate[:, 2] * attn_full
    normed_two, inv_two = layer_norm(resid_mid)
    hidden_two = (
        (normed_two * (1.0 + modulate[:, 4]) + modulate[:, 3]).reshape(tok_rows, D).astype(bfloat)
    )
    upward = jnp.dot(hidden_two, mlp_w[0], preferred_element_type=single)
    activ_low = jax.nn.gelu(upward, approximate=False).astype(bfloat)
    mlp_out = lax.psum(
        jnp.einsum("rf,df->rd", activ_low, mlp_w[1], preferred_element_type=single).astype(
            jnp.bfloat16
        ),
        "tp",
    ).astype(jnp.float32)
    mlp_full = mlp_out.reshape(frames_dev, PATCHES, D)
    resid_out = resid_mid + modulate[:, 5] * mlp_full
    normed_three, inv_three = layer_norm(resid_out)
    final_low = (normed_three * vec_w[7]).reshape(tok_rows, D).astype(bfloat)
    pred = jnp.einsum("rd,pd->rp", final_low, io_w[1], preferred_element_type=single)
    diff = pred.reshape(frames_dev, PATCHES, feat_dim) - target
    error = jnp.mean(diff * diff, axis=2)
    weight_sum, error_sum = lax.psum(
        (PATCHES * jnp.sum(weight), jnp.sum(weight[:, None] * error)), "ctx"
    )
    loss_value = error_sum / weight_sum
    grad_pred = (
        (2.0 / feat_dim * weight[:, None, None] * diff / weight_sum)
        .reshape(tok_rows, feat_dim)
        .astype(bfloat)
    )
    grad_head = jnp.einsum("rp,rd->pd", grad_pred, final_low, preferred_element_type=single)
    grad_final = jnp.einsum("rp,pd->rd", grad_pred, io_w[1], preferred_element_type=single).reshape(
        frames_dev, PATCHES, D
    )
    grad_gain = jnp.sum(grad_final * normed_three, axis=(0, 1))
    grad_three = norm_back(grad_final * vec_w[7], normed_three, inv_three)
    grad_mlp_low = (modulate[:, 5] * grad_three).reshape(tok_rows, D).astype(bfloat)
    grad_gate_two = jnp.sum(grad_three * mlp_full, axis=1)
    grad_activ = jnp.einsum("rd,df->rf", grad_mlp_low, mlp_w[1], preferred_element_type=single)
    grad_down = jnp.einsum("rd,rf->df", grad_mlp_low, activ_low, preferred_element_type=single)
    grad_up_low = (grad_activ * gelu_slope(upward)).astype(bfloat)
    grad_up = jnp.einsum("rd,rf->df", hidden_two, grad_up_low, preferred_element_type=single)
    grad_hidden_two = lax.psum(
        jnp.einsum("rf,df->rd", grad_up_low, mlp_w[0], preferred_element_type=single).astype(
            jnp.bfloat16
        ),
        "tp",
    ).astype(jnp.float32)
    grad_hidden_two = grad_hidden_two.reshape(frames_dev, PATCHES, D)
    grad_shift_two = jnp.sum(grad_hidden_two, axis=1)
    grad_scale_two = jnp.sum(grad_hidden_two * normed_two, axis=1)
    grad_mid = grad_three + norm_back(grad_hidden_two * (1.0 + modulate[:, 4]), normed_two, inv_two)
    grad_attn_low = (modulate[:, 2] * grad_mid).reshape(tok_rows, D).astype(bfloat)
    grad_gate_one = jnp.sum(grad_mid * attn_full, axis=1)
    grad_outproj = jnp.einsum("rd,rh->dh", grad_attn_low, mix_low, preferred_element_type=single)
    grad_mix_low = jnp.einsum(
        "rd,dh->rh", grad_attn_low, attn_w[3], preferred_element_type=single
    ).astype(bfloat)
    delta_rows = jnp.sum(
        grad_mix_low.astype(single).reshape(tok_rows, heads_dev, HD) * mix_rows, axis=2
    )
    grad_stretches = grad_mix_low.reshape(2, stretch_rows, heads_dev, HD)
    delta_stretches = jnp.transpose(delta_rows.reshape(2, stretch_rows, heads_dev), (0, 2, 1))

    def span_back(key_block, value_block, key_stretch, grad_query_acc):
        key_sum = jnp.zeros((stretch_rows, heads_dev, HD), single)
        value_sum = jnp.zeros((stretch_rows, heads_dev, HD), single)
        query_parts = []
        for half_num in range(2):
            allowed = stretch_mask(local_stretches[half_num], key_stretch, stretch_frames, lengths)
            result = lax.cond(
                jnp.any(allowed),
                lambda keep_mask: pair_grads(
                    query_stretches[half_num],
                    grad_stretches[half_num],
                    lse_stretches[half_num],
                    delta_stretches[half_num],
                    key_block,
                    value_block,
                    expand_mask(keep_mask),
                    scale,
                ),
                lambda keep_mask: (jnp.zeros((stretch_rows, heads_dev, HD), single),) * 3,
                allowed,
            )
            query_parts.append(grad_query_acc[half_num] + result[0])
            key_sum = key_sum + result[1]
            value_sum = value_sum + result[2]
        return (
            jnp.stack(query_parts),
            key_sum.reshape(stretch_rows, local_width),
            value_sum.reshape(stretch_rows, local_width),
        )

    init_back = (
        jnp.zeros((2, stretch_rows, heads_dev, HD), single),
        jnp.zeros((ctx_count * tok_rows, local_width), single),
        jnp.zeros((ctx_count * tok_rows, local_width), single),
    )
    carry_state = init_back
    fold_key_piece = lax.all_gather(key_flat, "ctx", axis=0, tiled=True)
    fold_value_piece = lax.all_gather(value_flat, "ctx", axis=0, tiled=True)

    def per_stretch(block_num, carry_state):
        grad_query_acc, grad_keys_all, grad_values_all = carry_state
        key_block = lax.dynamic_slice_in_dim(
            fold_key_piece, block_num * stretch_rows, stretch_rows, 0
        ).reshape(stretch_rows, heads_dev, HD)
        value_block = lax.dynamic_slice_in_dim(
            fold_value_piece, block_num * stretch_rows, stretch_rows, 0
        ).reshape(stretch_rows, heads_dev, HD)
        key_stretch = lax.dynamic_index_in_dim(order, block_num, 0, keepdims=False)
        grad_query_acc, key_sum, value_sum = span_back(
            key_block, value_block, key_stretch, grad_query_acc
        )
        place = block_num * stretch_rows
        grad_keys_all = lax.dynamic_update_slice_in_dim(grad_keys_all, key_sum, place, 0)
        grad_values_all = lax.dynamic_update_slice_in_dim(grad_values_all, value_sum, place, 0)
        return (grad_query_acc, grad_keys_all, grad_values_all)

    grad_query_acc, grad_keys_all, grad_values_all = lax.fori_loop(
        0, fold_key_piece.shape[0] // stretch_rows, per_stretch, carry_state
    )
    grad_keys, grad_values = (
        lax.psum_scatter(
            grad_keys_all.astype(jnp.bfloat16), "ctx", scatter_dimension=0, tiled=True
        ).astype(jnp.float32),
        lax.psum_scatter(
            grad_values_all.astype(jnp.bfloat16), "ctx", scatter_dimension=0, tiled=True
        ).astype(jnp.float32),
    )
    grad_query = grad_query_acc.reshape(tok_rows, local_width)
    query_back = (
        rotate_back(grad_query.reshape(tok_rows, heads_dev, HD), cosine, sine)
        .reshape(tok_rows, local_width)
        .astype(bfloat)
    )
    key_back = (
        rotate_back(grad_keys.reshape(tok_rows, heads_dev, HD), cosine, sine)
        .reshape(tok_rows, local_width)
        .astype(bfloat)
    )
    value_back = grad_values.astype(bfloat)
    grad_wq = jnp.einsum("rd,rh->dh", hidden_one, query_back, preferred_element_type=single)
    grad_wk = jnp.einsum("rd,rh->dh", hidden_one, key_back, preferred_element_type=single)
    grad_wv = jnp.einsum("rd,rh->dh", hidden_one, value_back, preferred_element_type=single)
    partial_one = (
        jnp.einsum("rh,dh->rd", query_back, attn_w[0], preferred_element_type=single)
        + jnp.einsum("rh,dh->rd", key_back, attn_w[1], preferred_element_type=single)
        + jnp.einsum("rh,dh->rd", value_back, attn_w[2], preferred_element_type=single)
    )
    grad_hidden_one = (
        lax.psum(partial_one.astype(jnp.bfloat16), "tp")
        .astype(jnp.float32)
        .reshape(frames_dev, PATCHES, D)
    )
    grad_shift_one = jnp.sum(grad_hidden_one, axis=1)
    grad_scale_one = jnp.sum(grad_hidden_one * normed_one, axis=1)
    grad_in = grad_mid + norm_back(grad_hidden_one * (1.0 + modulate[:, 1]), normed_one, inv_one)
    grad_mod = jnp.stack(
        [
            grad_shift_one,
            grad_scale_one,
            grad_gate_one,
            grad_shift_two,
            grad_scale_two,
            grad_gate_two,
        ],
        axis=1,
    )
    grad_mod_w = jnp.einsum(
        "fd,fc->dc",
        cond_low,
        grad_mod.reshape(frames_dev, 6 * D).astype(bfloat),
        preferred_element_type=single,
    )
    grad_in_low = grad_in.reshape(tok_rows, D).astype(bfloat)
    grad_embed = jnp.einsum("rp,rd->pd", noisy_low, grad_in_low, preferred_element_type=single)
    grad_vec = jnp.concatenate(
        [jnp.sum(grad_mod, axis=0), jnp.sum(grad_in, axis=(0, 1))[None], grad_gain[None]], axis=0
    )
    grad_attn = jnp.stack([grad_wq, grad_wk, grad_wv, grad_outproj])
    grad_mlp = jnp.stack([grad_up, grad_down])
    grad_io = jnp.stack([grad_embed, grad_head])
    red_attn, red_mlp, red_mod, red_io, red_vec = (
        lax.psum_scatter(
            grad_attn.astype(jnp.bfloat16), "ctx", scatter_dimension=1, tiled=True
        ).astype(jnp.float32),
        lax.psum_scatter(
            grad_mlp.astype(jnp.bfloat16), "ctx", scatter_dimension=1, tiled=True
        ).astype(jnp.float32),
        lax.psum_scatter(
            grad_mod_w.astype(jnp.bfloat16), "ctx", scatter_dimension=0, tiled=True
        ).astype(jnp.float32),
        lax.psum_scatter(
            grad_io.astype(jnp.bfloat16), "ctx", scatter_dimension=2, tiled=True
        ).astype(jnp.float32),
        lax.psum_scatter(
            grad_vec.astype(jnp.bfloat16), "ctx", scatter_dimension=1, tiled=True
        ).astype(jnp.float32),
    )
    shared_sq = jnp.sum(red_mod * red_mod) + jnp.sum(red_io * red_io) + jnp.sum(red_vec * red_vec)
    own_sq = (
        jnp.sum(red_attn * red_attn)
        + jnp.sum(red_mlp * red_mlp)
        + jnp.where(tp_index == 0, shared_sq, 0.0)
    )
    grad_norm = jnp.sqrt(lax.psum(own_sq, ("ctx", "tp")))
    factor = jnp.minimum(1.0, clip_limit / (grad_norm + 1e-06))
    count = step[0].astype(single)
    attn_new = adam(w_attn, m_attn, v_attn, red_attn, factor, count, rate_matrix, decay_rate)
    mlp_new = adam(w_mlp, m_mlp, v_mlp, red_mlp, factor, count, rate_matrix, decay_rate)
    mod_new = adam(w_mod, m_mod, v_mod, red_mod, factor, count, rate_matrix, decay_rate)
    io_new = adam(w_io, m_io, v_io, red_io, factor, count, rate_matrix, decay_rate)
    vec_new = adam(vectors, m_vec, v_vec, red_vec, factor, count, rate_vector, 0.0)
    return (
        loss_value,
        grad_norm,
        attn_new[0],
        attn_new[1],
        attn_new[2],
        attn_new[3],
        mlp_new[0],
        mlp_new[1],
        mlp_new[2],
        mlp_new[3],
        mod_new[0],
        mod_new[1],
        mod_new[2],
        mod_new[3],
        io_new[0],
        io_new[1],
        io_new[2][0],
        io_new[2][1],
        io_new[3],
        vec_new[0],
        vec_new[1],
        vec_new[2],
        vec_new[3],
    )


def solution(mesh):
    placed = (
        P("ctx", None),
        P("ctx", None),
        P(),
        P(),
        P(),
        P(),
        P(None, "ctx", "tp"),
        P(None, "ctx", "tp"),
        P(None, "ctx", "tp"),
        P(None, "ctx", "tp"),
        P(None, "ctx", "tp"),
        P(None, "ctx", "tp"),
        P("ctx", None),
        P("ctx", None),
        P("ctx", None),
        P(None, None, "ctx"),
        P(None, None, "ctx"),
        P(None, None, "ctx"),
        P(None, "ctx"),
        P(None, "ctx"),
        P(None, "ctx"),
    )
    return jax.shard_map(
        shards,
        mesh=mesh,
        in_specs=placed,
        out_specs=(
            P(),
            P(),
            P(None, "ctx", "tp"),
            P(None, "ctx", "tp"),
            P(None, "ctx", "tp"),
            P(None, "ctx", "tp"),
            P(None, "ctx", "tp"),
            P(None, "ctx", "tp"),
            P(None, "ctx", "tp"),
            P(None, "ctx", "tp"),
            P("ctx", None),
            P("ctx", None),
            P("ctx", None),
            P("ctx", None),
            P(None, None, "ctx"),
            P(None, None, "ctx"),
            P(None, "ctx"),
            P(None, "ctx"),
            P(None, None, "ctx"),
            P(None, "ctx"),
            P(None, "ctx"),
            P(None, "ctx"),
            P(None, "ctx"),
        ),
        check_vma=False,
    )
```

profile of v0, /device:TPU:0, one launch (start us, length us, event | category | flops | bytes accessed | tf_op | source)
XLA Modules:
  0.0 2046.0 jit_solution(9829723480017865253)
XLA Ops:
  13.1 28.2 %all_gather.24 = bf16[8,1024]{1,0:T(8,128)(2,1)S(1)} all-gather(bf16[8,128]{1,0:T(8,128)(2,1)S(1)} %convert_element_type.325), channel_id=1, replica_groups=mesh['ctx'=8,'tp'=4] {'ctx'}, dimensions={1}, use_global_device_ids=true | all-gather | bytes 18432 | tf_op jit(solution)/shard_map/all_gather | solution.py:219
  41.4 32.1 %all_gather.23 = bf16[2,128,1024]{2,1,0:T(8,128)(2,1)S(1)} all-gather(bf16[2,128,128]{2,1,0:T(8,128)(2,1)S(1)} %convert_element_type.324), channel_id=1, replica_groups=mesh['ctx'=8,'tp'=4] {'ctx'}, dimensions={2}, use_global_device_ids=true | all-gather | bytes 589824 | tf_op jit(solution)/shard_map/all_gather | solution.py:218
  77.1 122.7 %all-gather.6.cloned.1.call-done = bf16[1024,6144]{1,0:T(8,128)(2,1)} async-done(((bf16[128,6144]{1,0:T(8,128)(2,1)}), bf16[1024,6144]{1,0:T(8,128)(2,1)}) %all-gather.6.cloned.1.call-update) | async-done | bytes 12582928 | tf_op jit(solution)/shard_map/all_gather | solution.py:217
  211.5 38.5 %all-gather.8.cloned.1.call-done = bf16[4,1024,256]{2,1,0:T(8,128)(2,1)} async-done(((bf16[4,128,256]{2,1,0:T(8,128)(2,1)}), bf16[4,1024,256]{2,1,0:T(8,128)(2,1)}) %all-gather.8.cloned.1.call-update) | async-done | bytes 2097168 | tf_op jit(solution)/shard_map/all_gather | solution.py:215
  265.5 59.9 %all-gather.12.cloned.1.call-done = bf16[8192,256]{1,0:T(8,128)(2,1)} async-done(((bf16[1024,256]{1,0:T(8,128)(2,1)}), bf16[8192,256]{1,0:T(8,128)(2,1)}) %all-gather.12.cloned.1.call-update) | async-done | bytes 4194320 | tf_op jit(solution)/shard_map/all_gather | solution.py:279
  331.8 67.9 %all-gather.10.cloned.1.call-done = bf16[8192,256]{0,1:T(8,128)(2,1)} async-done(((bf16[1024,256]{0,1:T(8,128)(2,1)}), bf16[8192,256]{0,1:T(8,128)(2,1)}) %all-gather.10.cloned.1.call-update) | async-done | bytes 4194320 | tf_op jit(solution)/shard_map/all_gather | solution.py:278
  399.9 144.5 %while.38 = (s32[]{:T(128)}, f32[2,4,512]{2,1,0:T(4,128)S(1)}, f32[2,4,512]{2,1,0:T(4,128)S(1)}, f32[2,512,4,64]{1,3,2,0:T(8,128)S(1)}, s32[16]{0:T(128)S(1)}, /...) while((s32[]{:T(128)}, f32[2,4,512]{2,1,0:T(4,128)S(1)}, ...), condition=%wide.region_18.19_spmd, body=%wide.region_5.18_spmd.sunk | while | flops 564940928 | bytes 36577892 | solution.py:310
  550.8 104.4 %all-reduce.6.cloned.1.call-done = bf16[1024,1024]{1,0:T(8,128)(2,1)} async-done(((bf16[1024,1024]{1,0:T(8,128)(2,1)}), bf16[1024,1024]{1,0:T(8,128)(2,1)}) %all-reduce.6.cloned.1.call-update) | async-done | bytes 2097168 | tf_op jit(solution)/shard_map/psum | solution.py:318
  661.7 69.9 %all-gather.14.cloned.1.call-done = bf16[2,1024,1024]{2,1,0:T(8,128)(2,1)} async-done(((bf16[2,128,1024]{2,1,0:T(8,128)(2,1)}), bf16[2,1024,1024]{2,1,0:T(8,128)(2,1)}) %all-gather.14.cloned.1.call-update) | async-done | bytes 4194320 | tf_op jit(solution)/shard_map/all_gather | solution.py:216
  731.5 13.5 fusion.92
  754.3 45.6 %all-reduce.8.cloned.1.call-done = bf16[1024,1024]{1,0:T(8,128)(2,1)} async-done(((bf16[1024,1024]{1,0:T(8,128)(2,1)}), bf16[1024,1024]{1,0:T(8,128)(2,1)}) %all-reduce.8.cloned.1.call-update) | async-done | bytes 2097168 | tf_op jit(solution)/shard_map/psum | solution.py:332
  812.4 22.0 %all-reduce = (f32[]{:T(128)}, f32[]{:T(128)}) all-reduce(f32[]{:T(128)} %multiply_reduce_fusion.10, f32[]{:T(128)S(6)} %mul_shard_map.3), channel_id=1, replica_groups=mesh['ctx'=8,'tp'=4] {'ctx'}, use_global_device_ids=true, to_apply=%region_27.28 | all-reduce | flops 2 | bytes 16 | tf_op jit(solution)/shard_map/psum | solution.py:345
  858.4 46.6 %all-reduce.10.cloned.1.call-done = bf16[1024,1024]{1,0:T(8,128)(2,1)} async-done(((bf16[1024,1024]{1,0:T(8,128)(2,1)}), bf16[1024,1024]{1,0:T(8,128)(2,1)}) %all-reduce.10.cloned.1.call-update) | async-done | bytes 2097168 | tf_op jit(solution)/shard_map/psum | solution.py:366
  925.9 210.3 %while.39 = (s32[]{:T(128)}, f32[2,512,4,64]{1,3,2,0:T(8,128)}, bf16[8192,256]{0,1:T(8,128)(2,1)}, bf16[8192,256]{0,1:T(8,128)(2,1)}, s32[16]{0:T(128)S(1)}, /*i...) while((s32[]{:T(128)}, f32[2,512,4,64]{1,3,2,0:T(8,128)}, ...), condition=%wide.region_45.46_spmd, body=%wide.region_36.45_spmd.sunk | while | flops 1364459520 | bytes 92922568 | solution.py:444
  1058.1 11.9 conditional.11
  1138.5 185.7 %reduce-scatter.12.cloned.1.call-done = bf16[1024,256]{0,1:T(8,128)(2,1)} async-done(((bf16[8192,256]{0,1:T(8,128)(2,1)}), bf16[1024,256]{0,1:T(8,128)(2,1)}) %reduce-scatter.12.cloned.1.call-update) | async-done | bytes 524304 | tf_op jit(solution)/shard_map/reduce_scatter | solution.py:448
  1332.5 83.4 %reduce-scatter.14.cloned.1.call-done = bf16[1024,256]{0,1:T(8,128)(2,1)} async-done(((bf16[8192,256]{0,1:T(8,128)(2,1)}), bf16[1024,256]{0,1:T(8,128)(2,1)}) %reduce-scatter.14.cloned.1.call-update) | async-done | bytes 524304 | tf_op jit(solution)/shard_map/reduce_scatter | solution.py:451
  1434.6 38.5 %all-reduce.12.cloned.1.call-done = bf16[1024,1024]{1,0:T(8,128)(2,1)} async-done(((bf16[1024,1024]{1,0:T(8,128)(2,1)}), bf16[1024,1024]{1,0:T(8,128)(2,1)}) %all-reduce.12.cloned.1.call-update) | async-done | bytes 2097168 | tf_op jit(solution)/shard_map/psum | solution.py:476
  1505.7 58.9 %reduce-scatter.18.cloned.1.call-done = bf16[2,128,1024]{2,1,0:T(8,128)(2,1)} async-done(((bf16[2,1024,1024]{2,1,0:T(8,128)(2,1)}), bf16[2,128,1024]{2,1,0:T(8,128)(2,1)}) %reduce-scatter.18.cloned.1.call-update) | async-done | bytes 524304 | tf_op jit(solution)/shard_map/reduce_scatter | solution.py:512
  1566.5 63.3 %reduce-scatter.24.cloned.1.call-done = bf16[128,8]{1,0:T(8,128)(2,1)} async-done(((bf16[1024,8]{1,0:T(8,128)(2,1)}), bf16[128,8]{1,0:T(8,128)(2,1)}) %reduce-scatter.24.cloned.1.call-update) | async-done | bytes 2064
  1631.2 63.7 %reduce-scatter.22.cloned.1.call-done = bf16[128,256]{1,0:T(8,128)(2,1)} async-done(((bf16[1024,256]{1,0:T(8,128)(2,1)}), bf16[128,256]{1,0:T(8,128)(2,1)}) %reduce-scatter.22.cloned.1.call-update) | async-done | bytes 65552
  1696.6 69.6 %reduce-scatter.16.cloned.1.call-done = bf16[4,128,256]{2,1,0:T(8,128)(2,1)} async-done(((bf16[4,1024,256]{2,1,0:T(8,128)(2,1)}), bf16[4,128,256]{2,1,0:T(8,128)(2,1)}) %reduce-scatter.16.cloned.1.call-update) | async-done | bytes 262160 | tf_op jit(solution)/shard_map/reduce_scatter | solution.py:509
  1769.2 206.7 %reduce-scatter.20.cloned.1.call-done = bf16[128,6144]{1,0:T(8,128)(2,1)} async-done(((bf16[1024,6144]{1,0:T(8,128)(2,1)}), bf16[128,6144]{1,0:T(8,128)(2,1)}) %reduce-scatter.20.cloned.1.call-update) | async-done | bytes 1572880 | tf_op jit(solution)/shard_map/reduce_scatter | solution.py:515
  1982.0 39.4 %psum.55 = f32[]{:T(128)} all-reduce(f32[]{:T(128)S(6)} %add.630), channel_id=1, replica_groups=mesh['ctx'=8,'tp'=4] {'ctx','tp'}, use_global_device_ids=true, to_apply=%region_70.71 | all-reduce | flops 1 | bytes 8 | tf_op jit(solution)/shard_map/psum | solution.py:531
  (1025 shorter events, 569.4 us)
Async XLA Ops:
  7.3 192.5 %all-gather.6.cloned.1.call-start = ((), (), s32[]{:S(2)}) async-start(), calls=%async_computation.7 | async-start | bytes 14155776 | tf_op jit(solution)/shard_map/all_gather | solution.py:217
  10.7 239.3 %all-gather.8.cloned.1.call-start = ((), (), s32[]{:S(2)}) async-start(), calls=%async_computation.8 | async-start | bytes 2359296 | tf_op jit(solution)/shard_map/all_gather | solution.py:215
  11.5 314.0 %all-gather.12.cloned.1.call-start = ((), (), s32[]{:S(2)}) async-start(), calls=%async_computation.10 | async-start | bytes 4718592 | tf_op jit(solution)/shard_map/all_gather | solution.py:279
  253.3 146.4 %all-gather.10.cloned.1.call-start = ((), (), s32[]{:S(2)}) async-start(), calls=%async_computation.9 | async-start | bytes 4718592 | tf_op jit(solution)/shard_map/all_gather | solution.py:278
  263.3 391.9 %all-reduce.6.cloned.1.call-start = ((), (), s32[]{:S(2)}) async-start(), calls=%async_computation.11 | async-start | bytes 4194304 | tf_op jit(solution)/shard_map/psum | solution.py:318
  549.5 182.0 %all-gather.14.cloned.1.call-start = ((), (), s32[]{:S(2)}) async-start(), calls=%async_computation.12 | async-start | bytes 4718592 | tf_op jit(solution)/shard_map/all_gather | solution.py:216
  550.5 249.5 %all-reduce.8.cloned.1.call-start = ((), (), s32[]{:S(2)}) async-start(), calls=%async_computation.13 | async-start | bytes 4194304 | tf_op jit(solution)/shard_map/psum | solution.py:332
  750.2 154.8 %all-reduce.10.cloned.1.call-start = ((), (), s32[]{:S(2)}) async-start(), calls=%async_computation.14 | async-start | bytes 4194304 | tf_op jit(solution)/shard_map/psum | solution.py:366
  857.0 467.1 %reduce-scatter.12.cloned.1.call-start = ((), (), s32[]{:S(2)}) async-start(), calls=%async_computation.15 | async-start | bytes 4718592 | tf_op jit(solution)/shard_map/reduce_scatter | solution.py:448
  1136.2 279.7 %reduce-scatter.14.cloned.1.call-start = ((), (), s32[]{:S(2)}) async-start(), calls=%async_computation.16 | async-start | bytes 4718592 | tf_op jit(solution)/shard_map/reduce_scatter | solution.py:451
  1136.8 336.2 %all-reduce.12.cloned.1.call-start = ((), (), s32[]{:S(2)}) async-start(), calls=%async_computation.19 | async-start | bytes 4194304 | tf_op jit(solution)/shard_map/psum | solution.py:476
  1421.7 142.8 %reduce-scatter.18.cloned.1.call-start = ((), (), s32[]{:S(2)}) async-start(), calls=%async_computation.18 | async-start | bytes 4718592 | tf_op jit(solution)/shard_map/reduce_scatter | solution.py:512
  1431.4 198.4 %reduce-scatter.24.cloned.1.call-start = ((), (), s32[]{:S(2)}) async-start(), calls=%async_computation.22 | async-start | bytes 294912
  1487.6 207.3 %reduce-scatter.22.cloned.1.call-start = ((), (), s32[]{:S(2)}) async-start(), calls=%async_computation.21 | async-start | bytes 589824
  1491.7 274.5 %reduce-scatter.16.cloned.1.call-start = ((), (), s32[]{:S(2)}) async-start(), calls=%async_computation.17 | async-start | bytes 2359296 | tf_op jit(solution)/shard_map/reduce_scatter | solution.py:509
  1498.0 477.9 %reduce-scatter.20.cloned.1.call-start = ((), (), s32[]{:S(2)}) async-start(), calls=%async_computation.20 | async-start | bytes 14155776 | tf_op jit(solution)/shard_map/reduce_scatter | solution.py:515
  1504.7 517.4 %copy-start.54 = (f32[2,128,128]{2,1,0:T(8,128)S(1)}, f32[2,128,128]{2,1,0:T(8,128)}, u32[]{:S(2)}) copy-start(f32[2,128,128]{2,1,0:T(8,128)} %param.48) | copy-start | bytes 393220
  1504.7 517.4 %copy-start.57 = (f32[2,128,128]{2,1,0:T(8,128)S(1)}, f32[2,128,128]{2,1,0:T(8,128)}, u32[]{:S(2)}) copy-start(f32[2,128,128]{2,1,0:T(8,128)} %param.50) | copy-start | bytes 393220
  1504.7 519.8 %copy-start.74 = (f32[8,128]{1,0:T(8,128)S(1)}, f32[8,128]{1,0:T(8,128)}, u32[]{:S(2)}) copy-start(f32[8,128]{1,0:T(8,128)} %param.51) | copy-start | bytes 12292
  1504.7 519.8 %copy-start.75 = (f32[8,128]{1,0:T(8,128)S(1)}, f32[8,128]{1,0:T(8,128)}, u32[]{:S(2)}) copy-start(f32[8,128]{1,0:T(8,128)} %param.53) | copy-start | bytes 12292
  1504.7 519.8 %copy-start.76 = (f32[8,128]{1,0:T(8,128)S(1)}, f32[8,128]{1,0:T(8,128)}, u32[]{:S(2)}) copy-start(f32[8,128]{1,0:T(8,128)} %param.52) | copy-start | bytes 12292
  1504.7 520.4 %copy-start.37 = (f32[4,128,256]{2,1,0:T(8,128)S(1)}, f32[4,128,256]{2,1,0:T(8,128)}, u32[]{:S(2)}) copy-start(f32[4,128,256]{2,1,0:T(8,128)} %param.39) | copy-start | bytes 1572868
  1504.8 523.3 %copy-start.23 = (f32[2,128,1024]{2,1,0:T(8,128)S(1)}, f32[2,128,1024]{2,1,0:T(8,128)}, u32[]{:S(2)}) copy-start(f32[2,128,1024]{2,1,0:T(8,128)} %param.42) | copy-start | bytes 3145732
  1504.8 523.3 %copy-start.44 = (f32[2,128,1024]{2,1,0:T(8,128)S(1)}, f32[2,128,1024]{2,1,0:T(8,128)}, u32[]{:S(2)}) copy-start(f32[2,128,1024]{2,1,0:T(8,128)} %param.44) | copy-start | bytes 3145732
  (89 other events, 2463.1 us)
Sparse Core Ops, SparseCore 0:
  10.9 188.8 all-gather.5
  202.5 47.4 all-gather.7
  253.5 71.9 all-gather.11
  328.0 71.6 all-gather.9
  549.7 105.5 all-reduce.5
  658.1 73.4 all-gather.13
  750.3 49.6 all-reduce.7
  857.2 47.7 all-reduce.9
  1136.3 187.7 reduce-scatter.11
  1327.7 88.2 reduce-scatter.13
  1421.9 51.1 all-reduce.11
  1476.5 87.9 reduce-scatter.17
  1568.8 60.9 reduce-scatter.23
  1633.9 60.9 reduce-scatter.21
  1698.9 67.2 reduce-scatter.15
  1769.6 206.1 reduce-scatter.19
where the time goes:
time: 2080 us; the launch traced here: 2050 us
  waiting for transfers between devices  1330 us (64%)
  other arithmetic  187 us (9%)
  local copies, waits for them, and re-layouts  178 us (9%)
  matrix products  140 us (7%)
  blocking collectives  122 us (6%)
  loops' own time  65.7 us (3%)
  between operations  26.1 us (1%)
    reduce_scatter x1, waiting for transfers between devices, shards(): lax.psum_scatter(grad_mod_w.astype(jnp.bfloat16), 'ctx', scatter_dimensio...  207 us
    reduce_scatter x1, waiting for transfers between devices, shards(): lax.psum_scatter(grad_keys_all.astype(jnp.bfloat16), 'ctx', scatter_dimen...  186 us
    unnamed x18, waiting for transfers between devices  128 us
    all_gather x1, waiting for transfers between devices, shards(): lax.all_gather(w_mod.astype(bfloat), 'ctx', axis=0, tiled=True)  123 us
    psum x1, waiting for transfers between devices, shards(): lax.psum(jnp.einsum('rh,dh->rd', mix_low, attn_w[3], preferred_element_ty...  104 us
    reduce_scatter x1, waiting for transfers between devices, shards(): lax.psum_scatter(grad_values_all.astype(jnp.bfloat16), 'ctx', scatter_dim...  83.4 us
    all_gather x1, waiting for transfers between devices, shards(): lax.all_gather(w_mlp.astype(bfloat), 'ctx', axis=1, tiled=True)  69.9 us
    reduce_scatter x1, waiting for transfers between devices, shards(): lax.psum_scatter(grad_attn.astype(jnp.bfloat16), 'ctx', scatter_dimension...  69.6 us
  transfers between devices with their start and end apart: 16, of which 16 were waited for; matrix products, arithmetic and copies ran while one was open for 5% of the time, Pallas kernels for 0%

commit v1 on v0

--- a/solution.py
+++ b/solution.py
@@ -3,6 +3,8 @@
 import jax
 import jax.numpy as jnp
 from jax import lax
+from jax.experimental import pallas as pl
+from jax.experimental.pallas import tpu as pltpu
 from jax.sharding import PartitionSpec as P
 
 D = 1024
@@ -563,7 +565,700 @@
     )
 
 
+RING = (0, 1, 3, 5, 7, 6, 4, 2)
+RING_NEXT = tuple((RING[i], RING[(i + 1) % 8]) for i in range(8))
+RING_PREV = tuple((b, a) for a, b in RING_NEXT)
+HALF_SLOTS = 16
+QKV_ROWS = 768
+FRONT_ROWS = 912
+NT = (((1,), (1,)), ((), ()))
+TN = (((0,), (0,)), ((), ()))
+
+
+def swap(values, axis, bit):
+    size = 8 if axis == "ctx" else 4
+    return lax.ppermute(values, axis, [(i, i ^ bit) for i in range(size)])
+
+
+def ring_position(index):
+    z, x = index // 2, index % 2
+    return jnp.where(x == 1, z + 1, (8 - z) % 8)
+
+
+def ring_member(position):
+    position = position % 8
+    return jnp.where(
+        position == 0, 0, jnp.where(position <= 4, 2 * position - 1, 2 * (8 - position))
+    )
+
+
+def ring_gather(shard):
+    half = shard.shape[0] // 2
+    ahead = [shard]
+    behind = [shard]
+    for _ in range(3):
+        ahead.append(lax.ppermute(ahead[-1], "ctx", RING_NEXT))
+        behind.append(lax.ppermute(behind[-1], "ctx", RING_PREV))
+    first = lax.ppermute(ahead[-1][:half], "ctx", RING_NEXT)
+    second = lax.ppermute(behind[-1][half:], "ctx", RING_PREV)
+    return ahead + behind[1:] + [jnp.concatenate([first, second], axis=0)]
+
+
+def ring_offsets(ctx_index):
+    position = ring_position(ctx_index)
+    return [ring_member(position + 8 + offset) for offset in (0, -1, -2, -3, 1, 2, 3, 4)]
+
+
+def reduce_blocks(blocks, ctx_index, wire):
+    x = ctx_index % 2
+    z = ctx_index // 2
+    pairs = blocks.reshape((4, 2) + blocks.shape[1:])
+    first, second = pairs[:, 0], pairs[:, 1]
+    even = x == 0
+    away = jnp.where(even, second, first).astype(wire)
+    held = jnp.where(even, first, second) + swap(away, "ctx", 1).astype(jnp.float32)
+    total = lax.dynamic_index_in_dim(held, z, 0, keepdims=False)
+    low = held.astype(wire)
+    for bit in (1, 2, 3):
+        piece = lax.dynamic_index_in_dim(low, z ^ bit, 0, keepdims=False)
+        total = total + swap(piece, "ctx", 2 * bit).astype(jnp.float32)
+    return total
+
+
+def spread_frames(own):
+    core = swap(own, "tp", 1)
+    across = swap(own, "tp", 2)
+    return [own, core, across, swap(across, "tp", 1)]
+
+
+def sum_frames(parts):
+    low = jnp.stack([parts[1], parts[3]]).astype(jnp.bfloat16)
+    came = swap(low, "tp", 1)
+    across = (parts[2] + came[1].astype(jnp.float32)).astype(jnp.bfloat16)
+    return parts[0] + came[0].astype(jnp.float32) + swap(across, "tp", 2).astype(jnp.float32)
+
+
+def reorder_four(items, index):
+    low_bit = (index & 1) == 1
+    high_bit = (index & 2) == 2
+    once = [jnp.where(low_bit, items[k ^ 1], items[k]) for k in range(4)]
+    return [jnp.where(high_bit, once[k ^ 2], once[k]) for k in range(4)]
+
+
+def sum_all(values):
+    for axis, bit in (("tp", 1), ("tp", 2), ("ctx", 1), ("ctx", 2), ("ctx", 4)):
+        values = values + swap(values, axis, bit)
+    return values
+
+
+def front_kernel(meta, *refs):
+    shards_in = refs[:8]
+    noisy, shift_scale, cosine, sine, weights, hidden, resid, heads, work = refs[8:]
+    for place in range(8):
+        weights[:, pl.ds(pl.multiple_of(meta[place] * 128, 128), 128)] = shards_in[place][...]
+    embed = weights[QKV_ROWS : QKV_ROWS + 128, :]
+    vec_rows = weights[QKV_ROWS + 128 : FRONT_ROWS, :].astype(jnp.float32)
+    for frame in range(4):
+        values = jnp.dot(noisy[frame], embed, preferred_element_type=jnp.float32) + vec_rows[6:7]
+        if frame == 0:
+            resid[...] = values
+        centred = values - jnp.mean(values, axis=-1, keepdims=True)
+        normed = centred * lax.rsqrt(jnp.mean(centred * centred, axis=-1, keepdims=True) + ln_eps)
+        shift = shift_scale[frame, 0:1, :] + vec_rows[0:1]
+        scale = shift_scale[frame, 1:2, :] + vec_rows[1:2]
+        low = (normed * (1.0 + scale) + shift).astype(jnp.bfloat16)
+        hidden[frame] = low
+        mixed = lax.dot_general(
+            weights[0:QKV_ROWS, :], low, NT, preferred_element_type=jnp.float32
+        )
+        cos_now = cosine[meta[8 + frame]]
+        sin_now = sine[meta[8 + frame]]
+        for head in range(4):
+            base = 192 * head
+            where_to = meta[12 + head]
+            cols = slice(256 * frame, 256 * frame + 256)
+            for part in range(2):
+                upper = mixed[base + 64 * part : base + 64 * part + 32]
+                lower = mixed[base + 64 * part + 32 : base + 64 * part + 64]
+                heads[where_to, 64 * part : 64 * part + 32, cols] = (
+                    upper * cos_now - lower * sin_now
+                ).astype(jnp.bfloat16)
+                heads[where_to, 64 * part + 32 : 64 * part + 64, cols] = (
+                    lower * cos_now + upper * sin_now
+                ).astype(jnp.bfloat16)
+            heads[where_to, 128:192, cols] = mixed[base + 128 : base + 192].astype(jnp.bfloat16)
+
+
+def call_front(meta, shard_list, noisy, shift_scale, cosine, sine):
+    vmem = pl.BlockSpec(memory_space=pltpu.VMEM)
+    return pl.pallas_call(
+        front_kernel,
+        out_shape=(
+            jax.ShapeDtypeStruct((FRONT_ROWS, D), jnp.bfloat16),
+            jax.ShapeDtypeStruct((4, PATCHES, D), jnp.bfloat16),
+            jax.ShapeDtypeStruct((PATCHES, D), jnp.float32),
+            jax.ShapeDtypeStruct((4, 192, 4 * PATCHES), jnp.bfloat16),
+        ),
+        in_specs=[pl.BlockSpec(memory_space=pltpu.SMEM)] + [vmem] * 12,
+        out_specs=(vmem,) * 4,
+        scratch_shapes=[pltpu.VMEM((8, 128), jnp.float32)],
+        compiler_params=pltpu.CompilerParams(vmem_limit_bytes=40 * 2**20),
+        cost_estimate=pl.CostEstimate(flops=2 * 10**9, bytes_accessed=10**7, transcendentals=0),
+        name="front",
+    )(meta, *shard_list, noisy, shift_scale, cosine, sine)
+
+
+def turn(block):
+    return block.astype(jnp.float32).T.astype(jnp.bfloat16)
+
+
+def query_rows(meta, pair):
+    first = 2 * pair
+    start_first = first - meta[2 + first]
+    start_second = first + 1 - meta[3 + first]
+    left = lax.broadcasted_iota(jnp.int32, (1, 2 * PATCHES), 1) < PATCHES
+    upto = jnp.where(left, first, first + 1)
+    since = jnp.where(left, start_first, start_second)
+    return jnp.minimum(start_first, start_second), since, upto
+
+
+def attend_kernel(meta, *refs):
+    blocks = refs[:4]
+    outs = refs[4:8]
+    lse, mixed, query, key, value = refs[8:]
+    for member in range(4):
+        for frame in range(4):
+            slot = 4 * (meta[0] ^ member) + (meta[1] ^ frame)
+            cols = slice(256 * frame, 256 * frame + 256)
+            lanes = pl.ds(pl.multiple_of((slot % 2) * 256, 256), 256)
+            query[slot // 2, :, lanes] = blocks[member][0:64, cols] * 0.125
+            key[slot] = turn(blocks[member][64:128, cols])
+            value[slot] = blocks[member][128:192, cols]
+
+    def per_pair(pair, carry):
+        low, since, upto = query_rows(meta, pair)
+        wanted = query[pair]
+
+        def per_key(slot, state):
+            top, total, acc = state
+            bias = jnp.where((slot >= since) & (slot <= upto), 0.0, neg_large)
+            scores = jnp.dot(key[slot], wanted, preferred_element_type=jnp.float32) + bias
+            new_top = jnp.maximum(top, jnp.max(scores, axis=0, keepdims=True))
+            probs = jnp.exp(scores - new_top)
+            shrink = jnp.exp(top - new_top)
+            total = total * shrink + jnp.sum(probs, axis=0, keepdims=True)
+            acc = acc * shrink + jnp.dot(
+                value[slot], probs.astype(jnp.bfloat16), preferred_element_type=jnp.float32
+            )
+            return (new_top, total, acc)
+
+        top, total, acc = lax.fori_loop(
+            low,
+            2 * pair + 2,
+            per_key,
+            (
+                jnp.full((1, 2 * PATCHES), neg_large, jnp.float32),
+                jnp.zeros((1, 2 * PATCHES), jnp.float32),
+                jnp.zeros((HD, 2 * PATCHES), jnp.float32),
+            ),
+        )
+        lse[pair] = top + jnp.log(total)
+        mixed[pair] = acc / total
+        return carry
+
+    lax.fori_loop(0, 8, per_pair, 0)
+    for member in range(4):
+        for frame in range(4):
+            slot = 4 * (meta[0] ^ member) + (meta[1] ^ frame)
+            lanes = pl.ds(pl.multiple_of((slot % 2) * 256, 256), 256)
+            outs[member][:, 256 * frame : 256 * frame + 256] = mixed[slot // 2, :, lanes].astype(
+                jnp.bfloat16
+            )
+
+
+def call_attend(meta, blocks):
+    vmem = pl.BlockSpec(memory_space=pltpu.VMEM)
+    result = pl.pallas_call(
+        attend_kernel,
+        out_shape=tuple(jax.ShapeDtypeStruct((HD, 4 * PATCHES), jnp.bfloat16) for _ in range(4))
+        + (
+            jax.ShapeDtypeStruct((8, 1, 2 * PATCHES), jnp.float32),
+            jax.ShapeDtypeStruct((8, HD, 2 * PATCHES), jnp.float32),
+        ),
+        in_specs=[pl.BlockSpec(memory_space=pltpu.SMEM)] + [vmem] * 4,
+        out_specs=(vmem,) * 6,
+        scratch_shapes=[
+            pltpu.VMEM((8, HD, 2 * PATCHES), jnp.bfloat16),
+            pltpu.VMEM((16, PATCHES, HD), jnp.bfloat16),
+            pltpu.VMEM((16, HD, PATCHES), jnp.bfloat16),
+        ],
+        compiler_params=pltpu.CompilerParams(vmem_limit_bytes=40 * 2**20),
+        cost_estimate=pl.CostEstimate(flops=9 * 10**9, bytes_accessed=5 * 10**6, transcendentals=10**7),
+        name="attend",
+    )(meta, *blocks)
+    return list(result[:4]), result[4], result[5]
+
+
+def attend_back_kernel(meta, *refs):
+    blocks = refs[:4]
+    grads = refs[4:8]
+    lse, mixed, cosine, sine = refs[8:12]
+    outs = refs[12:16]
+    query, query_flat, key, key_flat, value_flat, grad, grad_flat, sum_key, sum_value, sum_query = (
+        refs[16:]
+    )
+    for member in range(4):
+        for frame in range(4):
+            slot = 4 * (meta[0] ^ member) + (meta[1] ^ frame)
+            cols = slice(256 * frame, 256 * frame + 256)
+            place = pl.ds(pl.multiple_of((slot % 2) * 256, 256), 256)
+            part = blocks[member][0:64, cols] * 0.125
+            query[slot // 2, :, place] = part
+            query_flat[slot // 2, place, :] = turn(part)
+            part = blocks[member][64:128, cols]
+            key[slot] = part
+            key_flat[slot] = turn(part)
+            value_flat[slot] = turn(blocks[member][128:192, cols])
+            part = grads[member][:, cols]
+            grad[slot // 2, :, place] = part
+            grad_flat[slot // 2, place, :] = turn(part)
+    sum_key[...] = jnp.zeros_like(sum_key)
+    sum_value[...] = jnp.zeros_like(sum_value)
+
+    def per_pair(pair, carry):
+        low, since, upto = query_rows(meta, pair)
+        wanted = query[pair]
+        wanted_grad = grad[pair]
+        delta = jnp.sum(wanted_grad.astype(jnp.float32) * mixed[pair], axis=0, keepdims=True)
+        level = lse[pair]
+
+        def per_key(slot, acc):
+            bias = jnp.where((slot >= since) & (slot <= upto), -level, neg_large)
+            scores = jnp.dot(key_flat[slot], wanted, preferred_element_type=jnp.float32)
+            probs = jnp.exp(scores + bias)
+            grad_probs = jnp.dot(
+                value_flat[slot], wanted_grad, preferred_element_type=jnp.float32
+            )
+            grad_scores = (probs * (grad_probs - delta)).astype(jnp.bfloat16)
+            sum_value[slot] += jnp.dot(
+                probs.astype(jnp.bfloat16), grad_flat[pair], preferred_element_type=jnp.float32
+            )
+            sum_key[slot] += jnp.dot(
+                grad_scores, query_flat[pair], preferred_element_type=jnp.float32
+            )
+            return acc + jnp.dot(key[slot], grad_scores, preferred_element_type=jnp.float32)
+
+        sum_query[pair] = lax.fori_loop(
+            low, 2 * pair + 2, per_key, jnp.zeros((HD, 2 * PATCHES), jnp.float32)
+        )
+        return carry
+
+    lax.fori_loop(0, 8, per_pair, 0)
+    for member in range(4):
+        for frame in range(4):
+            slot = 4 * (meta[0] ^ member) + (meta[1] ^ frame)
+            cols = slice(256 * frame, 256 * frame + 256)
+            place = pl.ds(pl.multiple_of((slot % 2) * 256, 256), 256)
+            cos_now = cosine[slot]
+            sin_now = sine[slot]
+            for base, part in (
+                (0, sum_query[slot // 2, :, place] * 0.125),
+                (64, sum_key[slot].T),
+            ):
+                upper = part[0:32]
+                lower = part[32:64]
+                outs[member][base : base + 32, cols] = (
+                    upper * cos_now + lower * sin_now
+                ).astype(jnp.bfloat16)
+                outs[member][base + 32 : base + 64, cols] = (
+                    lower * cos_now - upper * sin_now
+                ).astype(jnp.bfloat16)
+            outs[member][128:192, cols] = sum_value[slot].T.astype(jnp.bfloat16)
+
+
+def call_attend_back(meta, blocks, grads, lse, mixed, cosine, sine):
+    vmem = pl.BlockSpec(memory_space=pltpu.VMEM)
+    flat_pair = pltpu.VMEM((8, 2 * PATCHES, HD), jnp.bfloat16)
+    turned_pair = pltpu.VMEM((8, HD, 2 * PATCHES), jnp.bfloat16)
+    flat = pltpu.VMEM((16, PATCHES, HD), jnp.bfloat16)
+    wide = pltpu.VMEM((16, PATCHES, HD), jnp.float32)
+    return list(
+        pl.pallas_call(
+            attend_back_kernel,
+            out_shape=tuple(
+                jax.ShapeDtypeStruct((192, 4 * PATCHES), jnp.bfloat16) for _ in range(4)
+            ),
+            in_specs=[pl.BlockSpec(memory_space=pltpu.SMEM)] + [vmem] * 12,
+            out_specs=(vmem,) * 4,
+            scratch_shapes=[
+                turned_pair,
+                flat_pair,
+                pltpu.VMEM((16, HD, PATCHES), jnp.bfloat16),
+                flat,
+                flat,
+                turned_pair,
+                flat_pair,
+                wide,
+                wide,
+                pltpu.VMEM((8, HD, 2 * PATCHES), jnp.float32),
+            ],
+            compiler_params=pltpu.CompilerParams(vmem_limit_bytes=48 * 2**20),
+            cost_estimate=pl.CostEstimate(
+                flops=22 * 10**9, bytes_accessed=10**7, transcendentals=10**7
+            ),
+            name="attend_back",
+        )(meta, *blocks, *grads, lse, mixed, cosine, sine)
+    )
+
+
+def assemble_kernel(meta, *refs):
+    for place in range(8):
+        refs[8][:, pl.ds(pl.multiple_of(meta[place] * 128, 128), 128)] = refs[place][...]
+
+
+def assemble(meta, shard_list):
+    vmem = pl.BlockSpec(memory_space=pltpu.VMEM)
+    rows = shard_list[0].shape[0]
+    return pl.pallas_call(
+        assemble_kernel,
+        out_shape=jax.ShapeDtypeStruct((rows, 8 * 128), shard_list[0].dtype),
+        in_specs=[pl.BlockSpec(memory_space=pltpu.SMEM)] + [vmem] * 8,
+        out_specs=vmem,
+        name="assemble",
+    )(meta, *shard_list)
+
+
+def place_frames(lengths, order, levels):
+    frames = levels.shape[0]
+    ids = jnp.arange(frames, dtype=jnp.int32)
+    ends = jnp.cumsum(lengths)
+    begins = ends - lengths
+    inside = (ids[:, None] >= begins[None, :]) & (ids[:, None] < ends[None, :])
+    start = jnp.sum(jnp.where(inside, begins[None, :], 0), axis=1)
+    is_long = jnp.sum(jnp.where(inside, lengths[None, :], 0), axis=1) == frames // 2
+    before = ids[None, :] < ids[:, None]
+    same = is_long[None, :] == is_long[:, None]
+    slot = jnp.sum((before & same).astype(jnp.int32), axis=1) + jnp.where(is_long, 0, frames // 2)
+    stretches = order.shape[0]
+    per_stretch = frames // stretches
+    held = order[None, :] == (ids // per_stretch)[:, None]
+    stored = (
+        jnp.sum(jnp.where(held, jnp.arange(stretches, dtype=jnp.int32)[None, :], 0), axis=1)
+        * per_stretch
+        + ids % per_stretch
+    )
+    table = jnp.stack([stored, ids - start, levels])
+    hit = slot[None, :] == ids[:, None]
+    return jnp.sum(jnp.where(hit[None], table[:, None, :], 0), axis=2)
+
+
+def shards_halves(
+    clean,
+    noise,
+    levels,
+    lengths,
+    order,
+    step,
+    w_attn,
+    m_attn,
+    v_attn,
+    w_mlp,
+    m_mlp,
+    v_mlp,
+    w_mod,
+    m_mod,
+    v_mod,
+    w_io,
+    m_io,
+    v_io,
+    vectors,
+    m_vec,
+    v_vec,
+):
+    bfloat = jnp.bfloat16
+    single = jnp.float32
+    ctx_index = lax.axis_index("ctx")
+    tp_index = lax.axis_index("tp")
+    member = ctx_index % 4
+    feat_dim = clean.shape[1]
+    offsets = ring_offsets(ctx_index)
+    relative = [tp_index ^ k for k in range(4)]
+
+    both = jnp.stack([clean.reshape(4, 4, 64, feat_dim), noise.reshape(4, 4, 64, feat_dim)], axis=1)
+    quarter = lax.dynamic_index_in_dim(both, tp_index, 2, keepdims=False)
+    token_ring = ring_gather(quarter.reshape(4 * 128, feat_dim))
+    front_shard = jnp.concatenate(
+        [
+            jnp.transpose(w_attn[:3].reshape(3, 128, 4, HD), (2, 0, 3, 1)).reshape(QKV_ROWS, 128),
+            w_io[0],
+            vectors,
+            jnp.zeros((8, 128), single),
+        ],
+        axis=0,
+    ).astype(bfloat)
+    front_ring = ring_gather(front_shard)
+
+    table = place_frames(lengths, order, levels)
+    stored, position, slot_levels = table[0], table[1], table[2]
+    half_base = (ctx_index // 4) * HALF_SLOTS
+    half_position = lax.dynamic_slice_in_dim(position, half_base, HALF_SLOTS, 0)
+    own_levels = lax.dynamic_slice_in_dim(slot_levels, 4 * ctx_index, 4, 0)
+    own_levels = jnp.stack(
+        [lax.dynamic_index_in_dim(own_levels, r, 0, keepdims=False) for r in relative]
+    )
+    own_stored = lax.dynamic_slice_in_dim(stored, 4 * ctx_index, 4, 0)
+    gathered = jnp.stack(token_ring).reshape(8 * 4, 128, feat_dim)
+    my_place = ring_position(ctx_index)
+    picked = []
+    for frame in relative:
+        at = lax.dynamic_index_in_dim(own_stored, frame, 0, keepdims=False)
+        distance = (ring_position(at // 4) - my_place) % 8
+        index = jnp.where(distance <= 4, distance + 3, 8 - distance)
+        index = jnp.where(distance == 0, 0, index)
+        picked.append(
+            lax.dynamic_index_in_dim(gathered, index * 4 + at % 4, 0, keepdims=False)
+        )
+    quarters = spread_frames(jnp.stack(picked))
+    by_source = [
+        jnp.stack([quarters[b][k ^ b] for k in range(4)]).reshape(4, 2, 64, feat_dim)
+        for b in range(4)
+    ]
+    pieces = reorder_four(by_source, tp_index)
+    tokens = jnp.concatenate(pieces, axis=2)
+
+    rows_of = jnp.concatenate(
+        [
+            slot_levels,
+            jnp.stack(
+                [
+                    lax.dynamic_index_in_dim(
+                        slot_levels, 4 * (ctx_index ^ a) + (tp_index ^ b), 0, keepdims=False
+                    )
+                    for a in range(8)
+                    for b in range(4)
+                ]
+            ),
+        ]
+    )
+    half_dim = D // 2
+    column = ctx_index * 128 + jnp.arange(128, dtype=jnp.int32)
+    frequency = jnp.exp(
+        -math.log(10000.0) * (column % half_dim).astype(single) / half_dim
+    )
+    angle = rows_of.astype(single)[:, None] * frequency[None, :]
+    cond = jax.nn.silu(jnp.where(column[None, :] < half_dim, jnp.cos(angle), jnp.sin(angle)))
+    cond_low = cond.astype(bfloat)
+    cond_slots, cond_relative = cond_low[:32], cond_low[32:]
+    quarter_cols = 6 * D // 4
+    mod_cols = lax.dynamic_slice_in_dim(w_mod, tp_index * quarter_cols, quarter_cols, 1)
+    mod_part = jnp.dot(cond_slots, mod_cols.astype(bfloat), preferred_element_type=single)
+    mod_own = reduce_blocks(mod_part.reshape(8, 4, quarter_cols), ctx_index, single)
+    mod_quarters = reorder_four(spread_frames(mod_own), tp_index)
+    mod_all = jnp.concatenate(mod_quarters, axis=1)
+    mod_rel = jnp.stack(reorder_four([mod_all[k] for k in range(4)], tp_index))
+    mod_rel = mod_rel.reshape(4, 6, D)
+
+    time_pairs = HD // 8
+    side_pairs = (HD // 2 - time_pairs) // 2
+
+    def frequencies(count):
+        return 10000.0 ** (-jnp.arange(count, dtype=single) / count)
+
+    patch = jnp.arange(PATCHES, dtype=jnp.int32)
+    time_angle = half_position.astype(single)[:, None] * frequencies(time_pairs)[None, :]
+    height_angle = frequencies(side_pairs)[:, None] * (patch // GRID).astype(single)[None, :]
+    width_angle = frequencies(side_pairs)[:, None] * (patch % GRID).astype(single)[None, :]
+    side_angle = jnp.concatenate([height_angle, width_angle], axis=0)
+
+    def full_table(time_part, side_part):
+        return jnp.concatenate(
+            [
+                jnp.broadcast_to(time_part[:, :, None], (HALF_SLOTS, time_pairs, PATCHES)),
+                jnp.broadcast_to(side_part[None], (HALF_SLOTS, 2 * side_pairs, PATCHES)),
+            ],
+            axis=1,
+        )
+
+    cosine = full_table(jnp.cos(time_angle), jnp.cos(side_angle))
+    sine = full_table(jnp.sin(time_angle), jnp.sin(side_angle))
+
+    signal_scale, noise_scale, weight = plan(own_levels)
+    clean_full = tokens[:, 0].astype(single)
+    noise_full = tokens[:, 1].astype(single)
+    noisy_low = (
+        signal_scale[:, None, None] * clean_full + noise_scale[:, None, None] * noise_full
+    ).astype(bfloat)
+    target = signal_scale[0] * noise_full[0] - noise_scale[0] * clean_full[0]
+    all_weight = plan(levels)[2]
+    weight_sum = PATCHES * jnp.sum(all_weight)
+
+    front_meta = jnp.stack(
+        offsets + [4 * member + r for r in relative] + [member ^ k for k in range(4)]
+    ).astype(jnp.int32)
+    front_all, hidden_frames, resid_in, head_blocks = call_front(
+        front_meta, front_ring, noisy_low, mod_rel[:, :2], cosine, sine
+    )
+    hidden_one = hidden_frames.reshape(4 * PATCHES, D)
+    qkv_w = front_all[:QKV_ROWS]
+    vec_w = front_all[QKV_ROWS + 128 : QKV_ROWS + 136].astype(single)
+    mod_own_frame = mod_rel[0] + vec_w[:6]
+    shift_one, scale_one, gate_one, shift_two, scale_two, gate_two = (
+        mod_own_frame[k : k + 1] for k in range(6)
+    )
+
+    mid_shard = jnp.concatenate([jnp.transpose(w_attn[3]), w_io[1]], axis=0).astype(bfloat)
+    mid_shard, front_all = lax.optimization_barrier((mid_shard, front_all))
+    mid_all = assemble(jnp.stack(offsets).astype(jnp.int32), ring_gather(mid_shard))
+    out_w, head_w = mid_all[:256], mid_all[256:]
+    mlp_w = lax.all_gather(w_mlp.astype(bfloat), "ctx", axis=1, tiled=True)
+    up_w, down_w = mlp_w[0], mlp_w[1]
+
+    def exchange(blocks):
+        return [blocks[0]] + [swap(blocks[k], "ctx", k) for k in (1, 2, 3)]
+
+    attend_meta = jnp.concatenate([jnp.stack([member, tp_index]), half_position]).astype(jnp.int32)
+    head_in = exchange([head_blocks[k] for k in range(4)])
+    mixed_blocks, lse, mixed = call_attend(attend_meta, head_in)
+    mix_low = jnp.concatenate(reorder_four(exchange(mixed_blocks), member), axis=0)
+
+    attn_part = lax.dot_general(mix_low, out_w, TN, preferred_element_type=single)
+    attn_out = sum_frames(attn_part.reshape(4, PATCHES, D))
+    resid_mid = resid_in + gate_one * attn_out
+    normed_two, inv_two = layer_norm(resid_mid)
+    hidden_own = (normed_two * (1.0 + scale_two) + shift_two).astype(bfloat)
+    hidden_two = jnp.concatenate(spread_frames(hidden_own), axis=0)
+    upward = jnp.dot(hidden_two, up_w, preferred_element_type=single)
+    activ_low = jax.nn.gelu(upward, approximate=False).astype(bfloat)
+    mlp_part = lax.dot_general(activ_low, down_w, NT, preferred_element_type=single)
+    mlp_out = sum_frames(mlp_part.reshape(4, PATCHES, D))
+    resid_out = resid_mid + gate_two * mlp_out
+    normed_three, inv_three = layer_norm(resid_out)
+    gain = vec_w[7:8]
+    final_low = (normed_three * gain).astype(bfloat)
+    pred = lax.dot_general(final_low, head_w, NT, preferred_element_type=single)
+    diff = pred - target
+    error_part = weight[0] * jnp.sum(jnp.mean(diff * diff, axis=1))
+    grad_pred = (2.0 / feat_dim * weight[0] * diff / weight_sum).astype(bfloat)
+    grad_head = lax.dot_general(grad_pred, final_low, TN, preferred_element_type=single)
+    grad_final = jnp.dot(grad_pred, head_w, preferred_element_type=single)
+    grad_gain = jnp.sum(grad_final * normed_three, axis=0)
+    grad_three = norm_back(grad_final * gain, normed_three, inv_three)
+    grad_gate_two = jnp.sum(grad_three * mlp_out, axis=0)
+    grad_mlp_low = jnp.concatenate(spread_frames((gate_two * grad_three).astype(bfloat)), axis=0)
+
+    grad_activ = jnp.dot(grad_mlp_low, down_w, preferred_element_type=single)
+    grad_up_low = (grad_activ * gelu_slope(upward)).astype(bfloat)
+    hidden_part = lax.dot_general(grad_up_low, up_w, NT, preferred_element_type=single)
+    grad_hidden_two = sum_frames(hidden_part.reshape(4, PATCHES, D))
+    grad_down = lax.dot_general(grad_mlp_low, activ_low, TN, preferred_element_type=single)
+    grad_up = lax.dot_general(hidden_two, grad_up_low, TN, preferred_element_type=single)
+    red_mlp = lax.psum_scatter(
+        jnp.stack([grad_up, grad_down]).astype(bfloat), "ctx", scatter_dimension=1, tiled=True
+    ).astype(single)
+
+    grad_shift_two = jnp.sum(grad_hidden_two, axis=0)
+    grad_scale_two = jnp.sum(grad_hidden_two * normed_two, axis=0)
+    grad_mid = grad_three + norm_back(grad_hidden_two * (1.0 + scale_two), normed_two, inv_two)
+    grad_gate_one = jnp.sum(grad_mid * attn_out, axis=0)
+    grad_attn_low = jnp.concatenate(spread_frames((gate_one * grad_mid).astype(bfloat)), axis=0)
+
+    grad_mix = lax.dot_general(out_w, grad_attn_low, NT, preferred_element_type=single).astype(
+        bfloat
+    )
+    grad_blocks = reorder_four([grad_mix[HD * k : HD * k + HD] for k in range(4)], member)
+    grad_in_blocks = exchange(grad_blocks)
+    grad_outproj = jnp.dot(mix_low, grad_attn_low, preferred_element_type=single)
+    back_blocks = call_attend_back(
+        attend_meta, head_in, grad_in_blocks, lse, mixed, cosine, sine
+    )
+    grad_qkv = jnp.concatenate(reorder_four(exchange(back_blocks), member), axis=0)
+
+    hidden_part = lax.dot_general(grad_qkv, qkv_w, TN, preferred_element_type=single)
+    grad_hidden_one = sum_frames(hidden_part.reshape(4, PATCHES, D))
+    grad_qkv_w = jnp.dot(grad_qkv, hidden_one, preferred_element_type=single)
+
+    def lane_blocks(values):
+        return jnp.transpose(values.reshape(values.shape[0], 8, 128), (1, 0, 2))
+
+    red_out = reduce_blocks(lane_blocks(grad_outproj), ctx_index, bfloat)
+    red_qkv = reduce_blocks(lane_blocks(grad_qkv_w), ctx_index, bfloat)
+    red_attn = jnp.concatenate(
+        [
+            jnp.transpose(red_qkv.reshape(4, 3, HD, 128), (1, 3, 0, 2)).reshape(3, 128, 256),
+            jnp.transpose(red_out)[None],
+        ],
+        axis=0,
+    )
+
+    grad_shift_one = jnp.sum(grad_hidden_one, axis=0)
+    normed_one, inv_one = layer_norm(resid_in)
+    grad_scale_one = jnp.sum(grad_hidden_one * normed_one, axis=0)
+    grad_in = grad_mid + norm_back(grad_hidden_one * (1.0 + scale_one), normed_one, inv_one)
+    grad_in_low = grad_in.astype(bfloat)
+    grad_embed = lax.dot_general(noisy_low[0], grad_in_low, TN, preferred_element_type=single)
+    grad_mod = jnp.stack(
+        [
+            grad_shift_one,
+            grad_scale_one,
+            grad_gate_one,
+            grad_shift_two,
+            grad_scale_two,
+            grad_gate_two,
+        ]
+    ).astype(bfloat)
+    mod_rows = jnp.stack(spread_frames(grad_mod))
+    for bit in (1, 2, 4):
+        mod_rows = jnp.concatenate([mod_rows, swap(mod_rows, "ctx", bit)], axis=0)
+    grad_mod_w = lax.dot_general(
+        cond_relative, mod_rows.reshape(32, 6 * D), TN, preferred_element_type=single
+    )
+    mod_cols = lax.dynamic_slice_in_dim(mod_rows, ctx_index * 128, 128, 2)
+    grad_mod_vec = jnp.sum(mod_cols.astype(single), axis=0)
+
+    def reduce_io(weight_grad, vector_grad):
+        rows = jnp.concatenate([weight_grad, vector_grad[None], jnp.zeros((15, D), single)], axis=0)
+        total = reduce_blocks(lane_blocks(rows), ctx_index, bfloat)
+        for bit in (1, 2):
+            total = total + swap(total, "tp", bit)
+        return total[:128], total[128:129]
+
+    red_head, red_gain = reduce_io(grad_head, grad_gain)
+    red_embed, red_bias = reduce_io(grad_embed, jnp.sum(grad_in, axis=0))
+    red_io = jnp.stack([red_embed, red_head])
+    red_vec = jnp.concatenate([grad_mod_vec, red_bias, red_gain], axis=0)
+
+    shared_sq = (
+        jnp.sum(grad_mod_w * grad_mod_w) + jnp.sum(red_io * red_io) + jnp.sum(red_vec * red_vec)
+    )
+    own_sq = (
+        jnp.sum(red_attn * red_attn)
+        + jnp.sum(red_mlp * red_mlp)
+        + jnp.where(tp_index == 0, shared_sq, 0.0)
+    )
+    sums = sum_all(
+        jnp.where(jnp.arange(128) < 64, own_sq, error_part).reshape(1, 128)
+    )
+    loss_value = sums[0, 64] / weight_sum
+    grad_norm = jnp.sqrt(sums[0, 0])
+    factor = jnp.minimum(1.0, clip_limit / (grad_norm + 1e-06))
+    count = step[0].astype(single)
+    attn_new = adam(w_attn, m_attn, v_attn, red_attn, factor, count, rate_matrix, decay_rate)
+    mlp_new = adam(w_mlp, m_mlp, v_mlp, red_mlp, factor, count, rate_matrix, decay_rate)
+    mod_new = adam(w_mod, m_mod, v_mod, grad_mod_w, factor, count, rate_matrix, decay_rate)
+    io_new = adam(w_io, m_io, v_io, red_io, factor, count, rate_matrix, decay_rate)
+    vec_new = adam(vectors, m_vec, v_vec, red_vec, factor, count, rate_vector, 0.0)
+    return (
+        (loss_value, grad_norm)
+        + attn_new
+        + mlp_new
+        + mod_new
+        + (io_new[0], io_new[1], io_new[2][0], io_new[2][1], io_new[3])
+        + vec_new
+    )
+
+
 def solution(mesh):
+    halves = mesh.shape["ctx"] == 8 and mesh.shape["tp"] == 4
     placed = (
         P("ctx", None),
         P("ctx", None),
@@ -588,7 +1283,7 @@
         P(None, "ctx"),
     )
     return jax.shard_map(
-        shards,
+        shards_halves if halves else shards,
         mesh=mesh,
         in_specs=placed,
         out_specs=(

time: 2080 us -> 636 us (0.31); the launches traced: 2050 us -> 625 us
  waiting for transfers between devices: 1330 us -> 208 us
  blocking collectives: 122 us -> 0 us
  other arithmetic: 187 us -> 79.9 us
  local copies, waits for them, and re-layouts: 178 us -> 76.2 us
  starting transfers between devices: 2.09 us -> 93.6 us
  matrix products: 140 us -> 52.2 us
  Pallas kernels: 0 us -> 76.2 us
  loops' own time: 65.7 us -> 0 us
    reduce_scatter x5 -> x1, waiting for transfers between devices: 604 us -> 0.02 us  [shards_halves(): lax.psum_scatter(jnp.stack([grad_up, grad_down]).astype(bfloat), 'ctx', s...]
    all_gather x5 -> x1, waiting for transfers between devices: 359 us -> 0.01 us  [shards_halves(): mlp_w = lax.all_gather(w_mlp.astype(bfloat), 'ctx', axis=1, tiled=True)]
    psum x4 -> x0, waiting for transfers between devices: 235 us -> none  [the longest x1 104 us: shards(): lax.psum(jnp.einsum('rh,dh->rd', mix_low, attn_w[3], preferred_element_ty...]
    ppermute x0 -> x94, waiting for transfers between devices: none -> 208 us  [the longest x70 152 us: swap(): return lax.ppermute(values, axis, [(i, i ^ bit) for i in range(size)])]
    unnamed x18 -> x2, waiting for transfers between devices: 128 us -> 0.03 us
    ppermute x0 -> x94, starting transfers between devices: none -> 93.5 us  [the longest x70 59.2 us: swap(): return lax.ppermute(values, axis, [(i, i ^ bit) for i in range(size)])]
    dot_general x53 -> x17, matrix products: 140 us -> 52.2 us  [the longest x1 15.2 us: shards_halves(): upward = jnp.dot(hidden_two, up_w, preferred_element_type=single)]
    pallas_call x0 -> x4, Pallas kernels: none -> 76.2 us  [the longest x1 34.8 us: call_attend(): pl.pallas_call(attend_kernel, out_shape=tuple((jax.ShapeDtypeStruct((HD,...]
  transfers between devices with their start and end apart: 16 -> 96, of which waited for: 16 -> 47; matrix products, arithmetic and copies ran while one was open for 5% -> 19% of each run, Pallas kernels for 0% -> 12%
where the time goes in v1:
time: 636 us; the launch traced here: 625 us
  waiting for transfers between devices  208 us (33%)
  starting transfers between devices  93.6 us (15%)
  other arithmetic  79.9 us (13%)
  local copies, waits for them, and re-layouts  76.2 us (12%)
  Pallas kernels  76.2 us (12%)
  matrix products  52.2 us (8%)
  between operations  38.3 us (6%)
    ppermute x70, waiting for transfers between devices, swap(): return lax.ppermute(values, axis, [(i, i ^ bit) for i in range(size)])  152 us
    ppermute x70, starting transfers between devices, swap(): return lax.ppermute(values, axis, [(i, i ^ bit) for i in range(size)])  59.2 us
    pallas_call x1, Pallas kernels, call_attend(): pl.pallas_call(attend_kernel, out_shape=tuple((jax.ShapeDtypeStruct((HD,...  34.8 us
    pallas_call x1, Pallas kernels, call_attend_back(): pl.pallas_call(attend_back_kernel, out_shape=tuple((jax.ShapeDtypeStruct(...  34.3 us
    unnamed x288, local copies, waits for them, and re-layouts  30.6 us
    ppermute x9, waiting for transfers between devices, ring_gather(): ahead.append(lax.ppermute(ahead[-1], 'ctx', RING_NEXT))  25.5 us
    concatenate x1, local copies, waits for them, and re-layouts, shards_halves(): jnp.concatenate([slot_levels, jnp.stack([lax.dynamic_index_in_dim(slot_le...  20.9 us
    ppermute x9, waiting for transfers between devices, ring_gather(): behind.append(lax.ppermute(behind[-1], 'ctx', RING_PREV))  18.4 us
  transfers between devices with their start and end apart: 96, of which 47 were waited for; matrix products, arithmetic and copies ran while one was open for 19% of the time, Pallas kernels for 12%

profile of v1, /device:TPU:0, one launch (start us, length us, event | category | flops | bytes accessed | tf_op | source)
XLA Modules:
  0.0 624.7 jit_solution(14246805219217789506)
XLA Ops:
  17.2 20.9 %concatenate.233 = s32[64]{0:T(128)S(1)} concatenate(s32[32]{0:T(128)S(1)} %get-tuple-element.278, s32[1]{0:T(128)} %bitcast.54, s32[1]{0:T(128)} %bitcast.55, s32[1]{0:T(128)} %bitcast.56, s32[1]{0:T(128)} %bitcast.57, s32[1]{0:T(128)} %bitcast.58, s32[1]{0:T(128)} %bitcast.59, s32[1]{0:T(128)} %bitcast.60, s32[1]{0:T(128)} %bitcast.61, s32[1]{0:T(128)} %bitcast.62, s32[1]{0:T(128)} %bitcast.63, ...), dimensions={0} | concatenate | bytes 512 | tf_op jit(solution)/shard_map/concatenate | solution.py:1029
  101.9 12.0 %collective-permute-done.5.refs_6_ = bf16[912,128]{1,0:T(8,128)(2,1)S(1)} collective-permute-done((bf16[912,128]{1,0:T(8,128)(2,1)S(1)}, bf16[912,128]{1,0:T(8,128)(2,1)S(1)}, u32[]{:S(2)}, u32[]{:S(2)}) %collective-permute-start.5) | collective-permute-done | bytes 233504 | tf_op jit(solution)/shard_map/ppermute | solution.py:601
  118.1 5.4 collective-permute-start.6
  135.8 4.7 front.1
  147.1 17.4 %collective-permute-done.29.refs_1_ = bf16[384,128]{1,0:T(8,128)(2,1)S(1)} collective-permute-done((bf16[384,128]{1,0:T(8,128)(2,1)S(1)}, bf16[384,128]{1,0:T(8,128)(2,1)S(1)}, u32[]{:S(2)}, u32[]{:S(2)}) %collective-permute-start.29) | collective-permute-done | bytes 98336 | tf_op jit(solution)/shard_map/ppermute | solution.py:600
  177.9 34.8 %attend.1 = (bf16[64,1024]{1,0:T(8,128)(2,1)S(1)}, bf16[64,1024]{1,0:T(8,128)(2,1)}, bf16[64,1024]{1,0:T(8,128)(2,1)}, bf16[64,1024]{1,0:T(8,128)(2,1)}, f32[8,1...) custom-call(s32[18]{0:T(128)S(1)} %pad_add_fusion.1.meta, bf16[192,1024]{1,0:T(8,128)(2,1)S(1)} %get-tuple-element.199.refs_0_, ...), custom_call_target="tpu_custom_call" | custom-call | flops 8999999488 | bytes 5000000 | tf_op jit(solution)/shard_map/attend/pallas_call | solution.py:781
  235.4 12.5 %collective-permute-done.41 = bf16[256,1024]{1,0:T(8,128)(2,1)S(1)} collective-permute-done((bf16[256,1024]{1,0:T(8,128)(2,1)S(1)}, bf16[256,1024]{1,0:T(8,128)(2,1)S(1)}, u32[]{:S(2)}, u32[]{:S(2)}) %collective-permute-start.41) | collective-permute-done | bytes 524320 | tf_op jit(solution)/shard_map/ppermute | solution.py:580
  252.6 12.4 %collective-permute-done.43 = bf16[256,1024]{1,0:T(8,128)(2,1)S(1)} collective-permute-done((bf16[256,1024]{1,0:T(8,128)(2,1)S(1)}, bf16[256,1024]{1,0:T(8,128)(2,1)S(1)}, u32[]{:S(2)}, u32[]{:S(2)}) %collective-permute-start.43) | collective-permute-done | bytes 524320 | tf_op jit(solution)/shard_map/ppermute | solution.py:580
  267.0 15.2 %fusion.2 = (bf16[1024,1024]{1,0:T(8,128)(2,1)S(1)}, f32[1024,1024]{1,0:T(8,128)}) fusion(bf16[2,1024,1024]{2,1,0:T(8,128)(2,1)} %all-gather.2.cloned.1.call-done, bf16[256,1024]{1,0:T(8,128)(2,1)} %collective-permute-done.44, bf16[256,1024]{1,0:T(8,128)(2,1)} %copy-done.115, bf16[256,1024]{1,0:T(8,128)(2,1)} %copy-done.117, bf16[256,1024]{1,0:T(8,128)(2,1)} %copy-done.63), kind=kOutput, calls=%fused_computation.5 | convolution fusion | flops 2224029696 | bytes 10485760 | tf_op jit(solution)/shard_map/dot_general | solution.py:1130
  294.4 8.6 %collective-permute-done.46 = bf16[256,1024]{1,0:T(8,128)(2,1)} collective-permute-done((bf16[256,1024]{1,0:T(8,128)(2,1)}, bf16[256,1024]{1,0:T(8,128)(2,1)}, u32[]{:S(2)}, u32[]{:S(2)}) %collective-permute-start.46) | collective-permute-done | bytes 524320 | tf_op jit(solution)/shard_map/ppermute | solution.py:580
  312.5 12.6 %collective-permute-done.48 = bf16[256,1024]{1,0:T(8,128)(2,1)S(1)} collective-permute-done((bf16[256,1024]{1,0:T(8,128)(2,1)S(1)}, bf16[256,1024]{1,0:T(8,128)(2,1)S(1)}, u32[]{:S(2)}, u32[]{:S(2)}) %collective-permute-start.48) | collective-permute-done | bytes 524320 | tf_op jit(solution)/shard_map/ppermute | solution.py:580
  327.8 5.7 fusion.8
  364.1 10.4 %collective-permute-done.53 = bf16[256,1024]{1,0:T(8,128)(2,1)} collective-permute-done((bf16[256,1024]{1,0:T(8,128)(2,1)}, bf16[256,1024]{1,0:T(8,128)(2,1)}, u32[]{:S(2)}, u32[]{:S(2)}) %collective-permute-start.53) | collective-permute-done | bytes 524320 | tf_op jit(solution)/shard_map/ppermute | solution.py:580
  394.1 6.2 collective-permute-done.56.refs_6_
  400.3 8.7 %collective-permute-done.57.refs_7_ = bf16[64,1024]{1,0:T(8,128)(2,1)S(1)} collective-permute-done((bf16[64,1024]{1,0:T(8,128)(2,1)S(1)}, bf16[64,1024]{1,0:T(8,128)(2,1)S(1)}, u32[]{:S(2)}, u32[]{:S(2)}) %collective-permute-start.57) | collective-permute-done | bytes 131104 | tf_op jit(solution)/shard_map/ppermute | solution.py:580
  409.0 34.3 %attend_back.1 = (bf16[192,1024]{1,0:T(8,128)(2,1)S(1)}, bf16[192,1024]{1,0:T(8,128)(2,1)S(1)}, bf16[192,1024]{1,0:T(8,128)(2,1)S(1)}, bf16[192,1024]{1,0:T(8,128)(2,1)S(1)}) custom-call(s32[18]{0:T(128)S(1)} %pad_add_fusion.1.meta, bf16[192,1024]{1,0:T(8,128)(2,1)S(1)} %get-tuple-element.199.refs_0_, bf16[192,1024]{1,0:T(8,128)(2,1)S(1)} %copy-done.9, ...), custom_call_target="tpu_custom_call" | custom-call | flops 22000001024 | bytes 10000000 | tf_op jit(solution)/shard_map/attend_back/pallas_call | solution.py:886
  449.1 7.3 %collective-permute-done.58 = bf16[192,1024]{1,0:T(8,128)(2,1)S(1)} collective-permute-done((bf16[192,1024]{1,0:T(8,128)(2,1)S(1)}, bf16[192,1024]{1,0:T(8,128)(2,1)S(1)}, u32[]{:S(2)}, u32[]{:S(2)}) %collective-permute-start.58) | collective-permute-done | bytes 393248 | tf_op jit(solution)/shard_map/ppermute | solution.py:580
  456.3 6.7 %collective-permute-done.59 = bf16[192,1024]{1,0:T(8,128)(2,1)S(1)} collective-permute-done((bf16[192,1024]{1,0:T(8,128)(2,1)S(1)}, bf16[192,1024]{1,0:T(8,128)(2,1)S(1)}, u32[]{:S(2)}, u32[]{:S(2)}) %collective-permute-start.59) | collective-permute-done | bytes 393248 | tf_op jit(solution)/shard_map/ppermute | solution.py:580
  463.0 5.2 collective-permute-done.60
  483.7 7.6 %collective-permute-done.67 = bf16[256,128]{1,0:T(8,128)(2,1)S(1)} collective-permute-done((bf16[256,128]{1,0:T(8,128)(2,1)S(1)}, bf16[256,128]{1,0:T(8,128)(2,1)S(1)}, u32[]{:S(2)}, u32[]{:S(2)}) %collective-permute-start.67) | collective-permute-done | bytes 65568 | tf_op jit(solution)/shard_map/ppermute | solution.py:580
  492.0 5.7 collective-permute-done.61
  518.3 5.0 collective-permute-done.74
  550.9 7.1 %collective-permute-done.76 = bf16[16,6,1024]{2,1,0:T(8,128)(2,1)S(1)} collective-permute-done((bf16[16,6,1024]{2,1,0:T(8,128)(2,1)S(1)}, bf16[16,6,1024]{2,1,0:T(8,128)(2,1)S(1)}, u32[]{:S(2)}, u32[]{:S(2)}) %collective-permute-start.76) | collective-permute-done | bytes 196640 | tf_op jit(solution)/shard_map/ppermute | solution.py:580
  605.3 7.5 %fusion.121 = (bf16[128,6144]{1,0:T(8,128)(2,1)}, f32[128,6144]{1,0:T(8,128)}, f32[128,6144]{1,0:T(8,128)}, f32[128,6144]{1,0:T(8,128)}) fusion(f32[128,6144]{1,0:T(8,128)} %param.33, f32[]{:T(128)} %bitcast.203, f32[]{:T(128)} %bitcast.202, f32[128,6144]{1,0:T(8,128)S(1)} %get-tuple-element.343, f32[]{:T(128)S(6)} %min.15, f32[128,6144]{1,0:T(8,128)} %param.35, ...), kind=kLoop, calls=%fused_computation.477 | loop fusion | flops 13369344 | bytes 23592972 | tf_op jit(solution)/shard_map/convert_element_type | solution.py:179
  (686 shorter events, 312.6 us)
Async XLA Ops:
  7.2 259.8 %all-gather.2.cloned.1.call-start = ((), (), s32[]{:S(2)}) async-start(), calls=%async_computation.1 | async-start | bytes 4718592 | tf_op jit(solution)/shard_map/all_gather | solution.py:1113
  8.2 62.8 %collective-permute-start.8 = (bf16[512,128]{1,0:T(8,128)(2,1)S(1)}, bf16[512,128]{1,0:T(8,128)(2,1)S(1)}, u32[]{:S(2)}, u32[]{:S(2)}) collective-permute-start(bf16[512,128]{1,0:T(8,128)(2,1)S(1)} %bitcast.515), channel_id=1, source_target_pairs={{0,4},{4,12},{12,20},{20,28},{28,24},{24,16},{16,8},{8,0},{1,5},{5... | collective-permute-start | bytes 393224 | tf_op jit(solution)/shard_map/ppermute | solution.py:600
  11.2 60.4 %collective-permute-start.11 = (bf16[512,128]{1,0:T(8,128)(2,1)S(1)}, bf16[512,128]{1,0:T(8,128)(2,1)S(1)}, u32[]{:S(2)}, u32[]{:S(2)}) collective-permute-start(bf16[512,128]{1,0:T(8,128)(2,1)S(1)} %bitcast.516), channel_id=1, source_target_pairs={{4,0},{12,4},{20,12},{28,20},{24,28},{16,24},{8,16},{0,8},{5,1},{1... | collective-permute-start | bytes 393224 | tf_op jit(solution)/shard_map/ppermute | solution.py:601
  43.8 525.2 %reduce-scatter.2.cloned.1.call-start = ((), (), s32[]{:S(2)}) async-start(), calls=%async_computation.2 | async-start | bytes 4718592 | tf_op jit(solution)/shard_map/reduce_scatter | solution.py:1155
  58.8 18.7 %collective-permute-start = (bf16[912,128]{1,0:T(8,128)(2,1)S(1)}, bf16[912,128]{1,0:T(8,128)(2,1)S(1)}, u32[]{:S(2)}, u32[]{:S(2)}) collective-permute-start(bf16[912,128]{1,0:T(8,128)(2,1)S(1)} %maximum_maximum_fusion.2.refs_0_), channel_id=1, source_target_pairs={{0,4},{4,12},{12,20},{20,28},{28,24},{24,16},{16,8},{8,0},{1,5},{5... | collective-permute-start | bytes 700424 | tf_op jit(solution)/shard_map/ppermute | solution.py:600
  77.5 22.3 %collective-permute-start.1 = (bf16[912,128]{1,0:T(8,128)(2,1)S(1)}, bf16[912,128]{1,0:T(8,128)(2,1)S(1)}, u32[]{:S(2)}, u32[]{:S(2)}) collective-permute-start(bf16[912,128]{1,0:T(8,128)(2,1)S(1)} %collective-permute-done.refs_1_), channel_id=1, source_target_pairs={{0,4},{4,12},{12,20},{20,28},{28,24},{24,16},{16,8},{8,0},{1,5},{5... | collective-permute-start | bytes 700424 | tf_op jit(solution)/shard_map/ppermute | solution.py:600
  77.5 23.2 %collective-permute-start.4 = (bf16[912,128]{1,0:T(8,128)(2,1)S(1)}, bf16[912,128]{1,0:T(8,128)(2,1)S(1)}, u32[]{:S(2)}, u32[]{:S(2)}) collective-permute-start(bf16[912,128]{1,0:T(8,128)(2,1)S(1)} %collective-permute-done.3.refs_4_), channel_id=1, source_target_pairs={{4,0},{12,4},{20,12},{28,20},{24,28},{16,24},{8,16},{0,8},{5,1},{1... | collective-permute-start | bytes 700424 | tf_op jit(solution)/shard_map/ppermute | solution.py:601
  99.8 18.3 %collective-permute-start.2 = (bf16[912,128]{1,0:T(8,128)(2,1)S(1)}, bf16[912,128]{1,0:T(8,128)(2,1)S(1)}, u32[]{:S(2)}, u32[]{:S(2)}) collective-permute-start(bf16[912,128]{1,0:T(8,128)(2,1)S(1)} %collective-permute-done.1.refs_2_), channel_id=1, source_target_pairs={{0,4},{4,12},{12,20},{20,28},{28,24},{24,16},{16,8},{8,0},{1,5},{5... | collective-permute-start | bytes 700424 | tf_op jit(solution)/shard_map/ppermute | solution.py:600
  101.8 21.7 %collective-permute-start.17 = (bf16[4,128,128]{2,1,0:T(8,128)(2,1)S(1)}, bf16[4,128,128]{2,1,0:T(8,128)(2,1)S(1)}, u32[]{:S(2)}, u32[]{:S(2)}) collective-permute-start(bf16[4,128,128]{2,1,0:T(8,128)(2,1)S(1)} %collective-permute-done.16), channel_id=1, source_target_pairs={{0,1},{1,0},{2,3},{3,2},{4,5},{5,4},{6,7},{7,6},{8,9},{9,8},{10,11... | collective-permute-start | bytes 393224 | tf_op jit(solution)/shard_map/ppermute | solution.py:580
  140.7 37.1 %collective-permute-start.26 = (bf16[192,1024]{1,0:T(8,128)(2,1)S(1)}, bf16[192,1024]{1,0:T(8,128)(2,1)S(1)}, u32[]{:S(2)}, u32[]{:S(2)}) collective-permute-start(bf16[192,1024]{1,0:T(8,128)(2,1)S(1)} %get-tuple-element.198), channel_id=1, source_target_pairs={{0,4},{4,0},{8,12},{12,8},{16,20},{20,16},{24,28},{28,24},{1,5},{5... | collective-permute-start | bytes 1179656 | tf_op jit(solution)/shard_map/ppermute | solution.py:580
  143.4 34.4 %collective-permute-start.27 = (bf16[192,1024]{1,0:T(8,128)(2,1)S(1)}, bf16[192,1024]{1,0:T(8,128)(2,1)S(1)}, u32[]{:S(2)}, u32[]{:S(2)}) collective-permute-start(bf16[192,1024]{1,0:T(8,128)(2,1)S(1)} %get-tuple-element.197), channel_id=1, source_target_pairs={{0,8},{4,12},{8,0},{12,4},{16,24},{20,28},{24,16},{28,20},{1,9},{5... | collective-permute-start | bytes 1179656 | tf_op jit(solution)/shard_map/ppermute | solution.py:580
  144.3 33.6 %collective-permute-start.28 = (bf16[192,1024]{1,0:T(8,128)(2,1)S(1)}, bf16[192,1024]{1,0:T(8,128)(2,1)S(1)}, u32[]{:S(2)}, u32[]{:S(2)}) collective-permute-start(bf16[192,1024]{1,0:T(8,128)(2,1)S(1)} %get-tuple-element.196), channel_id=1, source_target_pairs={{0,12},{4,8},{8,4},{12,0},{16,28},{20,24},{24,20},{28,16},{1,13},{... | collective-permute-start | bytes 1179656 | tf_op jit(solution)/shard_map/ppermute | solution.py:580
  145.0 19.4 %collective-permute-start.29 = (bf16[384,128]{1,0:T(8,128)(2,1)S(1)}, bf16[384,128]{1,0:T(8,128)(2,1)S(1)}, u32[]{:S(2)}, u32[]{:S(2)}) collective-permute-start(bf16[384,128]{1,0:T(8,128)(2,1)S(1)} %pad_maximum_fusion.29.refs_0_), channel_id=1, source_target_pairs={{0,4},{4,12},{12,20},{20,28},{28,24},{24,16},{16,8},{8,0},{1,5},{5... | collective-permute-start | bytes 294920 | tf_op jit(solution)/shard_map/ppermute | solution.py:600
  175.1 44.0 %collective-permute-start.36 = (bf16[192,128]{1,0:T(8,128)(2,1)}, bf16[192,128]{1,0:T(8,128)(2,1)}, u32[]{:S(2)}, u32[]{:S(2)}) collective-permute-start(bf16[192,128]{1,0:T(8,128)(2,1)} %slice.493), channel_id=1, source_target_pairs={{4,0},{12,4},{20,12},{28,20},{24,28},{16,24},{8,16},{0,8},{5,1},{1... | collective-permute-start | bytes 147464 | tf_op jit(solution)/shard_map/ppermute | solution.py:603
  177.5 41.6 %collective-permute-start.35 = (bf16[192,128]{1,0:T(8,128)(2,1)}, bf16[192,128]{1,0:T(8,128)(2,1)}, u32[]{:S(2)}, u32[]{:S(2)}) collective-permute-start(bf16[192,128]{1,0:T(8,128)(2,1)} %slice.492), channel_id=1, source_target_pairs={{0,4},{4,12},{12,20},{20,28},{28,24},{24,16},{16,8},{8,0},{1,5},{5... | collective-permute-start | bytes 147464 | tf_op jit(solution)/shard_map/ppermute | solution.py:602
  364.1 18.9 %collective-permute-start.52 = (bf16[256,1024]{1,0:T(8,128)(2,1)}, bf16[256,1024]{1,0:T(8,128)(2,1)}, u32[]{:S(2)}, u32[]{:S(2)}) collective-permute-start(bf16[256,1024]{1,0:T(8,128)(2,1)} %multiply_convert_fusion), channel_id=1, source_target_pairs={{0,1},{1,0},{2,3},{3,2},{4,5},{5,4},{6,7},{7,6},{8,9},{9,8},{10,11... | collective-permute-start | bytes 1572872 | tf_op jit(solution)/shard_map/ppermute | solution.py:580
  388.0 21.0 %collective-permute-start.57 = (bf16[64,1024]{1,0:T(8,128)(2,1)S(1)}, bf16[64,1024]{1,0:T(8,128)(2,1)S(1)}, u32[]{:S(2)}, u32[]{:S(2)}) collective-permute-start(bf16[64,1024]{1,0:T(8,128)(2,1)S(1)} %get-tuple-element.210), channel_id=1, source_target_pairs={{0,12},{4,8},{8,4},{12,0},{16,28},{20,24},{24,20},{28,16},{1,13},{... | collective-permute-start | bytes 393224 | tf_op jit(solution)/shard_map/ppermute | solution.py:580
  443.4 19.6 %collective-permute-start.59 = (bf16[192,1024]{1,0:T(8,128)(2,1)S(1)}, bf16[192,1024]{1,0:T(8,128)(2,1)S(1)}, u32[]{:S(2)}, u32[]{:S(2)}) collective-permute-start(bf16[192,1024]{1,0:T(8,128)(2,1)S(1)} %get-tuple-element.49), channel_id=1, source_target_pairs={{0,8},{4,12},{8,0},{12,4},{16,24},{20,28},{24,16},{28,20},{1,9},{5... | collective-permute-start | bytes 1179656 | tf_op jit(solution)/shard_map/ppermute | solution.py:580
  446.1 22.1 %collective-permute-start.60 = (bf16[192,1024]{1,0:T(8,128)(2,1)S(1)}, bf16[192,1024]{1,0:T(8,128)(2,1)S(1)}, u32[]{:S(2)}, u32[]{:S(2)}) collective-permute-start(bf16[192,1024]{1,0:T(8,128)(2,1)S(1)} %get-tuple-element.50), channel_id=1, source_target_pairs={{0,4},{4,0},{8,12},{12,8},{16,20},{20,16},{24,28},{28,24},{1,5},{5... | collective-permute-start | bytes 1179656 | tf_op jit(solution)/shard_map/ppermute | solution.py:580
  447.8 27.5 %collective-permute-start.65 = (bf16[4,256,128]{2,1,0:T(8,128)(2,1)S(1)}, bf16[4,256,128]{2,1,0:T(8,128)(2,1)S(1)}, u32[]{:S(2)}, u32[]{:S(2)}) collective-permute-start(bf16[4,256,128]{2,1,0:T(8,128)(2,1)S(1)} %fusion.50), channel_id=1, source_target_pairs={{0,4},{4,0},{8,12},{12,8},{16,20},{20,16},{24,28},{28,24},{1,5},{5... | collective-permute-start | bytes 786440 | tf_op jit(solution)/shard_map/ppermute | solution.py:580
  473.8 23.9 %collective-permute-start.61 = (bf16[4,768,128]{2,1,0:T(8,128)(2,1)S(1)}, bf16[4,768,128]{2,1,0:T(8,128)(2,1)S(1)}, u32[]{:S(2)}, u32[]{:S(2)}) collective-permute-start(bf16[4,768,128]{2,1,0:T(8,128)(2,1)S(1)} %fusion.38), channel_id=1, source_target_pairs={{0,4},{4,0},{8,12},{12,8},{16,20},{20,16},{24,28},{28,24},{1,5},{5... | collective-permute-start | bytes 2359304 | tf_op jit(solution)/shard_map/ppermute | solution.py:580
  480.1 22.7 %collective-permute-start.70 = (bf16[256,1024]{1,0:T(8,128)(2,1)S(1)}, bf16[256,1024]{1,0:T(8,128)(2,1)S(1)}, u32[]{:S(2)}, u32[]{:S(2)}) collective-permute-start(bf16[256,1024]{1,0:T(8,128)(2,1)S(1)} %fusion.30), channel_id=1, source_target_pairs={{0,2},{1,3},{2,0},{3,1},{4,6},{5,7},{6,4},{7,5},{8,10},{9,11},{10,... | collective-permute-start | bytes 1572872 | tf_op jit(solution)/shard_map/ppermute | solution.py:580
  499.9 38.2 %collective-permute-start.64 = (bf16[768,128]{1,0:T(8,128)(2,1)}, bf16[768,128]{1,0:T(8,128)(2,1)S(1)}, u32[]{:S(2)}, u32[]{:S(2)}) collective-permute-start(bf16[768,128]{1,0:T(8,128)(2,1)} %get-tuple-element.208), channel_id=1, source_target_pairs={{0,24},{4,28},{8,16},{12,20},{16,8},{20,12},{24,0},{28,4},{1,25},{... | collective-permute-start | bytes 589832 | tf_op jit(solution)/shard_map/ppermute | solution.py:580
  499.9 38.7 %collective-permute-start.63 = (bf16[768,128]{1,0:T(8,128)(2,1)}, bf16[768,128]{1,0:T(8,128)(2,1)}, u32[]{:S(2)}, u32[]{:S(2)}) collective-permute-start(bf16[768,128]{1,0:T(8,128)(2,1)} %get-tuple-element.209), channel_id=1, source_target_pairs={{0,16},{4,20},{8,24},{12,28},{16,0},{20,4},{24,8},{28,12},{1,17},{... | collective-permute-start | bytes 589832 | tf_op jit(solution)/shard_map/ppermute | solution.py:580
  (202 other events, 2436.2 us)
Sparse Core Ops, SparseCore 0:
  43.9 87.8 all-gather.1
  380.6 119.1 reduce-scatter.1

commit v2 on v0

--- a/solution.py
+++ b/solution.py
@@ -1,8 +1,11 @@
+import functools
 import math
 
 import jax
 import jax.numpy as jnp
 from jax import lax
+from jax.experimental import pallas as pl
+from jax.experimental.pallas import tpu as pltpu
 from jax.sharding import PartitionSpec as P
 
 D = 1024
@@ -563,7 +566,1382 @@
     )
 
 
+RING = (0, 1, 3, 5, 7, 6, 4, 2)
+RING_NEXT = tuple((RING[i], RING[(i + 1) % 8]) for i in range(8))
+RING_PREV = tuple((b, a) for a, b in RING_NEXT)
+HALF_SLOTS = 16
+QKV_ROWS = 768
+ATTN_ROWS = 1024
+FRONT_ROWS = 912
+TOKEN_ROWS = 512
+IO_ROWS = 80
+MOD_ROWS = 48
+RING_ROWS = TOKEN_ROWS + FRONT_ROWS + 384
+NT = (((1,), (1,)), ((), ()))
+TN = (((0,), (0,)), ((), ()))
+
+
+def swap(values, axis, bit):
+    size = 8 if axis == "ctx" else 4
+    return lax.ppermute(values, axis, [(i, i ^ bit) for i in range(size)])
+
+
+def after(values, *others):
+    return lax.optimization_barrier((values,) + others)[0]
+
+
+def ring_gather(shard):
+    half = shard.shape[0] // 2
+    ahead = [shard]
+    behind = [shard]
+    for _ in range(3):
+        ahead.append(lax.ppermute(ahead[-1], "ctx", RING_NEXT))
+        behind.append(lax.ppermute(behind[-1], "ctx", RING_PREV))
+    first = lax.ppermute(ahead[-1][:half], "ctx", RING_NEXT)
+    second = lax.ppermute(behind[-1][half:], "ctx", RING_PREV)
+    return ahead + behind[1:] + [jnp.concatenate([first, second], axis=0)]
+
+
+def reduce_blocks(blocks, ctx_index, wire):
+    return reduce_along_z(reduce_along_x(blocks, ctx_index, wire), ctx_index, wire)
+
+
+def reduce_along_x(blocks, ctx_index, wire):
+    x = ctx_index % 2
+    pairs = blocks.reshape((4, 2) + blocks.shape[1:])
+    first, second = pairs[:, 0], pairs[:, 1]
+    even = x == 0
+    away = jnp.where(even, second, first).astype(wire)
+    return jnp.where(even, first, second) + swap(away, "ctx", 1).astype(jnp.float32)
+
+
+def pieces_along_z(held, ctx_index, wire):
+    z = ctx_index // 2
+    low = held.astype(wire)
+    came = []
+    for bit in (1, 2, 3):
+        piece = lax.dynamic_index_in_dim(low, z ^ bit, 0, keepdims=False)
+        came.append(swap(piece, "ctx", 2 * bit))
+    return lax.dynamic_index_in_dim(held, z, 0, keepdims=False), came
+
+
+def reduce_along_z(held, ctx_index, wire):
+    total, came = pieces_along_z(held, ctx_index, wire)
+    for piece in came:
+        total = total + piece.astype(jnp.float32)
+    return total
+
+
+def spread_frames(own):
+    core = swap(own, "tp", 1)
+    across = swap(own, "tp", 2)
+    return [own, core, across, swap(across, "tp", 1)]
+
+
+def sum_across(far):
+    return (far[0] + swap(far[1], "tp", 1).astype(jnp.float32)).astype(jnp.bfloat16)
+
+
+def sum_frames(near, across):
+    return near[0], swap(near[1], "tp", 1), swap(across, "tp", 2)
+
+
+def reorder_four(items, index):
+    low_bit = (index & 1) == 1
+    high_bit = (index & 2) == 2
+    once = [jnp.where(low_bit, items[k ^ 1], items[k]) for k in range(4)]
+    return [jnp.where(high_bit, once[k ^ 2], once[k]) for k in range(4)]
+
+
+def sum_all(values):
+    for axis, bit in (("tp", 1), ("tp", 2), ("ctx", 1)):
+        values = values + swap(values, axis, bit)
+    return [values] + [swap(values, "ctx", bit) for bit in (2, 4, 6)]
+
+
+def prepare_kernel(meta, clean, noise, w_attn, w_io, vectors, ring):
+    front = ring.at[TOKEN_ROWS:RING_ROWS]
+    for frame in range(4):
+        rows = pl.ds(pl.multiple_of(256 * frame + 64 * meta[1], 64), 64)
+        ring[128 * frame : 128 * frame + 64, :] = clean[rows, :]
+        ring[128 * frame + 64 : 128 * frame + 128, :] = noise[rows, :]
+    for part in range(3):
+        front[256 * part : 256 * part + 256, :] = w_attn[part].T.astype(jnp.bfloat16)
+    base = QKV_ROWS
+    front[base : base + 128, :] = w_io[0].astype(jnp.bfloat16)
+    front[base + 128 : base + 144, :] = jnp.concatenate(
+        [vectors[...], jnp.zeros((8, 128), jnp.float32)], axis=0
+    ).astype(jnp.bfloat16)
+    for part in range(2):
+        base = FRONT_ROWS + 128 * part
+        front[base : base + 128, :] = w_attn[3, :, 128 * part : 128 * part + 128].astype(
+            jnp.bfloat16
+        )
+    front[FRONT_ROWS + 256 : FRONT_ROWS + 384, :] = w_io[1].T.astype(jnp.bfloat16)
+
+
+def vmem_specs(count):
+    return [pl.BlockSpec(memory_space=pltpu.VMEM)] * count
+
+
+def smem_specs(count):
+    return [pl.BlockSpec(memory_space=pltpu.SMEM)] * count
+
+
+def call_prepare(device, clean, noise, w_attn, w_io, vectors):
+    return pl.pallas_call(
+        prepare_kernel,
+        out_shape=jax.ShapeDtypeStruct((RING_ROWS, 128), jnp.bfloat16),
+        in_specs=smem_specs(1) + vmem_specs(5),
+        out_specs=vmem_specs(1)[0],
+        name="prepare",
+    )(device, clean, noise, w_attn, w_io, vectors)
+
+
+def place_kernel(device, lengths, order, levels, front, attend, rows, inverse, stored, position, level):
+    ctx, tp = device[0], device[1]
+    frames, stretches, clips = levels.shape[0], order.shape[0], lengths.shape[0]
+    per_stretch = frames // stretches
+    half = frames // 2
+
+    def per_stretch_place(place, carry):
+        inverse[order[place]] = place
+        return carry
+
+    lax.fori_loop(0, stretches, per_stretch_place, 0)
+
+    def per_frame(frame, counts):
+        long_count, short_count = counts
+        begin, start, length = jnp.int32(0), jnp.int32(0), jnp.int32(0)
+        for clip in range(clips):
+            size = lengths[clip]
+            inside = (frame >= begin) & (frame < begin + size)
+            start = jnp.where(inside, begin, start)
+            length = jnp.where(inside, size, length)
+            begin = begin + size
+        is_long = length == half
+        slot = jnp.where(is_long, long_count, half + short_count)
+        stored[slot] = inverse[lax.div(frame, jnp.int32(per_stretch))] * per_stretch + lax.rem(
+            frame, jnp.int32(per_stretch)
+        )
+        position[slot] = frame - start
+        level[slot] = levels[frame]
+        grown = is_long.astype(jnp.int32)
+        return (long_count + grown, short_count + 1 - grown)
+
+    lax.fori_loop(0, frames, per_frame, (jnp.int32(0), jnp.int32(0)))
+
+    def where_on_ring(index):
+        z, x = index >> 1, index & 1
+        return jnp.where(x == 1, z + 1, (8 - z) & 7)
+
+    mine = where_on_ring(ctx)
+    member = ctx & 3
+    for place, offset in enumerate((0, 7, 6, 5, 1, 2, 3, 4)):
+        at = (mine + offset) & 7
+        front[place] = jnp.where(
+            at == 0, 0, jnp.where(at <= 4, 2 * at - 1, 2 * (8 - at))
+        )
+    for k in range(4):
+        front[8 + k] = 4 * member + (tp ^ k)
+        front[12 + k] = member ^ k
+        at = stored[4 * ctx + (tp ^ k)]
+        distance = (where_on_ring(at >> 2) - mine) & 7
+        place = jnp.where(distance == 0, 0, jnp.where(distance <= 4, distance + 3, 8 - distance))
+        front[16 + k] = place * 4 + (at & 3)
+        front[20 + k] = tp ^ k
+    attend[0] = member
+    attend[1] = tp
+    base = lax.div(ctx, jnp.int32(4)) * half
+
+    def per_slot(slot, carry):
+        attend[2 + slot] = position[base + slot]
+        return carry
+
+    lax.fori_loop(0, half, per_slot, 0)
+
+    def per_row(row, carry):
+        rows[row] = level[row]
+        rows[frames + row] = level[4 * (ctx ^ (row & 7)) + (tp ^ (row >> 3))]
+        return carry
+
+    lax.fori_loop(0, frames, per_row, 0)
+
+
+def call_place(device, lengths, order, levels):
+    frames = levels.shape[0]
+    return pl.pallas_call(
+        place_kernel,
+        out_shape=(
+            jax.ShapeDtypeStruct((24,), jnp.int32),
+            jax.ShapeDtypeStruct((2 + frames // 2,), jnp.int32),
+            jax.ShapeDtypeStruct((2 * frames,), jnp.int32),
+        ),
+        in_specs=smem_specs(4),
+        out_specs=smem_specs(3),
+        scratch_shapes=[pltpu.SMEM((order.shape[0],), jnp.int32)]
+        + [pltpu.SMEM((frames,), jnp.int32)] * 3,
+        name="place",
+    )(device, lengths, order, levels)
+
+
+def pick_kernel(meta, *refs):
+    out, sems = refs[8:]
+    for frame in range(4):
+        wanted = meta[16 + frame]
+        for place in range(8):
+
+            @pl.when((wanted >> 2) == place)
+            def _():
+                start = pl.multiple_of((wanted & 3) * 128, 128)
+                pltpu.make_async_copy(
+                    refs[place].at[pl.ds(start, 128), :],
+                    out.at[128 * frame : 128 * frame + 128, :],
+                    sems.at[frame],
+                ).start()
+
+    for frame in range(4):
+        pltpu.make_async_copy(
+            refs[0].at[0:128, :], out.at[128 * frame : 128 * frame + 128, :], sems.at[frame]
+        ).wait()
+
+
+def hbm_specs(count):
+    return [pl.BlockSpec(memory_space=pltpu.HBM)] * count
+
+
+def call_pick(meta, pieces):
+    return pl.pallas_call(
+        pick_kernel,
+        out_shape=jax.ShapeDtypeStruct((TOKEN_ROWS, 128), jnp.bfloat16),
+        in_specs=smem_specs(1) + hbm_specs(8),
+        out_specs=vmem_specs(1)[0],
+        scratch_shapes=[pltpu.SemaphoreType.DMA((4,))],
+        compiler_params=pltpu.CompilerParams(vmem_limit_bytes=56 * 2**20),
+        name="pick",
+    )(meta, *pieces)
+
+
+def centred_norm(values):
+    centred = values - jnp.mean(values, axis=-1, keepdims=True)
+    inv_std = lax.rsqrt(jnp.mean(centred * centred, axis=-1, keepdims=True) + ln_eps)
+    return centred * inv_std, inv_std
+
+
+def front_kernel(meta, scales, *refs):
+    pieces, quarters = refs[:8], refs[8:12]
+    mod, cosine, sine = refs[12:15]
+    weights_out, mid_out, hidden_out, resid_out = refs[15:19]
+    head_outs = refs[19:23]
+    noisy_out, target_out, mod_out = refs[23:26]
+    tokens, heads, weights, mid, hidden, resid, target, mod_own, held, sems, out_sems = refs[26:]
+    copies = [
+        pltpu.make_async_copy(
+            pieces[place].at[TOKEN_ROWS:RING_ROWS, :], held.at[place], sems.at[place]
+        )
+        for place in range(8)
+    ]
+    for copy in copies:
+        copy.start()
+    for source in range(4):
+        rows = pl.ds(pl.multiple_of(meta[20 + source] * 64, 64), 64)
+        for frame in range(4):
+            base = 128 * (frame ^ source)
+            clean = quarters[source][base : base + 64, :].astype(jnp.float32)
+            noise = quarters[source][base + 64 : base + 128, :].astype(jnp.float32)
+            mixed = scales[frame] * clean + scales[4 + frame] * noise
+            tokens[frame, rows, :] = mixed.astype(jnp.bfloat16)
+            if frame == 0:
+                target[rows, :] = scales[0] * noise - scales[4] * clean
+    outs = [
+        pltpu.make_async_copy(tokens.at[0], noisy_out, out_sems.at[0]),
+        pltpu.make_async_copy(target, target_out, out_sems.at[1]),
+        pltpu.make_async_copy(weights, weights_out, out_sems.at[2]),
+        pltpu.make_async_copy(resid, resid_out, out_sems.at[3]),
+    ] + [
+        pltpu.make_async_copy(hidden.at[frame], hidden_out.at[frame], out_sems.at[4 + frame])
+        for frame in range(4)
+    ]
+    outs.append(pltpu.make_async_copy(mod_own, mod_out, out_sems.at[8]))
+    outs.append(pltpu.make_async_copy(mid, mid_out, out_sems.at[9]))
+    for place in range(8):
+        copies[place].wait()
+        block = pl.ds(pl.multiple_of(meta[place] * 128, 128), 128)
+        weights[:, block] = held[place, 0:FRONT_ROWS, :]
+        for part in range(3):
+            base = FRONT_ROWS + 128 * part
+            mid[block, 128 * part : 128 * part + 128] = held[place, base : base + 128, :]
+    for index in (0, 1, 2, 9):
+        outs[index].start()
+    embed = weights[QKV_ROWS : QKV_ROWS + 128, :]
+    vec_rows = weights[QKV_ROWS + 128 : FRONT_ROWS, :].astype(jnp.float32)
+    mod_own[0:6, :] = mod[0] + vec_rows[0:6]
+    mod_own[6:8, :] = vec_rows[6:8]
+    outs[8].start()
+    for frame in range(4):
+        values = jnp.dot(tokens[frame], embed, preferred_element_type=jnp.float32) + vec_rows[6:7]
+        if frame == 0:
+            resid[...] = values
+            outs[3].start()
+        normed, _ = centred_norm(values)
+        shift = mod[frame, 0:1, :] + vec_rows[0:1]
+        scale = mod[frame, 1:2, :] + vec_rows[1:2]
+        low = (normed * (1.0 + scale) + shift).astype(jnp.bfloat16)
+        hidden[frame] = low
+        outs[4 + frame].start()
+        mixed = lax.dot_general(
+            weights[0:QKV_ROWS, :], low, NT, preferred_element_type=jnp.float32
+        )
+        cos_now = cosine[meta[8 + frame]]
+        sin_now = sine[meta[8 + frame]]
+        cols = slice(256 * frame, 256 * frame + 256)
+        for head in range(4):
+            where_to = head
+            for part in range(2):
+                base = 256 * part + 64 * head
+                upper = mixed[base : base + 32]
+                lower = mixed[base + 32 : base + 64]
+                heads[where_to, 64 * part : 64 * part + 32, cols] = (
+                    upper * cos_now - lower * sin_now
+                ).astype(jnp.bfloat16)
+                heads[where_to, 64 * part + 32 : 64 * part + 64, cols] = (
+                    lower * cos_now + upper * sin_now
+                ).astype(jnp.bfloat16)
+            base = 512 + 64 * head
+            heads[where_to, 128:192, cols] = mixed[base : base + 64].astype(jnp.bfloat16)
+    for k in range(4):
+        outs.append(pltpu.make_async_copy(heads.at[meta[12 + k]], head_outs[k], out_sems.at[10 + k]))
+        outs[10 + k].start()
+    for copy in outs:
+        copy.wait()
+
+
+def call_front(meta, scales, pieces, quarters, mod, cosine, sine):
+    return pl.pallas_call(
+        front_kernel,
+        out_shape=(
+            jax.ShapeDtypeStruct((FRONT_ROWS, D), jnp.bfloat16),
+            jax.ShapeDtypeStruct((D, 384), jnp.bfloat16),
+            jax.ShapeDtypeStruct((4, PATCHES, D), jnp.bfloat16),
+            jax.ShapeDtypeStruct((PATCHES, D), jnp.float32),
+        )
+        + (jax.ShapeDtypeStruct((192, 4 * PATCHES), jnp.bfloat16),) * 4
+        + (
+            jax.ShapeDtypeStruct((PATCHES, 128), jnp.bfloat16),
+            jax.ShapeDtypeStruct((PATCHES, 128), jnp.float32),
+            jax.ShapeDtypeStruct((8, D), jnp.float32),
+        ),
+        in_specs=smem_specs(2) + hbm_specs(8) + vmem_specs(7),
+        out_specs=hbm_specs(11),
+        scratch_shapes=[
+            pltpu.VMEM((4, PATCHES, 128), jnp.bfloat16),
+            pltpu.VMEM((4, 192, 4 * PATCHES), jnp.bfloat16),
+            pltpu.VMEM((FRONT_ROWS, D), jnp.bfloat16),
+            pltpu.VMEM((D, 384), jnp.bfloat16),
+            pltpu.VMEM((4, PATCHES, D), jnp.bfloat16),
+            pltpu.VMEM((PATCHES, D), jnp.float32),
+            pltpu.VMEM((PATCHES, 128), jnp.float32),
+            pltpu.VMEM((8, D), jnp.float32),
+            pltpu.VMEM((8, FRONT_ROWS + 384, 128), jnp.bfloat16),
+            pltpu.SemaphoreType.DMA((8,)),
+            pltpu.SemaphoreType.DMA((14,)),
+        ],
+        compiler_params=pltpu.CompilerParams(vmem_limit_bytes=52 * 2**20),
+        cost_estimate=pl.CostEstimate(flops=2 * 10**9, bytes_accessed=10**7, transcendentals=0),
+        name="front",
+    )(meta, scales, *pieces, *quarters, mod, cosine, sine)
+
+
+def total_own(held, came, across):
+    return held[...] + came[...].astype(jnp.float32) + across[...].astype(jnp.float32)
+
+
+def middle_kernel(held, came, across, resid, mod, attn_out, resid_mid, hidden):
+    total = total_own(held, came, across)
+    attn_out[...] = total
+    values = resid[...] + mod[2:3, :] * total
+    resid_mid[...] = values
+    normed, _ = centred_norm(values)
+    hidden[...] = (normed * (1.0 + mod[4:5, :]) + mod[3:4, :]).astype(jnp.bfloat16)
+
+
+def row_call(kernel, name, outs, *operands, smem=0):
+    return pl.pallas_call(
+        kernel,
+        out_shape=tuple(outs),
+        in_specs=smem_specs(smem) + vmem_specs(len(operands) - smem),
+        out_specs=vmem_specs(len(outs)),
+        compiler_params=pltpu.CompilerParams(vmem_limit_bytes=16 * 2**20),
+        cost_estimate=pl.CostEstimate(flops=10**9, bytes_accessed=4 * 10**6, transcendentals=0),
+        name=name,
+    )(*operands)
+
+
+def frame_f32():
+    return jax.ShapeDtypeStruct((PATCHES, D), jnp.float32)
+
+
+def frame_low():
+    return jax.ShapeDtypeStruct((PATCHES, D), jnp.bfloat16)
+
+
+def back_through_norm(grad, normed, inv_std):
+    mean_grad = jnp.mean(grad, axis=-1, keepdims=True)
+    mean_proj = jnp.mean(grad * normed, axis=-1, keepdims=True)
+    return inv_std * (grad - mean_grad - normed * mean_proj)
+
+
+def column_sum(values):
+    return jnp.sum(values, axis=0, keepdims=True)
+
+
+def loss_kernel(
+    scales, held, came, across, resid_mid, mod, mid, target, grad_low, grad_three, io_rows, gate, error
+):
+    mlp_out = total_own(held, came, across)
+    values = resid_mid[...] + mod[5:6, :] * mlp_out
+    normed, inv_std = centred_norm(values)
+    gain = mod[7:8, :]
+    final = (normed * gain).astype(jnp.bfloat16)
+    head = mid[:, 256:384]
+    pred = jnp.dot(final, head, preferred_element_type=jnp.float32)
+    diff = pred - target[...]
+    per_token = jnp.sum(diff * diff, axis=1, keepdims=True)
+    error[...] = jnp.broadcast_to(
+        scales[0] * jnp.sum(per_token, axis=0, keepdims=True) / diff.shape[1], error.shape
+    )
+    grad_pred = (scales[1] * diff).astype(jnp.bfloat16)
+    grad_final = lax.dot_general(grad_pred, head, NT, preferred_element_type=jnp.float32)
+    grad_gain = column_sum(grad_final * normed)
+    grad = back_through_norm(grad_final * gain, normed, inv_std)
+    grad_three[...] = grad
+    grad_low[...] = (mod[5:6, :] * grad).astype(jnp.bfloat16)
+    gate[...] = column_sum(grad * mlp_out)
+    io_rows[0:128, :] = lax.dot_general(grad_pred, final, TN, preferred_element_type=jnp.float32)
+    io_rows[128:136, :] = jnp.concatenate([grad_gain, jnp.zeros((7, D), jnp.float32)], axis=0)
+
+
+def second_kernel(
+    held, came, across, resid_mid, mod, grad_three, attn_out, grad_low, grad_mid, rows
+):
+    grad_hidden = total_own(held, came, across)
+    normed, inv_std = centred_norm(resid_mid[...])
+    grad = grad_three[...] + back_through_norm(grad_hidden * (1.0 + mod[4:5, :]), normed, inv_std)
+    grad_mid[...] = grad
+    grad_low[...] = (mod[2:3, :] * grad).astype(jnp.bfloat16)
+    rows[0:1, :] = column_sum(grad * attn_out[...])
+    rows[1:2, :] = column_sum(grad_hidden)
+    rows[2:3, :] = column_sum(grad_hidden * normed)
+
+
+def first_kernel(
+    device,
+    held,
+    came,
+    across,
+    resid,
+    mod,
+    grad_mid,
+    noisy,
+    rows_two,
+    gate_two,
+    head_rows,
+    mod_rows,
+    near_held,
+    near_away,
+    far_held,
+    far_away,
+    io_rows,
+):
+    grad_hidden = total_own(held, came, across)
+    normed, inv_std = centred_norm(resid[...])
+    grad = grad_mid[...] + back_through_norm(grad_hidden * (1.0 + mod[1:2, :]), normed, inv_std)
+    rows = [
+        column_sum(grad_hidden),
+        column_sum(grad_hidden * normed),
+        rows_two[0:1, :],
+        rows_two[1:2, :],
+        rows_two[2:3, :],
+        gate_two[...],
+    ]
+    blocks = [row[:, 128 * k : 128 * k + 128] for row in rows for k in range(8)]
+    mod_rows[...] = jnp.concatenate(blocks, axis=0).astype(jnp.bfloat16)
+    io_rows[0:128, :] = lax.dot_general(
+        noisy[...], grad.astype(jnp.bfloat16), TN, preferred_element_type=jnp.float32
+    )
+    io_rows[128:256, :] = head_rows[0:128, :]
+    io_rows[256:264, :] = jnp.concatenate(
+        [column_sum(grad), head_rows[128:129, :], jnp.zeros((6, D), jnp.float32)], axis=0
+    )
+    io_rows[264:320, :] = jnp.zeros((56, D), jnp.float32)
+    for k, out in enumerate((near_held, near_away, far_held, far_away)):
+        group = pl.ds(pl.multiple_of(IO_ROWS * (device[1] ^ k), 16), IO_ROWS)
+        out[...] = io_rows[group, :].astype(out.dtype)
+
+
+def side_kernel(device, held, came, across, mod_rows, keep, away):
+    total = total_own(held, came, across)
+    side = device[0] & 1
+    for block in range(8):
+        piece = total[:, 128 * block : 128 * block + 128]
+
+        @pl.when(side == block % 2)
+        def _():
+            keep[block // 2] = piece
+
+        @pl.when(side != block % 2)
+        def _():
+            away[IO_ROWS * (block // 2) : IO_ROWS * (block // 2) + IO_ROWS, :] = piece.astype(
+                jnp.bfloat16
+            )
+
+    away[4 * IO_ROWS :, :] = mod_rows[...]
+
+
+def merge_kernel(
+    device, held, came, out_held, out_came, io_held, io_came, mod_rows, own, io_own, *outs
+):
+    z = device[0] >> 1
+    for bit in range(4):
+        total = jnp.concatenate(
+            [
+                held[z ^ bit] + came[z ^ bit].astype(jnp.float32),
+                out_held[z ^ bit] + out_came[z ^ bit].astype(jnp.float32),
+            ],
+            axis=0,
+        )
+        rows = pl.ds(pl.multiple_of(IO_ROWS * (z ^ bit), 16), IO_ROWS)
+        io_total = io_held[z ^ bit] + io_came[rows, :].astype(jnp.float32)
+        if bit == 0:
+            own[...] = total
+            io_own[...] = io_total
+        else:
+            out = outs[bit]
+            out[0:ATTN_ROWS, :] = total.astype(jnp.bfloat16)
+            out[ATTN_ROWS : ATTN_ROWS + IO_ROWS, :] = io_total.astype(jnp.bfloat16)
+            base = ATTN_ROWS + IO_ROWS
+            out[base : base + MOD_ROWS, :] = mod_rows[...]
+            out[base + MOD_ROWS : base + 2 * MOD_ROWS, :] = io_came[4 * IO_ROWS :, :]
+    outs[0][0:MOD_ROWS, :] = mod_rows[...]
+    outs[0][MOD_ROWS : 2 * MOD_ROWS, :] = io_came[4 * IO_ROWS :, :]
+
+
+def mod_grad_kernel(device, cond, *refs):
+    parts = refs[:4]
+    grad, vector, io_grad, square, rows = refs[4:]
+    for index in range(4):
+        for frame in range(8):
+            block = parts[index][MOD_ROWS * frame : MOD_ROWS * frame + MOD_ROWS, :].astype(
+                jnp.float32
+            )
+            at = 8 * index + frame
+            for k in range(MOD_ROWS):
+                rows[at : at + 1, 128 * k : 128 * k + 128] = block[k : k + 1, :]
+        base = 8 * MOD_ROWS
+        group = pl.ds(pl.multiple_of(IO_ROWS * (device[1] ^ index), 16), IO_ROWS)
+        io_grad[group, :] = parts[index][base : base + IO_ROWS, :].astype(jnp.float32) + parts[
+            index
+        ][base + IO_ROWS : base + 2 * IO_ROWS, :].astype(jnp.float32)
+    total = jnp.zeros((1, 1), jnp.float32)
+    for index in range(6):
+        cols = slice(D * index, D * index + D)
+        part = lax.dot_general(
+            cond[...], rows[:, cols].astype(jnp.bfloat16), TN, preferred_element_type=jnp.float32
+        )
+        grad[:, cols] = part
+        total = total + jnp.sum(column_sum(part * part), axis=1, keepdims=True)
+        own = pl.ds(pl.multiple_of(D * index + 128 * device[0], 128), 128)
+        vector[index : index + 1, :] = column_sum(rows[:, own])
+    vector[6:8, :] = io_grad[256:258, :]
+    mixed = vector[0:6, :]
+    total = total + jnp.sum(column_sum(mixed * mixed), axis=1, keepdims=True)
+    square[...] = jnp.broadcast_to(total, square.shape)
+
+
+def call_mod_grad(device, cond, parts):
+    return pl.pallas_call(
+        mod_grad_kernel,
+        out_shape=(
+            jax.ShapeDtypeStruct((128, 6 * D), jnp.float32),
+            jax.ShapeDtypeStruct((8, 128), jnp.float32),
+            jax.ShapeDtypeStruct((4 * IO_ROWS, 128), jnp.float32),
+            jax.ShapeDtypeStruct((1, 128), jnp.float32),
+        ),
+        in_specs=smem_specs(1) + vmem_specs(5),
+        out_specs=vmem_specs(4),
+        scratch_shapes=[pltpu.VMEM((32, 6 * D), jnp.float32)],
+        compiler_params=pltpu.CompilerParams(vmem_limit_bytes=12 * 2**20),
+        cost_estimate=pl.CostEstimate(flops=10**8, bytes_accessed=4 * 10**6, transcendentals=0),
+        name="mod_grad",
+    )(device, cond, *parts)
+
+
+def mlp_kernel(first, second, weights, held, away, active, slope):
+    for frame, source in enumerate((first, second)):
+        rows = slice(256 * frame, 256 * frame + 256)
+        upward = jnp.dot(source[...], weights[0], preferred_element_type=jnp.float32)
+        inner = 0.5 * (1.0 + lax.erf(upward * (1.0 / math.sqrt(2.0))))
+        low = (upward * inner).astype(jnp.bfloat16)
+        active[rows, :] = low
+        change = inner + upward * jnp.exp(-0.5 * upward * upward) * (
+            1.0 / math.sqrt(2.0 * math.pi)
+        )
+        slope[rows, :] = change.astype(jnp.bfloat16)
+        part = lax.dot_general(low, weights[1], NT, preferred_element_type=jnp.float32)
+        if frame:
+            away[...] = part.astype(jnp.bfloat16)
+        else:
+            held[...] = part
+
+
+def mlp_back_kernel(first, second, weights, slope, held, away, grad_up):
+    for frame, source in enumerate((first, second)):
+        rows = slice(256 * frame, 256 * frame + 256)
+        grad = jnp.dot(source[...], weights[1], preferred_element_type=jnp.float32)
+        low = (grad * slope[rows, :].astype(jnp.float32)).astype(jnp.bfloat16)
+        grad_up[rows, :] = low
+        part = lax.dot_general(low, weights[0], NT, preferred_element_type=jnp.float32)
+        if frame:
+            away[...] = part.astype(jnp.bfloat16)
+        else:
+            held[...] = part
+
+
+def call_mlp(kernel, name, outs, *operands):
+    return pl.pallas_call(
+        kernel,
+        out_shape=(frame_f32(), frame_low()) + outs,
+        in_specs=vmem_specs(len(operands)),
+        out_specs=vmem_specs(2 + len(outs)),
+        compiler_params=pltpu.CompilerParams(vmem_limit_bytes=16 * 2**20),
+        cost_estimate=pl.CostEstimate(
+            flops=4 * 10**9, bytes_accessed=2 * 10**7, transcendentals=10**6
+        ),
+        name=name,
+    )(*operands)
+
+
+def weight_grad_kernel(*refs):
+    hidden, grads = refs[:4], refs[4:8]
+    grad_up, active = refs[8:10], refs[10:12]
+    result, out, sems = refs[12:]
+    width = active[0].shape[1]
+    copies = []
+    for index, (left, right) in enumerate(((hidden, grad_up), (grads, active))):
+        total = jnp.zeros((D, width), jnp.float32)
+        for frame in range(4):
+            rows = slice(256 * (frame % 2), 256 * (frame % 2) + 256)
+            total = total + lax.dot_general(
+                left[frame][...],
+                right[frame // 2][rows, :],
+                TN,
+                preferred_element_type=jnp.float32,
+            )
+        out[index] = total.astype(jnp.bfloat16)
+        copies.append(
+            pltpu.make_async_copy(
+                out.at[index], result.at[:, width * index : width * index + width], sems.at[index]
+            )
+        )
+        copies[index].start()
+    for copy in copies:
+        copy.wait()
+
+
+def call_weight_grad(hidden, grads, grad_up, active):
+    operands = (*hidden, *grads, *grad_up, *active)
+    return pl.pallas_call(
+        weight_grad_kernel,
+        out_shape=jax.ShapeDtypeStruct((D, 2 * active[0].shape[1]), jnp.bfloat16),
+        in_specs=vmem_specs(len(operands)),
+        out_specs=hbm_specs(1)[0],
+        scratch_shapes=[
+            pltpu.VMEM((2, D, active[0].shape[1]), jnp.bfloat16),
+            pltpu.SemaphoreType.DMA((2,)),
+        ],
+        compiler_params=pltpu.CompilerParams(vmem_limit_bytes=20 * 2**20),
+        cost_estimate=pl.CostEstimate(flops=5 * 10**9, bytes_accessed=2 * 10**7, transcendentals=0),
+        name="weight_grad",
+    )(*operands)
+
+
+def side_blocks(device, total, held, away):
+    side = device[0] & 1
+    for z in range(4):
+        held[z] = total[:, pl.ds(pl.multiple_of(256 * z + 128 * side, 128), 128)]
+        away[z] = total[:, pl.ds(pl.multiple_of(256 * z + 128 * (1 - side), 128), 128)].astype(
+            jnp.bfloat16
+        )
+
+
+def head_grad_kernel(device, left, right, held, away, total):
+    total[...] = jnp.dot(left[...], right[...], preferred_element_type=jnp.float32)
+    side_blocks(device, total, held, away)
+
+
+def call_head_grad(device, left, right):
+    rows = left.shape[0]
+    return pl.pallas_call(
+        head_grad_kernel,
+        out_shape=(
+            jax.ShapeDtypeStruct((4, rows, 128), jnp.float32),
+            jax.ShapeDtypeStruct((4, rows, 128), jnp.bfloat16),
+        ),
+        in_specs=smem_specs(1) + vmem_specs(2),
+        out_specs=vmem_specs(2),
+        scratch_shapes=[pltpu.VMEM((rows, D), jnp.float32)],
+        compiler_params=pltpu.CompilerParams(vmem_limit_bytes=12 * 2**20),
+        cost_estimate=pl.CostEstimate(flops=2 * 10**9, bytes_accessed=10**7, transcendentals=0),
+        name="head_grad",
+    )(device, left, right)
+
+
+def qkv_back_kernel(meta, *refs):
+    blocks, weights = refs[:4], refs[4]
+    grads, near_held, near_away, far_held, far_away = refs[5:]
+    for k in range(4):
+        head = meta[0] ^ k
+        for part in range(3):
+            rows = pl.ds(pl.multiple_of(256 * part + 64 * head, 64), 64)
+            grads[rows, :] = blocks[k][64 * part : 64 * part + 64, :]
+    for frame, out in ((2, far_held), (3, far_away), (0, near_held), (1, near_away)):
+        part = lax.dot_general(
+            grads[:, 256 * frame : 256 * frame + 256],
+            weights[0:QKV_ROWS, :],
+            TN,
+            preferred_element_type=jnp.float32,
+        )
+        out[...] = part.astype(out.dtype)
+
+
+def call_qkv_back(meta, blocks, weights):
+    return row_call(
+        qkv_back_kernel,
+        "qkv_back",
+        (
+            jax.ShapeDtypeStruct((QKV_ROWS, 4 * PATCHES), jnp.bfloat16),
+            frame_f32(),
+            frame_low(),
+            frame_f32(),
+            frame_low(),
+        ),
+        meta,
+        *blocks,
+        weights,
+        smem=1,
+    )
+
+
+def adam_step(weight_now, first_mom, second_mom, grad, scale, rate, decay):
+    factor, first_fix, second_fix = scale
+    grad = grad * factor
+    first_mom = beta_one * first_mom + (1.0 - beta_one) * grad
+    second_mom = beta_two * second_mom + (1.0 - beta_two) * grad * grad
+    updated = weight_now - rate * (
+        first_mom * first_fix / (jnp.sqrt(second_mom * second_fix) + adam_eps) + decay * weight_now
+    )
+    return updated, first_mom, second_mom, updated.astype(jnp.bfloat16)
+
+
+def adam_kernel(*refs):
+    fixes, sums = refs[0], refs[1:5]
+    groups = [refs[5 + 4 * k : 9 + 4 * k] for k in range(3)]
+    io_in, vec_in = refs[17:21], refs[21:25]
+    outs = [refs[25 + 4 * k : 29 + 4 * k] for k in range(3)]
+    io_out, vec_out, norm_out = refs[37:42], refs[42:46], refs[46]
+    slots, low_slots, sems = refs[47:]
+    total = (sums[0][...] + sums[1][...]) + (sums[2][...] + sums[3][...])
+    norm = jnp.sqrt(total)
+    norm_out[0:1, :] = norm
+    norm_out[1:2, :] = total
+    factor = jnp.minimum(1.0, clip_limit / (norm[:, 0:1] + 1e-06))
+    scale = (factor, fixes[0], fixes[1])
+    tasks = []
+    for k, group in enumerate(groups):
+        rows, width = group[0].shape[-2:]
+        for lead in range(group[0].shape[0] if len(group[0].shape) == 3 else 1):
+            for col in range(0, width, 1024):
+                span = min(1024, width - col)
+                tasks.append((k, lead, col, span))
+    running = {}
+    for number, (k, lead, col, span) in enumerate(tasks):
+        slot = number % 4
+        if number >= 4:
+            for copy in running.pop(number - 4):
+                copy.wait()
+        cut = (slice(None), slice(col, col + span))
+        if len(groups[k][0].shape) == 3:
+            cut = (lead,) + cut
+        values = [ref[cut].astype(jnp.float32) for ref in groups[k]]
+        results = adam_step(*values, scale, rate_matrix, decay_rate)
+        copies = []
+        for index, result in enumerate(results):
+            source = low_slots.at[slot] if index == 3 else slots.at[slot, index]
+            source = source.at[:, 0:span]
+            source[...] = result
+            copies.append(
+                pltpu.make_async_copy(source, outs[k][index].at[cut], sems.at[slot, index])
+            )
+            copies[index].start()
+        running[number] = copies
+    results = adam_step(*(ref[...] for ref in io_in), scale, rate_matrix, decay_rate)
+    io_out[0][...] = results[0]
+    io_out[1][...] = results[1]
+    io_out[2][...] = results[2][0]
+    io_out[3][...] = results[2][1]
+    io_out[4][...] = results[3]
+    results = adam_step(*(ref[...] for ref in vec_in), scale, rate_vector, 0.0)
+    for out, result in zip(vec_out, results):
+        out[...] = result
+    for copies in running.values():
+        for copy in copies:
+            copy.wait()
+
+
+def call_adam(fixes, sums, groups, io_group, vec_group):
+    operands = [*sums, *(array for group in groups for array in group), *io_group, *vec_group]
+
+    def results(group):
+        low = jax.ShapeDtypeStruct(group[0].shape, jnp.bfloat16)
+        return (jax.ShapeDtypeStruct(group[0].shape, jnp.float32),) * 3 + (low,)
+
+    io_like = results(io_group)
+    half = jax.ShapeDtypeStruct(io_group[0].shape[1:], jnp.float32)
+    out_shape = sum((results(group) for group in groups), ())
+    out_shape = out_shape + io_like[:2] + (half, half) + io_like[3:] + results(vec_group)
+    out_shape = out_shape + (jax.ShapeDtypeStruct((2, 128), jnp.float32),)
+    return pl.pallas_call(
+        adam_kernel,
+        out_shape=out_shape,
+        in_specs=smem_specs(1) + vmem_specs(len(operands)),
+        out_specs=hbm_specs(12) + vmem_specs(10),
+        scratch_shapes=[
+            pltpu.VMEM((4, 3, 128, 1024), jnp.float32),
+            pltpu.VMEM((4, 128, 1024), jnp.bfloat16),
+            pltpu.SemaphoreType.DMA((4, 4)),
+        ],
+        compiler_params=pltpu.CompilerParams(vmem_limit_bytes=20 * 2**20),
+        cost_estimate=pl.CostEstimate(flops=10**7, bytes_accessed=2 * 10**7, transcendentals=0),
+        name="adam",
+    )(fixes, *operands)
+
+
+def finish_kernel(*refs):
+    own, io_own, mod_own, pieces = refs[0], refs[1], refs[2], refs[3:6]
+    scattered, grad, spread, square = refs[6:]
+    total = own[...]
+    io_total = io_own[...]
+    spread[0 : 2 * MOD_ROWS, :] = mod_own[...]
+    for index, piece in enumerate(pieces):
+        total = total + piece[0:ATTN_ROWS, :].astype(jnp.float32)
+        base = ATTN_ROWS + IO_ROWS
+        io_total = io_total + piece[ATTN_ROWS:base, :].astype(jnp.float32)
+        spread[2 * MOD_ROWS * (index + 1) : 2 * MOD_ROWS * (index + 2), :] = piece[base:, :]
+    high = io_total.astype(jnp.bfloat16)
+    base = 8 * MOD_ROWS
+    spread[base : base + IO_ROWS, :] = high
+    spread[base + IO_ROWS :, :] = (io_total - high.astype(jnp.float32)).astype(jnp.bfloat16)
+    for part in range(4):
+        grad[part] = total[256 * part : 256 * part + 256].T
+    rest = scattered[...].astype(jnp.float32)
+    squares = jnp.zeros((1, 1), jnp.float32)
+    for values in (total, rest, io_total):
+        squares = squares + jnp.sum(column_sum(values * values), axis=1, keepdims=True)
+    square[...] = jnp.broadcast_to(squares, square.shape)
+
+
+def turn(block):
+    return block.astype(jnp.float32).T.astype(jnp.bfloat16)
+
+
+def query_rows(meta, pair):
+    first = 2 * pair
+    start_first = first - meta[2 + first]
+    start_second = first + 1 - meta[3 + first]
+    left = lax.broadcasted_iota(jnp.int32, (1, 2 * PATCHES), 1) < PATCHES
+    upto = jnp.where(left, first, first + 1)
+    since = jnp.where(left, start_first, start_second)
+    return jnp.minimum(start_first, start_second), since, upto
+
+
+def attend_kernel(meta, *refs):
+    blocks = refs[:4]
+    outs = refs[4:8]
+    lse, mixed, query, key, value = refs[8:]
+    for member in range(4):
+        for frame in range(4):
+            slot = 4 * (meta[0] ^ member) + (meta[1] ^ frame)
+            cols = slice(256 * frame, 256 * frame + 256)
+            lanes = pl.ds(pl.multiple_of((slot % 2) * 256, 256), 256)
+            query[slot // 2, :, lanes] = blocks[member][0:64, cols] * 0.125
+            key[slot // 2, lanes, :] = turn(blocks[member][64:128, cols])
+            value[slot // 2, :, lanes] = blocks[member][128:192, cols]
+
+    def per_pair(pair, carry):
+        low, since, upto = query_rows(meta, pair)
+        wanted = query[pair]
+
+        def per_keys(keys, state):
+            top, total, acc = state
+            both = jnp.dot(key[keys], wanted, preferred_element_type=jnp.float32)
+            scores = []
+            new_top = top
+            for side in range(2):
+                slot = 2 * keys + side
+                bias = jnp.where((slot >= since) & (slot <= upto), 0.0, neg_large)
+                scores.append(both[256 * side : 256 * side + 256] + bias)
+                new_top = jnp.maximum(new_top, jnp.max(scores[side], axis=0, keepdims=True))
+            probs = [jnp.exp(values - new_top) for values in scores]
+            shrink = jnp.exp(top - new_top)
+            total = total * shrink + jnp.sum(probs[0] + probs[1], axis=0, keepdims=True)
+            low_probs = jnp.concatenate([values.astype(jnp.bfloat16) for values in probs], axis=0)
+            acc = acc * shrink + jnp.dot(
+                value[keys], low_probs, preferred_element_type=jnp.float32
+            )
+            return (new_top, total, acc)
+
+        top, total, acc = lax.fori_loop(
+            low // 2,
+            pair + 1,
+            per_keys,
+            (
+                jnp.full((1, 2 * PATCHES), neg_large, jnp.float32),
+                jnp.zeros((1, 2 * PATCHES), jnp.float32),
+                jnp.zeros((HD, 2 * PATCHES), jnp.float32),
+            ),
+        )
+        lse[pair] = top + jnp.log(total)
+        mixed[pair] = acc / total
+        return carry
+
+    lax.fori_loop(0, 8, per_pair, 0)
+    for member in range(4):
+        for frame in range(4):
+            slot = 4 * (meta[0] ^ member) + (meta[1] ^ frame)
+            lanes = pl.ds(pl.multiple_of((slot % 2) * 256, 256), 256)
+            outs[member][:, 256 * frame : 256 * frame + 256] = mixed[slot // 2, :, lanes].astype(
+                jnp.bfloat16
+            )
+
+
+def call_attend(meta, blocks):
+    vmem = pl.BlockSpec(memory_space=pltpu.VMEM)
+    result = pl.pallas_call(
+        attend_kernel,
+        out_shape=tuple(jax.ShapeDtypeStruct((HD, 4 * PATCHES), jnp.bfloat16) for _ in range(4))
+        + (
+            jax.ShapeDtypeStruct((8, 1, 2 * PATCHES), jnp.float32),
+            jax.ShapeDtypeStruct((8, HD, 2 * PATCHES), jnp.float32),
+        ),
+        in_specs=[pl.BlockSpec(memory_space=pltpu.SMEM)] + [vmem] * 4,
+        out_specs=(vmem,) * 6,
+        scratch_shapes=[
+            pltpu.VMEM((8, HD, 2 * PATCHES), jnp.bfloat16),
+            pltpu.VMEM((8, 2 * PATCHES, HD), jnp.bfloat16),
+            pltpu.VMEM((8, HD, 2 * PATCHES), jnp.bfloat16),
+        ],
+        compiler_params=pltpu.CompilerParams(vmem_limit_bytes=16 * 2**20),
+        cost_estimate=pl.CostEstimate(flops=9 * 10**9, bytes_accessed=5 * 10**6, transcendentals=10**7),
+        name="attend",
+    )(meta, *blocks)
+    return list(result[:4]), result[4], result[5]
+
+
+def attend_back_kernel(meta, *refs):
+    blocks = refs[:4]
+    grads = refs[4:8]
+    lse, mixed, cosine, sine = refs[8:12]
+    outs = refs[12:16]
+    query, query_flat, key, key_flat, value_flat, grad, grad_flat, sum_key, sum_value, sum_query = (
+        refs[16:]
+    )
+    for member in range(4):
+        for frame in range(4):
+            slot = 4 * (meta[0] ^ member) + (meta[1] ^ frame)
+            cols = slice(256 * frame, 256 * frame + 256)
+            place = pl.ds(pl.multiple_of((slot % 2) * 256, 256), 256)
+            part = blocks[member][0:64, cols] * 0.125
+            query[slot // 2, :, place] = part
+            query_flat[slot // 2, place, :] = turn(part)
+            part = blocks[member][64:128, cols]
+            key[slot // 2, :, place] = part
+            key_flat[slot // 2, place, :] = turn(part)
+            value_flat[slot // 2, place, :] = turn(blocks[member][128:192, cols])
+            part = grads[member][:, cols]
+            grad[slot // 2, :, place] = part
+            grad_flat[slot // 2, place, :] = turn(part)
+    sum_key[...] = jnp.zeros_like(sum_key)
+    sum_value[...] = jnp.zeros_like(sum_value)
+
+    def per_pair(pair, carry):
+        low, since, upto = query_rows(meta, pair)
+        wanted = query[pair]
+        wanted_grad = grad[pair]
+        delta = jnp.sum(wanted_grad.astype(jnp.float32) * mixed[pair], axis=0, keepdims=True)
+        level = lse[pair]
+
+        def per_keys(keys, acc):
+            scores = jnp.dot(key_flat[keys], wanted, preferred_element_type=jnp.float32)
+            grad_probs = jnp.dot(
+                value_flat[keys], wanted_grad, preferred_element_type=jnp.float32
+            )
+            low_probs, low_scores = [], []
+            for side in range(2):
+                rows = slice(256 * side, 256 * side + 256)
+                slot = 2 * keys + side
+                bias = jnp.where((slot >= since) & (slot <= upto), -level, neg_large)
+                probs = jnp.exp(scores[rows] + bias)
+                low_probs.append(probs.astype(jnp.bfloat16))
+                low_scores.append((probs * (grad_probs[rows] - delta)).astype(jnp.bfloat16))
+            all_probs = jnp.concatenate(low_probs, axis=0)
+            all_scores = jnp.concatenate(low_scores, axis=0)
+            sum_value[keys] += jnp.dot(
+                all_probs, grad_flat[pair], preferred_element_type=jnp.float32
+            )
+            sum_key[keys] += jnp.dot(
+                all_scores, query_flat[pair], preferred_element_type=jnp.float32
+            )
+            return acc + jnp.dot(key[keys], all_scores, preferred_element_type=jnp.float32)
+
+        sum_query[pair] = lax.fori_loop(
+            low // 2, pair + 1, per_keys, jnp.zeros((HD, 2 * PATCHES), jnp.float32)
+        )
+        return carry
+
+    lax.fori_loop(0, 8, per_pair, 0)
+    for member in range(4):
+        for frame in range(4):
+            slot = 4 * (meta[0] ^ member) + (meta[1] ^ frame)
+            cols = slice(256 * frame, 256 * frame + 256)
+            place = pl.ds(pl.multiple_of((slot % 2) * 256, 256), 256)
+            cos_now = cosine[slot]
+            sin_now = sine[slot]
+            for base, part in (
+                (0, sum_query[slot // 2, :, place] * 0.125),
+                (64, sum_key[slot // 2, place, :].T),
+            ):
+                upper = part[0:32]
+                lower = part[32:64]
+                outs[member][base : base + 32, cols] = (
+                    upper * cos_now + lower * sin_now
+                ).astype(jnp.bfloat16)
+                outs[member][base + 32 : base + 64, cols] = (
+                    lower * cos_now - upper * sin_now
+                ).astype(jnp.bfloat16)
+            outs[member][128:192, cols] = sum_value[slot // 2, place, :].T.astype(jnp.bfloat16)
+
+
+def call_attend_back(meta, blocks, grads, lse, mixed, cosine, sine):
+    vmem = pl.BlockSpec(memory_space=pltpu.VMEM)
+    flat_pair = pltpu.VMEM((8, 2 * PATCHES, HD), jnp.bfloat16)
+    turned_pair = pltpu.VMEM((8, HD, 2 * PATCHES), jnp.bfloat16)
+    wide = pltpu.VMEM((8, 2 * PATCHES, HD), jnp.float32)
+    return list(
+        pl.pallas_call(
+            attend_back_kernel,
+            out_shape=tuple(
+                jax.ShapeDtypeStruct((192, 4 * PATCHES), jnp.bfloat16) for _ in range(4)
+            ),
+            in_specs=[pl.BlockSpec(memory_space=pltpu.SMEM)] + [vmem] * 12,
+            out_specs=(vmem,) * 4,
+            scratch_shapes=[
+                turned_pair,
+                flat_pair,
+                turned_pair,
+                flat_pair,
+                flat_pair,
+                turned_pair,
+                flat_pair,
+                wide,
+                wide,
+                pltpu.VMEM((8, HD, 2 * PATCHES), jnp.float32),
+            ],
+            compiler_params=pltpu.CompilerParams(vmem_limit_bytes=20 * 2**20),
+            cost_estimate=pl.CostEstimate(
+                flops=22 * 10**9, bytes_accessed=10**7, transcendentals=10**7
+            ),
+            name="attend_back",
+        )(meta, *blocks, *grads, lse, mixed, cosine, sine)
+    )
+
+
+def shards_halves(
+    clean,
+    noise,
+    levels,
+    lengths,
+    order,
+    step,
+    w_attn,
+    m_attn,
+    v_attn,
+    w_mlp,
+    m_mlp,
+    v_mlp,
+    w_mod,
+    m_mod,
+    v_mod,
+    w_io,
+    m_io,
+    v_io,
+    vectors,
+    m_vec,
+    v_vec,
+):
+    bfloat = jnp.bfloat16
+    single = jnp.float32
+    ctx_index = lax.axis_index("ctx")
+    tp_index = lax.axis_index("tp")
+    member = ctx_index % 4
+    device = jnp.stack([ctx_index, tp_index]).astype(jnp.int32)
+
+    pieces = ring_gather(call_prepare(device, clean, noise, w_attn, w_io, vectors))
+    front_meta, attend_meta, row_levels = call_place(device, lengths, order, levels)
+
+    half_dim = D // 2
+    column = ctx_index * 128 + jnp.arange(128, dtype=jnp.int32)
+    frequency = jnp.exp(-math.log(10000.0) * (column % half_dim).astype(single) / half_dim)
+    angle = row_levels.astype(single)[:, None] * frequency[None, :]
+    cond = jax.nn.silu(jnp.where(column[None, :] < half_dim, jnp.cos(angle), jnp.sin(angle)))
+    cond_low = cond.astype(bfloat)
+    cond_slots, cond_relative = cond_low[:32], cond_low[32:]
+    quarter_cols = 6 * D // 4
+    mod_cols = lax.dynamic_slice_in_dim(w_mod, tp_index * quarter_cols, quarter_cols, 1)
+    mod_part = jnp.dot(cond_slots, mod_cols.astype(bfloat), preferred_element_type=single)
+    mod_held = reduce_along_x(mod_part.reshape(8, 4, quarter_cols), ctx_index, single)
+    mod_held = after(mod_held, pieces[2], pieces[5])
+    mod_own = after(reduce_along_z(mod_held, ctx_index, single), pieces[3], pieces[6])
+    mod_quarters = reorder_four(spread_frames(mod_own), tp_index)
+    mod_all = jnp.concatenate(mod_quarters, axis=1)
+    mod_rel = jnp.stack(reorder_four([mod_all[k] for k in range(4)], tp_index))
+    mod_rel = mod_rel.reshape(4, 6, D)
+
+    time_pairs = HD // 8
+    side_pairs = (HD // 2 - time_pairs) // 2
+
+    def frequencies(count):
+        return 10000.0 ** (-jnp.arange(count, dtype=single) / count)
+
+    patch = jnp.arange(PATCHES, dtype=jnp.int32)
+    half_position = attend_meta[2:].astype(single)
+    time_angle = half_position[:, None] * frequencies(time_pairs)[None, :]
+    height_angle = frequencies(side_pairs)[:, None] * (patch // GRID).astype(single)[None, :]
+    width_angle = frequencies(side_pairs)[:, None] * (patch % GRID).astype(single)[None, :]
+    side_angle = jnp.concatenate([height_angle, width_angle], axis=0)
+
+    def full_table(time_part, side_part):
+        return jnp.concatenate(
+            [
+                jnp.broadcast_to(time_part[:, :, None], (HALF_SLOTS, time_pairs, PATCHES)),
+                jnp.broadcast_to(side_part[None], (HALF_SLOTS, 2 * side_pairs, PATCHES)),
+            ],
+            axis=1,
+        )
+
+    cosine = full_table(jnp.cos(time_angle), jnp.cos(side_angle))
+    sine = full_table(jnp.sin(time_angle), jnp.sin(side_angle))
+    signal_scale, noise_scale, weight = plan(row_levels)
+    weight_sum = PATCHES * jnp.sum(weight[:32])
+    token_scales = jnp.concatenate([signal_scale[32::8], noise_scale[32::8]])
+    loss_scales = jnp.stack([weight[32], 2.0 / clean.shape[1] * weight[32] / weight_sum])
+
+    front_meta = after(front_meta, mod_rel, cosine, sine, token_scales)
+    quarters = spread_frames(call_pick(front_meta, pieces))
+    front_all, mid_all, hidden_frames, resid_in, *head_blocks, noisy_low, target, mod_own = (
+        call_front(front_meta, token_scales, pieces, quarters, mod_rel, cosine, sine)
+    )
+    hidden_one = hidden_frames.reshape(4 * PATCHES, D)
+
+    out_w = mid_all[:, :256]
+
+    def exchange(blocks):
+        return [blocks[0]] + [swap(blocks[k], "ctx", k) for k in (1, 2, 3)]
+
+    head_in = exchange(head_blocks)
+    mlp_shard = after(w_mlp.astype(bfloat), *head_in)
+    mlp_w = lax.all_gather(mlp_shard, "ctx", axis=1, tiled=True)
+    mixed_blocks, lse, mixed = call_attend(attend_meta, head_in)
+    mix_low = jnp.concatenate(reorder_four(exchange(mixed_blocks), member), axis=0)
+
+    def project(left, right, dims):
+        pairs = []
+        for base in (2 * PATCHES, 0):
+            part = lax.dot_general(
+                left[:, base : base + 2 * PATCHES], right, dims, preferred_element_type=single
+            )
+            pairs.append((part[:PATCHES], part[PATCHES:].astype(bfloat)))
+        return pairs[1], pairs[0]
+
+    near, far = project(mix_low, out_w, (((0,), (1,)), ((), ())))
+    attn_out, resid_mid, hidden_own = row_call(
+        middle_kernel,
+        "middle",
+        (frame_f32(), frame_f32(), frame_low()),
+        *sum_frames(near, sum_across(far)),
+        resid_in,
+        mod_own,
+    )
+    hidden_list = spread_frames(hidden_own)
+    wide = (2 * PATCHES, w_mlp.shape[2])
+    wide_low = jax.ShapeDtypeStruct(wide, bfloat)
+    near = call_mlp(mlp_kernel, "mlp", (wide_low, wide_low), *hidden_list[:2], mlp_w)
+    far = call_mlp(mlp_kernel, "mlp", (wide_low, wide_low), *hidden_list[2:], mlp_w)
+    active, slope = (near[2], far[2]), (near[3], far[3])
+    grad_own, grad_three, head_rows, grad_gate_two, error_part = row_call(
+        loss_kernel,
+        "loss",
+        (
+            frame_low(),
+            frame_f32(),
+            jax.ShapeDtypeStruct((136, D), single),
+            jax.ShapeDtypeStruct((1, D), single),
+            jax.ShapeDtypeStruct((1, 128), single),
+        ),
+        loss_scales,
+        *sum_frames(near[:2], sum_across(far)),
+        resid_mid,
+        mod_own,
+        mid_all,
+        target,
+        smem=1,
+    )
+    grad_list = spread_frames(grad_own)
+    near = call_mlp(mlp_back_kernel, "mlp_back", (wide_low,), *grad_list[:2], mlp_w, slope[0])
+    far = call_mlp(mlp_back_kernel, "mlp_back", (wide_low,), *grad_list[2:], mlp_w, slope[1])
+    across = sum_across(far)
+    weight_grad = call_weight_grad(
+        hidden_list, grad_list, (near[2], after(far[2], across)), active
+    )
+    scattered = lax.psum_scatter(weight_grad, "ctx", scatter_dimension=0, tiled=True)
+    grad_low, grad_mid, rows_two = row_call(
+        second_kernel,
+        "second",
+        (frame_low(), frame_f32(), jax.ShapeDtypeStruct((3, D), single)),
+        *sum_frames(near[:2], across),
+        after(resid_mid, weight_grad),
+        mod_own,
+        grad_three,
+        attn_out,
+    )
+    back_list = spread_frames(grad_low)
+    grad_attn_low = jnp.concatenate(back_list, axis=0)
+    grad_mix = lax.dot_general(
+        out_w, grad_attn_low, (((0,), (1,)), ((), ())), preferred_element_type=single
+    ).astype(bfloat)
+    grad_blocks = reorder_four([grad_mix[HD * k : HD * k + HD] for k in range(4)], member)
+    grad_in_blocks = exchange(grad_blocks)
+    out_held, out_away = call_head_grad(device, mix_low, after(grad_attn_low, grad_mix))
+    out_came = swap(out_away, "ctx", 1)
+    grad_in_blocks[0] = after(grad_in_blocks[0], out_held)
+    back_blocks = call_attend_back(attend_meta, head_in, grad_in_blocks, lse, mixed, cosine, sine)
+    grad_qkv, *parts = call_qkv_back(
+        attend_meta, exchange(back_blocks), after(front_all, out_came)
+    )
+    near, far = parts[:2], parts[2:]
+    across = sum_across(far)
+    first_terms = sum_frames(near, across)
+    qkv_held, qkv_away = call_head_grad(device, after(grad_qkv, across), hidden_one)
+    qkv_came = swap(qkv_away, "ctx", 1)
+    group_f32 = jax.ShapeDtypeStruct((IO_ROWS, D), single)
+    group_low = jax.ShapeDtypeStruct((IO_ROWS, D), bfloat)
+    mod_rows, *io_parts, _ = row_call(
+        first_kernel,
+        "first",
+        (
+            jax.ShapeDtypeStruct((MOD_ROWS, 128), bfloat),
+            group_f32,
+            group_low,
+            group_f32,
+            group_low,
+            jax.ShapeDtypeStruct((4 * IO_ROWS, D), single),
+        ),
+        device,
+        *first_terms,
+        after(resid_in, qkv_held),
+        mod_own,
+        grad_mid,
+        noisy_low,
+        rows_two,
+        grad_gate_two,
+        head_rows,
+        smem=1,
+    )
+    io_held, io_away = row_call(
+        side_kernel,
+        "side",
+        (
+            jax.ShapeDtypeStruct((4, IO_ROWS, 128), single),
+            jax.ShapeDtypeStruct((4 * IO_ROWS + MOD_ROWS, 128), bfloat),
+        ),
+        device,
+        *sum_frames(io_parts[:2], sum_across(io_parts[2:])),
+        mod_rows,
+        smem=1,
+    )
+    z_rows = jax.ShapeDtypeStruct((ATTN_ROWS + IO_ROWS + 2 * MOD_ROWS, 128), bfloat)
+    qkv_own, io_own, *z_pieces = row_call(
+        merge_kernel,
+        "merge",
+        (
+            jax.ShapeDtypeStruct((ATTN_ROWS, 128), single),
+            jax.ShapeDtypeStruct((IO_ROWS, 128), single),
+            jax.ShapeDtypeStruct((2 * MOD_ROWS, 128), bfloat),
+            z_rows,
+            z_rows,
+            z_rows,
+        ),
+        device,
+        qkv_held,
+        qkv_came,
+        out_held,
+        out_came,
+        io_held,
+        swap(io_away, "ctx", 1),
+        mod_rows,
+        smem=1,
+    )
+    red_attn, spread, matrix_sq = row_call(
+        finish_kernel,
+        "finish",
+        (
+            jax.ShapeDtypeStruct((4, 128, 256), single),
+            jax.ShapeDtypeStruct((8 * MOD_ROWS + 2 * IO_ROWS, 128), bfloat),
+            jax.ShapeDtypeStruct((1, 128), single),
+        ),
+        qkv_own,
+        io_own,
+        z_pieces[0],
+        *(swap(piece, "ctx", 2 * bit) for bit, piece in zip((1, 2, 3), z_pieces[1:])),
+        scattered,
+    )
+    grad_mod_w, red_vec, io_grad, mod_sq = call_mod_grad(
+        device, cond_relative, spread_frames(spread)
+    )
+    red_io = io_grad[: 2 * 128].reshape(2, 128, 128)
+    own_sq = matrix_sq + jnp.where(tp_index == 0, mod_sq, 0.0)
+    sums = sum_all(jnp.where(jnp.arange(128)[None, :] < 64, own_sq, error_part))
+    count = step[0].astype(single)
+    fixes = jnp.stack([1.0 / (1.0 - beta_one**count), 1.0 / (1.0 - beta_two**count)])
+    hidden_width = w_mlp.shape[2]
+    red_mlp = jnp.stack(
+        [scattered[:, :hidden_width], scattered[:, hidden_width : 2 * hidden_width]]
+    )
+    updated = call_adam(
+        fixes,
+        sums,
+        (
+            (w_attn, m_attn, v_attn, red_attn),
+            (w_mlp, m_mlp, v_mlp, red_mlp),
+            (w_mod, m_mod, v_mod, grad_mod_w),
+        ),
+        (w_io, m_io, v_io, red_io),
+        (vectors, m_vec, v_vec, red_vec),
+    )
+    return (updated[21][1, 64] / weight_sum, updated[21][0, 0], *updated[:21])
+
+
 def solution(mesh):
+    halves = mesh.shape["ctx"] == 8 and mesh.shape["tp"] == 4
     placed = (
         P("ctx", None),
         P("ctx", None),
@@ -588,7 +1966,7 @@
         P(None, "ctx"),
     )
     return jax.shard_map(
-        shards,
+        shards_halves if halves else shards,
         mesh=mesh,
         in_specs=placed,
         out_specs=(

time: 2080 us -> 493 us (0.24); the launches traced: 2050 us -> 485 us
  waiting for transfers between devices: 1330 us -> 218 us
  other arithmetic: 187 us -> 12.3 us
  matrix products: 140 us -> 3.06 us
  local copies, waits for them, and re-layouts: 178 us -> 49 us
  blocking collectives: 122 us -> 0 us
  Pallas kernels: 0 us -> 116 us
  loops' own time: 65.7 us -> 0 us
  starting transfers between devices: 2.09 us -> 66.8 us
    reduce_scatter x5 -> x1, waiting for transfers between devices: 604 us -> 0.01 us  [shards_halves(): lax.psum_scatter(weight_grad, 'ctx', scatter_dimension=0, tiled=True)]
    all_gather x5 -> x1, waiting for transfers between devices: 359 us -> 6.92 us  [shards_halves(): mlp_w = lax.all_gather(mlp_shard, 'ctx', axis=1, tiled=True)]
    psum x4 -> x0, waiting for transfers between devices: 235 us -> none  [the longest x1 104 us: shards(): lax.psum(jnp.einsum('rh,dh->rd', mix_low, attn_w[3], preferred_element_ty...]
    ppermute x0 -> x69, waiting for transfers between devices: none -> 211 us  [the longest x61 188 us: swap(): return lax.ppermute(values, axis, [(i, i ^ bit) for i in range(size)])]
    dot_general x53 -> x4, matrix products: 140 us -> 3.06 us  [the longest x1 1.32 us: shards_halves(): jnp.dot(cond_slots, mod_cols.astype(bfloat), preferred_element_type=single)]
    unnamed x18 -> x2, waiting for transfers between devices: 128 us -> 0.03 us
    pallas_call x0 -> x23, Pallas kernels: none -> 116 us  [the longest x1 30.7 us: call_attend_back(): pl.pallas_call(attend_back_kernel, out_shape=tuple((jax.ShapeDtypeStruct(...]
    dynamic_slice x80 -> x0, local copies, waits for them, and re-layouts: 67.2 us -> none  [the longest x32 18.9 us: per_stretch(): key_stretch = lax.dynamic_index_in_dim(order, block_num, 0, keepdims=False)]
  transfers between devices with their start and end apart: 16 -> 71, of which waited for: 16 -> 48; matrix products, arithmetic and copies ran while one was open for 5% -> 4% of each run, Pallas kernels for 0% -> 17%
where the time goes in v2:
time: 493 us; the launch traced here: 485 us
  waiting for transfers between devices  218 us (44%)
  Pallas kernels  116 us (24%)
  starting transfers between devices  66.8 us (14%)
  local copies, waits for them, and re-layouts  49 us (10%)
  between operations  19.4 us (4%)
  other arithmetic  12.3 us (2%)
    ppermute x61, waiting for transfers between devices, swap(): return lax.ppermute(values, axis, [(i, i ^ bit) for i in range(size)])  188 us
    ppermute x61, starting transfers between devices, swap(): return lax.ppermute(values, axis, [(i, i ^ bit) for i in range(size)])  57.1 us
    unnamed x189, local copies, waits for them, and re-layouts  44.6 us
    pallas_call x1, Pallas kernels, call_attend_back(): pl.pallas_call(attend_back_kernel, out_shape=tuple((jax.ShapeDtypeStruct(...  30.7 us
    pallas_call x1, Pallas kernels, call_attend(): pl.pallas_call(attend_kernel, out_shape=tuple((jax.ShapeDtypeStruct((HD,...  24.7 us
    ppermute x3, waiting for transfers between devices, ring_gather(): ahead.append(lax.ppermute(ahead[-1], 'ctx', RING_NEXT))  14.6 us
    pallas_call x4, Pallas kernels, call_mlp(): pl.pallas_call(kernel, out_shape=(frame_f32(), frame_low()) + outs, in_sp...  12.9 us
    pallas_call x8, Pallas kernels, row_call(): pl.pallas_call(kernel, out_shape=tuple(outs), in_specs=smem_specs(smem) +...  12.1 us
  transfers between devices with their start and end apart: 71, of which 48 were waited for; matrix products, arithmetic and copies ran while one was open for 4% of the time, Pallas kernels for 17%

profile of v2, /device:TPU:0, one launch (start us, length us, event | category | flops | bytes accessed | tf_op | source)
XLA Modules:
  0.0 484.7 jit_solution(16729245490416605536)
XLA Ops:
  27.8 7.8 %collective-permute-done.2.refs_2_ = bf16[1808,128]{1,0:T(8,128)(2,1)S(1)} collective-permute-done((bf16[1808,128]{1,0:T(8,128)(2,1)S(1)}, bf16[1808,128]{1,0:T(8,128)(2,1)S(1)}, u32[]{:S(2)}, u32[]{:S(2)}) %collective-permute-start.2) | collective-permute-done | bytes 462880 | tf_op jit(solution)/shard_map/ppermute | solution.py:598
  58.5 5.5 %collective-permute-done.13 = bf16[904,128]{1,0:T(8,128)(2,1)S(1)} collective-permute-done((bf16[904,128]{1,0:T(8,128)(2,1)S(1)}, bf16[904,128]{1,0:T(8,128)(2,1)S(1)}, u32[]{:S(2)}, u32[]{:S(2)}) %collective-permute-start.13) | collective-permute-done | bytes 231456 | tf_op jit(solution)/shard_map/ppermute | solution.py:600
  75.9 8.2 %front.1 = (bf16[912,1024]{1,0:T(8,128)(2,1)}, bf16[1024,384]{1,0:T(8,128)(2,1)}, bf16[4,256,1024]{2,1,0:T(8,128)(2,1)}, f32[256,1024]{1,0:T(8,128)}, bf16[192,1...) custom-call(s32[24]{0:T(128)S(1)} %copy-done.40, ...), custom_call_target="tpu_custom_call" | custom-call | flops 2000000000 | bytes 10000000 | tf_op jit(solution)/shard_map/front/pallas_call | solution.py:920
  89.9 6.8 %collective-permute-done.18.refs_1_ = bf16[192,1024]{1,0:T(8,128)(2,1)S(1)} collective-permute-done((bf16[192,1024]{1,0:T(8,128)(2,1)S(1)}, bf16[192,1024]{1,0:T(8,128)(2,1)S(1)}, u32[]{:S(2)}, u32[]{:S(2)}) %collective-permute-start.18) | collective-permute-done | bytes 393248 | tf_op jit(solution)/shard_map/ppermute | solution.py:586
  99.5 7.0 %collective-permute-done.20.refs_3_ = bf16[192,1024]{1,0:T(8,128)(2,1)S(1)} collective-permute-done((bf16[192,1024]{1,0:T(8,128)(2,1)}, bf16[192,1024]{1,0:T(8,128)(2,1)S(1)}, u32[]{:S(2)}, u32[]{:S(2)}) %collective-permute-start.20) | collective-permute-done | bytes 393248 | tf_op jit(solution)/shard_map/ppermute | solution.py:586
  106.6 24.7 %attend.1 = (bf16[64,1024]{1,0:T(8,128)(2,1)S(1)}, bf16[64,1024]{1,0:T(8,128)(2,1)S(1)}, bf16[64,1024]{1,0:T(8,128)(2,1)S(1)}, bf16[64,1024]{1,0:T(8,128)(2,1)S(...) custom-call(s32[18]{0:T(128)S(1)} %copy-done.66, bf16[192,1024]{1,0:T(8,128)(2,1)S(1)} %copy-done.70, ...), custom_call_target="tpu_custom_call" | custom-call | flops 8999999488 | bytes 5000000 | tf_op jit(solution)/shard_map/attend/pallas_call | solution.py:1529
  136.5 4.9 %collective-permute-done.21 = bf16[64,1024]{1,0:T(8,128)(2,1)S(1)} collective-permute-done((bf16[64,1024]{1,0:T(8,128)(2,1)S(1)}, bf16[64,1024]{1,0:T(8,128)(2,1)S(1)}, u32[]{:S(2)}, u32[]{:S(2)}) %collective-permute-start.21) | collective-permute-done | bytes 131104 | tf_op jit(solution)/shard_map/ppermute | solution.py:586
  146.6 12.4 %collective-permute-done.26.across = bf16[256,1024]{1,0:T(8,128)(2,1)S(1)} collective-permute-done((bf16[256,1024]{1,0:T(8,128)(2,1)S(1)}, bf16[256,1024]{1,0:T(8,128)(2,1)S(1)}, u32[]{:S(2)}, u32[]{:S(2)}) %collective-permute-start.26) | collective-permute-done | bytes 524320 | tf_op jit(solution)/shard_map/ppermute | solution.py:586
  162.8 12.0 %collective-permute-done.29.first.refs_2_ = bf16[256,1024]{1,0:T(8,128)(2,1)S(1)} collective-permute-done((bf16[256,1024]{1,0:T(8,128)(2,1)}, bf16[256,1024]{1,0:T(8,128)(2,1)S(1)}, u32[]{:S(2)}, u32[]{:S(2)}) %collective-permute-start.29) | collective-permute-done | bytes 524320 | tf_op jit(solution)/shard_map/ppermute | solution.py:586
  177.6 6.9 %all-gather.2.cloned.1.call-done.weights = bf16[2,1024,1024]{2,1,0:T(8,128)(2,1)} async-done(((bf16[2,128,1024]{2,1,0:T(8,128)(2,1)}), bf16[2,1024,1024]{2,1,0:T(8,128)(2,1)}) %all-gather.2.cloned.1.call-update) | async-done | bytes 4194320 | tf_op jit(solution)/shard_map/all_gather | solution.py:1762
  192.7 5.2 %mlp.2 = (f32[256,1024]{1,0:T(8,128)S(1)}, bf16[256,1024]{1,0:T(8,128)(2,1)}, bf16[512,1024]{1,0:T(8,128)(2,1)S(1)}, bf16[512,1024]{1,0:T(8,128)(2,1)S(1)}) custom-call(bf16[256,1024]{1,0:T(8,128)(2,1)} %get-tuple-element.151.first.refs_0_, bf16[256,1024]{1,0:T(8,128)(2,1)} %collective-permute-done.27.second.refs_1_, bf16[2,1024,1024]{2,1,0:T(8,128)(2,1)S(1)} %copy-done.44), custom_call_target="tpu_custom_call" | custom-call | flops 4000000000 | bytes 20000000 | tf_op jit(solution)/shard_map/mlp/pallas_call | solution.py:1211
  204.8 9.8 %collective-permute-done.32.across = bf16[256,1024]{1,0:T(8,128)(2,1)} collective-permute-done((bf16[256,1024]{1,0:T(8,128)(2,1)}, bf16[256,1024]{1,0:T(8,128)(2,1)}, u32[]{:S(2)}, u32[]{:S(2)}) %collective-permute-start.32) | collective-permute-done | bytes 524320 | tf_op jit(solution)/shard_map/ppermute | solution.py:586
  222.6 11.9 %collective-permute-done.35.first.refs_6_ = bf16[256,1024]{1,0:T(8,128)(2,1)S(1)} collective-permute-done((bf16[256,1024]{1,0:T(8,128)(2,1)S(1)}, bf16[256,1024]{1,0:T(8,128)(2,1)S(1)}, u32[]{:S(2)}, u32[]{:S(2)}) %collective-permute-start.35) | collective-permute-done | bytes 524320 | tf_op jit(solution)/shard_map/ppermute | solution.py:586
  246.1 6.8 %weight_grad.1 = bf16[1024,2048]{1,0:T(8,128)(2,1)S(1)} custom-call(bf16[256,1024]{1,0:T(8,128)(2,1)} %get-tuple-element.151.first.refs_0_, bf16[256,1024]{1,0:T(8,128)(2,1)} %collective-permute-done.27.second.refs_1_, bf16[256,1024]{1,0:T(8,128)(2,1)S(1)} %copy-done.49, bf16[256,1024]{1,0:T(8,128)(2,1)S(1)} %copy-done.52, ...), custom_call_target="tpu_custom_call" | custom-call | flops 5000000000 | bytes 20000000 | tf_op jit(solution)/shard_map/weight_grad/pallas_call | solution.py:1253
  257.2 12.4 %collective-permute-done.38.across = bf16[256,1024]{1,0:T(8,128)(2,1)S(1)} collective-permute-done((bf16[256,1024]{1,0:T(8,128)(2,1)}, bf16[256,1024]{1,0:T(8,128)(2,1)S(1)}, u32[]{:S(2)}, u32[]{:S(2)}) %collective-permute-start.38) | collective-permute-done | bytes 524320 | tf_op jit(solution)/shard_map/ppermute | solution.py:586
  275.8 11.8 %collective-permute-done.40 = bf16[256,1024]{1,0:T(8,128)(2,1)S(1)} collective-permute-done((bf16[256,1024]{1,0:T(8,128)(2,1)S(1)}, bf16[256,1024]{1,0:T(8,128)(2,1)S(1)}, u32[]{:S(2)}, u32[]{:S(2)}) %collective-permute-start.40) | collective-permute-done | bytes 524320 | tf_op jit(solution)/shard_map/ppermute | solution.py:586
  303.0 30.7 %attend_back.1 = (bf16[192,1024]{1,0:T(8,128)(2,1)S(1)}, bf16[192,1024]{1,0:T(8,128)(2,1)S(1)}, bf16[192,1024]{1,0:T(8,128)(2,1)S(1)}, bf16[192,1024]{1,0:T(8,128)(2,1)S(1)}) custom-call(s32[18]{0:T(128)S(1)} %copy-done.66, bf16[192,1024]{1,0:T(8,128)(2,1)S(1)} %copy-done.71, bf16[192,1024]{1,0:T(8,128)(2,1)S(1)} %copy-done.55, ...), custom_call_target="tpu_custom_call" | custom-call | flops 22000001024 | bytes 10000000 | tf_op jit(solution)/shard_map/attend_back/pallas_call | solution.py:1640
  337.9 12.5 %collective-permute-done.48.out_came = bf16[4,256,128]{2,1,0:T(8,128)(2,1)S(1)} collective-permute-done((bf16[4,256,128]{2,1,0:T(8,128)(2,1)S(1)}, bf16[4,256,128]{2,1,0:T(8,128)(2,1)S(1)}, u32[]{:S(2)}, u32[]{:S(2)}) %collective-permute-start.48) | collective-permute-done | bytes 262176 | tf_op jit(solution)/shard_map/ppermute | solution.py:586
  354.7 8.6 %collective-permute-done.47.refs_3_ = bf16[192,1024]{1,0:T(8,128)(2,1)S(1)} collective-permute-done((bf16[192,1024]{1,0:T(8,128)(2,1)S(1)}, bf16[192,1024]{1,0:T(8,128)(2,1)S(1)}, u32[]{:S(2)}, u32[]{:S(2)}) %collective-permute-start.47) | collective-permute-done | bytes 393248 | tf_op jit(solution)/shard_map/ppermute | solution.py:586
  373.0 8.9 %collective-permute-done.52.across = bf16[256,1024]{1,0:T(8,128)(2,1)S(1)} collective-permute-done((bf16[256,1024]{1,0:T(8,128)(2,1)S(1)}, bf16[256,1024]{1,0:T(8,128)(2,1)S(1)}, u32[]{:S(2)}, u32[]{:S(2)}) %collective-permute-start.52) | collective-permute-done | bytes 524320 | tf_op jit(solution)/shard_map/ppermute | solution.py:586
  403.1 6.2 %collective-permute-done.57.refs_3_ = bf16[1200,128]{1,0:T(8,128)(2,1)S(1)} collective-permute-done((bf16[1200,128]{1,0:T(8,128)(2,1)S(1)}, bf16[1200,128]{1,0:T(8,128)(2,1)S(1)}, u32[]{:S(2)}, u32[]{:S(2)}) %collective-permute-start.57) | collective-permute-done | bytes 307232 | tf_op jit(solution)/shard_map/ppermute | solution.py:586
  410.0 11.5 %collective-permute-done.58.refs_4_ = bf16[1200,128]{1,0:T(8,128)(2,1)S(1)} collective-permute-done((bf16[1200,128]{1,0:T(8,128)(2,1)S(1)}, bf16[1200,128]{1,0:T(8,128)(2,1)S(1)}, u32[]{:S(2)}, u32[]{:S(2)}) %collective-permute-start.58) | collective-permute-done | bytes 307232 | tf_op jit(solution)/shard_map/ppermute | solution.py:586
  448.0 5.2 %collective-permute-start.66 = (f32[1,128]{1,0:T(1,128)S(1)}, f32[1,128]{1,0:T(1,128)S(1)}, u32[]{:S(2)}, u32[]{:S(2)}) collective-permute-start(f32[1,128]{1,0:T(1,128)S(1)} %add.139.refs_1_), channel_id=1, source_target_pairs={{0,8},{4,12},{8,0},{12,4},{16,24},{20,28},{24,16},{28,20},{1,9},{5... | collective-permute-start | bytes 1544 | tf_op jit(solution)/shard_map/ppermute | solution.py:586
  467.3 8.0 %adam.1 = (f32[4,128,256]{2,1,0:T(8,128)}, f32[4,128,256]{2,1,0:T(8,128)}, f32[4,128,256]{2,1,0:T(8,128)}, bf16[4,128,256]{2,1,0:T(8,128)(2,1)}, f32[2,128,1024]...) custom-call(f32[2]{0:T(128)S(1)} %pad_maximum_fusion.6.refs_0_, ...), custom_call_target="tpu_custom_call" | custom-call | flops 10000000 | bytes 20000000 | tf_op jit(solution)/shard_map/adam/pallas_call | solution.py:1413
  (400 shorter events, 219.7 us)
Async XLA Ops:
  7.2 177.4 %all-gather.2.cloned.1.call-start = ((), (), s32[]{:S(2)}) async-start(), calls=%async_computation.1 | async-start | bytes 4718592 | tf_op jit(solution)/shard_map/all_gather | solution.py:1762
  10.0 14.2 %collective-permute-start.1 = (bf16[1808,128]{1,0:T(8,128)(2,1)}, bf16[1808,128]{1,0:T(8,128)(2,1)S(1)}, u32[]{:S(2)}, u32[]{:S(2)}) collective-permute-start(bf16[1808,128]{1,0:T(8,128)(2,1)} %prepare.1.refs_0_), channel_id=1, source_target_pairs={{0,4},{4,12},{12,20},{20,28},{28,24},{24,16},{16,8},{8,0},{1,5},{5... | collective-permute-start | bytes 1388552 | tf_op jit(solution)/shard_map/ppermute | solution.py:598
  12.9 13.6 %collective-permute-start.3 = (bf16[1808,128]{1,0:T(8,128)(2,1)}, bf16[1808,128]{1,0:T(8,128)(2,1)S(1)}, u32[]{:S(2)}, u32[]{:S(2)}) collective-permute-start(bf16[1808,128]{1,0:T(8,128)(2,1)} %prepare.1.refs_0_), channel_id=1, source_target_pairs={{4,0},{12,4},{20,12},{28,20},{24,28},{16,24},{8,16},{0,8},{5,1},{1... | collective-permute-start | bytes 1388552 | tf_op jit(solution)/shard_map/ppermute | solution.py:599
  24.2 11.5 %collective-permute-start.2 = (bf16[1808,128]{1,0:T(8,128)(2,1)S(1)}, bf16[1808,128]{1,0:T(8,128)(2,1)S(1)}, u32[]{:S(2)}, u32[]{:S(2)}) collective-permute-start(bf16[1808,128]{1,0:T(8,128)(2,1)S(1)} %collective-permute-done.1.refs_1_), channel_id=1, source_target_pairs={{0,4},{4,12},{12,20},{20,28},{28,24},{24,16},{16,8},{8,0},{1,5},{5... | collective-permute-start | bytes 1388552 | tf_op jit(solution)/shard_map/ppermute | solution.py:598
  85.5 11.2 %collective-permute-start.18 = (bf16[192,1024]{1,0:T(8,128)(2,1)S(1)}, bf16[192,1024]{1,0:T(8,128)(2,1)S(1)}, u32[]{:S(2)}, u32[]{:S(2)}) collective-permute-start(bf16[192,1024]{1,0:T(8,128)(2,1)S(1)} %get-tuple-element.141), channel_id=1, source_target_pairs={{0,4},{4,0},{8,12},{12,8},{16,20},{20,16},{24,28},{28,24},{1,5},{5... | collective-permute-start | bytes 1179656 | tf_op jit(solution)/shard_map/ppermute | solution.py:586
  87.3 12.2 %collective-permute-start.19 = (bf16[192,1024]{1,0:T(8,128)(2,1)}, bf16[192,1024]{1,0:T(8,128)(2,1)S(1)}, u32[]{:S(2)}, u32[]{:S(2)}) collective-permute-start(bf16[192,1024]{1,0:T(8,128)(2,1)} %get-tuple-element.142), channel_id=1, source_target_pairs={{0,8},{4,12},{8,0},{12,4},{16,24},{20,28},{24,16},{28,20},{1,9},{5... | collective-permute-start | bytes 1179656 | tf_op jit(solution)/shard_map/ppermute | solution.py:586
  87.9 18.6 %collective-permute-start.20 = (bf16[192,1024]{1,0:T(8,128)(2,1)}, bf16[192,1024]{1,0:T(8,128)(2,1)S(1)}, u32[]{:S(2)}, u32[]{:S(2)}) collective-permute-start(bf16[192,1024]{1,0:T(8,128)(2,1)} %get-tuple-element.143), channel_id=1, source_target_pairs={{0,12},{4,8},{8,4},{12,0},{16,28},{20,24},{24,20},{28,16},{1,13},{... | collective-permute-start | bytes 1179656 | tf_op jit(solution)/shard_map/ppermute | solution.py:586
  106.5 316.4 %reduce-scatter.2.cloned.1.call-start = ((), (), s32[]{:S(2)}) async-start(), calls=%async_computation.2 | async-start | bytes 4718592 | tf_op jit(solution)/shard_map/reduce_scatter | solution.py:1815
  145.0 14.0 %collective-permute-start.26 = (bf16[256,1024]{1,0:T(8,128)(2,1)S(1)}, bf16[256,1024]{1,0:T(8,128)(2,1)S(1)}, u32[]{:S(2)}, u32[]{:S(2)}) collective-permute-start(bf16[256,1024]{1,0:T(8,128)(2,1)S(1)} %fusion), channel_id=1, source_target_pairs={{0,2},{1,3},{2,0},{3,1},{4,6},{5,7},{6,4},{7,5},{8,10},{9,11},{10,... | collective-permute-start | bytes 1572872 | tf_op jit(solution)/shard_map/ppermute | solution.py:586
  161.4 13.5 %collective-permute-start.29 = (bf16[256,1024]{1,0:T(8,128)(2,1)}, bf16[256,1024]{1,0:T(8,128)(2,1)S(1)}, u32[]{:S(2)}, u32[]{:S(2)}) collective-permute-start(bf16[256,1024]{1,0:T(8,128)(2,1)} %get-tuple-element.151.first.refs_0_), channel_id=1, source_target_pairs={{0,2},{1,3},{2,0},{3,1},{4,6},{5,7},{6,4},{7,5},{8,10},{9,11},{10,... | collective-permute-start | bytes 1572872 | tf_op jit(solution)/shard_map/ppermute | solution.py:586
  175.7 16.9 %collective-permute-start.27 = (bf16[256,1024]{1,0:T(8,128)(2,1)}, bf16[256,1024]{1,0:T(8,128)(2,1)}, u32[]{:S(2)}, u32[]{:S(2)}) collective-permute-start(bf16[256,1024]{1,0:T(8,128)(2,1)} %get-tuple-element.151.first.refs_0_), channel_id=1, source_target_pairs={{0,1},{1,0},{2,3},{3,2},{4,5},{5,4},{6,7},{7,6},{8,9},{9,8},{10,11... | collective-permute-start | bytes 1572872 | tf_op jit(solution)/shard_map/ppermute | solution.py:586
  200.1 14.5 %collective-permute-start.32 = (bf16[256,1024]{1,0:T(8,128)(2,1)}, bf16[256,1024]{1,0:T(8,128)(2,1)}, u32[]{:S(2)}, u32[]{:S(2)}) collective-permute-start(bf16[256,1024]{1,0:T(8,128)(2,1)} %add_convert_fusion.2), channel_id=1, source_target_pairs={{0,2},{1,3},{2,0},{3,1},{4,6},{5,7},{6,4},{7,5},{8,10},{9,11},{10,... | collective-permute-start | bytes 1572872 | tf_op jit(solution)/shard_map/ppermute | solution.py:586
  221.2 13.4 %collective-permute-start.35 = (bf16[256,1024]{1,0:T(8,128)(2,1)S(1)}, bf16[256,1024]{1,0:T(8,128)(2,1)S(1)}, u32[]{:S(2)}, u32[]{:S(2)}) collective-permute-start(bf16[256,1024]{1,0:T(8,128)(2,1)S(1)} %get-tuple-element.159.first.refs_4_), channel_id=1, source_target_pairs={{0,2},{1,3},{2,0},{3,1},{4,6},{5,7},{6,4},{7,5},{8,10},{9,11},{10,... | collective-permute-start | bytes 1572872 | tf_op jit(solution)/shard_map/ppermute | solution.py:586
  255.4 14.2 %collective-permute-start.38 = (bf16[256,1024]{1,0:T(8,128)(2,1)}, bf16[256,1024]{1,0:T(8,128)(2,1)S(1)}, u32[]{:S(2)}, u32[]{:S(2)}) collective-permute-start(bf16[256,1024]{1,0:T(8,128)(2,1)} %add_convert_fusion.1), channel_id=1, source_target_pairs={{0,2},{1,3},{2,0},{3,1},{4,6},{5,7},{6,4},{7,5},{8,10},{9,11},{10,... | collective-permute-start | bytes 1572872 | tf_op jit(solution)/shard_map/ppermute | solution.py:586
  274.3 13.3 %collective-permute-start.40 = (bf16[256,1024]{1,0:T(8,128)(2,1)S(1)}, bf16[256,1024]{1,0:T(8,128)(2,1)S(1)}, u32[]{:S(2)}, u32[]{:S(2)}) collective-permute-start(bf16[256,1024]{1,0:T(8,128)(2,1)S(1)} %get-tuple-element.174), channel_id=1, source_target_pairs={{0,2},{1,3},{2,0},{3,1},{4,6},{5,7},{6,4},{7,5},{8,10},{9,11},{10,... | collective-permute-start | bytes 1572872 | tf_op jit(solution)/shard_map/ppermute | solution.py:586
  275.8 11.8 %collective-permute-start.39 = (bf16[256,1024]{1,0:T(8,128)(2,1)S(1)}, bf16[256,1024]{1,0:T(8,128)(2,1)S(1)}, u32[]{:S(2)}, u32[]{:S(2)}) collective-permute-start(bf16[256,1024]{1,0:T(8,128)(2,1)S(1)} %get-tuple-element.174), channel_id=1, source_target_pairs={{0,1},{1,0},{2,3},{3,2},{4,5},{5,4},{6,7},{7,6},{8,9},{9,8},{10,11... | collective-permute-start | bytes 1572872 | tf_op jit(solution)/shard_map/ppermute | solution.py:586
  333.7 16.6 %collective-permute-start.45 = (bf16[192,1024]{1,0:T(8,128)(2,1)S(1)}, bf16[192,1024]{1,0:T(8,128)(2,1)S(1)}, u32[]{:S(2)}, u32[]{:S(2)}) collective-permute-start(bf16[192,1024]{1,0:T(8,128)(2,1)S(1)} %get-tuple-element.181), channel_id=1, source_target_pairs={{0,4},{4,0},{8,12},{12,8},{16,20},{20,16},{24,28},{28,24},{1,5},{5... | collective-permute-start | bytes 1179656 | tf_op jit(solution)/shard_map/ppermute | solution.py:586
  334.4 20.3 %collective-permute-start.46 = (bf16[192,1024]{1,0:T(8,128)(2,1)S(1)}, bf16[192,1024]{1,0:T(8,128)(2,1)S(1)}, u32[]{:S(2)}, u32[]{:S(2)}) collective-permute-start(bf16[192,1024]{1,0:T(8,128)(2,1)S(1)} %get-tuple-element.182), channel_id=1, source_target_pairs={{0,8},{4,12},{8,0},{12,4},{16,24},{20,28},{24,16},{28,20},{1,9},{5... | collective-permute-start | bytes 1179656 | tf_op jit(solution)/shard_map/ppermute | solution.py:586
  334.7 28.6 %collective-permute-start.47 = (bf16[192,1024]{1,0:T(8,128)(2,1)S(1)}, bf16[192,1024]{1,0:T(8,128)(2,1)S(1)}, u32[]{:S(2)}, u32[]{:S(2)}) collective-permute-start(bf16[192,1024]{1,0:T(8,128)(2,1)S(1)} %get-tuple-element.183), channel_id=1, source_target_pairs={{0,12},{4,8},{8,4},{12,0},{16,28},{20,24},{24,20},{28,16},{1,13},{... | collective-permute-start | bytes 1179656 | tf_op jit(solution)/shard_map/ppermute | solution.py:586
  337.3 13.1 %collective-permute-start.48 = (bf16[4,256,128]{2,1,0:T(8,128)(2,1)S(1)}, bf16[4,256,128]{2,1,0:T(8,128)(2,1)S(1)}, u32[]{:S(2)}, u32[]{:S(2)}) collective-permute-start(bf16[4,256,128]{2,1,0:T(8,128)(2,1)S(1)} %get-tuple-element.185), channel_id=1, source_target_pairs={{0,4},{4,0},{8,12},{12,8},{16,20},{20,16},{24,28},{28,24},{1,5},{5... | collective-permute-start | bytes 786440 | tf_op jit(solution)/shard_map/ppermute | solution.py:586
  367.9 14.0 %collective-permute-start.52 = (bf16[256,1024]{1,0:T(8,128)(2,1)S(1)}, bf16[256,1024]{1,0:T(8,128)(2,1)S(1)}, u32[]{:S(2)}, u32[]{:S(2)}) collective-permute-start(bf16[256,1024]{1,0:T(8,128)(2,1)S(1)} %add_convert_fusion), channel_id=1, source_target_pairs={{0,2},{1,3},{2,0},{3,1},{4,6},{5,7},{6,4},{7,5},{8,10},{9,11},{10,... | collective-permute-start | bytes 1572872 | tf_op jit(solution)/shard_map/ppermute | solution.py:586
  372.3 21.5 %collective-permute-start.50 = (bf16[4,768,128]{2,1,0:T(8,128)(2,1)S(1)}, bf16[4,768,128]{2,1,0:T(8,128)(2,1)S(1)}, u32[]{:S(2)}, u32[]{:S(2)}) collective-permute-start(bf16[4,768,128]{2,1,0:T(8,128)(2,1)S(1)} %get-tuple-element.193), channel_id=1, source_target_pairs={{0,4},{4,0},{8,12},{12,8},{16,20},{20,16},{24,28},{28,24},{1,5},{5... | collective-permute-start | bytes 2359304 | tf_op jit(solution)/shard_map/ppermute | solution.py:586
  398.7 22.7 %collective-permute-start.58 = (bf16[1200,128]{1,0:T(8,128)(2,1)S(1)}, bf16[1200,128]{1,0:T(8,128)(2,1)S(1)}, u32[]{:S(2)}, u32[]{:S(2)}) collective-permute-start(bf16[1200,128]{1,0:T(8,128)(2,1)S(1)} %get-tuple-element.213), channel_id=1, source_target_pairs={{0,16},{4,20},{8,24},{12,28},{16,0},{20,4},{24,8},{28,12},{1,17},{... | collective-permute-start | bytes 921608 | tf_op jit(solution)/shard_map/ppermute | solution.py:586
  398.8 23.4 %collective-permute-start.59 = (bf16[1200,128]{1,0:T(8,128)(2,1)S(1)}, bf16[1200,128]{1,0:T(8,128)(2,1)S(1)}, u32[]{:S(2)}, u32[]{:S(2)}) collective-permute-start(bf16[1200,128]{1,0:T(8,128)(2,1)S(1)} %get-tuple-element.214), channel_id=1, source_target_pairs={{0,24},{4,28},{8,16},{12,20},{16,8},{20,12},{24,0},{28,4},{1,25},{... | collective-permute-start | bytes 921608 | tf_op jit(solution)/shard_map/ppermute | solution.py:586
  (138 other events, 1068.3 us)
Sparse Core Ops, SparseCore 0:
  106.7 77.8 all-gather.1
  255.1 100.3 reduce-scatter.1

commit v3 on v2

--- a/solution.py
+++ b/solution.py
@@ -653,9 +653,8 @@
     return [jnp.where(high_bit, once[k ^ 2], once[k]) for k in range(4)]
 
 
-def sum_all(values):
-    for axis, bit in (("tp", 1), ("tp", 2), ("ctx", 1)):
-        values = values + swap(values, axis, bit)
+def sum_terms(values):
+    values = values + swap(values, "ctx", 1)
     return [values] + [swap(values, "ctx", bit) for bit in (2, 4, 6)]
 
 
@@ -762,10 +761,12 @@
 
     def per_row(row, carry):
         rows[row] = level[row]
-        rows[frames + row] = level[4 * (ctx ^ (row & 7)) + (tp ^ (row >> 3))]
+        rows[frames + row] = level[4 * (ctx ^ (row & 7)) + (row >> 3)]
         return carry
 
     lax.fori_loop(0, frames, per_row, 0)
+    for k in range(8):
+        rows[2 * frames + k] = level[4 * ctx + (tp ^ (k & 3))]
 
 
 def call_place(device, lengths, order, levels):
@@ -775,7 +776,7 @@
         out_shape=(
             jax.ShapeDtypeStruct((24,), jnp.int32),
             jax.ShapeDtypeStruct((2 + frames // 2,), jnp.int32),
-            jax.ShapeDtypeStruct((2 * frames,), jnp.int32),
+            jax.ShapeDtypeStruct((2 * frames + 8,), jnp.int32),
         ),
         in_specs=smem_specs(4),
         out_specs=smem_specs(3),
@@ -1128,48 +1129,51 @@
 
 def mod_grad_kernel(device, cond, *refs):
     parts = refs[:4]
-    grad, vector, io_grad, square, rows = refs[4:]
+    rows_out, vector, io_grad, square, rows = refs[4:]
+    base = 8 * MOD_ROWS + 2 * IO_ROWS
+    terms = []
     for index in range(4):
+        owner = device[1] ^ index
+        block = parts[index][0 : 8 * MOD_ROWS, :].astype(jnp.float32)
         for frame in range(8):
-            block = parts[index][MOD_ROWS * frame : MOD_ROWS * frame + MOD_ROWS, :].astype(
-                jnp.float32
-            )
-            at = 8 * index + frame
             for k in range(MOD_ROWS):
-                rows[at : at + 1, 128 * k : 128 * k + 128] = block[k : k + 1, :]
-        base = 8 * MOD_ROWS
-        group = pl.ds(pl.multiple_of(IO_ROWS * (device[1] ^ index), 16), IO_ROWS)
-        io_grad[group, :] = parts[index][base : base + IO_ROWS, :].astype(jnp.float32) + parts[
-            index
-        ][base + IO_ROWS : base + 2 * IO_ROWS, :].astype(jnp.float32)
+                at = MOD_ROWS * frame + k
+                rows[owner, frame : frame + 1, 128 * k : 128 * k + 128] = block[at : at + 1, :]
+        group = pl.ds(pl.multiple_of(IO_ROWS * owner, 16), IO_ROWS)
+        high = parts[index][8 * MOD_ROWS : 8 * MOD_ROWS + IO_ROWS, :].astype(jnp.float32)
+        rest = parts[index][8 * MOD_ROWS + IO_ROWS : base, :].astype(jnp.float32)
+        io_grad[group, :] = high + rest
+        terms.append(column_sum(parts[index][base : base + 16, :].astype(jnp.float32)))
     total = jnp.zeros((1, 1), jnp.float32)
     for index in range(6):
         cols = slice(D * index, D * index + D)
+        low = rows[:, :, cols].reshape(32, D)
+        rows_out[:, cols] = low.astype(jnp.bfloat16)
         part = lax.dot_general(
-            cond[...], rows[:, cols].astype(jnp.bfloat16), TN, preferred_element_type=jnp.float32
+            cond[32:64, :], low.astype(jnp.bfloat16), TN, preferred_element_type=jnp.float32
         )
-        grad[:, cols] = part
         total = total + jnp.sum(column_sum(part * part), axis=1, keepdims=True)
         own = pl.ds(pl.multiple_of(D * index + 128 * device[0], 128), 128)
-        vector[index : index + 1, :] = column_sum(rows[:, own])
+        vector[index : index + 1, :] = column_sum(rows[:, :, own].reshape(32, 128))
     vector[6:8, :] = io_grad[256:258, :]
     mixed = vector[0:6, :]
     total = total + jnp.sum(column_sum(mixed * mixed), axis=1, keepdims=True)
-    square[...] = jnp.broadcast_to(total, square.shape)
+    left = lax.broadcasted_iota(jnp.int32, (1, 128), 1) < 64
+    square[...] = ((terms[0] + terms[1]) + (terms[2] + terms[3])) + jnp.where(left, total, 0.0)
 
 
 def call_mod_grad(device, cond, parts):
     return pl.pallas_call(
         mod_grad_kernel,
         out_shape=(
-            jax.ShapeDtypeStruct((128, 6 * D), jnp.float32),
+            jax.ShapeDtypeStruct((32, 6 * D), jnp.bfloat16),
             jax.ShapeDtypeStruct((8, 128), jnp.float32),
             jax.ShapeDtypeStruct((4 * IO_ROWS, 128), jnp.float32),
             jax.ShapeDtypeStruct((1, 128), jnp.float32),
         ),
         in_specs=smem_specs(1) + vmem_specs(5),
         out_specs=vmem_specs(4),
-        scratch_shapes=[pltpu.VMEM((32, 6 * D), jnp.float32)],
+        scratch_shapes=[pltpu.VMEM((4, 8, 6 * D), jnp.float32)],
         compiler_params=pltpu.CompilerParams(vmem_limit_bytes=12 * 2**20),
         cost_estimate=pl.CostEstimate(flops=10**8, bytes_accessed=4 * 10**6, transcendentals=0),
         name="mod_grad",
@@ -1345,35 +1349,71 @@
 
 def adam_kernel(*refs):
     fixes, sums = refs[0], refs[1:5]
-    groups = [refs[5 + 4 * k : 9 + 4 * k] for k in range(3)]
-    io_in, vec_in = refs[17:21], refs[21:25]
-    outs = [refs[25 + 4 * k : 29 + 4 * k] for k in range(3)]
-    io_out, vec_out, norm_out = refs[37:42], refs[42:46], refs[46]
-    slots, low_slots, sems = refs[47:]
+    attn_grad, mlp_grad, cond, mod_rows = refs[5:9]
+    io_in, vec_in = refs[9:13], refs[13:17]
+    groups = [refs[17 + 3 * k : 20 + 3 * k] for k in range(3)]
+    outs = [refs[26 + 4 * k : 30 + 4 * k] for k in range(3)]
+    io_out, vec_out, norm_out = refs[38:43], refs[43:47], refs[47]
+    held, slots, low_slots, in_sems, sems = refs[48:]
+    depth = held.shape[0]
+    tasks = []
+    for k in (2, 1, 0):
+        width = groups[k][0].shape[-1]
+        for lead in range(groups[k][0].shape[0] if k < 2 else 1):
+            for col in range(0, width, 1024):
+                tasks.append((k, lead, col, min(1024, width - col)))
+
+    def fetches(number):
+        k, lead, col, span = tasks[number]
+        cut = ((lead,) if k < 2 else ()) + (slice(None), slice(col, col + span))
+        slot = number % depth
+        return [
+            pltpu.make_async_copy(
+                groups[k][index].at[cut], held.at[slot, index, :, 0:span], in_sems.at[slot, index]
+            )
+            for index in range(3)
+        ]
+
+    for number in range(min(depth, len(tasks))):
+        for copy in fetches(number):
+            copy.start()
     total = (sums[0][...] + sums[1][...]) + (sums[2][...] + sums[3][...])
     norm = jnp.sqrt(total)
     norm_out[0:1, :] = norm
     norm_out[1:2, :] = total
     factor = jnp.minimum(1.0, clip_limit / (norm[:, 0:1] + 1e-06))
     scale = (factor, fixes[0], fixes[1])
-    tasks = []
-    for k, group in enumerate(groups):
-        rows, width = group[0].shape[-2:]
-        for lead in range(group[0].shape[0] if len(group[0].shape) == 3 else 1):
-            for col in range(0, width, 1024):
-                span = min(1024, width - col)
-                tasks.append((k, lead, col, span))
+    results = adam_step(*(ref[...] for ref in io_in), scale, rate_matrix, decay_rate)
+    io_out[0][...] = results[0]
+    io_out[1][...] = results[1]
+    io_out[2][...] = results[2][0]
+    io_out[3][...] = results[2][1]
+    io_out[4][...] = results[3]
+    results = adam_step(*(ref[...] for ref in vec_in), scale, rate_vector, 0.0)
+    for out, result in zip(vec_out, results):
+        out[...] = result
     running = {}
     for number, (k, lead, col, span) in enumerate(tasks):
-        slot = number % 4
-        if number >= 4:
-            for copy in running.pop(number - 4):
-                copy.wait()
-        cut = (slice(None), slice(col, col + span))
-        if len(groups[k][0].shape) == 3:
-            cut = (lead,) + cut
-        values = [ref[cut].astype(jnp.float32) for ref in groups[k]]
-        results = adam_step(*values, scale, rate_matrix, decay_rate)
+        slot = number % depth
+        for copy in fetches(number):
+            copy.wait()
+        for copy in running.pop(number - depth, ()):
+            copy.wait()
+        cut = ((lead,) if k < 2 else ()) + (slice(None), slice(col, col + span))
+        if k == 0:
+            grad = attn_grad[lead]
+        elif k == 1:
+            base = groups[1][0].shape[-1] * lead + col
+            grad = mlp_grad[:, base : base + span].astype(jnp.float32)
+        else:
+            grad = lax.dot_general(
+                cond[32:64, :],
+                mod_rows[:, col : col + span],
+                TN,
+                preferred_element_type=jnp.float32,
+            )
+        values = [held[slot, index, :, 0:span] for index in range(3)]
+        results = adam_step(*values, grad, scale, rate_matrix, decay_rate)
         copies = []
         for index, result in enumerate(results):
             source = low_slots.at[slot] if index == 3 else slots.at[slot, index]
@@ -1384,22 +1424,17 @@
             )
             copies[index].start()
         running[number] = copies
-    results = adam_step(*(ref[...] for ref in io_in), scale, rate_matrix, decay_rate)
-    io_out[0][...] = results[0]
-    io_out[1][...] = results[1]
-    io_out[2][...] = results[2][0]
-    io_out[3][...] = results[2][1]
-    io_out[4][...] = results[3]
-    results = adam_step(*(ref[...] for ref in vec_in), scale, rate_vector, 0.0)
-    for out, result in zip(vec_out, results):
-        out[...] = result
+        if number + depth < len(tasks):
+            for copy in fetches(number + depth):
+                copy.start()
     for copies in running.values():
         for copy in copies:
             copy.wait()
 
 
-def call_adam(fixes, sums, groups, io_group, vec_group):
-    operands = [*sums, *(array for group in groups for array in group), *io_group, *vec_group]
+def call_adam(fixes, sums, grads, io_group, vec_group, groups):
+    held = [array for group in groups for array in group]
+    inside = [*sums, *grads, *io_group, *vec_group]
 
     def results(group):
         low = jax.ShapeDtypeStruct(group[0].shape, jnp.bfloat16)
@@ -1413,22 +1448,24 @@
     return pl.pallas_call(
         adam_kernel,
         out_shape=out_shape,
-        in_specs=smem_specs(1) + vmem_specs(len(operands)),
+        in_specs=smem_specs(1) + vmem_specs(len(inside)) + hbm_specs(9),
         out_specs=hbm_specs(12) + vmem_specs(10),
         scratch_shapes=[
-            pltpu.VMEM((4, 3, 128, 1024), jnp.float32),
-            pltpu.VMEM((4, 128, 1024), jnp.bfloat16),
-            pltpu.SemaphoreType.DMA((4, 4)),
+            pltpu.VMEM((6, 3, 128, 1024), jnp.float32),
+            pltpu.VMEM((6, 3, 128, 1024), jnp.float32),
+            pltpu.VMEM((6, 128, 1024), jnp.bfloat16),
+            pltpu.SemaphoreType.DMA((6, 3)),
+            pltpu.SemaphoreType.DMA((6, 4)),
         ],
-        compiler_params=pltpu.CompilerParams(vmem_limit_bytes=20 * 2**20),
+        compiler_params=pltpu.CompilerParams(vmem_limit_bytes=52 * 2**20),
         cost_estimate=pl.CostEstimate(flops=10**7, bytes_accessed=2 * 10**7, transcendentals=0),
         name="adam",
-    )(fixes, *operands)
+    )(fixes, *inside, *held)
 
 
 def finish_kernel(*refs):
     own, io_own, mod_own, pieces = refs[0], refs[1], refs[2], refs[3:6]
-    scattered, grad, spread, square = refs[6:]
+    scattered, error, grad, spread = refs[6:]
     total = own[...]
     io_total = io_own[...]
     spread[0 : 2 * MOD_ROWS, :] = mod_own[...]
@@ -1440,14 +1477,23 @@
     high = io_total.astype(jnp.bfloat16)
     base = 8 * MOD_ROWS
     spread[base : base + IO_ROWS, :] = high
-    spread[base + IO_ROWS :, :] = (io_total - high.astype(jnp.float32)).astype(jnp.bfloat16)
+    base = base + IO_ROWS
+    spread[base : base + IO_ROWS, :] = (io_total - high.astype(jnp.float32)).astype(jnp.bfloat16)
     for part in range(4):
         grad[part] = total[256 * part : 256 * part + 256].T
     rest = scattered[...].astype(jnp.float32)
     squares = jnp.zeros((1, 1), jnp.float32)
     for values in (total, rest, io_total):
         squares = squares + jnp.sum(column_sum(values * values), axis=1, keepdims=True)
-    square[...] = jnp.broadcast_to(squares, square.shape)
+    left = lax.broadcasted_iota(jnp.int32, (1, 128), 1) < 64
+    value = jnp.where(left, squares, error[...])
+    terms = []
+    for _ in range(3):
+        terms.append(value.astype(jnp.bfloat16).astype(jnp.float32))
+        value = value - terms[-1]
+    spread[base + IO_ROWS :, :] = jnp.concatenate(
+        terms + [jnp.zeros((13, 128), jnp.float32)], axis=0
+    ).astype(jnp.bfloat16)
 
 
 def turn(block):
@@ -1467,7 +1513,7 @@
 def attend_kernel(meta, *refs):
     blocks = refs[:4]
     outs = refs[4:8]
-    lse, mixed, query, key, value = refs[8:]
+    lse, mixed, query, key, value, scores = refs[8:]
     for member in range(4):
         for frame in range(4):
             slot = 4 * (meta[0] ^ member) + (meta[1] ^ frame)
@@ -1481,35 +1527,40 @@
         low, since, upto = query_rows(meta, pair)
         wanted = query[pair]
 
-        def per_keys(keys, state):
-            top, total, acc = state
+        def first_pass(keys, top):
             both = jnp.dot(key[keys], wanted, preferred_element_type=jnp.float32)
-            scores = []
-            new_top = top
             for side in range(2):
                 slot = 2 * keys + side
                 bias = jnp.where((slot >= since) & (slot <= upto), 0.0, neg_large)
-                scores.append(both[256 * side : 256 * side + 256] + bias)
-                new_top = jnp.maximum(new_top, jnp.max(scores[side], axis=0, keepdims=True))
-            probs = [jnp.exp(values - new_top) for values in scores]
-            shrink = jnp.exp(top - new_top)
-            total = total * shrink + jnp.sum(probs[0] + probs[1], axis=0, keepdims=True)
-            low_probs = jnp.concatenate([values.astype(jnp.bfloat16) for values in probs], axis=0)
-            acc = acc * shrink + jnp.dot(
-                value[keys], low_probs, preferred_element_type=jnp.float32
+                part = both[256 * side : 256 * side + 256] + bias
+                scores[keys, 256 * side : 256 * side + 256, :] = part
+                top = jnp.maximum(top, jnp.max(part.reshape(32, 8, 2 * PATCHES), axis=0))
+            return top
+
+        tops = lax.fori_loop(
+            low // 2, pair + 1, first_pass, jnp.full((8, 2 * PATCHES), neg_large, jnp.float32)
+        )
+        top = jnp.max(tops, axis=0, keepdims=True)
+
+        def second_pass(keys, state):
+            total, acc = state
+            probs = jnp.exp(scores[keys] - top)
+            total = total + jnp.sum(probs.reshape(64, 8, 2 * PATCHES), axis=0)
+            acc = acc + jnp.dot(
+                value[keys], probs.astype(jnp.bfloat16), preferred_element_type=jnp.float32
             )
-            return (new_top, total, acc)
-
-        top, total, acc = lax.fori_loop(
+            return (total, acc)
+
+        totals, acc = lax.fori_loop(
             low // 2,
             pair + 1,
-            per_keys,
+            second_pass,
             (
-                jnp.full((1, 2 * PATCHES), neg_large, jnp.float32),
-                jnp.zeros((1, 2 * PATCHES), jnp.float32),
+                jnp.zeros((8, 2 * PATCHES), jnp.float32),
                 jnp.zeros((HD, 2 * PATCHES), jnp.float32),
             ),
         )
+        total = jnp.sum(totals, axis=0, keepdims=True)
         lse[pair] = top + jnp.log(total)
         mixed[pair] = acc / total
         return carry
@@ -1525,7 +1576,7 @@
 
 
 def call_attend(meta, blocks):
-    vmem = pl.BlockSpec(memory_space=pltpu.VMEM)
+    vmem = pl.BlockSpec()
     result = pl.pallas_call(
         attend_kernel,
         out_shape=tuple(jax.ShapeDtypeStruct((HD, 4 * PATCHES), jnp.bfloat16) for _ in range(4))
@@ -1539,8 +1590,9 @@
             pltpu.VMEM((8, HD, 2 * PATCHES), jnp.bfloat16),
             pltpu.VMEM((8, 2 * PATCHES, HD), jnp.bfloat16),
             pltpu.VMEM((8, HD, 2 * PATCHES), jnp.bfloat16),
+            pltpu.VMEM((8, 2 * PATCHES, 2 * PATCHES), jnp.float32),
         ],
-        compiler_params=pltpu.CompilerParams(vmem_limit_bytes=16 * 2**20),
+        compiler_params=pltpu.CompilerParams(vmem_limit_bytes=48 * 2**20),
         cost_estimate=pl.CostEstimate(flops=9 * 10**9, bytes_accessed=5 * 10**6, transcendentals=10**7),
         name="attend",
     )(meta, *blocks)
@@ -1552,9 +1604,7 @@
     grads = refs[4:8]
     lse, mixed, cosine, sine = refs[8:12]
     outs = refs[12:16]
-    query, query_flat, key, key_flat, value_flat, grad, grad_flat, sum_key, sum_value, sum_query = (
-        refs[16:]
-    )
+    query, key, key_flat, value_flat, grad, sum_key, sum_value, sum_query = refs[16:]
     for member in range(4):
         for frame in range(4):
             slot = 4 * (meta[0] ^ member) + (meta[1] ^ frame)
@@ -1562,14 +1612,12 @@
             place = pl.ds(pl.multiple_of((slot % 2) * 256, 256), 256)
             part = blocks[member][0:64, cols] * 0.125
             query[slot // 2, :, place] = part
-            query_flat[slot // 2, place, :] = turn(part)
             part = blocks[member][64:128, cols]
             key[slot // 2, :, place] = part
             key_flat[slot // 2, place, :] = turn(part)
             value_flat[slot // 2, place, :] = turn(blocks[member][128:192, cols])
             part = grads[member][:, cols]
             grad[slot // 2, :, place] = part
-            grad_flat[slot // 2, place, :] = turn(part)
     sum_key[...] = jnp.zeros_like(sum_key)
     sum_value[...] = jnp.zeros_like(sum_value)
 
@@ -1595,11 +1643,11 @@
                 low_scores.append((probs * (grad_probs[rows] - delta)).astype(jnp.bfloat16))
             all_probs = jnp.concatenate(low_probs, axis=0)
             all_scores = jnp.concatenate(low_scores, axis=0)
-            sum_value[keys] += jnp.dot(
-                all_probs, grad_flat[pair], preferred_element_type=jnp.float32
+            sum_value[keys] += lax.dot_general(
+                wanted_grad, all_probs, NT, preferred_element_type=jnp.float32
             )
-            sum_key[keys] += jnp.dot(
-                all_scores, query_flat[pair], preferred_element_type=jnp.float32
+            sum_key[keys] += lax.dot_general(
+                wanted, all_scores, NT, preferred_element_type=jnp.float32
             )
             return acc + jnp.dot(key[keys], all_scores, preferred_element_type=jnp.float32)
 
@@ -1618,7 +1666,7 @@
             sin_now = sine[slot]
             for base, part in (
                 (0, sum_query[slot // 2, :, place] * 0.125),
-                (64, sum_key[slot // 2, place, :].T),
+                (64, sum_key[slot // 2, :, place]),
             ):
                 upper = part[0:32]
                 lower = part[32:64]
@@ -1628,14 +1676,14 @@
                 outs[member][base + 32 : base + 64, cols] = (
                     lower * cos_now - upper * sin_now
                 ).astype(jnp.bfloat16)
-            outs[member][128:192, cols] = sum_value[slot // 2, place, :].T.astype(jnp.bfloat16)
+            outs[member][128:192, cols] = sum_value[slot // 2, :, place].astype(jnp.bfloat16)
 
 
 def call_attend_back(meta, blocks, grads, lse, mixed, cosine, sine):
-    vmem = pl.BlockSpec(memory_space=pltpu.VMEM)
+    vmem = pl.BlockSpec()
     flat_pair = pltpu.VMEM((8, 2 * PATCHES, HD), jnp.bfloat16)
     turned_pair = pltpu.VMEM((8, HD, 2 * PATCHES), jnp.bfloat16)
-    wide = pltpu.VMEM((8, 2 * PATCHES, HD), jnp.float32)
+    wide = pltpu.VMEM((8, HD, 2 * PATCHES), jnp.float32)
     return list(
         pl.pallas_call(
             attend_back_kernel,
@@ -1646,19 +1694,17 @@
             out_specs=(vmem,) * 4,
             scratch_shapes=[
                 turned_pair,
-                flat_pair,
                 turned_pair,
                 flat_pair,
                 flat_pair,
                 turned_pair,
-                flat_pair,
                 wide,
                 wide,
                 pltpu.VMEM((8, HD, 2 * PATCHES), jnp.float32),
             ],
-            compiler_params=pltpu.CompilerParams(vmem_limit_bytes=20 * 2**20),
+            compiler_params=pltpu.CompilerParams(vmem_limit_bytes=48 * 2**20),
             cost_estimate=pl.CostEstimate(
-                flops=22 * 10**9, bytes_accessed=10**7, transcendentals=10**7
+                flops=30 * 10**9, bytes_accessed=10**7, transcendentals=10**7
             ),
             name="attend_back",
         )(meta, *blocks, *grads, lse, mixed, cosine, sine)
@@ -1698,13 +1744,16 @@
     pieces = ring_gather(call_prepare(device, clean, noise, w_attn, w_io, vectors))
     front_meta, attend_meta, row_levels = call_place(device, lengths, order, levels)
 
+    count = step[0].astype(single)
+    fixes = jnp.stack([1.0 / (1.0 - beta_one**count), 1.0 / (1.0 - beta_two**count)])
+
     half_dim = D // 2
     column = ctx_index * 128 + jnp.arange(128, dtype=jnp.int32)
     frequency = jnp.exp(-math.log(10000.0) * (column % half_dim).astype(single) / half_dim)
     angle = row_levels.astype(single)[:, None] * frequency[None, :]
     cond = jax.nn.silu(jnp.where(column[None, :] < half_dim, jnp.cos(angle), jnp.sin(angle)))
     cond_low = cond.astype(bfloat)
-    cond_slots, cond_relative = cond_low[:32], cond_low[32:]
+    cond_slots = cond_low[:32]
     quarter_cols = 6 * D // 4
     mod_cols = lax.dynamic_slice_in_dim(w_mod, tp_index * quarter_cols, quarter_cols, 1)
     mod_part = jnp.dot(cond_slots, mod_cols.astype(bfloat), preferred_element_type=single)
@@ -1742,10 +1791,10 @@
     sine = full_table(jnp.sin(time_angle), jnp.sin(side_angle))
     signal_scale, noise_scale, weight = plan(row_levels)
     weight_sum = PATCHES * jnp.sum(weight[:32])
-    token_scales = jnp.concatenate([signal_scale[32::8], noise_scale[32::8]])
-    loss_scales = jnp.stack([weight[32], 2.0 / clean.shape[1] * weight[32] / weight_sum])
-
-    front_meta = after(front_meta, mod_rel, cosine, sine, token_scales)
+    token_scales = jnp.concatenate([signal_scale[64:68], noise_scale[64:68]])
+    loss_scales = jnp.stack([weight[64], 2.0 / clean.shape[1] * weight[64] / weight_sum])
+
+    front_meta = after(front_meta, mod_rel, cosine, sine, token_scales, loss_scales, fixes)
     quarters = spread_frames(call_pick(front_meta, pieces))
     front_all, mid_all, hidden_frames, resid_in, *head_blocks, noisy_low, target, mod_own = (
         call_front(front_meta, token_scales, pieces, quarters, mod_rel, cosine, sine)
@@ -1784,8 +1833,16 @@
     hidden_list = spread_frames(hidden_own)
     wide = (2 * PATCHES, w_mlp.shape[2])
     wide_low = jax.ShapeDtypeStruct(wide, bfloat)
-    near = call_mlp(mlp_kernel, "mlp", (wide_low, wide_low), *hidden_list[:2], mlp_w)
     far = call_mlp(mlp_kernel, "mlp", (wide_low, wide_low), *hidden_list[2:], mlp_w)
+    across = sum_across(far)
+    near = call_mlp(
+        mlp_kernel,
+        "mlp",
+        (wide_low, wide_low),
+        after(hidden_list[0], across),
+        hidden_list[1],
+        mlp_w,
+    )
     active, slope = (near[2], far[2]), (near[3], far[3])
     grad_own, grad_three, head_rows, grad_gate_two, error_part = row_call(
         loss_kernel,
@@ -1798,7 +1855,7 @@
             jax.ShapeDtypeStruct((1, 128), single),
         ),
         loss_scales,
-        *sum_frames(near[:2], sum_across(far)),
+        *sum_frames(near[:2], across),
         resid_mid,
         mod_own,
         mid_all,
@@ -1807,7 +1864,15 @@
     )
     grad_list = spread_frames(grad_own)
     near = call_mlp(mlp_back_kernel, "mlp_back", (wide_low,), *grad_list[:2], mlp_w, slope[0])
-    far = call_mlp(mlp_back_kernel, "mlp_back", (wide_low,), *grad_list[2:], mlp_w, slope[1])
+    far = call_mlp(
+        mlp_back_kernel,
+        "mlp_back",
+        (wide_low,),
+        after(grad_list[2], near[0]),
+        grad_list[3],
+        mlp_w,
+        slope[1],
+    )
     across = sum_across(far)
     weight_grad = call_weight_grad(
         hidden_list, grad_list, (near[2], after(far[2], across)), active
@@ -1900,42 +1965,28 @@
         mod_rows,
         smem=1,
     )
-    red_attn, spread, matrix_sq = row_call(
+    red_attn, spread = row_call(
         finish_kernel,
         "finish",
         (
             jax.ShapeDtypeStruct((4, 128, 256), single),
-            jax.ShapeDtypeStruct((8 * MOD_ROWS + 2 * IO_ROWS, 128), bfloat),
-            jax.ShapeDtypeStruct((1, 128), single),
+            jax.ShapeDtypeStruct((8 * MOD_ROWS + 2 * IO_ROWS + 16, 128), bfloat),
         ),
         qkv_own,
         io_own,
         z_pieces[0],
         *(swap(piece, "ctx", 2 * bit) for bit, piece in zip((1, 2, 3), z_pieces[1:])),
         scattered,
-    )
-    grad_mod_w, red_vec, io_grad, mod_sq = call_mod_grad(
-        device, cond_relative, spread_frames(spread)
-    )
-    red_io = io_grad[: 2 * 128].reshape(2, 128, 128)
-    own_sq = matrix_sq + jnp.where(tp_index == 0, mod_sq, 0.0)
-    sums = sum_all(jnp.where(jnp.arange(128)[None, :] < 64, own_sq, error_part))
-    count = step[0].astype(single)
-    fixes = jnp.stack([1.0 / (1.0 - beta_one**count), 1.0 / (1.0 - beta_two**count)])
-    hidden_width = w_mlp.shape[2]
-    red_mlp = jnp.stack(
-        [scattered[:, :hidden_width], scattered[:, hidden_width : 2 * hidden_width]]
-    )
+        error_part,
+    )
+    all_rows, red_vec, io_grad, square = call_mod_grad(device, cond_low, spread_frames(spread))
     updated = call_adam(
         fixes,
-        sums,
-        (
-            (w_attn, m_attn, v_attn, red_attn),
-            (w_mlp, m_mlp, v_mlp, red_mlp),
-            (w_mod, m_mod, v_mod, grad_mod_w),
-        ),
-        (w_io, m_io, v_io, red_io),
+        sum_terms(square),
+        (red_attn, scattered, cond_low, all_rows),
+        (w_io, m_io, v_io, io_grad[: 2 * 128].reshape(2, 128, 128)),
         (vectors, m_vec, v_vec, red_vec),
+        ((w_attn, m_attn, v_attn), (w_mlp, m_mlp, v_mlp), (w_mod, m_mod, v_mod)),
     )
     return (updated[21][1, 64] / weight_sum, updated[21][0, 0], *updated[:21])
 

time: 493 us -> 465 us (0.943)
  local copies, waits for them, and re-layouts: 49 us -> 24.2 us
    unnamed x189 -> x125, local copies, waits for them, and re-layouts: 44.6 us -> 21.6 us
    ppermute x3, waiting for transfers between devices: 14.6 us -> 2.83 us  [ring_gather(): ahead.append(lax.ppermute(ahead[-1], 'ctx', RING_NEXT))]
    ppermute x3, waiting for transfers between devices: 1.82 us -> 13.2 us  [ring_gather(): behind.append(lax.ppermute(behind[-1], 'ctx', RING_PREV))]
    ppermute x61 -> x59, starting transfers between devices: 57.1 us -> 58.4 us  [swap(): return lax.ppermute(values, axis, [(i, i ^ bit) for i in range(size)])]
    ppermute x61 -> x59, waiting for transfers between devices: 188 us -> 188 us  [swap(): return lax.ppermute(values, axis, [(i, i ^ bit) for i in range(size)])]
  transfers between devices with their start and end apart: 71 -> 69, of which waited for: 48 -> 44; matrix products, arithmetic and copies ran while one was open for 4% -> 3% of each run, Pallas kernels for 17% -> 18%
where the time goes in v3:
time: 465 us; the launch traced here: 458 us
  waiting for transfers between devices  220 us (47%)
  Pallas kernels  115 us (25%)
  starting transfers between devices  67.6 us (15%)
  local copies, waits for them, and re-layouts  24.2 us (5%)
  between operations  19.2 us (4%)
  other arithmetic  8.63 us (2%)
    ppermute x59, waiting for transfers between devices, swap(): return lax.ppermute(values, axis, [(i, i ^ bit) for i in range(size)])  188 us
    ppermute x59, starting transfers between devices, swap(): return lax.ppermute(values, axis, [(i, i ^ bit) for i in range(size)])  58.4 us
    pallas_call x1, Pallas kernels, call_attend_back(): pl.pallas_call(attend_back_kernel, out_shape=tuple((jax.ShapeDtypeStruct(...  30.1 us
    pallas_call x1, Pallas kernels, call_attend(): pl.pallas_call(attend_kernel, out_shape=tuple((jax.ShapeDtypeStruct((HD,...  22.6 us
    unnamed x125, local copies, waits for them, and re-layouts  21.6 us
    ppermute x3, waiting for transfers between devices, ring_gather(): behind.append(lax.ppermute(behind[-1], 'ctx', RING_PREV))  13.2 us
    pallas_call x1, Pallas kernels, call_adam(): pl.pallas_call(adam_kernel, out_shape=out_shape, in_specs=smem_specs(1) +...  12.5 us
    pallas_call x8, Pallas kernels, row_call(): pl.pallas_call(kernel, out_shape=tuple(outs), in_specs=smem_specs(smem) +...  11.9 us
  transfers between devices with their start and end apart: 69, of which 44 were waited for; matrix products, arithmetic and copies ran while one was open for 3% of the time, Pallas kernels for 18%

profile of v3, /device:TPU:0, one launch (start us, length us, event | category | flops | bytes accessed | tf_op | source)
XLA Modules:
  0.0 458.0 jit_solution(18041323646198894967)
XLA Ops:
  29.3 6.6 %collective-permute-done.4.refs_5_ = bf16[1808,128]{1,0:T(8,128)(2,1)} collective-permute-done((bf16[1808,128]{1,0:T(8,128)(2,1)S(1)}, bf16[1808,128]{1,0:T(8,128)(2,1)}, u32[]{:S(2)}, u32[]{:S(2)}) %collective-permute-start.4) | collective-permute-done | bytes 462880 | tf_op jit(solution)/shard_map/ppermute | solution.py:599
  60.0 7.3 %collective-permute-done.13 = bf16[904,128]{1,0:T(8,128)(2,1)S(1)} collective-permute-done((bf16[904,128]{1,0:T(8,128)(2,1)}, bf16[904,128]{1,0:T(8,128)(2,1)S(1)}, u32[]{:S(2)}, u32[]{:S(2)}) %collective-permute-start.13) | collective-permute-done | bytes 231456 | tf_op jit(solution)/shard_map/ppermute | solution.py:600
  78.0 8.2 %front.1 = (bf16[912,1024]{1,0:T(8,128)(2,1)}, bf16[1024,384]{1,0:T(8,128)(2,1)}, bf16[4,256,1024]{2,1,0:T(8,128)(2,1)}, f32[256,1024]{1,0:T(8,128)}, bf16[192,1...) custom-call(s32[24]{0:T(128)S(1)} %copy-done.24, ...), custom_call_target="tpu_custom_call" | custom-call | flops 2000000000 | bytes 10000000 | tf_op jit(solution)/shard_map/front/pallas_call | solution.py:921
  91.3 6.8 %collective-permute-done.18.refs_1_ = bf16[192,1024]{1,0:T(8,128)(2,1)S(1)} collective-permute-done((bf16[192,1024]{1,0:T(8,128)(2,1)S(1)}, bf16[192,1024]{1,0:T(8,128)(2,1)S(1)}, u32[]{:S(2)}, u32[]{:S(2)}) %collective-permute-start.18) | collective-permute-done | bytes 393248 | tf_op jit(solution)/shard_map/ppermute | solution.py:586
  99.4 8.5 %collective-permute-done.20.refs_3_ = bf16[192,1024]{1,0:T(8,128)(2,1)S(1)} collective-permute-done((bf16[192,1024]{1,0:T(8,128)(2,1)}, bf16[192,1024]{1,0:T(8,128)(2,1)S(1)}, u32[]{:S(2)}, u32[]{:S(2)}) %collective-permute-start.20) | collective-permute-done | bytes 393248 | tf_op jit(solution)/shard_map/ppermute | solution.py:586
  108.0 22.6 %attend.1 = (bf16[64,1024]{1,0:T(8,128)(2,1)S(1)}, bf16[64,1024]{1,0:T(8,128)(2,1)S(1)}, bf16[64,1024]{1,0:T(8,128)(2,1)S(1)}, bf16[64,1024]{1,0:T(8,128)(2,1)S(...) custom-call(s32[18]{0:T(128)S(1)} %copy-done.41, bf16[192,1024]{1,0:T(8,128)(2,1)S(1)} %get-tuple-element.141.refs_0_, ...), custom_call_target="tpu_custom_call" | custom-call | flops 8999999488 | bytes 5000000 | tf_op jit(solution)/shard_map/attend/pallas_call | solution.py:1580
  136.4 5.6 %collective-permute-done.21 = bf16[64,1024]{1,0:T(8,128)(2,1)S(1)} collective-permute-done((bf16[64,1024]{1,0:T(8,128)(2,1)S(1)}, bf16[64,1024]{1,0:T(8,128)(2,1)S(1)}, u32[]{:S(2)}, u32[]{:S(2)}) %collective-permute-start.21) | collective-permute-done | bytes 131104 | tf_op jit(solution)/shard_map/ppermute | solution.py:586
  147.4 12.4 %collective-permute-done.26.across = bf16[256,1024]{1,0:T(8,128)(2,1)S(1)} collective-permute-done((bf16[256,1024]{1,0:T(8,128)(2,1)S(1)}, bf16[256,1024]{1,0:T(8,128)(2,1)S(1)}, u32[]{:S(2)}, u32[]{:S(2)}) %collective-permute-start.26) | collective-permute-done | bytes 524320 | tf_op jit(solution)/shard_map/ppermute | solution.py:586
  162.5 11.8 %collective-permute-done.27.first.refs_2_ = bf16[256,1024]{1,0:T(8,128)(2,1)S(1)} collective-permute-done((bf16[256,1024]{1,0:T(8,128)(2,1)S(1)}, bf16[256,1024]{1,0:T(8,128)(2,1)S(1)}, u32[]{:S(2)}, u32[]{:S(2)}) %collective-permute-start.27) | collective-permute-done | bytes 524320 | tf_op jit(solution)/shard_map/ppermute | solution.py:586
  177.1 8.3 %all-gather.2.cloned.1.call-done.weights = bf16[2,1024,1024]{2,1,0:T(8,128)(2,1)} async-done(((bf16[2,128,1024]{2,1,0:T(8,128)(2,1)}), bf16[2,1024,1024]{2,1,0:T(8,128)(2,1)}) %all-gather.2.cloned.1.call-update) | async-done | bytes 4194320 | tf_op jit(solution)/shard_map/all_gather | solution.py:1811
  199.2 9.5 %collective-permute-done.32.across = bf16[256,1024]{1,0:T(8,128)(2,1)S(1)} collective-permute-done((bf16[256,1024]{1,0:T(8,128)(2,1)S(1)}, bf16[256,1024]{1,0:T(8,128)(2,1)S(1)}, u32[]{:S(2)}, u32[]{:S(2)}) %collective-permute-start.32) | collective-permute-done | bytes 524320 | tf_op jit(solution)/shard_map/ppermute | solution.py:586
  213.9 11.6 %collective-permute-done.35.first.refs_6_ = bf16[256,1024]{1,0:T(8,128)(2,1)S(1)} collective-permute-done((bf16[256,1024]{1,0:T(8,128)(2,1)S(1)}, bf16[256,1024]{1,0:T(8,128)(2,1)S(1)}, u32[]{:S(2)}, u32[]{:S(2)}) %collective-permute-start.35) | collective-permute-done | bytes 524320 | tf_op jit(solution)/shard_map/ppermute | solution.py:586
  236.8 5.6 %weight_grad.1 = bf16[1024,2048]{1,0:T(8,128)(2,1)S(1)} custom-call(bf16[256,1024]{1,0:T(8,128)(2,1)S(1)} %copy-done.28, bf16[256,1024]{1,0:T(8,128)(2,1)S(1)} %collective-permute-done.30.second.refs_1_, bf16[256,1024]{1,0:T(8,128)(2,1)S(1)} %copy-done.31, bf16[256,1024]{1,0:T(8,128)(2,1)S(1)} %copy-done.34, ...), custom_call_target="tpu_custom_call" | custom-call | flops 5000000000 | bytes 20000000 | tf_op jit(solution)/shard_map/weight_grad/pallas_call | solution.py:1257
  256.1 11.9 %collective-permute-done.40 = bf16[256,1024]{1,0:T(8,128)(2,1)S(1)} collective-permute-done((bf16[256,1024]{1,0:T(8,128)(2,1)S(1)}, bf16[256,1024]{1,0:T(8,128)(2,1)S(1)}, u32[]{:S(2)}, u32[]{:S(2)}) %collective-permute-start.40) | collective-permute-done | bytes 524320 | tf_op jit(solution)/shard_map/ppermute | solution.py:586
  276.0 8.7 %collective-permute-done.44.refs_7_ = bf16[64,1024]{1,0:T(8,128)(2,1)S(1)} collective-permute-done((bf16[64,1024]{1,0:T(8,128)(2,1)S(1)}, bf16[64,1024]{1,0:T(8,128)(2,1)S(1)}, u32[]{:S(2)}, u32[]{:S(2)}) %collective-permute-start.44) | collective-permute-done | bytes 131104 | tf_op jit(solution)/shard_map/ppermute | solution.py:586
  284.6 5.8 %collective-permute-done.43.refs_6_ = bf16[64,1024]{1,0:T(8,128)(2,1)S(1)} collective-permute-done((bf16[64,1024]{1,0:T(8,128)(2,1)S(1)}, bf16[64,1024]{1,0:T(8,128)(2,1)S(1)}, u32[]{:S(2)}, u32[]{:S(2)}) %collective-permute-start.43) | collective-permute-done | bytes 131104 | tf_op jit(solution)/shard_map/ppermute | solution.py:586
  290.5 30.1 %attend_back.1 = (bf16[192,1024]{1,0:T(8,128)(2,1)S(1)}, bf16[192,1024]{1,0:T(8,128)(2,1)S(1)}, bf16[192,1024]{1,0:T(8,128)(2,1)S(1)}, bf16[192,1024]{1,0:T(8,128)(2,1)S(1)}) custom-call(s32[18]{0:T(128)S(1)} %copy-done.41, bf16[192,1024]{1,0:T(8,128)(2,1)S(1)} %copy-done.47, bf16[192,1024]{1,0:T(8,128)(2,1)S(1)} %copy-done.36, ...), custom_call_target="tpu_custom_call" | custom-call | flops 30000001024 | bytes 10000000 | tf_op jit(solution)/shard_map/attend_back/pallas_call | solution.py:1688
  325.6 12.0 %collective-permute-done.48.out_came = bf16[4,256,128]{2,1,0:T(8,128)(2,1)S(1)} collective-permute-done((bf16[4,256,128]{2,1,0:T(8,128)(2,1)S(1)}, bf16[4,256,128]{2,1,0:T(8,128)(2,1)S(1)}, u32[]{:S(2)}, u32[]{:S(2)}) %collective-permute-start.48) | collective-permute-done | bytes 262176 | tf_op jit(solution)/shard_map/ppermute | solution.py:586
  337.6 6.7 %collective-permute-done.46.refs_2_ = bf16[192,1024]{1,0:T(8,128)(2,1)S(1)} collective-permute-done((bf16[192,1024]{1,0:T(8,128)(2,1)S(1)}, bf16[192,1024]{1,0:T(8,128)(2,1)S(1)}, u32[]{:S(2)}, u32[]{:S(2)}) %collective-permute-start.46) | collective-permute-done | bytes 393248 | tf_op jit(solution)/shard_map/ppermute | solution.py:586
  344.3 7.6 %collective-permute-done.47.refs_3_ = bf16[192,1024]{1,0:T(8,128)(2,1)S(1)} collective-permute-done((bf16[192,1024]{1,0:T(8,128)(2,1)S(1)}, bf16[192,1024]{1,0:T(8,128)(2,1)S(1)}, u32[]{:S(2)}, u32[]{:S(2)}) %collective-permute-start.47) | collective-permute-done | bytes 393248 | tf_op jit(solution)/shard_map/ppermute | solution.py:586
  362.6 8.0 %collective-permute-done.52.across = bf16[256,1024]{1,0:T(8,128)(2,1)S(1)} collective-permute-done((bf16[256,1024]{1,0:T(8,128)(2,1)S(1)}, bf16[256,1024]{1,0:T(8,128)(2,1)S(1)}, u32[]{:S(2)}, u32[]{:S(2)}) %collective-permute-start.52) | collective-permute-done | bytes 524320 | tf_op jit(solution)/shard_map/ppermute | solution.py:586
  392.5 6.1 %collective-permute-done.57.refs_3_ = bf16[1200,128]{1,0:T(8,128)(2,1)S(1)} collective-permute-done((bf16[1200,128]{1,0:T(8,128)(2,1)S(1)}, bf16[1200,128]{1,0:T(8,128)(2,1)S(1)}, u32[]{:S(2)}, u32[]{:S(2)}) %collective-permute-start.57) | collective-permute-done | bytes 307232 | tf_op jit(solution)/shard_map/ppermute | solution.py:586
  398.6 12.3 %collective-permute-done.58.refs_4_ = bf16[1200,128]{1,0:T(8,128)(2,1)S(1)} collective-permute-done((bf16[1200,128]{1,0:T(8,128)(2,1)S(1)}, bf16[1200,128]{1,0:T(8,128)(2,1)S(1)}, u32[]{:S(2)}, u32[]{:S(2)}) %collective-permute-start.58) | collective-permute-done | bytes 307232 | tf_op jit(solution)/shard_map/ppermute | solution.py:586
  436.1 12.5 %adam.1 = (f32[4,128,256]{2,1,0:T(8,128)}, f32[4,128,256]{2,1,0:T(8,128)}, f32[4,128,256]{2,1,0:T(8,128)}, bf16[4,128,256]{2,1,0:T(8,128)(2,1)}, f32[2,128,1024]...) custom-call(f32[2]{0:T(128)S(1)} %pad_maximum_fusion.5.refs_0_, ...), custom_call_target="tpu_custom_call" | custom-call | flops 10000000 | bytes 20000000 | tf_op jit(solution)/shard_map/adam/pallas_call | solution.py:1448
  (326 shorter events, 192.2 us)
Async XLA Ops:
  7.2 178.2 %all-gather.2.cloned.1.call-start = ((), (), s32[]{:S(2)}) async-start(), calls=%async_computation.1 | async-start | bytes 4718592 | tf_op jit(solution)/shard_map/all_gather | solution.py:1811
  10.0 14.6 %collective-permute-start.3 = (bf16[1808,128]{1,0:T(8,128)(2,1)}, bf16[1808,128]{1,0:T(8,128)(2,1)S(1)}, u32[]{:S(2)}, u32[]{:S(2)}) collective-permute-start(bf16[1808,128]{1,0:T(8,128)(2,1)} %prepare.1.refs_0_), channel_id=1, source_target_pairs={{4,0},{12,4},{20,12},{28,20},{24,28},{16,24},{8,16},{0,8},{5,1},{1... | collective-permute-start | bytes 1388552 | tf_op jit(solution)/shard_map/ppermute | solution.py:599
  13.0 12.6 %collective-permute-start.1 = (bf16[1808,128]{1,0:T(8,128)(2,1)}, bf16[1808,128]{1,0:T(8,128)(2,1)S(1)}, u32[]{:S(2)}, u32[]{:S(2)}) collective-permute-start(bf16[1808,128]{1,0:T(8,128)(2,1)} %prepare.1.refs_0_), channel_id=1, source_target_pairs={{0,4},{4,12},{12,20},{20,28},{28,24},{24,16},{16,8},{8,0},{1,5},{5... | collective-permute-start | bytes 1388552 | tf_op jit(solution)/shard_map/ppermute | solution.py:598
  87.2 12.2 %collective-permute-start.19 = (bf16[192,1024]{1,0:T(8,128)(2,1)}, bf16[192,1024]{1,0:T(8,128)(2,1)S(1)}, u32[]{:S(2)}, u32[]{:S(2)}) collective-permute-start(bf16[192,1024]{1,0:T(8,128)(2,1)} %get-tuple-element.143), channel_id=1, source_target_pairs={{0,8},{4,12},{8,0},{12,4},{16,24},{20,28},{24,16},{28,20},{1,9},{5... | collective-permute-start | bytes 1179656 | tf_op jit(solution)/shard_map/ppermute | solution.py:586
  87.5 20.4 %collective-permute-start.20 = (bf16[192,1024]{1,0:T(8,128)(2,1)}, bf16[192,1024]{1,0:T(8,128)(2,1)S(1)}, u32[]{:S(2)}, u32[]{:S(2)}) collective-permute-start(bf16[192,1024]{1,0:T(8,128)(2,1)} %get-tuple-element.144), channel_id=1, source_target_pairs={{0,12},{4,8},{8,4},{12,0},{16,28},{20,24},{24,20},{28,16},{1,13},{... | collective-permute-start | bytes 1179656 | tf_op jit(solution)/shard_map/ppermute | solution.py:586
  107.9 303.0 %reduce-scatter.2.cloned.1.call-start = ((), (), s32[]{:S(2)}) async-start(), calls=%async_computation.2 | async-start | bytes 4718592 | tf_op jit(solution)/shard_map/reduce_scatter | solution.py:1880
  145.8 14.0 %collective-permute-start.26 = (bf16[256,1024]{1,0:T(8,128)(2,1)S(1)}, bf16[256,1024]{1,0:T(8,128)(2,1)S(1)}, u32[]{:S(2)}, u32[]{:S(2)}) collective-permute-start(bf16[256,1024]{1,0:T(8,128)(2,1)S(1)} %fusion), channel_id=1, source_target_pairs={{0,2},{1,3},{2,0},{3,1},{4,6},{5,7},{6,4},{7,5},{8,10},{9,11},{10,... | collective-permute-start | bytes 1572872 | tf_op jit(solution)/shard_map/ppermute | solution.py:586
  161.1 13.2 %collective-permute-start.27 = (bf16[256,1024]{1,0:T(8,128)(2,1)S(1)}, bf16[256,1024]{1,0:T(8,128)(2,1)S(1)}, u32[]{:S(2)}, u32[]{:S(2)}) collective-permute-start(bf16[256,1024]{1,0:T(8,128)(2,1)S(1)} %get-tuple-element.156.first.refs_0_), channel_id=1, source_target_pairs={{0,2},{1,3},{2,0},{3,1},{4,6},{5,7},{6,4},{7,5},{8,10},{9,11},{10,... | collective-permute-start | bytes 1572872 | tf_op jit(solution)/shard_map/ppermute | solution.py:586
  194.7 14.0 %collective-permute-start.32 = (bf16[256,1024]{1,0:T(8,128)(2,1)S(1)}, bf16[256,1024]{1,0:T(8,128)(2,1)S(1)}, u32[]{:S(2)}, u32[]{:S(2)}) collective-permute-start(bf16[256,1024]{1,0:T(8,128)(2,1)S(1)} %add_convert_fusion.2), channel_id=1, source_target_pairs={{0,2},{1,3},{2,0},{3,1},{4,6},{5,7},{6,4},{7,5},{8,10},{9,11},{10,... | collective-permute-start | bytes 1572872 | tf_op jit(solution)/shard_map/ppermute | solution.py:586
  212.4 13.1 %collective-permute-start.35 = (bf16[256,1024]{1,0:T(8,128)(2,1)S(1)}, bf16[256,1024]{1,0:T(8,128)(2,1)S(1)}, u32[]{:S(2)}, u32[]{:S(2)}) collective-permute-start(bf16[256,1024]{1,0:T(8,128)(2,1)S(1)} %get-tuple-element.161.first.refs_4_), channel_id=1, source_target_pairs={{0,2},{1,3},{2,0},{3,1},{4,6},{5,7},{6,4},{7,5},{8,10},{9,11},{10,... | collective-permute-start | bytes 1572872 | tf_op jit(solution)/shard_map/ppermute | solution.py:586
  235.3 14.5 %collective-permute-start.38 = (bf16[256,1024]{1,0:T(8,128)(2,1)}, bf16[256,1024]{1,0:T(8,128)(2,1)}, u32[]{:S(2)}, u32[]{:S(2)}) collective-permute-start(bf16[256,1024]{1,0:T(8,128)(2,1)} %add_convert_fusion.1), channel_id=1, source_target_pairs={{0,2},{1,3},{2,0},{3,1},{4,6},{5,7},{6,4},{7,5},{8,10},{9,11},{10,... | collective-permute-start | bytes 1572872 | tf_op jit(solution)/shard_map/ppermute | solution.py:586
  254.6 13.5 %collective-permute-start.40 = (bf16[256,1024]{1,0:T(8,128)(2,1)S(1)}, bf16[256,1024]{1,0:T(8,128)(2,1)S(1)}, u32[]{:S(2)}, u32[]{:S(2)}) collective-permute-start(bf16[256,1024]{1,0:T(8,128)(2,1)S(1)} %get-tuple-element.177), channel_id=1, source_target_pairs={{0,2},{1,3},{2,0},{3,1},{4,6},{5,7},{6,4},{7,5},{8,10},{9,11},{10,... | collective-permute-start | bytes 1572872 | tf_op jit(solution)/shard_map/ppermute | solution.py:586
  256.1 12.0 %collective-permute-start.39 = (bf16[256,1024]{1,0:T(8,128)(2,1)S(1)}, bf16[256,1024]{1,0:T(8,128)(2,1)S(1)}, u32[]{:S(2)}, u32[]{:S(2)}) collective-permute-start(bf16[256,1024]{1,0:T(8,128)(2,1)S(1)} %get-tuple-element.177), channel_id=1, source_target_pairs={{0,1},{1,0},{2,3},{3,2},{4,5},{5,4},{6,7},{7,6},{8,9},{9,8},{10,11... | collective-permute-start | bytes 1572872 | tf_op jit(solution)/shard_map/ppermute | solution.py:586
  270.8 13.8 %collective-permute-start.44 = (bf16[64,1024]{1,0:T(8,128)(2,1)S(1)}, bf16[64,1024]{1,0:T(8,128)(2,1)S(1)}, u32[]{:S(2)}, u32[]{:S(2)}) collective-permute-start(bf16[64,1024]{1,0:T(8,128)(2,1)S(1)} %get-tuple-element.251), channel_id=1, source_target_pairs={{0,12},{4,8},{8,4},{12,0},{16,28},{20,24},{24,20},{28,16},{1,13},{... | collective-permute-start | bytes 393224 | tf_op jit(solution)/shard_map/ppermute | solution.py:586
  271.9 12.8 %collective-permute-start.42 = (bf16[64,1024]{1,0:T(8,128)(2,1)S(1)}, bf16[64,1024]{1,0:T(8,128)(2,1)S(1)}, u32[]{:S(2)}, u32[]{:S(2)}) collective-permute-start(bf16[64,1024]{1,0:T(8,128)(2,1)S(1)} %get-tuple-element.253), channel_id=1, source_target_pairs={{0,4},{4,0},{8,12},{12,8},{16,20},{20,16},{24,28},{28,24},{1,5},{5... | collective-permute-start | bytes 393224 | tf_op jit(solution)/shard_map/ppermute | solution.py:586
  273.5 16.9 %collective-permute-start.43 = (bf16[64,1024]{1,0:T(8,128)(2,1)S(1)}, bf16[64,1024]{1,0:T(8,128)(2,1)S(1)}, u32[]{:S(2)}, u32[]{:S(2)}) collective-permute-start(bf16[64,1024]{1,0:T(8,128)(2,1)S(1)} %get-tuple-element.254), channel_id=1, source_target_pairs={{0,8},{4,12},{8,0},{12,4},{16,24},{20,28},{24,16},{28,20},{1,9},{5... | collective-permute-start | bytes 393224 | tf_op jit(solution)/shard_map/ppermute | solution.py:586
  320.6 17.1 %collective-permute-start.45 = (bf16[192,1024]{1,0:T(8,128)(2,1)S(1)}, bf16[192,1024]{1,0:T(8,128)(2,1)S(1)}, u32[]{:S(2)}, u32[]{:S(2)}) collective-permute-start(bf16[192,1024]{1,0:T(8,128)(2,1)S(1)} %get-tuple-element.184), channel_id=1, source_target_pairs={{0,4},{4,0},{8,12},{12,8},{16,20},{20,16},{24,28},{28,24},{1,5},{5... | collective-permute-start | bytes 1179656 | tf_op jit(solution)/shard_map/ppermute | solution.py:586
  322.1 22.2 %collective-permute-start.46 = (bf16[192,1024]{1,0:T(8,128)(2,1)S(1)}, bf16[192,1024]{1,0:T(8,128)(2,1)S(1)}, u32[]{:S(2)}, u32[]{:S(2)}) collective-permute-start(bf16[192,1024]{1,0:T(8,128)(2,1)S(1)} %get-tuple-element.185), channel_id=1, source_target_pairs={{0,8},{4,12},{8,0},{12,4},{16,24},{20,28},{24,16},{28,20},{1,9},{5... | collective-permute-start | bytes 1179656 | tf_op jit(solution)/shard_map/ppermute | solution.py:586
  322.1 29.8 %collective-permute-start.47 = (bf16[192,1024]{1,0:T(8,128)(2,1)S(1)}, bf16[192,1024]{1,0:T(8,128)(2,1)S(1)}, u32[]{:S(2)}, u32[]{:S(2)}) collective-permute-start(bf16[192,1024]{1,0:T(8,128)(2,1)S(1)} %get-tuple-element.186), channel_id=1, source_target_pairs={{0,12},{4,8},{8,4},{12,0},{16,28},{20,24},{24,20},{28,16},{1,13},{... | collective-permute-start | bytes 1179656 | tf_op jit(solution)/shard_map/ppermute | solution.py:586
  324.1 13.5 %collective-permute-start.48 = (bf16[4,256,128]{2,1,0:T(8,128)(2,1)S(1)}, bf16[4,256,128]{2,1,0:T(8,128)(2,1)S(1)}, u32[]{:S(2)}, u32[]{:S(2)}) collective-permute-start(bf16[4,256,128]{2,1,0:T(8,128)(2,1)S(1)} %get-tuple-element.188), channel_id=1, source_target_pairs={{0,4},{4,0},{8,12},{12,8},{16,20},{20,16},{24,28},{28,24},{1,5},{5... | collective-permute-start | bytes 786440 | tf_op jit(solution)/shard_map/ppermute | solution.py:586
  356.6 14.0 %collective-permute-start.52 = (bf16[256,1024]{1,0:T(8,128)(2,1)S(1)}, bf16[256,1024]{1,0:T(8,128)(2,1)S(1)}, u32[]{:S(2)}, u32[]{:S(2)}) collective-permute-start(bf16[256,1024]{1,0:T(8,128)(2,1)S(1)} %add_convert_fusion), channel_id=1, source_target_pairs={{0,2},{1,3},{2,0},{3,1},{4,6},{5,7},{6,4},{7,5},{8,10},{9,11},{10,... | collective-permute-start | bytes 1572872 | tf_op jit(solution)/shard_map/ppermute | solution.py:586
  361.0 22.5 %collective-permute-start.50 = (bf16[4,768,128]{2,1,0:T(8,128)(2,1)S(1)}, bf16[4,768,128]{2,1,0:T(8,128)(2,1)S(1)}, u32[]{:S(2)}, u32[]{:S(2)}) collective-permute-start(bf16[4,768,128]{2,1,0:T(8,128)(2,1)S(1)} %get-tuple-element.196), channel_id=1, source_target_pairs={{0,4},{4,0},{8,12},{12,8},{16,20},{20,16},{24,28},{28,24},{1,5},{5... | collective-permute-start | bytes 2359304 | tf_op jit(solution)/shard_map/ppermute | solution.py:586
  388.5 22.3 %collective-permute-start.58 = (bf16[1200,128]{1,0:T(8,128)(2,1)S(1)}, bf16[1200,128]{1,0:T(8,128)(2,1)S(1)}, u32[]{:S(2)}, u32[]{:S(2)}) collective-permute-start(bf16[1200,128]{1,0:T(8,128)(2,1)S(1)} %get-tuple-element.216), channel_id=1, source_target_pairs={{0,16},{4,20},{8,24},{12,28},{16,0},{20,4},{24,8},{28,12},{1,17},{... | collective-permute-start | bytes 921608 | tf_op jit(solution)/shard_map/ppermute | solution.py:586
  388.6 22.3 %collective-permute-start.59 = (bf16[1200,128]{1,0:T(8,128)(2,1)S(1)}, bf16[1200,128]{1,0:T(8,128)(2,1)S(1)}, u32[]{:S(2)}, u32[]{:S(2)}) collective-permute-start(bf16[1200,128]{1,0:T(8,128)(2,1)S(1)} %get-tuple-element.217), channel_id=1, source_target_pairs={{0,24},{4,28},{8,16},{12,20},{16,8},{20,12},{24,0},{28,4},{1,25},{... | collective-permute-start | bytes 921608 | tf_op jit(solution)/shard_map/ppermute | solution.py:586
  (104 other events, 1019.0 us)
Sparse Core Ops, SparseCore 0:
  108.0 77.3 all-gather.1
  244.5 100.9 reduce-scatter.1

commit v4 on v3

--- a/solution.py
+++ b/solution.py
@@ -566,9 +566,6 @@
     )
 
 
-RING = (0, 1, 3, 5, 7, 6, 4, 2)
-RING_NEXT = tuple((RING[i], RING[(i + 1) % 8]) for i in range(8))
-RING_PREV = tuple((b, a) for a, b in RING_NEXT)
 HALF_SLOTS = 16
 QKV_ROWS = 768
 ATTN_ROWS = 1024
@@ -576,7 +573,6 @@
 TOKEN_ROWS = 512
 IO_ROWS = 80
 MOD_ROWS = 48
-RING_ROWS = TOKEN_ROWS + FRONT_ROWS + 384
 NT = (((1,), (1,)), ((), ()))
 TN = (((0,), (0,)), ((), ()))
 
@@ -590,16 +586,10 @@
     return lax.optimization_barrier((values,) + others)[0]
 
 
-def ring_gather(shard):
-    half = shard.shape[0] // 2
-    ahead = [shard]
-    behind = [shard]
-    for _ in range(3):
-        ahead.append(lax.ppermute(ahead[-1], "ctx", RING_NEXT))
-        behind.append(lax.ppermute(behind[-1], "ctx", RING_PREV))
-    first = lax.ppermute(ahead[-1][:half], "ctx", RING_NEXT)
-    second = lax.ppermute(behind[-1][half:], "ctx", RING_PREV)
-    return ahead + behind[1:] + [jnp.concatenate([first, second], axis=0)]
+def gather_swaps(shard):
+    along_x = swap(shard, "ctx", 1)
+    along_z = [swap(shard, "ctx", bit) for bit in (2, 4, 6)]
+    return [shard, along_x, *along_z, swap(jnp.concatenate(along_z, axis=0), "ctx", 1)]
 
 
 def reduce_blocks(blocks, ctx_index, wire):
@@ -658,12 +648,14 @@
     return [values] + [swap(values, "ctx", bit) for bit in (2, 4, 6)]
 
 
-def prepare_kernel(meta, clean, noise, w_attn, w_io, vectors, ring):
-    front = ring.at[TOKEN_ROWS:RING_ROWS]
+def token_kernel(meta, clean, noise, ring):
     for frame in range(4):
         rows = pl.ds(pl.multiple_of(256 * frame + 64 * meta[1], 64), 64)
         ring[128 * frame : 128 * frame + 64, :] = clean[rows, :]
         ring[128 * frame + 64 : 128 * frame + 128, :] = noise[rows, :]
+
+
+def prepare_kernel(w_attn, w_io, vectors, front):
     for part in range(3):
         front[256 * part : 256 * part + 256, :] = w_attn[part].T.astype(jnp.bfloat16)
     base = QKV_ROWS
@@ -687,14 +679,24 @@
     return [pl.BlockSpec(memory_space=pltpu.SMEM)] * count
 
 
-def call_prepare(device, clean, noise, w_attn, w_io, vectors):
+def call_tokens(device, clean, noise):
+    return pl.pallas_call(
+        token_kernel,
+        out_shape=jax.ShapeDtypeStruct((TOKEN_ROWS, 128), jnp.bfloat16),
+        in_specs=smem_specs(1) + vmem_specs(2),
+        out_specs=vmem_specs(1)[0],
+        name="tokens",
+    )(device, clean, noise)
+
+
+def call_prepare(w_attn, w_io, vectors):
     return pl.pallas_call(
         prepare_kernel,
-        out_shape=jax.ShapeDtypeStruct((RING_ROWS, 128), jnp.bfloat16),
-        in_specs=smem_specs(1) + vmem_specs(5),
+        out_shape=jax.ShapeDtypeStruct((FRONT_ROWS + 384, 128), jnp.bfloat16),
+        in_specs=vmem_specs(3),
         out_specs=vmem_specs(1)[0],
         name="prepare",
-    )(device, clean, noise, w_attn, w_io, vectors)
+    )(w_attn, w_io, vectors)
 
 
 def place_kernel(device, lengths, order, levels, front, attend, rows, inverse, stored, position, level):
@@ -730,25 +732,15 @@
 
     lax.fori_loop(0, frames, per_frame, (jnp.int32(0), jnp.int32(0)))
 
-    def where_on_ring(index):
-        z, x = index >> 1, index & 1
-        return jnp.where(x == 1, z + 1, (8 - z) & 7)
-
-    mine = where_on_ring(ctx)
     member = ctx & 3
-    for place, offset in enumerate((0, 7, 6, 5, 1, 2, 3, 4)):
-        at = (mine + offset) & 7
-        front[place] = jnp.where(
-            at == 0, 0, jnp.where(at <= 4, 2 * at - 1, 2 * (8 - at))
-        )
     for k in range(4):
         front[8 + k] = 4 * member + (tp ^ k)
         front[12 + k] = member ^ k
         at = stored[4 * ctx + (tp ^ k)]
-        distance = (where_on_ring(at >> 2) - mine) & 7
-        place = jnp.where(distance == 0, 0, jnp.where(distance <= 4, distance + 3, 8 - distance))
-        front[16 + k] = place * 4 + (at & 3)
+        front[16 + k] = ((at >> 2) ^ ctx) * 4 + (at & 3)
         front[20 + k] = tp ^ k
+    for k in range(8):
+        front[k] = 0
     attend[0] = member
     attend[1] = tp
     base = lax.div(ctx, jnp.int32(4)) * half
@@ -787,16 +779,19 @@
 
 
 def pick_kernel(meta, *refs):
-    out, sems = refs[8:]
+    out, sems = refs[6:]
+    places = [(refs[0], 0), (refs[1], 0)]
+    for bit in range(3):
+        places += [(refs[2 + bit], 0), (refs[5], TOKEN_ROWS * bit)]
     for frame in range(4):
         wanted = meta[16 + frame]
-        for place in range(8):
+        for place, (source, base) in enumerate(places):
 
             @pl.when((wanted >> 2) == place)
             def _():
-                start = pl.multiple_of((wanted & 3) * 128, 128)
+                start = pl.multiple_of(base + (wanted & 3) * 128, 128)
                 pltpu.make_async_copy(
-                    refs[place].at[pl.ds(start, 128), :],
+                    source.at[pl.ds(start, 128), :],
                     out.at[128 * frame : 128 * frame + 128, :],
                     sems.at[frame],
                 ).start()
@@ -815,7 +810,7 @@
     return pl.pallas_call(
         pick_kernel,
         out_shape=jax.ShapeDtypeStruct((TOKEN_ROWS, 128), jnp.bfloat16),
-        in_specs=smem_specs(1) + hbm_specs(8),
+        in_specs=smem_specs(1) + hbm_specs(6),
         out_specs=vmem_specs(1)[0],
         scratch_shapes=[pltpu.SemaphoreType.DMA((4,))],
         compiler_params=pltpu.CompilerParams(vmem_limit_bytes=56 * 2**20),
@@ -830,16 +825,14 @@
 
 
 def front_kernel(meta, scales, *refs):
-    pieces, quarters = refs[:8], refs[8:12]
-    mod, cosine, sine = refs[12:15]
-    weights_out, mid_out, hidden_out, resid_out = refs[15:19]
-    head_outs = refs[19:23]
-    noisy_out, target_out, mod_out = refs[23:26]
-    tokens, heads, weights, mid, hidden, resid, target, mod_own, held, sems, out_sems = refs[26:]
+    pieces, quarters = refs[0], refs[1:5]
+    mod, cosine, sine = refs[5:8]
+    weights_out, mid_out, hidden_out, resid_out = refs[8:12]
+    head_outs = refs[12:16]
+    noisy_out, target_out, mod_out = refs[16:19]
+    tokens, heads, weights, mid, hidden, resid, target, mod_own, held, sems, out_sems = refs[19:]
     copies = [
-        pltpu.make_async_copy(
-            pieces[place].at[TOKEN_ROWS:RING_ROWS, :], held.at[place], sems.at[place]
-        )
+        pltpu.make_async_copy(pieces.at[place], held.at[place], sems.at[place])
         for place in range(8)
     ]
     for copy in copies:
@@ -867,7 +860,7 @@
     outs.append(pltpu.make_async_copy(mid, mid_out, out_sems.at[9]))
     for place in range(8):
         copies[place].wait()
-        block = pl.ds(pl.multiple_of(meta[place] * 128, 128), 128)
+        block = slice(128 * place, 128 * place + 128)
         weights[:, block] = held[place, 0:FRONT_ROWS, :]
         for part in range(3):
             base = FRONT_ROWS + 128 * part
@@ -932,7 +925,7 @@
             jax.ShapeDtypeStruct((PATCHES, 128), jnp.float32),
             jax.ShapeDtypeStruct((8, D), jnp.float32),
         ),
-        in_specs=smem_specs(2) + hbm_specs(8) + vmem_specs(7),
+        in_specs=smem_specs(2) + hbm_specs(1) + vmem_specs(7),
         out_specs=hbm_specs(11),
         scratch_shapes=[
             pltpu.VMEM((4, PATCHES, 128), jnp.bfloat16),
@@ -950,7 +943,7 @@
         compiler_params=pltpu.CompilerParams(vmem_limit_bytes=52 * 2**20),
         cost_estimate=pl.CostEstimate(flops=2 * 10**9, bytes_accessed=10**7, transcendentals=0),
         name="front",
-    )(meta, scales, *pieces, *quarters, mod, cosine, sine)
+    )(meta, scales, pieces, *quarters, mod, cosine, sine)
 
 
 def total_own(held, came, across):
@@ -1347,6 +1340,30 @@
     return updated, first_mom, second_mom, updated.astype(jnp.bfloat16)
 
 
+def preload_kernel(*refs):
+    sources, targets, sems = refs[:3], refs[4:7], refs[7]
+    copies = [
+        pltpu.make_async_copy(sources[k], targets[k], sems.at[k]) for k in range(3)
+    ]
+    for copy in copies:
+        copy.start()
+    for copy in copies:
+        copy.wait()
+
+
+def call_preload(arrays, values):
+    return pl.pallas_call(
+        preload_kernel,
+        out_shape=tuple(jax.ShapeDtypeStruct(a.shape, a.dtype) for a in arrays),
+        in_specs=hbm_specs(3) + vmem_specs(1),
+        out_specs=vmem_specs(3),
+        scratch_shapes=[pltpu.SemaphoreType.DMA((3,))],
+        compiler_params=pltpu.CompilerParams(vmem_limit_bytes=4 * 2**20),
+        cost_estimate=pl.CostEstimate(flops=10**6, bytes_accessed=10**7, transcendentals=0),
+        name="preload",
+    )(*arrays, values)
+
+
 def adam_kernel(*refs):
     fixes, sums = refs[0], refs[1:5]
     attn_grad, mlp_grad, cond, mod_rows = refs[5:9]
@@ -1357,7 +1374,7 @@
     held, slots, low_slots, in_sems, sems = refs[48:]
     depth = held.shape[0]
     tasks = []
-    for k in (2, 1, 0):
+    for k in (1, 0, 2):
         width = groups[k][0].shape[-1]
         for lead in range(groups[k][0].shape[0] if k < 2 else 1):
             for col in range(0, width, 1024):
@@ -1367,6 +1384,8 @@
         k, lead, col, span = tasks[number]
         cut = ((lead,) if k < 2 else ()) + (slice(None), slice(col, col + span))
         slot = number % depth
+        if k == 2:
+            return []
         return [
             pltpu.make_async_copy(
                 groups[k][index].at[cut], held.at[slot, index, :, 0:span], in_sems.at[slot, index]
@@ -1412,7 +1431,10 @@
                 TN,
                 preferred_element_type=jnp.float32,
             )
-        values = [held[slot, index, :, 0:span] for index in range(3)]
+        if k == 2:
+            values = [ref[:, col : col + span] for ref in groups[2]]
+        else:
+            values = [held[slot, index, :, 0:span] for index in range(3)]
         results = adam_step(*values, grad, scale, rate_matrix, decay_rate)
         copies = []
         for index, result in enumerate(results):
@@ -1448,7 +1470,7 @@
     return pl.pallas_call(
         adam_kernel,
         out_shape=out_shape,
-        in_specs=smem_specs(1) + vmem_specs(len(inside)) + hbm_specs(9),
+        in_specs=smem_specs(1) + vmem_specs(len(inside)) + hbm_specs(6) + vmem_specs(3),
         out_specs=hbm_specs(12) + vmem_specs(10),
         scratch_shapes=[
             pltpu.VMEM((6, 3, 128, 1024), jnp.float32),
@@ -1457,15 +1479,22 @@
             pltpu.SemaphoreType.DMA((6, 3)),
             pltpu.SemaphoreType.DMA((6, 4)),
         ],
-        compiler_params=pltpu.CompilerParams(vmem_limit_bytes=52 * 2**20),
+        compiler_params=pltpu.CompilerParams(vmem_limit_bytes=28 * 2**20),
         cost_estimate=pl.CostEstimate(flops=10**7, bytes_accessed=2 * 10**7, transcendentals=0),
         name="adam",
     )(fixes, *inside, *held)
 
 
+def square_kernel(scattered, square):
+    rest = scattered[...].astype(jnp.float32)
+    square[...] = jnp.broadcast_to(
+        jnp.sum(column_sum(rest * rest), axis=1, keepdims=True), square.shape
+    )
+
+
 def finish_kernel(*refs):
     own, io_own, mod_own, pieces = refs[0], refs[1], refs[2], refs[3:6]
-    scattered, error, grad, spread = refs[6:]
+    rest, error, grad, spread = refs[6:]
     total = own[...]
     io_total = io_own[...]
     spread[0 : 2 * MOD_ROWS, :] = mod_own[...]
@@ -1481,9 +1510,8 @@
     spread[base : base + IO_ROWS, :] = (io_total - high.astype(jnp.float32)).astype(jnp.bfloat16)
     for part in range(4):
         grad[part] = total[256 * part : 256 * part + 256].T
-    rest = scattered[...].astype(jnp.float32)
-    squares = jnp.zeros((1, 1), jnp.float32)
-    for values in (total, rest, io_total):
+    squares = rest[:, 0:1]
+    for values in (total, io_total):
         squares = squares + jnp.sum(column_sum(values * values), axis=1, keepdims=True)
     left = lax.broadcasted_iota(jnp.int32, (1, 128), 1) < 64
     value = jnp.where(left, squares, error[...])
@@ -1741,8 +1769,13 @@
     member = ctx_index % 4
     device = jnp.stack([ctx_index, tp_index]).astype(jnp.int32)
 
-    pieces = ring_gather(call_prepare(device, clean, noise, w_attn, w_io, vectors))
-    front_meta, attend_meta, row_levels = call_place(device, lengths, order, levels)
+    front_shard = call_prepare(w_attn, w_io, vectors)
+    token_shard = call_tokens(after(device, front_shard), clean, noise)
+    pieces = gather_swaps(token_shard)
+    front_pieces = lax.all_gather(front_shard, "ctx", axis=0)
+    front_meta, attend_meta, row_levels = call_place(
+        after(device, pieces[1]), lengths, order, levels
+    )
 
     count = step[0].astype(single)
     fixes = jnp.stack([1.0 / (1.0 - beta_one**count), 1.0 / (1.0 - beta_two**count)])
@@ -1758,8 +1791,7 @@
     mod_cols = lax.dynamic_slice_in_dim(w_mod, tp_index * quarter_cols, quarter_cols, 1)
     mod_part = jnp.dot(cond_slots, mod_cols.astype(bfloat), preferred_element_type=single)
     mod_held = reduce_along_x(mod_part.reshape(8, 4, quarter_cols), ctx_index, single)
-    mod_held = after(mod_held, pieces[2], pieces[5])
-    mod_own = after(reduce_along_z(mod_held, ctx_index, single), pieces[3], pieces[6])
+    mod_own = reduce_along_z(mod_held, ctx_index, single)
     mod_quarters = reorder_four(spread_frames(mod_own), tp_index)
     mod_all = jnp.concatenate(mod_quarters, axis=1)
     mod_rel = jnp.stack(reorder_four([mod_all[k] for k in range(4)], tp_index))
@@ -1797,7 +1829,7 @@
     front_meta = after(front_meta, mod_rel, cosine, sine, token_scales, loss_scales, fixes)
     quarters = spread_frames(call_pick(front_meta, pieces))
     front_all, mid_all, hidden_frames, resid_in, *head_blocks, noisy_low, target, mod_own = (
-        call_front(front_meta, token_scales, pieces, quarters, mod_rel, cosine, sine)
+        call_front(front_meta, token_scales, front_pieces, quarters, mod_rel, cosine, sine)
     )
     hidden_one = hidden_frames.reshape(4 * PATCHES, D)
 
@@ -1976,17 +2008,19 @@
         io_own,
         z_pieces[0],
         *(swap(piece, "ctx", 2 * bit) for bit, piece in zip((1, 2, 3), z_pieces[1:])),
-        scattered,
+        row_call(square_kernel, "square", (jax.ShapeDtypeStruct((1, 128), single),), scattered)[0],
         error_part,
     )
     all_rows, red_vec, io_grad, square = call_mod_grad(device, cond_low, spread_frames(spread))
+    terms = sum_terms(square)
+    loaded = call_preload((w_mod, m_mod, v_mod), terms[0])
     updated = call_adam(
         fixes,
-        sum_terms(square),
+        terms,
         (red_attn, scattered, cond_low, all_rows),
         (w_io, m_io, v_io, io_grad[: 2 * 128].reshape(2, 128, 128)),
         (vectors, m_vec, v_vec, red_vec),
-        ((w_attn, m_attn, v_attn), (w_mlp, m_mlp, v_mlp), (w_mod, m_mod, v_mod)),
+        ((w_attn, m_attn, v_attn), (w_mlp, m_mlp, v_mlp), loaded),
     )
     return (updated[21][1, 64] / weight_sum, updated[21][0, 0], *updated[:21])
 

time: 465 us -> 455 us (0.978)
  waiting for transfers between devices: 220 us -> 211 us
    ppermute x8 -> x0, waiting for transfers between devices: 23.3 us -> none  [the longest x3 13.2 us: ring_gather(): behind.append(lax.ppermute(behind[-1], 'ctx', RING_PREV))]
    ppermute x8 -> x0, starting transfers between devices: 9.21 us -> none  [the longest x3 5.36 us: ring_gather(): behind.append(lax.ppermute(behind[-1], 'ctx', RING_PREV))]
    all_gather x0 -> x1, waiting for transfers between devices: none -> 9.15 us  [shards_halves(): front_pieces = lax.all_gather(front_shard, 'ctx', axis=0)]
    ppermute x59 -> x64, starting transfers between devices: 58.4 us -> 65.7 us  [swap(): return lax.ppermute(values, axis, [(i, i ^ bit) for i in range(size)])]
    unnamed x125 -> x148, local copies, waits for them, and re-layouts: 21.6 us -> 26.4 us
    ppermute x59 -> x64, waiting for transfers between devices: 188 us -> 193 us  [swap(): return lax.ppermute(values, axis, [(i, i ^ bit) for i in range(size)])]
    pallas_call x8 -> x9, Pallas kernels: 11.9 us -> 10.6 us  [row_call(): pl.pallas_call(kernel, out_shape=tuple(outs), in_specs=smem_specs(smem) +...]
  transfers between devices with their start and end apart: 69 -> 67, of which waited for: 44 -> 43; matrix products, arithmetic and copies ran while one was open for 3% -> 3% of each run, Pallas kernels for 18% -> 17%
where the time goes in v4:
time: 455 us; the launch traced here: 448 us
  waiting for transfers between devices  211 us (46%)
  Pallas kernels  112 us (25%)
  starting transfers between devices  65.9 us (14%)
  local copies, waits for them, and re-layouts  28.4 us (6%)
  between operations  19 us (4%)
  other arithmetic  8 us (2%)
    ppermute x64, waiting for transfers between devices, swap(): return lax.ppermute(values, axis, [(i, i ^ bit) for i in range(size)])  193 us
    ppermute x64, starting transfers between devices, swap(): return lax.ppermute(values, axis, [(i, i ^ bit) for i in range(size)])  65.7 us
    pallas_call x1, Pallas kernels, call_attend_back(): pl.pallas_call(attend_back_kernel, out_shape=tuple((jax.ShapeDtypeStruct(...  30 us
    unnamed x148, local copies, waits for them, and re-layouts  26.4 us
    pallas_call x1, Pallas kernels, call_attend(): pl.pallas_call(attend_kernel, out_shape=tuple((jax.ShapeDtypeStruct((HD,...  22.6 us
    pallas_call x4, Pallas kernels, call_mlp(): pl.pallas_call(kernel, out_shape=(frame_f32(), frame_low()) + outs, in_sp...  10.7 us
    pallas_call x9, Pallas kernels, row_call(): pl.pallas_call(kernel, out_shape=tuple(outs), in_specs=smem_specs(smem) +...  10.6 us
    pallas_call x1, Pallas kernels, call_adam(): pl.pallas_call(adam_kernel, out_shape=out_shape, in_specs=smem_specs(1) +...  9.24 us
  transfers between devices with their start and end apart: 67, of which 43 were waited for; matrix products, arithmetic and copies ran while one was open for 3% of the time, Pallas kernels for 17%

profile of v4, /device:TPU:0, one launch (start us, length us, event | category | flops | bytes accessed | tf_op | source)
XLA Modules:
  0.0 447.7 jit_solution(15655684621953290895)
XLA Ops:
  11.6 5.0 %collective-permute-start.10 = (bf16[512,128]{1,0:T(8,128)(2,1)}, bf16[512,128]{1,0:T(8,128)(2,1)S(1)}, u32[]{:S(2)}, u32[]{:S(2)}) collective-permute-start(bf16[512,128]{1,0:T(8,128)(2,1)} %tokens.1.refs_0_), channel_id=1, source_target_pairs={{0,24},{4,28},{8,16},{12,20},{16,8},{20,12},{24,0},{28,4},{1,25},{... | collective-permute-start | bytes 393224 | tf_op jit(solution)/shard_map/ppermute | solution.py:582
  28.9 6.4 %collective-permute-done.9.refs_3_ = bf16[512,128]{1,0:T(8,128)(2,1)S(1)} collective-permute-done((bf16[512,128]{1,0:T(8,128)(2,1)}, bf16[512,128]{1,0:T(8,128)(2,1)S(1)}, u32[]{:S(2)}, u32[]{:S(2)}) %collective-permute-start.9) | collective-permute-done | bytes 131104 | tf_op jit(solution)/shard_map/ppermute | solution.py:582
  63.3 9.2 %all-gather.6.cloned.1.call-done = bf16[10368,128]{1,0:T(8,128)(2,1)} async-done(((bf16[1296,128]{1,0:T(8,128)(2,1)}), bf16[10368,128]{1,0:T(8,128)(2,1)}) %all-gather.6.cloned.1.call-update) | async-done | bytes 2654224 | tf_op jit(solution)/shard_map/all_gather | solution.py:1775
  73.3 8.3 %front.1 = (bf16[912,1024]{1,0:T(8,128)(2,1)}, bf16[1024,384]{1,0:T(8,128)(2,1)}, bf16[4,256,1024]{2,1,0:T(8,128)(2,1)}, f32[256,1024]{1,0:T(8,128)}, bf16[192,1...) custom-call(s32[24]{0:T(128)S(1)} %copy-done.35, ...), custom_call_target="tpu_custom_call" | custom-call | flops 2000000000 | bytes 10000000 | tf_op jit(solution)/shard_map/front/pallas_call | solution.py:914
  87.4 6.6 %collective-permute-done.15.refs_1_ = bf16[192,1024]{1,0:T(8,128)(2,1)S(1)} collective-permute-done((bf16[192,1024]{1,0:T(8,128)(2,1)S(1)}, bf16[192,1024]{1,0:T(8,128)(2,1)S(1)}, u32[]{:S(2)}, u32[]{:S(2)}) %collective-permute-start.15) | collective-permute-done | bytes 393248 | tf_op jit(solution)/shard_map/ppermute | solution.py:582
  95.9 6.6 %collective-permute-done.17.refs_3_ = bf16[192,1024]{1,0:T(8,128)(2,1)S(1)} collective-permute-done((bf16[192,1024]{1,0:T(8,128)(2,1)}, bf16[192,1024]{1,0:T(8,128)(2,1)S(1)}, u32[]{:S(2)}, u32[]{:S(2)}) %collective-permute-start.17) | collective-permute-done | bytes 393248 | tf_op jit(solution)/shard_map/ppermute | solution.py:582
  102.6 22.6 %attend.1 = (bf16[64,1024]{1,0:T(8,128)(2,1)S(1)}, bf16[64,1024]{1,0:T(8,128)(2,1)S(1)}, bf16[64,1024]{1,0:T(8,128)(2,1)S(1)}, bf16[64,1024]{1,0:T(8,128)(2,1)S(...) custom-call(s32[18]{0:T(128)S(1)} %copy-done.53, bf16[192,1024]{1,0:T(8,128)(2,1)S(1)} %copy-done.59, ...), custom_call_target="tpu_custom_call" | custom-call | flops 8999999488 | bytes 5000000 | tf_op jit(solution)/shard_map/attend/pallas_call | solution.py:1608
  130.5 6.5 %collective-permute-done.18 = bf16[64,1024]{1,0:T(8,128)(2,1)S(1)} collective-permute-done((bf16[64,1024]{1,0:T(8,128)(2,1)S(1)}, bf16[64,1024]{1,0:T(8,128)(2,1)S(1)}, u32[]{:S(2)}, u32[]{:S(2)}) %collective-permute-start.18) | collective-permute-done | bytes 131104 | tf_op jit(solution)/shard_map/ppermute | solution.py:582
  141.8 12.4 %collective-permute-done.23.across = bf16[256,1024]{1,0:T(8,128)(2,1)S(1)} collective-permute-done((bf16[256,1024]{1,0:T(8,128)(2,1)S(1)}, bf16[256,1024]{1,0:T(8,128)(2,1)S(1)}, u32[]{:S(2)}, u32[]{:S(2)}) %collective-permute-start.23) | collective-permute-done | bytes 524320 | tf_op jit(solution)/shard_map/ppermute | solution.py:582
  157.9 11.8 %collective-permute-done.24.first.refs_2_ = bf16[256,1024]{1,0:T(8,128)(2,1)S(1)} collective-permute-done((bf16[256,1024]{1,0:T(8,128)(2,1)S(1)}, bf16[256,1024]{1,0:T(8,128)(2,1)S(1)}, u32[]{:S(2)}, u32[]{:S(2)}) %collective-permute-start.24) | collective-permute-done | bytes 524320 | tf_op jit(solution)/shard_map/ppermute | solution.py:582
  172.5 9.0 %all-gather.4.cloned.1.call-done.weights = bf16[2,1024,1024]{2,1,0:T(8,128)(2,1)} async-done(((bf16[2,128,1024]{2,1,0:T(8,128)(2,1)}), bf16[2,1024,1024]{2,1,0:T(8,128)(2,1)}) %all-gather.4.cloned.1.call-update) | async-done | bytes 4194320 | tf_op jit(solution)/shard_map/all_gather | solution.py:1843
  195.3 9.5 %collective-permute-done.29.across = bf16[256,1024]{1,0:T(8,128)(2,1)S(1)} collective-permute-done((bf16[256,1024]{1,0:T(8,128)(2,1)S(1)}, bf16[256,1024]{1,0:T(8,128)(2,1)S(1)}, u32[]{:S(2)}, u32[]{:S(2)}) %collective-permute-start.29) | collective-permute-done | bytes 524320 | tf_op jit(solution)/shard_map/ppermute | solution.py:582
  210.0 11.6 %collective-permute-done.32.first.refs_6_ = bf16[256,1024]{1,0:T(8,128)(2,1)S(1)} collective-permute-done((bf16[256,1024]{1,0:T(8,128)(2,1)S(1)}, bf16[256,1024]{1,0:T(8,128)(2,1)S(1)}, u32[]{:S(2)}, u32[]{:S(2)}) %collective-permute-start.32) | collective-permute-done | bytes 524320 | tf_op jit(solution)/shard_map/ppermute | solution.py:582
  231.5 5.6 %weight_grad.1 = bf16[1024,2048]{1,0:T(8,128)(2,1)S(1)} custom-call(bf16[256,1024]{1,0:T(8,128)(2,1)S(1)} %copy-done.39, bf16[256,1024]{1,0:T(8,128)(2,1)S(1)} %collective-permute-done.27.second.refs_1_, bf16[256,1024]{1,0:T(8,128)(2,1)S(1)} %copy-done.42, bf16[256,1024]{1,0:T(8,128)(2,1)S(1)} %copy-done.45, ...), custom_call_target="tpu_custom_call" | custom-call | flops 5000000000 | bytes 20000000 | tf_op jit(solution)/shard_map/weight_grad/pallas_call | solution.py:1250
  241.3 12.4 %collective-permute-done.35.across = bf16[256,1024]{1,0:T(8,128)(2,1)S(1)} collective-permute-done((bf16[256,1024]{1,0:T(8,128)(2,1)}, bf16[256,1024]{1,0:T(8,128)(2,1)S(1)}, u32[]{:S(2)}, u32[]{:S(2)}) %collective-permute-start.35) | collective-permute-done | bytes 524320 | tf_op jit(solution)/shard_map/ppermute | solution.py:582
  260.1 11.8 %collective-permute-done.37 = bf16[256,1024]{1,0:T(8,128)(2,1)S(1)} collective-permute-done((bf16[256,1024]{1,0:T(8,128)(2,1)S(1)}, bf16[256,1024]{1,0:T(8,128)(2,1)S(1)}, u32[]{:S(2)}, u32[]{:S(2)}) %collective-permute-start.37) | collective-permute-done | bytes 524320 | tf_op jit(solution)/shard_map/ppermute | solution.py:582
  286.2 30.0 %attend_back.1 = (bf16[192,1024]{1,0:T(8,128)(2,1)S(1)}, bf16[192,1024]{1,0:T(8,128)(2,1)S(1)}, bf16[192,1024]{1,0:T(8,128)(2,1)S(1)}, bf16[192,1024]{1,0:T(8,128)(2,1)S(1)}) custom-call(s32[18]{0:T(128)S(1)} %copy-done.53, bf16[192,1024]{1,0:T(8,128)(2,1)S(1)} %copy-done.60, bf16[192,1024]{1,0:T(8,128)(2,1)S(1)} %copy-done.48, ...), custom_call_target="tpu_custom_call" | custom-call | flops 30000001024 | bytes 10000000 | tf_op jit(solution)/shard_map/attend_back/pallas_call | solution.py:1716
  321.3 11.8 %collective-permute-done.45.out_came = bf16[4,256,128]{2,1,0:T(8,128)(2,1)S(1)} collective-permute-done((bf16[4,256,128]{2,1,0:T(8,128)(2,1)S(1)}, bf16[4,256,128]{2,1,0:T(8,128)(2,1)S(1)}, u32[]{:S(2)}, u32[]{:S(2)}) %collective-permute-start.45) | collective-permute-done | bytes 262176 | tf_op jit(solution)/shard_map/ppermute | solution.py:582
  337.8 9.2 %collective-permute-done.44.refs_3_ = bf16[192,1024]{1,0:T(8,128)(2,1)S(1)} collective-permute-done((bf16[192,1024]{1,0:T(8,128)(2,1)S(1)}, bf16[192,1024]{1,0:T(8,128)(2,1)S(1)}, u32[]{:S(2)}, u32[]{:S(2)}) %collective-permute-start.44) | collective-permute-done | bytes 393248 | tf_op jit(solution)/shard_map/ppermute | solution.py:582
  357.3 8.4 %collective-permute-done.49.across = bf16[256,1024]{1,0:T(8,128)(2,1)S(1)} collective-permute-done((bf16[256,1024]{1,0:T(8,128)(2,1)S(1)}, bf16[256,1024]{1,0:T(8,128)(2,1)S(1)}, u32[]{:S(2)}, u32[]{:S(2)}) %collective-permute-start.49) | collective-permute-done | bytes 524320 | tf_op jit(solution)/shard_map/ppermute | solution.py:582
  371.4 4.8 %collective-permute-done.52.across = bf16[80,1024]{1,0:T(8,128)(2,1)S(1)} collective-permute-done((bf16[80,1024]{1,0:T(8,128)(2,1)S(1)}, bf16[80,1024]{1,0:T(8,128)(2,1)S(1)}, u32[]{:S(2)}, u32[]{:S(2)}) %collective-permute-start.52) | collective-permute-done | bytes 163872 | tf_op jit(solution)/shard_map/ppermute | solution.py:582
  388.6 5.2 %collective-permute-done.54.refs_3_ = bf16[1200,128]{1,0:T(8,128)(2,1)S(1)} collective-permute-done((bf16[1200,128]{1,0:T(8,128)(2,1)S(1)}, bf16[1200,128]{1,0:T(8,128)(2,1)S(1)}, u32[]{:S(2)}, u32[]{:S(2)}) %collective-permute-start.54) | collective-permute-done | bytes 307232 | tf_op jit(solution)/shard_map/ppermute | solution.py:582
  393.7 12.0 %collective-permute-done.55.refs_4_ = bf16[1200,128]{1,0:T(8,128)(2,1)S(1)} collective-permute-done((bf16[1200,128]{1,0:T(8,128)(2,1)S(1)}, bf16[1200,128]{1,0:T(8,128)(2,1)S(1)}, u32[]{:S(2)}, u32[]{:S(2)}) %collective-permute-start.55) | collective-permute-done | bytes 307232 | tf_op jit(solution)/shard_map/ppermute | solution.py:582
  429.4 9.2 %adam.1 = (f32[4,128,256]{2,1,0:T(8,128)}, f32[4,128,256]{2,1,0:T(8,128)}, f32[4,128,256]{2,1,0:T(8,128)}, bf16[4,128,256]{2,1,0:T(8,128)(2,1)}, f32[2,128,1024]...) custom-call(f32[2]{0:T(128)S(1)} %get-tuple-element.285.refs_0_, ...), custom_call_target="tpu_custom_call" | custom-call | flops 10000000 | bytes 20000000 | tf_op jit(solution)/shard_map/adam/pallas_call | solution.py:1470
  (346 shorter events, 182.6 us)
Async XLA Ops:
  7.2 65.2 %all-gather.6.cloned.1.call-start = ((), (), s32[]{:S(2)}) async-start(), calls=%async_computation.3 | async-start | bytes 2985984 | tf_op jit(solution)/shard_map/all_gather | solution.py:1775
  9.2 172.3 %all-gather.4.cloned.1.call-start = ((), (), s32[]{:S(2)}) async-start(), calls=%async_computation.1 | async-start | bytes 4718592 | tf_op jit(solution)/shard_map/all_gather | solution.py:1843
  11.6 17.3 %collective-permute-start.10 = (bf16[512,128]{1,0:T(8,128)(2,1)}, bf16[512,128]{1,0:T(8,128)(2,1)S(1)}, u32[]{:S(2)}, u32[]{:S(2)}) collective-permute-start(bf16[512,128]{1,0:T(8,128)(2,1)} %tokens.1.refs_0_), channel_id=1, source_target_pairs={{0,24},{4,28},{8,16},{12,20},{16,8},{20,12},{24,0},{28,4},{1,25},{... | collective-permute-start | bytes 393224 | tf_op jit(solution)/shard_map/ppermute | solution.py:582
  16.6 18.7 %collective-permute-start.9 = (bf16[512,128]{1,0:T(8,128)(2,1)}, bf16[512,128]{1,0:T(8,128)(2,1)S(1)}, u32[]{:S(2)}, u32[]{:S(2)}) collective-permute-start(bf16[512,128]{1,0:T(8,128)(2,1)} %tokens.1.refs_0_), channel_id=1, source_target_pairs={{0,16},{4,20},{8,24},{12,28},{16,0},{20,4},{24,8},{28,12},{1,17},{... | collective-permute-start | bytes 393224 | tf_op jit(solution)/shard_map/ppermute | solution.py:582
  16.6 18.7 %collective-permute-start.8 = (bf16[512,128]{1,0:T(8,128)(2,1)}, bf16[512,128]{1,0:T(8,128)(2,1)S(1)}, u32[]{:S(2)}, u32[]{:S(2)}) collective-permute-start(bf16[512,128]{1,0:T(8,128)(2,1)} %tokens.1.refs_0_), channel_id=1, source_target_pairs={{0,8},{4,12},{8,0},{12,4},{16,24},{20,28},{24,16},{28,20},{1,9},{5... | collective-permute-start | bytes 393224 | tf_op jit(solution)/shard_map/ppermute | solution.py:582
  27.1 12.0 %collective-permute-start.1 = (f32[4,4,1536]{2,1,0:T(4,128)S(1)}, f32[4,4,1536]{2,1,0:T(4,128)S(1)}, u32[]{:S(2)}, u32[]{:S(2)}) collective-permute-start(f32[4,4,1536]{2,1,0:T(4,128)S(1)} %select_bitcast_fusion), channel_id=1, source_target_pairs={{0,4},{4,0},{8,12},{12,8},{16,20},{20,16},{24,28},{28,24},{1,5},{5... | collective-permute-start | bytes 294920 | tf_op jit(solution)/shard_map/ppermute | solution.py:582
  35.3 17.8 %collective-permute-start.11 = (bf16[1536,128]{1,0:T(8,128)(2,1)S(1)}, bf16[1536,128]{1,0:T(8,128)(2,1)S(1)}, u32[]{:S(2)}, u32[]{:S(2)}) collective-permute-start(bf16[1536,128]{1,0:T(8,128)(2,1)S(1)} %pad_maximum_fusion.3), channel_id=1, source_target_pairs={{0,4},{4,0},{8,12},{12,8},{16,20},{20,16},{24,28},{28,24},{1,5},{5... | collective-permute-start | bytes 1179656 | tf_op jit(solution)/shard_map/ppermute | solution.py:582
  83.6 12.3 %collective-permute-start.16 = (bf16[192,1024]{1,0:T(8,128)(2,1)}, bf16[192,1024]{1,0:T(8,128)(2,1)S(1)}, u32[]{:S(2)}, u32[]{:S(2)}) collective-permute-start(bf16[192,1024]{1,0:T(8,128)(2,1)} %get-tuple-element.146), channel_id=1, source_target_pairs={{0,8},{4,12},{8,0},{12,4},{16,24},{20,28},{24,16},{28,20},{1,9},{5... | collective-permute-start | bytes 1179656 | tf_op jit(solution)/shard_map/ppermute | solution.py:582
  85.1 17.4 %collective-permute-start.17 = (bf16[192,1024]{1,0:T(8,128)(2,1)}, bf16[192,1024]{1,0:T(8,128)(2,1)S(1)}, u32[]{:S(2)}, u32[]{:S(2)}) collective-permute-start(bf16[192,1024]{1,0:T(8,128)(2,1)} %get-tuple-element.147), channel_id=1, source_target_pairs={{0,12},{4,8},{8,4},{12,0},{16,28},{20,24},{24,20},{28,16},{1,13},{... | collective-permute-start | bytes 1179656 | tf_op jit(solution)/shard_map/ppermute | solution.py:582
  102.5 284.9 %reduce-scatter.2.cloned.1.call-start = ((), (), s32[]{:S(2)}) async-start(), calls=%async_computation.2 | async-start | bytes 4718592 | tf_op jit(solution)/shard_map/reduce_scatter | solution.py:1912
  140.1 14.0 %collective-permute-start.23 = (bf16[256,1024]{1,0:T(8,128)(2,1)S(1)}, bf16[256,1024]{1,0:T(8,128)(2,1)S(1)}, u32[]{:S(2)}, u32[]{:S(2)}) collective-permute-start(bf16[256,1024]{1,0:T(8,128)(2,1)S(1)} %fusion), channel_id=1, source_target_pairs={{0,2},{1,3},{2,0},{3,1},{4,6},{5,7},{6,4},{7,5},{8,10},{9,11},{10,... | collective-permute-start | bytes 1572872 | tf_op jit(solution)/shard_map/ppermute | solution.py:582
  156.5 13.2 %collective-permute-start.24 = (bf16[256,1024]{1,0:T(8,128)(2,1)S(1)}, bf16[256,1024]{1,0:T(8,128)(2,1)S(1)}, u32[]{:S(2)}, u32[]{:S(2)}) collective-permute-start(bf16[256,1024]{1,0:T(8,128)(2,1)S(1)} %get-tuple-element.159.first.refs_0_), channel_id=1, source_target_pairs={{0,2},{1,3},{2,0},{3,1},{4,6},{5,7},{6,4},{7,5},{8,10},{9,11},{10,... | collective-permute-start | bytes 1572872 | tf_op jit(solution)/shard_map/ppermute | solution.py:582
  190.8 14.0 %collective-permute-start.29 = (bf16[256,1024]{1,0:T(8,128)(2,1)S(1)}, bf16[256,1024]{1,0:T(8,128)(2,1)S(1)}, u32[]{:S(2)}, u32[]{:S(2)}) collective-permute-start(bf16[256,1024]{1,0:T(8,128)(2,1)S(1)} %add_convert_fusion.2), channel_id=1, source_target_pairs={{0,2},{1,3},{2,0},{3,1},{4,6},{5,7},{6,4},{7,5},{8,10},{9,11},{10,... | collective-permute-start | bytes 1572872 | tf_op jit(solution)/shard_map/ppermute | solution.py:582
  208.5 13.1 %collective-permute-start.32 = (bf16[256,1024]{1,0:T(8,128)(2,1)S(1)}, bf16[256,1024]{1,0:T(8,128)(2,1)S(1)}, u32[]{:S(2)}, u32[]{:S(2)}) collective-permute-start(bf16[256,1024]{1,0:T(8,128)(2,1)S(1)} %get-tuple-element.164.first.refs_4_), channel_id=1, source_target_pairs={{0,2},{1,3},{2,0},{3,1},{4,6},{5,7},{6,4},{7,5},{8,10},{9,11},{10,... | collective-permute-start | bytes 1572872 | tf_op jit(solution)/shard_map/ppermute | solution.py:582
  239.6 14.2 %collective-permute-start.35 = (bf16[256,1024]{1,0:T(8,128)(2,1)}, bf16[256,1024]{1,0:T(8,128)(2,1)S(1)}, u32[]{:S(2)}, u32[]{:S(2)}) collective-permute-start(bf16[256,1024]{1,0:T(8,128)(2,1)} %add_convert_fusion.1), channel_id=1, source_target_pairs={{0,2},{1,3},{2,0},{3,1},{4,6},{5,7},{6,4},{7,5},{8,10},{9,11},{10,... | collective-permute-start | bytes 1572872 | tf_op jit(solution)/shard_map/ppermute | solution.py:582
  258.5 13.3 %collective-permute-start.37 = (bf16[256,1024]{1,0:T(8,128)(2,1)S(1)}, bf16[256,1024]{1,0:T(8,128)(2,1)S(1)}, u32[]{:S(2)}, u32[]{:S(2)}) collective-permute-start(bf16[256,1024]{1,0:T(8,128)(2,1)S(1)} %get-tuple-element.180), channel_id=1, source_target_pairs={{0,2},{1,3},{2,0},{3,1},{4,6},{5,7},{6,4},{7,5},{8,10},{9,11},{10,... | collective-permute-start | bytes 1572872 | tf_op jit(solution)/shard_map/ppermute | solution.py:582
  316.2 16.9 %collective-permute-start.42 = (bf16[192,1024]{1,0:T(8,128)(2,1)S(1)}, bf16[192,1024]{1,0:T(8,128)(2,1)S(1)}, u32[]{:S(2)}, u32[]{:S(2)}) collective-permute-start(bf16[192,1024]{1,0:T(8,128)(2,1)S(1)} %get-tuple-element.187), channel_id=1, source_target_pairs={{0,4},{4,0},{8,12},{12,8},{16,20},{20,16},{24,28},{28,24},{1,5},{5... | collective-permute-start | bytes 1179656 | tf_op jit(solution)/shard_map/ppermute | solution.py:582
  317.8 19.9 %collective-permute-start.43 = (bf16[192,1024]{1,0:T(8,128)(2,1)S(1)}, bf16[192,1024]{1,0:T(8,128)(2,1)S(1)}, u32[]{:S(2)}, u32[]{:S(2)}) collective-permute-start(bf16[192,1024]{1,0:T(8,128)(2,1)S(1)} %get-tuple-element.188), channel_id=1, source_target_pairs={{0,8},{4,12},{8,0},{12,4},{16,24},{20,28},{24,16},{28,20},{1,9},{5... | collective-permute-start | bytes 1179656 | tf_op jit(solution)/shard_map/ppermute | solution.py:582
  318.9 28.0 %collective-permute-start.44 = (bf16[192,1024]{1,0:T(8,128)(2,1)S(1)}, bf16[192,1024]{1,0:T(8,128)(2,1)S(1)}, u32[]{:S(2)}, u32[]{:S(2)}) collective-permute-start(bf16[192,1024]{1,0:T(8,128)(2,1)S(1)} %get-tuple-element.189), channel_id=1, source_target_pairs={{0,12},{4,8},{8,4},{12,0},{16,28},{20,24},{24,20},{28,16},{1,13},{... | collective-permute-start | bytes 1179656 | tf_op jit(solution)/shard_map/ppermute | solution.py:582
  319.8 13.3 %collective-permute-start.45 = (bf16[4,256,128]{2,1,0:T(8,128)(2,1)S(1)}, bf16[4,256,128]{2,1,0:T(8,128)(2,1)S(1)}, u32[]{:S(2)}, u32[]{:S(2)}) collective-permute-start(bf16[4,256,128]{2,1,0:T(8,128)(2,1)S(1)} %get-tuple-element.191), channel_id=1, source_target_pairs={{0,4},{4,0},{8,12},{12,8},{16,20},{20,16},{24,28},{28,24},{1,5},{5... | collective-permute-start | bytes 786440 | tf_op jit(solution)/shard_map/ppermute | solution.py:582
  351.6 14.0 %collective-permute-start.49 = (bf16[256,1024]{1,0:T(8,128)(2,1)S(1)}, bf16[256,1024]{1,0:T(8,128)(2,1)S(1)}, u32[]{:S(2)}, u32[]{:S(2)}) collective-permute-start(bf16[256,1024]{1,0:T(8,128)(2,1)S(1)} %add_convert_fusion), channel_id=1, source_target_pairs={{0,2},{1,3},{2,0},{3,1},{4,6},{5,7},{6,4},{7,5},{8,10},{9,11},{10,... | collective-permute-start | bytes 1572872 | tf_op jit(solution)/shard_map/ppermute | solution.py:582
  356.1 21.9 %collective-permute-start.47 = (bf16[4,768,128]{2,1,0:T(8,128)(2,1)S(1)}, bf16[4,768,128]{2,1,0:T(8,128)(2,1)S(1)}, u32[]{:S(2)}, u32[]{:S(2)}) collective-permute-start(bf16[4,768,128]{2,1,0:T(8,128)(2,1)S(1)} %get-tuple-element.199), channel_id=1, source_target_pairs={{0,4},{4,0},{8,12},{12,8},{16,20},{20,16},{24,28},{28,24},{1,5},{5... | collective-permute-start | bytes 2359304 | tf_op jit(solution)/shard_map/ppermute | solution.py:582
  383.0 22.7 %collective-permute-start.55 = (bf16[1200,128]{1,0:T(8,128)(2,1)S(1)}, bf16[1200,128]{1,0:T(8,128)(2,1)S(1)}, u32[]{:S(2)}, u32[]{:S(2)}) collective-permute-start(bf16[1200,128]{1,0:T(8,128)(2,1)S(1)} %get-tuple-element.219), channel_id=1, source_target_pairs={{0,16},{4,20},{8,24},{12,28},{16,0},{20,4},{24,8},{28,12},{1,17},{... | collective-permute-start | bytes 921608 | tf_op jit(solution)/shard_map/ppermute | solution.py:582
  383.0 22.7 %collective-permute-start.56 = (bf16[1200,128]{1,0:T(8,128)(2,1)S(1)}, bf16[1200,128]{1,0:T(8,128)(2,1)S(1)}, u32[]{:S(2)}, u32[]{:S(2)}) collective-permute-start(bf16[1200,128]{1,0:T(8,128)(2,1)S(1)} %get-tuple-element.220), channel_id=1, source_target_pairs={{0,24},{4,28},{8,16},{12,20},{16,8},{20,12},{24,0},{28,4},{1,25},{... | collective-permute-start | bytes 921608 | tf_op jit(solution)/shard_map/ppermute | solution.py:582
  (114 other events, 773.3 us)
Sparse Core Ops, SparseCore 0:
  10.8 61.6 all-gather.5
  102.6 78.8 all-gather.3
  239.3 101.5 reduce-scatter.1

commit v5 on v4

--- a/solution.py
+++ b/solution.py
@@ -1839,7 +1839,7 @@
         return [blocks[0]] + [swap(blocks[k], "ctx", k) for k in (1, 2, 3)]
 
     head_in = exchange(head_blocks)
-    mlp_shard = after(w_mlp.astype(bfloat), *head_in)
+    mlp_shard = after(w_mlp.astype(bfloat), head_in[1], head_in[2])
     mlp_w = lax.all_gather(mlp_shard, "ctx", axis=1, tiled=True)
     mixed_blocks, lse, mixed = call_attend(attend_meta, head_in)
     mix_low = jnp.concatenate(reorder_four(exchange(mixed_blocks), member), axis=0)
@@ -1894,14 +1894,15 @@
         target,
         smem=1,
     )
-    grad_list = spread_frames(grad_own)
-    near = call_mlp(mlp_back_kernel, "mlp_back", (wide_low,), *grad_list[:2], mlp_w, slope[0])
+    grad_list = [grad_own, swap(grad_own, "tp", 1)]
+    near = call_mlp(mlp_back_kernel, "mlp_back", (wide_low,), *grad_list, mlp_w, slope[0])
+    grad_across = after(swap(grad_own, "tp", 2), near[0])
+    grad_list += [grad_across, swap(grad_across, "tp", 1)]
     far = call_mlp(
         mlp_back_kernel,
         "mlp_back",
         (wide_low,),
-        after(grad_list[2], near[0]),
-        grad_list[3],
+        *grad_list[2:],
         mlp_w,
         slope[1],
     )
@@ -1909,7 +1910,6 @@
     weight_grad = call_weight_grad(
         hidden_list, grad_list, (near[2], after(far[2], across)), active
     )
-    scattered = lax.psum_scatter(weight_grad, "ctx", scatter_dimension=0, tiled=True)
     grad_low, grad_mid, rows_two = row_call(
         second_kernel,
         "second",
@@ -1930,10 +1930,11 @@
     out_held, out_away = call_head_grad(device, mix_low, after(grad_attn_low, grad_mix))
     out_came = swap(out_away, "ctx", 1)
     grad_in_blocks[0] = after(grad_in_blocks[0], out_held)
+    scattered = lax.psum_scatter(
+        after(weight_grad, grad_low), "ctx", scatter_dimension=0, tiled=True
+    )
     back_blocks = call_attend_back(attend_meta, head_in, grad_in_blocks, lse, mixed, cosine, sine)
-    grad_qkv, *parts = call_qkv_back(
-        attend_meta, exchange(back_blocks), after(front_all, out_came)
-    )
+    grad_qkv, *parts = call_qkv_back(attend_meta, exchange(back_blocks), front_all)
     near, far = parts[:2], parts[2:]
     across = sum_across(far)
     first_terms = sum_frames(near, across)

time: 455 us -> 441 us (0.969)
  waiting for transfers between devices: 211 us -> 192 us
    ppermute x64, waiting for transfers between devices: 193 us -> 183 us  [swap(): return lax.ppermute(values, axis, [(i, i ^ bit) for i in range(size)])]
    all_gather x1, waiting for transfers between devices: 9.05 us -> 0.01 us  [shards_halves(): mlp_w = lax.all_gather(mlp_shard, 'ctx', axis=1, tiled=True)]
    unnamed x148 -> x160, local copies, waits for them, and re-layouts: 26.4 us -> 28.3 us
  transfers between devices with their start and end apart: 67 -> 67, of which waited for: 43 -> 44; matrix products, arithmetic and copies ran while one was open for 3% -> 3% of each run, Pallas kernels for 17% -> 19%
where the time goes in v5:
time: 441 us; the launch traced here: 434 us
  waiting for transfers between devices  192 us (44%)
  Pallas kernels  115 us (26%)
  starting transfers between devices  67.1 us (15%)
  local copies, waits for them, and re-layouts  30.2 us (7%)
  between operations  19 us (4%)
  other arithmetic  7.96 us (2%)
    ppermute x64, waiting for transfers between devices, swap(): return lax.ppermute(values, axis, [(i, i ^ bit) for i in range(size)])  183 us
    ppermute x64, starting transfers between devices, swap(): return lax.ppermute(values, axis, [(i, i ^ bit) for i in range(size)])  66.9 us
    pallas_call x1, Pallas kernels, call_attend_back(): pl.pallas_call(attend_back_kernel, out_shape=tuple((jax.ShapeDtypeStruct(...  30 us
    unnamed x160, local copies, waits for them, and re-layouts  28.3 us
    pallas_call x1, Pallas kernels, call_attend(): pl.pallas_call(attend_kernel, out_shape=tuple((jax.ShapeDtypeStruct((HD,...  22.6 us
    pallas_call x9, Pallas kernels, row_call(): pl.pallas_call(kernel, out_shape=tuple(outs), in_specs=smem_specs(smem) +...  12.5 us
    pallas_call x4, Pallas kernels, call_mlp(): pl.pallas_call(kernel, out_shape=(frame_f32(), frame_low()) + outs, in_sp...  11.4 us
    pallas_call x1, Pallas kernels, call_adam(): pl.pallas_call(adam_kernel, out_shape=out_shape, in_specs=smem_specs(1) +...  9.24 us
  transfers between devices with their start and end apart: 67, of which 44 were waited for; matrix products, arithmetic and copies ran while one was open for 3% of the time, Pallas kernels for 19%

profile of v5, /device:TPU:0, one launch (start us, length us, event | category | flops | bytes accessed | tf_op | source)
XLA Modules:
  0.0 434.0 jit_solution(2097689181866675073)
XLA Ops:
  11.6 5.0 %collective-permute-start.10 = (bf16[512,128]{1,0:T(8,128)(2,1)}, bf16[512,128]{1,0:T(8,128)(2,1)S(1)}, u32[]{:S(2)}, u32[]{:S(2)}) collective-permute-start(bf16[512,128]{1,0:T(8,128)(2,1)} %tokens.1.refs_0_), channel_id=1, source_target_pairs={{0,24},{4,28},{8,16},{12,20},{16,8},{20,12},{24,0},{28,4},{1,25},{... | collective-permute-start | bytes 393224 | tf_op jit(solution)/shard_map/ppermute | solution.py:582
  28.9 6.4 %collective-permute-done.9.refs_3_ = bf16[512,128]{1,0:T(8,128)(2,1)S(1)} collective-permute-done((bf16[512,128]{1,0:T(8,128)(2,1)}, bf16[512,128]{1,0:T(8,128)(2,1)S(1)}, u32[]{:S(2)}, u32[]{:S(2)}) %collective-permute-start.9) | collective-permute-done | bytes 131104 | tf_op jit(solution)/shard_map/ppermute | solution.py:582
  63.3 9.2 %all-gather.6.cloned.1.call-done = bf16[10368,128]{1,0:T(8,128)(2,1)} async-done(((bf16[1296,128]{1,0:T(8,128)(2,1)}), bf16[10368,128]{1,0:T(8,128)(2,1)}) %all-gather.6.cloned.1.call-update) | async-done | bytes 2654224 | tf_op jit(solution)/shard_map/all_gather | solution.py:1775
  73.3 8.3 %front.1 = (bf16[912,1024]{1,0:T(8,128)(2,1)}, bf16[1024,384]{1,0:T(8,128)(2,1)}, bf16[4,256,1024]{2,1,0:T(8,128)(2,1)}, f32[256,1024]{1,0:T(8,128)}, bf16[192,1...) custom-call(s32[24]{0:T(128)S(1)} %copy-done.39, ...), custom_call_target="tpu_custom_call" | custom-call | flops 2000000000 | bytes 10000000 | tf_op jit(solution)/shard_map/front/pallas_call | solution.py:914
  86.0 6.7 %collective-permute-done.15.refs_1_ = bf16[192,1024]{1,0:T(8,128)(2,1)S(1)} collective-permute-done((bf16[192,1024]{1,0:T(8,128)(2,1)S(1)}, bf16[192,1024]{1,0:T(8,128)(2,1)S(1)}, u32[]{:S(2)}, u32[]{:S(2)}) %collective-permute-start.15) | collective-permute-done | bytes 393248 | tf_op jit(solution)/shard_map/ppermute | solution.py:582
  95.8 6.9 %collective-permute-done.17.refs_3_ = bf16[192,1024]{1,0:T(8,128)(2,1)S(1)} collective-permute-done((bf16[192,1024]{1,0:T(8,128)(2,1)S(1)}, bf16[192,1024]{1,0:T(8,128)(2,1)S(1)}, u32[]{:S(2)}, u32[]{:S(2)}) %collective-permute-start.17) | collective-permute-done | bytes 393248 | tf_op jit(solution)/shard_map/ppermute | solution.py:582
  102.6 22.6 %attend.1 = (bf16[64,1024]{1,0:T(8,128)(2,1)S(1)}, bf16[64,1024]{1,0:T(8,128)(2,1)S(1)}, bf16[64,1024]{1,0:T(8,128)(2,1)S(1)}, bf16[64,1024]{1,0:T(8,128)(2,1)S(...) custom-call(s32[18]{0:T(128)S(1)} %copy-done.56, bf16[192,1024]{1,0:T(8,128)(2,1)S(1)} %copy-done.64, ...), custom_call_target="tpu_custom_call" | custom-call | flops 8999999488 | bytes 5000000 | tf_op jit(solution)/shard_map/attend/pallas_call | solution.py:1608
  141.5 12.3 %collective-permute-done.23.across = bf16[256,1024]{1,0:T(8,128)(2,1)S(1)} collective-permute-done((bf16[256,1024]{1,0:T(8,128)(2,1)S(1)}, bf16[256,1024]{1,0:T(8,128)(2,1)S(1)}, u32[]{:S(2)}, u32[]{:S(2)}) %collective-permute-start.23) | collective-permute-done | bytes 524320 | tf_op jit(solution)/shard_map/ppermute | solution.py:582
  157.6 11.7 %collective-permute-done.24.first.refs_2_ = bf16[256,1024]{1,0:T(8,128)(2,1)S(1)} collective-permute-done((bf16[256,1024]{1,0:T(8,128)(2,1)S(1)}, bf16[256,1024]{1,0:T(8,128)(2,1)S(1)}, u32[]{:S(2)}, u32[]{:S(2)}) %collective-permute-start.24) | collective-permute-done | bytes 524320 | tf_op jit(solution)/shard_map/ppermute | solution.py:582
  185.8 9.5 %collective-permute-done.29.across = bf16[256,1024]{1,0:T(8,128)(2,1)S(1)} collective-permute-done((bf16[256,1024]{1,0:T(8,128)(2,1)S(1)}, bf16[256,1024]{1,0:T(8,128)(2,1)S(1)}, u32[]{:S(2)}, u32[]{:S(2)}) %collective-permute-start.29) | collective-permute-done | bytes 524320 | tf_op jit(solution)/shard_map/ppermute | solution.py:582
  205.0 8.3 %collective-permute-done.32.first.refs_6_ = bf16[256,1024]{1,0:T(8,128)(2,1)S(1)} collective-permute-done((bf16[256,1024]{1,0:T(8,128)(2,1)S(1)}, bf16[256,1024]{1,0:T(8,128)(2,1)S(1)}, u32[]{:S(2)}, u32[]{:S(2)}) %collective-permute-start.32) | collective-permute-done | bytes 524320 | tf_op jit(solution)/shard_map/ppermute | solution.py:582
  222.3 5.6 %weight_grad.1 = bf16[1024,2048]{1,0:T(8,128)(2,1)S(1)} custom-call(bf16[256,1024]{1,0:T(8,128)(2,1)S(1)} %copy-done.43, bf16[256,1024]{1,0:T(8,128)(2,1)S(1)} %collective-permute-done.27.second.refs_1_, bf16[256,1024]{1,0:T(8,128)(2,1)S(1)} %copy-done.46, bf16[256,1024]{1,0:T(8,128)(2,1)S(1)} %copy-done.49, ...), custom_call_target="tpu_custom_call" | custom-call | flops 5000000000 | bytes 20000000 | tf_op jit(solution)/shard_map/weight_grad/pallas_call | solution.py:1250
  229.9 5.1 %collective-permute-done.35.across = bf16[256,1024]{1,0:T(8,128)(2,1)} collective-permute-done((bf16[256,1024]{1,0:T(8,128)(2,1)}, bf16[256,1024]{1,0:T(8,128)(2,1)}, u32[]{:S(2)}, u32[]{:S(2)}) %collective-permute-start.35) | collective-permute-done | bytes 524320 | tf_op jit(solution)/shard_map/ppermute | solution.py:582
  245.3 11.6 %collective-permute-done.37 = bf16[256,1024]{1,0:T(8,128)(2,1)S(1)} collective-permute-done((bf16[256,1024]{1,0:T(8,128)(2,1)S(1)}, bf16[256,1024]{1,0:T(8,128)(2,1)S(1)}, u32[]{:S(2)}, u32[]{:S(2)}) %collective-permute-start.37) | collective-permute-done | bytes 524320 | tf_op jit(solution)/shard_map/ppermute | solution.py:582
  265.1 8.0 %collective-permute-done.41.refs_7_ = bf16[64,1024]{1,0:T(8,128)(2,1)S(1)} collective-permute-done((bf16[64,1024]{1,0:T(8,128)(2,1)S(1)}, bf16[64,1024]{1,0:T(8,128)(2,1)S(1)}, u32[]{:S(2)}, u32[]{:S(2)}) %collective-permute-start.41) | collective-permute-done | bytes 131104 | tf_op jit(solution)/shard_map/ppermute | solution.py:582
  273.1 6.4 %collective-permute-done.40.refs_6_ = bf16[64,1024]{1,0:T(8,128)(2,1)S(1)} collective-permute-done((bf16[64,1024]{1,0:T(8,128)(2,1)S(1)}, bf16[64,1024]{1,0:T(8,128)(2,1)S(1)}, u32[]{:S(2)}, u32[]{:S(2)}) %collective-permute-start.40) | collective-permute-done | bytes 131104 | tf_op jit(solution)/shard_map/ppermute | solution.py:582
  279.5 30.0 %attend_back.1 = (bf16[192,1024]{1,0:T(8,128)(2,1)S(1)}, bf16[192,1024]{1,0:T(8,128)(2,1)S(1)}, bf16[192,1024]{1,0:T(8,128)(2,1)S(1)}, bf16[192,1024]{1,0:T(8,128)(2,1)S(1)}) custom-call(s32[18]{0:T(128)S(1)} %copy-done.56, bf16[192,1024]{1,0:T(8,128)(2,1)S(1)} %copy-done.65, bf16[192,1024]{1,0:T(8,128)(2,1)S(1)} %copy-done.51, ...), custom_call_target="tpu_custom_call" | custom-call | flops 30000001024 | bytes 10000000 | tf_op jit(solution)/shard_map/attend_back/pallas_call | solution.py:1716
  313.1 7.7 %collective-permute-done.42.refs_1_ = bf16[192,1024]{1,0:T(8,128)(2,1)S(1)} collective-permute-done((bf16[192,1024]{1,0:T(8,128)(2,1)S(1)}, bf16[192,1024]{1,0:T(8,128)(2,1)S(1)}, u32[]{:S(2)}, u32[]{:S(2)}) %collective-permute-start.42) | collective-permute-done | bytes 393248 | tf_op jit(solution)/shard_map/ppermute | solution.py:582
  323.1 7.0 %collective-permute-done.44.refs_3_ = bf16[192,1024]{1,0:T(8,128)(2,1)S(1)} collective-permute-done((bf16[192,1024]{1,0:T(8,128)(2,1)S(1)}, bf16[192,1024]{1,0:T(8,128)(2,1)S(1)}, u32[]{:S(2)}, u32[]{:S(2)}) %collective-permute-start.44) | collective-permute-done | bytes 393248 | tf_op jit(solution)/shard_map/ppermute | solution.py:582
  340.9 7.8 %collective-permute-done.49.across = bf16[256,1024]{1,0:T(8,128)(2,1)S(1)} collective-permute-done((bf16[256,1024]{1,0:T(8,128)(2,1)S(1)}, bf16[256,1024]{1,0:T(8,128)(2,1)S(1)}, u32[]{:S(2)}, u32[]{:S(2)}) %collective-permute-start.49) | collective-permute-done | bytes 524320 | tf_op jit(solution)/shard_map/ppermute | solution.py:582
  374.1 7.3 %collective-permute-done.54.refs_3_ = bf16[1200,128]{1,0:T(8,128)(2,1)S(1)} collective-permute-done((bf16[1200,128]{1,0:T(8,128)(2,1)}, bf16[1200,128]{1,0:T(8,128)(2,1)S(1)}, u32[]{:S(2)}, u32[]{:S(2)}) %collective-permute-start.54) | collective-permute-done | bytes 307232 | tf_op jit(solution)/shard_map/ppermute | solution.py:582
  381.3 11.7 %collective-permute-done.55.refs_4_ = bf16[1200,128]{1,0:T(8,128)(2,1)S(1)} collective-permute-done((bf16[1200,128]{1,0:T(8,128)(2,1)S(1)}, bf16[1200,128]{1,0:T(8,128)(2,1)S(1)}, u32[]{:S(2)}, u32[]{:S(2)}) %collective-permute-start.55) | collective-permute-done | bytes 307232 | tf_op jit(solution)/shard_map/ppermute | solution.py:582
  406.4 5.1 %collective-permute-start.62 = (f32[1,128]{1,0:T(1,128)S(1)}, f32[1,128]{1,0:T(1,128)S(1)}, u32[]{:S(2)}, u32[]{:S(2)}) collective-permute-start(f32[1,128]{1,0:T(1,128)S(1)} %add.127.refs_3_.refs_1_), channel_id=1, source_target_pairs={{0,16},{4,20},{8,24},{12,28},{16,0},{20,4},{24,8},{28,12},{1,17},{... | collective-permute-start | bytes 1544 | tf_op jit(solution)/shard_map/ppermute | solution.py:582
  415.7 9.2 %adam.1 = (f32[4,128,256]{2,1,0:T(8,128)}, f32[4,128,256]{2,1,0:T(8,128)}, f32[4,128,256]{2,1,0:T(8,128)}, bf16[4,128,256]{2,1,0:T(8,128)(2,1)}, f32[2,128,1024]...) custom-call(f32[2]{0:T(128)S(1)} %get-tuple-element.285.refs_0_, ...), custom_call_target="tpu_custom_call" | custom-call | flops 10000000 | bytes 20000000 | tf_op jit(solution)/shard_map/adam/pallas_call | solution.py:1470
  (358 shorter events, 185.8 us)
Async XLA Ops:
  7.2 65.2 %all-gather.6.cloned.1.call-start = ((), (), s32[]{:S(2)}) async-start(), calls=%async_computation.3 | async-start | bytes 2985984 | tf_op jit(solution)/shard_map/all_gather | solution.py:1775
  9.2 162.8 %all-gather.4.cloned.1.call-start = ((), (), s32[]{:S(2)}) async-start(), calls=%async_computation.1 | async-start | bytes 4718592 | tf_op jit(solution)/shard_map/all_gather | solution.py:1843
  11.6 17.3 %collective-permute-start.10 = (bf16[512,128]{1,0:T(8,128)(2,1)}, bf16[512,128]{1,0:T(8,128)(2,1)S(1)}, u32[]{:S(2)}, u32[]{:S(2)}) collective-permute-start(bf16[512,128]{1,0:T(8,128)(2,1)} %tokens.1.refs_0_), channel_id=1, source_target_pairs={{0,24},{4,28},{8,16},{12,20},{16,8},{20,12},{24,0},{28,4},{1,25},{... | collective-permute-start | bytes 393224 | tf_op jit(solution)/shard_map/ppermute | solution.py:582
  16.6 18.7 %collective-permute-start.9 = (bf16[512,128]{1,0:T(8,128)(2,1)}, bf16[512,128]{1,0:T(8,128)(2,1)S(1)}, u32[]{:S(2)}, u32[]{:S(2)}) collective-permute-start(bf16[512,128]{1,0:T(8,128)(2,1)} %tokens.1.refs_0_), channel_id=1, source_target_pairs={{0,16},{4,20},{8,24},{12,28},{16,0},{20,4},{24,8},{28,12},{1,17},{... | collective-permute-start | bytes 393224 | tf_op jit(solution)/shard_map/ppermute | solution.py:582
  16.6 18.7 %collective-permute-start.8 = (bf16[512,128]{1,0:T(8,128)(2,1)}, bf16[512,128]{1,0:T(8,128)(2,1)S(1)}, u32[]{:S(2)}, u32[]{:S(2)}) collective-permute-start(bf16[512,128]{1,0:T(8,128)(2,1)} %tokens.1.refs_0_), channel_id=1, source_target_pairs={{0,8},{4,12},{8,0},{12,4},{16,24},{20,28},{24,16},{28,20},{1,9},{5... | collective-permute-start | bytes 393224 | tf_op jit(solution)/shard_map/ppermute | solution.py:582
  27.1 12.0 %collective-permute-start.1 = (f32[4,4,1536]{2,1,0:T(4,128)S(1)}, f32[4,4,1536]{2,1,0:T(4,128)S(1)}, u32[]{:S(2)}, u32[]{:S(2)}) collective-permute-start(f32[4,4,1536]{2,1,0:T(4,128)S(1)} %select_bitcast_fusion), channel_id=1, source_target_pairs={{0,4},{4,0},{8,12},{12,8},{16,20},{20,16},{24,28},{28,24},{1,5},{5... | collective-permute-start | bytes 294920 | tf_op jit(solution)/shard_map/ppermute | solution.py:582
  35.3 17.8 %collective-permute-start.11 = (bf16[1536,128]{1,0:T(8,128)(2,1)S(1)}, bf16[1536,128]{1,0:T(8,128)(2,1)S(1)}, u32[]{:S(2)}, u32[]{:S(2)}) collective-permute-start(bf16[1536,128]{1,0:T(8,128)(2,1)S(1)} %pad_maximum_fusion.3), channel_id=1, source_target_pairs={{0,4},{4,0},{8,12},{12,8},{16,20},{20,16},{24,28},{28,24},{1,5},{5... | collective-permute-start | bytes 1179656 | tf_op jit(solution)/shard_map/ppermute | solution.py:582
  93.2 279.7 %reduce-scatter.2.cloned.1.call-start = ((), (), s32[]{:S(2)}) async-start(), calls=%async_computation.2 | async-start | bytes 4718592 | tf_op jit(solution)/shard_map/reduce_scatter | solution.py:1933
  139.8 14.0 %collective-permute-start.23 = (bf16[256,1024]{1,0:T(8,128)(2,1)S(1)}, bf16[256,1024]{1,0:T(8,128)(2,1)S(1)}, u32[]{:S(2)}, u32[]{:S(2)}) collective-permute-start(bf16[256,1024]{1,0:T(8,128)(2,1)S(1)} %fusion), channel_id=1, source_target_pairs={{0,2},{1,3},{2,0},{3,1},{4,6},{5,7},{6,4},{7,5},{8,10},{9,11},{10,... | collective-permute-start | bytes 1572872 | tf_op jit(solution)/shard_map/ppermute | solution.py:582
  156.1 13.2 %collective-permute-start.24 = (bf16[256,1024]{1,0:T(8,128)(2,1)S(1)}, bf16[256,1024]{1,0:T(8,128)(2,1)S(1)}, u32[]{:S(2)}, u32[]{:S(2)}) collective-permute-start(bf16[256,1024]{1,0:T(8,128)(2,1)S(1)} %get-tuple-element.159.first.refs_0_), channel_id=1, source_target_pairs={{0,2},{1,3},{2,0},{3,1},{4,6},{5,7},{6,4},{7,5},{8,10},{9,11},{10,... | collective-permute-start | bytes 1572872 | tf_op jit(solution)/shard_map/ppermute | solution.py:582
  181.3 14.0 %collective-permute-start.29 = (bf16[256,1024]{1,0:T(8,128)(2,1)S(1)}, bf16[256,1024]{1,0:T(8,128)(2,1)S(1)}, u32[]{:S(2)}, u32[]{:S(2)}) collective-permute-start(bf16[256,1024]{1,0:T(8,128)(2,1)S(1)} %add_convert_fusion.2), channel_id=1, source_target_pairs={{0,2},{1,3},{2,0},{3,1},{4,6},{5,7},{6,4},{7,5},{8,10},{9,11},{10,... | collective-permute-start | bytes 1572872 | tf_op jit(solution)/shard_map/ppermute | solution.py:582
  199.0 14.3 %collective-permute-start.32 = (bf16[256,1024]{1,0:T(8,128)(2,1)S(1)}, bf16[256,1024]{1,0:T(8,128)(2,1)S(1)}, u32[]{:S(2)}, u32[]{:S(2)}) collective-permute-start(bf16[256,1024]{1,0:T(8,128)(2,1)S(1)} %get-tuple-element.164.first.refs_4_), channel_id=1, source_target_pairs={{0,2},{1,3},{2,0},{3,1},{4,6},{5,7},{6,4},{7,5},{8,10},{9,11},{10,... | collective-permute-start | bytes 1572872 | tf_op jit(solution)/shard_map/ppermute | solution.py:582
  218.1 11.9 %collective-permute-start.31 = (bf16[256,1024]{1,0:T(8,128)(2,1)}, bf16[256,1024]{1,0:T(8,128)(2,1)}, u32[]{:S(2)}, u32[]{:S(2)}) collective-permute-start(bf16[256,1024]{1,0:T(8,128)(2,1)} %get-tuple-element.167), channel_id=1, source_target_pairs={{0,1},{1,0},{2,3},{3,2},{4,5},{5,4},{6,7},{7,6},{8,9},{9,8},{10,11... | collective-permute-start | bytes 1572872 | tf_op jit(solution)/shard_map/ppermute | solution.py:582
  220.8 14.3 %collective-permute-start.35 = (bf16[256,1024]{1,0:T(8,128)(2,1)}, bf16[256,1024]{1,0:T(8,128)(2,1)}, u32[]{:S(2)}, u32[]{:S(2)}) collective-permute-start(bf16[256,1024]{1,0:T(8,128)(2,1)} %add_convert_fusion.1), channel_id=1, source_target_pairs={{0,2},{1,3},{2,0},{3,1},{4,6},{5,7},{6,4},{7,5},{8,10},{9,11},{10,... | collective-permute-start | bytes 1572872 | tf_op jit(solution)/shard_map/ppermute | solution.py:582
  243.7 13.1 %collective-permute-start.37 = (bf16[256,1024]{1,0:T(8,128)(2,1)S(1)}, bf16[256,1024]{1,0:T(8,128)(2,1)S(1)}, u32[]{:S(2)}, u32[]{:S(2)}) collective-permute-start(bf16[256,1024]{1,0:T(8,128)(2,1)S(1)} %copy-done.29), channel_id=1, source_target_pairs={{0,2},{1,3},{2,0},{3,1},{4,6},{5,7},{6,4},{7,5},{8,10},{9,11},{10,... | collective-permute-start | bytes 1572872 | tf_op jit(solution)/shard_map/ppermute | solution.py:582
  259.7 13.4 %collective-permute-start.41 = (bf16[64,1024]{1,0:T(8,128)(2,1)S(1)}, bf16[64,1024]{1,0:T(8,128)(2,1)S(1)}, u32[]{:S(2)}, u32[]{:S(2)}) collective-permute-start(bf16[64,1024]{1,0:T(8,128)(2,1)S(1)} %get-tuple-element.257), channel_id=1, source_target_pairs={{0,12},{4,8},{8,4},{12,0},{16,28},{20,24},{24,20},{28,16},{1,13},{... | collective-permute-start | bytes 393224 | tf_op jit(solution)/shard_map/ppermute | solution.py:582
  263.5 16.0 %collective-permute-start.40 = (bf16[64,1024]{1,0:T(8,128)(2,1)S(1)}, bf16[64,1024]{1,0:T(8,128)(2,1)S(1)}, u32[]{:S(2)}, u32[]{:S(2)}) collective-permute-start(bf16[64,1024]{1,0:T(8,128)(2,1)S(1)} %get-tuple-element.260), channel_id=1, source_target_pairs={{0,8},{4,12},{8,0},{12,4},{16,24},{20,28},{24,16},{28,20},{1,9},{5... | collective-permute-start | bytes 393224 | tf_op jit(solution)/shard_map/ppermute | solution.py:582
  311.1 12.0 %collective-permute-start.43 = (bf16[192,1024]{1,0:T(8,128)(2,1)S(1)}, bf16[192,1024]{1,0:T(8,128)(2,1)S(1)}, u32[]{:S(2)}, u32[]{:S(2)}) collective-permute-start(bf16[192,1024]{1,0:T(8,128)(2,1)S(1)} %get-tuple-element.188), channel_id=1, source_target_pairs={{0,8},{4,12},{8,0},{12,4},{16,24},{20,28},{24,16},{28,20},{1,9},{5... | collective-permute-start | bytes 1179656 | tf_op jit(solution)/shard_map/ppermute | solution.py:582
  311.1 19.0 %collective-permute-start.44 = (bf16[192,1024]{1,0:T(8,128)(2,1)S(1)}, bf16[192,1024]{1,0:T(8,128)(2,1)S(1)}, u32[]{:S(2)}, u32[]{:S(2)}) collective-permute-start(bf16[192,1024]{1,0:T(8,128)(2,1)S(1)} %get-tuple-element.189), channel_id=1, source_target_pairs={{0,12},{4,8},{8,4},{12,0},{16,28},{20,24},{24,20},{28,16},{1,13},{... | collective-permute-start | bytes 1179656 | tf_op jit(solution)/shard_map/ppermute | solution.py:582
  334.7 14.0 %collective-permute-start.49 = (bf16[256,1024]{1,0:T(8,128)(2,1)S(1)}, bf16[256,1024]{1,0:T(8,128)(2,1)S(1)}, u32[]{:S(2)}, u32[]{:S(2)}) collective-permute-start(bf16[256,1024]{1,0:T(8,128)(2,1)S(1)} %add_convert_fusion), channel_id=1, source_target_pairs={{0,2},{1,3},{2,0},{3,1},{4,6},{5,7},{6,4},{7,5},{8,10},{9,11},{10,... | collective-permute-start | bytes 1572872 | tf_op jit(solution)/shard_map/ppermute | solution.py:582
  339.2 26.0 %collective-permute-start.46 = (bf16[4,768,128]{2,1,0:T(8,128)(2,1)S(1)}, bf16[4,768,128]{2,1,0:T(8,128)(2,1)S(1)}, u32[]{:S(2)}, u32[]{:S(2)}) collective-permute-start(bf16[4,768,128]{2,1,0:T(8,128)(2,1)S(1)} %get-tuple-element.197), channel_id=1, source_target_pairs={{0,4},{4,0},{8,12},{12,8},{16,20},{20,16},{24,28},{28,24},{1,5},{5... | collective-permute-start | bytes 2359304 | tf_op jit(solution)/shard_map/ppermute | solution.py:582
  368.5 12.8 %collective-permute-start.54 = (bf16[1200,128]{1,0:T(8,128)(2,1)}, bf16[1200,128]{1,0:T(8,128)(2,1)S(1)}, u32[]{:S(2)}, u32[]{:S(2)}) collective-permute-start(bf16[1200,128]{1,0:T(8,128)(2,1)} %get-tuple-element.217), channel_id=1, source_target_pairs={{0,8},{4,12},{8,0},{12,4},{16,24},{20,28},{24,16},{28,20},{1,9},{5... | collective-permute-start | bytes 921608 | tf_op jit(solution)/shard_map/ppermute | solution.py:582
  368.8 24.3 %collective-permute-start.55 = (bf16[1200,128]{1,0:T(8,128)(2,1)S(1)}, bf16[1200,128]{1,0:T(8,128)(2,1)S(1)}, u32[]{:S(2)}, u32[]{:S(2)}) collective-permute-start(bf16[1200,128]{1,0:T(8,128)(2,1)S(1)} %get-tuple-element.218), channel_id=1, source_target_pairs={{0,16},{4,20},{8,24},{12,28},{16,0},{20,4},{24,8},{28,12},{1,17},{... | collective-permute-start | bytes 921608 | tf_op jit(solution)/shard_map/ppermute | solution.py:582
  368.8 24.3 %collective-permute-start.56 = (bf16[1200,128]{1,0:T(8,128)(2,1)S(1)}, bf16[1200,128]{1,0:T(8,128)(2,1)S(1)}, u32[]{:S(2)}, u32[]{:S(2)}) collective-permute-start(bf16[1200,128]{1,0:T(8,128)(2,1)S(1)} %get-tuple-element.219), channel_id=1, source_target_pairs={{0,24},{4,28},{8,16},{12,20},{16,8},{20,12},{24,0},{28,4},{1,25},{... | collective-permute-start | bytes 921608 | tf_op jit(solution)/shard_map/ppermute | solution.py:582
  (120 other events, 870.4 us)
Sparse Core Ops, SparseCore 0:
  10.8 61.6 all-gather.5
  93.3 78.3 all-gather.3
  242.8 112.8 reduce-scatter.1

commit v6 on v5

--- a/solution.py
+++ b/solution.py
@@ -831,11 +831,17 @@
     head_outs = refs[12:16]
     noisy_out, target_out, mod_out = refs[16:19]
     tokens, heads, weights, mid, hidden, resid, target, mod_own, held, sems, out_sems = refs[19:]
+    spans = (slice(QKV_ROWS, FRONT_ROWS + 384), slice(0, QKV_ROWS))
     copies = [
-        pltpu.make_async_copy(pieces.at[place], held.at[place], sems.at[place])
-        for place in range(8)
+        [
+            pltpu.make_async_copy(
+                pieces.at[place, span, :], held.at[place, span, :], sems.at[place, index]
+            )
+            for place in range(8)
+        ]
+        for index, span in enumerate(spans)
     ]
-    for copy in copies:
+    for copy in copies[0] + copies[1]:
         copy.start()
     for source in range(4):
         rows = pl.ds(pl.multiple_of(meta[20 + source] * 64, 64), 64)
@@ -859,13 +865,13 @@
     outs.append(pltpu.make_async_copy(mod_own, mod_out, out_sems.at[8]))
     outs.append(pltpu.make_async_copy(mid, mid_out, out_sems.at[9]))
     for place in range(8):
-        copies[place].wait()
+        copies[0][place].wait()
         block = slice(128 * place, 128 * place + 128)
-        weights[:, block] = held[place, 0:FRONT_ROWS, :]
+        weights[QKV_ROWS:FRONT_ROWS, block] = held[place, QKV_ROWS:FRONT_ROWS, :]
         for part in range(3):
             base = FRONT_ROWS + 128 * part
             mid[block, 128 * part : 128 * part + 128] = held[place, base : base + 128, :]
-    for index in (0, 1, 2, 9):
+    for index in (0, 1, 9):
         outs[index].start()
     embed = weights[QKV_ROWS : QKV_ROWS + 128, :]
     vec_rows = weights[QKV_ROWS + 128 : FRONT_ROWS, :].astype(jnp.float32)
@@ -883,8 +889,13 @@
         low = (normed * (1.0 + scale) + shift).astype(jnp.bfloat16)
         hidden[frame] = low
         outs[4 + frame].start()
+    for place in range(8):
+        copies[1][place].wait()
+        weights[0:QKV_ROWS, 128 * place : 128 * place + 128] = held[place, 0:QKV_ROWS, :]
+    outs[2].start()
+    for frame in range(4):
         mixed = lax.dot_general(
-            weights[0:QKV_ROWS, :], low, NT, preferred_element_type=jnp.float32
+            weights[0:QKV_ROWS, :], hidden[frame], NT, preferred_element_type=jnp.float32
         )
         cos_now = cosine[meta[8 + frame]]
         sin_now = sine[meta[8 + frame]]
@@ -937,7 +948,7 @@
             pltpu.VMEM((PATCHES, 128), jnp.float32),
             pltpu.VMEM((8, D), jnp.float32),
             pltpu.VMEM((8, FRONT_ROWS + 384, 128), jnp.bfloat16),
-            pltpu.SemaphoreType.DMA((8,)),
+            pltpu.SemaphoreType.DMA((8, 2)),
             pltpu.SemaphoreType.DMA((14,)),
         ],
         compiler_params=pltpu.CompilerParams(vmem_limit_bytes=52 * 2**20),
@@ -952,7 +963,7 @@
 
 def middle_kernel(held, came, across, resid, mod, attn_out, resid_mid, hidden):
     total = total_own(held, came, across)
-    attn_out[...] = total
+    attn_out[...] = total.astype(jnp.bfloat16)
     values = resid[...] + mod[2:3, :] * total
     resid_mid[...] = values
     normed, _ = centred_norm(values)
@@ -1023,7 +1034,7 @@
     grad = grad_three[...] + back_through_norm(grad_hidden * (1.0 + mod[4:5, :]), normed, inv_std)
     grad_mid[...] = grad
     grad_low[...] = (mod[2:3, :] * grad).astype(jnp.bfloat16)
-    rows[0:1, :] = column_sum(grad * attn_out[...])
+    rows[0:1, :] = column_sum(grad * attn_out[...].astype(jnp.float32))
     rows[1:2, :] = column_sum(grad_hidden)
     rows[2:3, :] = column_sum(grad_hidden * normed)
 
@@ -1334,8 +1345,10 @@
     grad = grad * factor
     first_mom = beta_one * first_mom + (1.0 - beta_one) * grad
     second_mom = beta_two * second_mom + (1.0 - beta_two) * grad * grad
+    second_hat = second_mom * second_fix
     updated = weight_now - rate * (
-        first_mom * first_fix / (jnp.sqrt(second_mom * second_fix) + adam_eps) + decay * weight_now
+        first_mom * first_fix / (second_hat * lax.rsqrt(second_hat) + adam_eps)
+        + decay * weight_now
     )
     return updated, first_mom, second_mom, updated.astype(jnp.bfloat16)
 
@@ -1857,7 +1870,7 @@
     attn_out, resid_mid, hidden_own = row_call(
         middle_kernel,
         "middle",
-        (frame_f32(), frame_f32(), frame_low()),
+        (frame_low(), frame_f32(), frame_low()),
         *sum_frames(near, sum_across(far)),
         resid_in,
         mod_own,

time: 441 us -> 441 us (level)
  transfers between devices with their start and end apart: 67 -> 67, of which waited for: 44 -> 43; matrix products, arithmetic and copies ran while one was open for 3% -> 3% of each run, Pallas kernels for 19% -> 19%
where the time goes in v6:
time: 441 us; the launch traced here: 433 us
  waiting for transfers between devices  196 us (44%)
  Pallas kernels  114 us (26%)
  starting transfers between devices  63.1 us (14%)
  local copies, waits for them, and re-layouts  29.9 us (7%)
  between operations  19 us (4%)
  other arithmetic  7.96 us (2%)
    ppermute x64, waiting for transfers between devices, swap(): return lax.ppermute(values, axis, [(i, i ^ bit) for i in range(size)])  187 us
    ppermute x64, starting transfers between devices, swap(): return lax.ppermute(values, axis, [(i, i ^ bit) for i in range(size)])  63 us
    pallas_call x1, Pallas kernels, call_attend_back(): pl.pallas_call(attend_back_kernel, out_shape=tuple((jax.ShapeDtypeStruct(...  30 us
    unnamed x160, local copies, waits for them, and re-layouts  28 us
    pallas_call x1, Pallas kernels, call_attend(): pl.pallas_call(attend_kernel, out_shape=tuple((jax.ShapeDtypeStruct((HD,...  22.6 us
    pallas_call x9, Pallas kernels, row_call(): pl.pallas_call(kernel, out_shape=tuple(outs), in_specs=smem_specs(smem) +...  12.5 us
    pallas_call x4, Pallas kernels, call_mlp(): pl.pallas_call(kernel, out_shape=(frame_f32(), frame_low()) + outs, in_sp...  11.4 us
    all_gather x1, waiting for transfers between devices, shards_halves(): front_pieces = lax.all_gather(front_shard, 'ctx', axis=0)  9.15 us
  transfers between devices with their start and end apart: 67, of which 43 were waited for; matrix products, arithmetic and copies ran while one was open for 3% of the time, Pallas kernels for 19%

profile of v6, /device:TPU:0, one launch (start us, length us, event | category | flops | bytes accessed | tf_op | source)
XLA Modules:
  0.0 433.3 jit_solution(11774235740772134303)
XLA Ops:
  28.9 6.4 %collective-permute-done.9.refs_3_ = bf16[512,128]{1,0:T(8,128)(2,1)S(1)} collective-permute-done((bf16[512,128]{1,0:T(8,128)(2,1)}, bf16[512,128]{1,0:T(8,128)(2,1)S(1)}, u32[]{:S(2)}, u32[]{:S(2)}) %collective-permute-start.9) | collective-permute-done | bytes 131104 | tf_op jit(solution)/shard_map/ppermute | solution.py:582
  63.3 9.2 %all-gather.6.cloned.1.call-done = bf16[10368,128]{1,0:T(8,128)(2,1)} async-done(((bf16[1296,128]{1,0:T(8,128)(2,1)}), bf16[10368,128]{1,0:T(8,128)(2,1)}) %all-gather.6.cloned.1.call-update) | async-done | bytes 2654224 | tf_op jit(solution)/shard_map/all_gather | solution.py:1788
  73.3 8.4 %front.1 = (bf16[912,1024]{1,0:T(8,128)(2,1)}, bf16[1024,384]{1,0:T(8,128)(2,1)}, bf16[4,256,1024]{2,1,0:T(8,128)(2,1)}, f32[256,1024]{1,0:T(8,128)}, bf16[192,1...) custom-call(s32[24]{0:T(128)S(1)} %copy-done.39, ...), custom_call_target="tpu_custom_call" | custom-call | flops 2000000000 | bytes 10000000 | tf_op jit(solution)/shard_map/front/pallas_call | solution.py:925
  86.1 6.7 %collective-permute-done.15.refs_1_ = bf16[192,1024]{1,0:T(8,128)(2,1)S(1)} collective-permute-done((bf16[192,1024]{1,0:T(8,128)(2,1)S(1)}, bf16[192,1024]{1,0:T(8,128)(2,1)S(1)}, u32[]{:S(2)}, u32[]{:S(2)}) %collective-permute-start.15) | collective-permute-done | bytes 393248 | tf_op jit(solution)/shard_map/ppermute | solution.py:582
  95.8 6.8 %collective-permute-done.17.refs_3_ = bf16[192,1024]{1,0:T(8,128)(2,1)S(1)} collective-permute-done((bf16[192,1024]{1,0:T(8,128)(2,1)S(1)}, bf16[192,1024]{1,0:T(8,128)(2,1)S(1)}, u32[]{:S(2)}, u32[]{:S(2)}) %collective-permute-start.17) | collective-permute-done | bytes 393248 | tf_op jit(solution)/shard_map/ppermute | solution.py:582
  102.7 22.6 %attend.1 = (bf16[64,1024]{1,0:T(8,128)(2,1)S(1)}, bf16[64,1024]{1,0:T(8,128)(2,1)S(1)}, bf16[64,1024]{1,0:T(8,128)(2,1)S(1)}, bf16[64,1024]{1,0:T(8,128)(2,1)S(...) custom-call(s32[18]{0:T(128)S(1)} %copy-done.56, bf16[192,1024]{1,0:T(8,128)(2,1)S(1)} %copy-done.64, ...), custom_call_target="tpu_custom_call" | custom-call | flops 8999999488 | bytes 5000000 | tf_op jit(solution)/shard_map/attend/pallas_call | solution.py:1621
  134.1 5.3 %collective-permute-done.19 = bf16[64,1024]{1,0:T(8,128)(2,1)S(1)} collective-permute-done((bf16[64,1024]{1,0:T(8,128)(2,1)S(1)}, bf16[64,1024]{1,0:T(8,128)(2,1)S(1)}, u32[]{:S(2)}, u32[]{:S(2)}) %collective-permute-start.19) | collective-permute-done | bytes 131104 | tf_op jit(solution)/shard_map/ppermute | solution.py:582
  144.3 12.1 %collective-permute-done.23.across = bf16[256,1024]{1,0:T(8,128)(2,1)S(1)} collective-permute-done((bf16[256,1024]{1,0:T(8,128)(2,1)S(1)}, bf16[256,1024]{1,0:T(8,128)(2,1)S(1)}, u32[]{:S(2)}, u32[]{:S(2)}) %collective-permute-start.23) | collective-permute-done | bytes 524320 | tf_op jit(solution)/shard_map/ppermute | solution.py:582
  160.2 11.6 %collective-permute-done.24.first.refs_2_ = bf16[256,1024]{1,0:T(8,128)(2,1)S(1)} collective-permute-done((bf16[256,1024]{1,0:T(8,128)(2,1)S(1)}, bf16[256,1024]{1,0:T(8,128)(2,1)S(1)}, u32[]{:S(2)}, u32[]{:S(2)}) %collective-permute-start.24) | collective-permute-done | bytes 524320 | tf_op jit(solution)/shard_map/ppermute | solution.py:582
  188.5 9.4 %collective-permute-done.29.across = bf16[256,1024]{1,0:T(8,128)(2,1)S(1)} collective-permute-done((bf16[256,1024]{1,0:T(8,128)(2,1)S(1)}, bf16[256,1024]{1,0:T(8,128)(2,1)S(1)}, u32[]{:S(2)}, u32[]{:S(2)}) %collective-permute-start.29) | collective-permute-done | bytes 524320 | tf_op jit(solution)/shard_map/ppermute | solution.py:582
  207.6 8.3 %collective-permute-done.32.first.refs_6_ = bf16[256,1024]{1,0:T(8,128)(2,1)S(1)} collective-permute-done((bf16[256,1024]{1,0:T(8,128)(2,1)S(1)}, bf16[256,1024]{1,0:T(8,128)(2,1)S(1)}, u32[]{:S(2)}, u32[]{:S(2)}) %collective-permute-start.32) | collective-permute-done | bytes 524320 | tf_op jit(solution)/shard_map/ppermute | solution.py:582
  224.9 5.6 %weight_grad.1 = bf16[1024,2048]{1,0:T(8,128)(2,1)S(1)} custom-call(bf16[256,1024]{1,0:T(8,128)(2,1)S(1)} %copy-done.43, bf16[256,1024]{1,0:T(8,128)(2,1)S(1)} %collective-permute-done.27.second.refs_1_, bf16[256,1024]{1,0:T(8,128)(2,1)S(1)} %copy-done.46, bf16[256,1024]{1,0:T(8,128)(2,1)S(1)} %copy-done.49, ...), custom_call_target="tpu_custom_call" | custom-call | flops 5000000000 | bytes 20000000 | tf_op jit(solution)/shard_map/weight_grad/pallas_call | solution.py:1261
  232.5 5.1 %collective-permute-done.35.across = bf16[256,1024]{1,0:T(8,128)(2,1)} collective-permute-done((bf16[256,1024]{1,0:T(8,128)(2,1)}, bf16[256,1024]{1,0:T(8,128)(2,1)}, u32[]{:S(2)}, u32[]{:S(2)}) %collective-permute-start.35) | collective-permute-done | bytes 524320 | tf_op jit(solution)/shard_map/ppermute | solution.py:582
  247.7 11.5 %collective-permute-done.37 = bf16[256,1024]{1,0:T(8,128)(2,1)S(1)} collective-permute-done((bf16[256,1024]{1,0:T(8,128)(2,1)S(1)}, bf16[256,1024]{1,0:T(8,128)(2,1)S(1)}, u32[]{:S(2)}, u32[]{:S(2)}) %collective-permute-start.37) | collective-permute-done | bytes 524320 | tf_op jit(solution)/shard_map/ppermute | solution.py:582
  267.2 6.2 %collective-permute-done.41.refs_7_ = bf16[64,1024]{1,0:T(8,128)(2,1)S(1)} collective-permute-done((bf16[64,1024]{1,0:T(8,128)(2,1)S(1)}, bf16[64,1024]{1,0:T(8,128)(2,1)S(1)}, u32[]{:S(2)}, u32[]{:S(2)}) %collective-permute-start.41) | collective-permute-done | bytes 131104 | tf_op jit(solution)/shard_map/ppermute | solution.py:582
  273.4 5.6 %collective-permute-done.40.refs_6_ = bf16[64,1024]{1,0:T(8,128)(2,1)S(1)} collective-permute-done((bf16[64,1024]{1,0:T(8,128)(2,1)S(1)}, bf16[64,1024]{1,0:T(8,128)(2,1)S(1)}, u32[]{:S(2)}, u32[]{:S(2)}) %collective-permute-start.40) | collective-permute-done | bytes 131104 | tf_op jit(solution)/shard_map/ppermute | solution.py:582
  279.1 30.0 %attend_back.1 = (bf16[192,1024]{1,0:T(8,128)(2,1)S(1)}, bf16[192,1024]{1,0:T(8,128)(2,1)S(1)}, bf16[192,1024]{1,0:T(8,128)(2,1)S(1)}, bf16[192,1024]{1,0:T(8,128)(2,1)S(1)}) custom-call(s32[18]{0:T(128)S(1)} %copy-done.56, bf16[192,1024]{1,0:T(8,128)(2,1)S(1)} %copy-done.65, bf16[192,1024]{1,0:T(8,128)(2,1)S(1)} %copy-done.51, ...), custom_call_target="tpu_custom_call" | custom-call | flops 30000001024 | bytes 10000000 | tf_op jit(solution)/shard_map/attend_back/pallas_call | solution.py:1729
  312.7 7.6 %collective-permute-done.42.refs_1_ = bf16[192,1024]{1,0:T(8,128)(2,1)S(1)} collective-permute-done((bf16[192,1024]{1,0:T(8,128)(2,1)S(1)}, bf16[192,1024]{1,0:T(8,128)(2,1)S(1)}, u32[]{:S(2)}, u32[]{:S(2)}) %collective-permute-start.42) | collective-permute-done | bytes 393248 | tf_op jit(solution)/shard_map/ppermute | solution.py:582
  322.3 7.6 %collective-permute-done.44.refs_3_ = bf16[192,1024]{1,0:T(8,128)(2,1)S(1)} collective-permute-done((bf16[192,1024]{1,0:T(8,128)(2,1)S(1)}, bf16[192,1024]{1,0:T(8,128)(2,1)S(1)}, u32[]{:S(2)}, u32[]{:S(2)}) %collective-permute-start.44) | collective-permute-done | bytes 393248 | tf_op jit(solution)/shard_map/ppermute | solution.py:582
  339.7 8.9 %collective-permute-done.49.across = bf16[256,1024]{1,0:T(8,128)(2,1)S(1)} collective-permute-done((bf16[256,1024]{1,0:T(8,128)(2,1)S(1)}, bf16[256,1024]{1,0:T(8,128)(2,1)S(1)}, u32[]{:S(2)}, u32[]{:S(2)}) %collective-permute-start.49) | collective-permute-done | bytes 524320 | tf_op jit(solution)/shard_map/ppermute | solution.py:582
  373.9 7.5 %collective-permute-done.54.refs_3_ = bf16[1200,128]{1,0:T(8,128)(2,1)S(1)} collective-permute-done((bf16[1200,128]{1,0:T(8,128)(2,1)}, bf16[1200,128]{1,0:T(8,128)(2,1)S(1)}, u32[]{:S(2)}, u32[]{:S(2)}) %collective-permute-start.54) | collective-permute-done | bytes 307232 | tf_op jit(solution)/shard_map/ppermute | solution.py:582
  381.4 11.5 %collective-permute-done.55.refs_4_ = bf16[1200,128]{1,0:T(8,128)(2,1)S(1)} collective-permute-done((bf16[1200,128]{1,0:T(8,128)(2,1)S(1)}, bf16[1200,128]{1,0:T(8,128)(2,1)S(1)}, u32[]{:S(2)}, u32[]{:S(2)}) %collective-permute-start.55) | collective-permute-done | bytes 307232 | tf_op jit(solution)/shard_map/ppermute | solution.py:582
  406.2 5.1 %collective-permute-start.62 = (f32[1,128]{1,0:T(1,128)S(1)}, f32[1,128]{1,0:T(1,128)S(1)}, u32[]{:S(2)}, u32[]{:S(2)}) collective-permute-start(f32[1,128]{1,0:T(1,128)S(1)} %add.127.refs_3_.refs_1_), channel_id=1, source_target_pairs={{0,16},{4,20},{8,24},{12,28},{16,0},{20,4},{24,8},{28,12},{1,17},{... | collective-permute-start | bytes 1544 | tf_op jit(solution)/shard_map/ppermute | solution.py:582
  415.5 8.6 %adam.1 = (f32[4,128,256]{2,1,0:T(8,128)}, f32[4,128,256]{2,1,0:T(8,128)}, f32[4,128,256]{2,1,0:T(8,128)}, bf16[4,128,256]{2,1,0:T(8,128)(2,1)}, f32[2,128,1024]...) custom-call(f32[2]{0:T(128)S(1)} %get-tuple-element.285.refs_0_, ...), custom_call_target="tpu_custom_call" | custom-call | flops 10000000 | bytes 20000000 | tf_op jit(solution)/shard_map/adam/pallas_call | solution.py:1483
  (358 shorter events, 186.4 us)
Async XLA Ops:
  7.2 65.2 %all-gather.6.cloned.1.call-start = ((), (), s32[]{:S(2)}) async-start(), calls=%async_computation.3 | async-start | bytes 2985984 | tf_op jit(solution)/shard_map/all_gather | solution.py:1788
  9.2 165.4 %all-gather.4.cloned.1.call-start = ((), (), s32[]{:S(2)}) async-start(), calls=%async_computation.1 | async-start | bytes 4718592 | tf_op jit(solution)/shard_map/all_gather | solution.py:1856
  11.6 17.3 %collective-permute-start.10 = (bf16[512,128]{1,0:T(8,128)(2,1)}, bf16[512,128]{1,0:T(8,128)(2,1)S(1)}, u32[]{:S(2)}, u32[]{:S(2)}) collective-permute-start(bf16[512,128]{1,0:T(8,128)(2,1)} %tokens.1.refs_0_), channel_id=1, source_target_pairs={{0,24},{4,28},{8,16},{12,20},{16,8},{20,12},{24,0},{28,4},{1,25},{... | collective-permute-start | bytes 393224 | tf_op jit(solution)/shard_map/ppermute | solution.py:582
  16.6 18.7 %collective-permute-start.9 = (bf16[512,128]{1,0:T(8,128)(2,1)}, bf16[512,128]{1,0:T(8,128)(2,1)S(1)}, u32[]{:S(2)}, u32[]{:S(2)}) collective-permute-start(bf16[512,128]{1,0:T(8,128)(2,1)} %tokens.1.refs_0_), channel_id=1, source_target_pairs={{0,16},{4,20},{8,24},{12,28},{16,0},{20,4},{24,8},{28,12},{1,17},{... | collective-permute-start | bytes 393224 | tf_op jit(solution)/shard_map/ppermute | solution.py:582
  16.6 18.7 %collective-permute-start.8 = (bf16[512,128]{1,0:T(8,128)(2,1)}, bf16[512,128]{1,0:T(8,128)(2,1)S(1)}, u32[]{:S(2)}, u32[]{:S(2)}) collective-permute-start(bf16[512,128]{1,0:T(8,128)(2,1)} %tokens.1.refs_0_), channel_id=1, source_target_pairs={{0,8},{4,12},{8,0},{12,4},{16,24},{20,28},{24,16},{28,20},{1,9},{5... | collective-permute-start | bytes 393224 | tf_op jit(solution)/shard_map/ppermute | solution.py:582
  27.1 12.0 %collective-permute-start.1 = (f32[4,4,1536]{2,1,0:T(4,128)S(1)}, f32[4,4,1536]{2,1,0:T(4,128)S(1)}, u32[]{:S(2)}, u32[]{:S(2)}) collective-permute-start(f32[4,4,1536]{2,1,0:T(4,128)S(1)} %select_bitcast_fusion), channel_id=1, source_target_pairs={{0,4},{4,0},{8,12},{12,8},{16,20},{20,16},{24,28},{28,24},{1,5},{5... | collective-permute-start | bytes 294920 | tf_op jit(solution)/shard_map/ppermute | solution.py:582
  35.3 17.8 %collective-permute-start.11 = (bf16[1536,128]{1,0:T(8,128)(2,1)S(1)}, bf16[1536,128]{1,0:T(8,128)(2,1)S(1)}, u32[]{:S(2)}, u32[]{:S(2)}) collective-permute-start(bf16[1536,128]{1,0:T(8,128)(2,1)S(1)} %pad_maximum_fusion.3), channel_id=1, source_target_pairs={{0,4},{4,0},{8,12},{12,8},{16,20},{20,16},{24,28},{28,24},{1,5},{5... | collective-permute-start | bytes 1179656 | tf_op jit(solution)/shard_map/ppermute | solution.py:582
  93.2 279.5 %reduce-scatter.2.cloned.1.call-start = ((), (), s32[]{:S(2)}) async-start(), calls=%async_computation.2 | async-start | bytes 4718592 | tf_op jit(solution)/shard_map/reduce_scatter | solution.py:1946
  142.2 14.2 %collective-permute-start.23 = (bf16[256,1024]{1,0:T(8,128)(2,1)S(1)}, bf16[256,1024]{1,0:T(8,128)(2,1)S(1)}, u32[]{:S(2)}, u32[]{:S(2)}) collective-permute-start(bf16[256,1024]{1,0:T(8,128)(2,1)S(1)} %fusion), channel_id=1, source_target_pairs={{0,2},{1,3},{2,0},{3,1},{4,6},{5,7},{6,4},{7,5},{8,10},{9,11},{10,... | collective-permute-start | bytes 1572872 | tf_op jit(solution)/shard_map/ppermute | solution.py:582
  158.5 13.4 %collective-permute-start.24 = (bf16[256,1024]{1,0:T(8,128)(2,1)S(1)}, bf16[256,1024]{1,0:T(8,128)(2,1)S(1)}, u32[]{:S(2)}, u32[]{:S(2)}) collective-permute-start(bf16[256,1024]{1,0:T(8,128)(2,1)S(1)} %get-tuple-element.159.first.refs_0_), channel_id=1, source_target_pairs={{0,2},{1,3},{2,0},{3,1},{4,6},{5,7},{6,4},{7,5},{8,10},{9,11},{10,... | collective-permute-start | bytes 1572872 | tf_op jit(solution)/shard_map/ppermute | solution.py:582
  183.9 14.0 %collective-permute-start.29 = (bf16[256,1024]{1,0:T(8,128)(2,1)S(1)}, bf16[256,1024]{1,0:T(8,128)(2,1)S(1)}, u32[]{:S(2)}, u32[]{:S(2)}) collective-permute-start(bf16[256,1024]{1,0:T(8,128)(2,1)S(1)} %add_convert_fusion.2), channel_id=1, source_target_pairs={{0,2},{1,3},{2,0},{3,1},{4,6},{5,7},{6,4},{7,5},{8,10},{9,11},{10,... | collective-permute-start | bytes 1572872 | tf_op jit(solution)/shard_map/ppermute | solution.py:582
  201.6 14.3 %collective-permute-start.32 = (bf16[256,1024]{1,0:T(8,128)(2,1)S(1)}, bf16[256,1024]{1,0:T(8,128)(2,1)S(1)}, u32[]{:S(2)}, u32[]{:S(2)}) collective-permute-start(bf16[256,1024]{1,0:T(8,128)(2,1)S(1)} %get-tuple-element.164.first.refs_4_), channel_id=1, source_target_pairs={{0,2},{1,3},{2,0},{3,1},{4,6},{5,7},{6,4},{7,5},{8,10},{9,11},{10,... | collective-permute-start | bytes 1572872 | tf_op jit(solution)/shard_map/ppermute | solution.py:582
  220.6 11.9 %collective-permute-start.31 = (bf16[256,1024]{1,0:T(8,128)(2,1)}, bf16[256,1024]{1,0:T(8,128)(2,1)}, u32[]{:S(2)}, u32[]{:S(2)}) collective-permute-start(bf16[256,1024]{1,0:T(8,128)(2,1)} %get-tuple-element.167), channel_id=1, source_target_pairs={{0,1},{1,0},{2,3},{3,2},{4,5},{5,4},{6,7},{7,6},{8,9},{9,8},{10,11... | collective-permute-start | bytes 1572872 | tf_op jit(solution)/shard_map/ppermute | solution.py:582
  223.3 14.3 %collective-permute-start.35 = (bf16[256,1024]{1,0:T(8,128)(2,1)}, bf16[256,1024]{1,0:T(8,128)(2,1)}, u32[]{:S(2)}, u32[]{:S(2)}) collective-permute-start(bf16[256,1024]{1,0:T(8,128)(2,1)} %add_convert_fusion.1), channel_id=1, source_target_pairs={{0,2},{1,3},{2,0},{3,1},{4,6},{5,7},{6,4},{7,5},{8,10},{9,11},{10,... | collective-permute-start | bytes 1572872 | tf_op jit(solution)/shard_map/ppermute | solution.py:582
  246.1 13.1 %collective-permute-start.37 = (bf16[256,1024]{1,0:T(8,128)(2,1)S(1)}, bf16[256,1024]{1,0:T(8,128)(2,1)S(1)}, u32[]{:S(2)}, u32[]{:S(2)}) collective-permute-start(bf16[256,1024]{1,0:T(8,128)(2,1)S(1)} %copy-done.29), channel_id=1, source_target_pairs={{0,2},{1,3},{2,0},{3,1},{4,6},{5,7},{6,4},{7,5},{8,10},{9,11},{10,... | collective-permute-start | bytes 1572872 | tf_op jit(solution)/shard_map/ppermute | solution.py:582
  247.7 11.6 %collective-permute-start.36 = (bf16[256,1024]{1,0:T(8,128)(2,1)S(1)}, bf16[256,1024]{1,0:T(8,128)(2,1)S(1)}, u32[]{:S(2)}, u32[]{:S(2)}) collective-permute-start(bf16[256,1024]{1,0:T(8,128)(2,1)S(1)} %copy-done.29), channel_id=1, source_target_pairs={{0,1},{1,0},{2,3},{3,2},{4,5},{5,4},{6,7},{7,6},{8,9},{9,8},{10,11... | collective-permute-start | bytes 1572872 | tf_op jit(solution)/shard_map/ppermute | solution.py:582
  264.7 14.3 %collective-permute-start.40 = (bf16[64,1024]{1,0:T(8,128)(2,1)S(1)}, bf16[64,1024]{1,0:T(8,128)(2,1)S(1)}, u32[]{:S(2)}, u32[]{:S(2)}) collective-permute-start(bf16[64,1024]{1,0:T(8,128)(2,1)S(1)} %get-tuple-element.260), channel_id=1, source_target_pairs={{0,8},{4,12},{8,0},{12,4},{16,24},{20,28},{24,16},{28,20},{1,9},{5... | collective-permute-start | bytes 393224 | tf_op jit(solution)/shard_map/ppermute | solution.py:582
  310.2 12.1 %collective-permute-start.43 = (bf16[192,1024]{1,0:T(8,128)(2,1)S(1)}, bf16[192,1024]{1,0:T(8,128)(2,1)S(1)}, u32[]{:S(2)}, u32[]{:S(2)}) collective-permute-start(bf16[192,1024]{1,0:T(8,128)(2,1)S(1)} %get-tuple-element.188), channel_id=1, source_target_pairs={{0,8},{4,12},{8,0},{12,4},{16,24},{20,28},{24,16},{28,20},{1,9},{5... | collective-permute-start | bytes 1179656 | tf_op jit(solution)/shard_map/ppermute | solution.py:582
  310.2 19.7 %collective-permute-start.44 = (bf16[192,1024]{1,0:T(8,128)(2,1)S(1)}, bf16[192,1024]{1,0:T(8,128)(2,1)S(1)}, u32[]{:S(2)}, u32[]{:S(2)}) collective-permute-start(bf16[192,1024]{1,0:T(8,128)(2,1)S(1)} %get-tuple-element.189), channel_id=1, source_target_pairs={{0,12},{4,8},{8,4},{12,0},{16,28},{20,24},{24,20},{28,16},{1,13},{... | collective-permute-start | bytes 1179656 | tf_op jit(solution)/shard_map/ppermute | solution.py:582
  334.5 14.0 %collective-permute-start.49 = (bf16[256,1024]{1,0:T(8,128)(2,1)S(1)}, bf16[256,1024]{1,0:T(8,128)(2,1)S(1)}, u32[]{:S(2)}, u32[]{:S(2)}) collective-permute-start(bf16[256,1024]{1,0:T(8,128)(2,1)S(1)} %add_convert_fusion), channel_id=1, source_target_pairs={{0,2},{1,3},{2,0},{3,1},{4,6},{5,7},{6,4},{7,5},{8,10},{9,11},{10,... | collective-permute-start | bytes 1572872 | tf_op jit(solution)/shard_map/ppermute | solution.py:582
  339.1 26.0 %collective-permute-start.46 = (bf16[4,768,128]{2,1,0:T(8,128)(2,1)S(1)}, bf16[4,768,128]{2,1,0:T(8,128)(2,1)S(1)}, u32[]{:S(2)}, u32[]{:S(2)}) collective-permute-start(bf16[4,768,128]{2,1,0:T(8,128)(2,1)S(1)} %get-tuple-element.197), channel_id=1, source_target_pairs={{0,4},{4,0},{8,12},{12,8},{16,20},{20,16},{24,28},{28,24},{1,5},{5... | collective-permute-start | bytes 2359304 | tf_op jit(solution)/shard_map/ppermute | solution.py:582
  368.4 13.1 %collective-permute-start.54 = (bf16[1200,128]{1,0:T(8,128)(2,1)}, bf16[1200,128]{1,0:T(8,128)(2,1)S(1)}, u32[]{:S(2)}, u32[]{:S(2)}) collective-permute-start(bf16[1200,128]{1,0:T(8,128)(2,1)} %get-tuple-element.217), channel_id=1, source_target_pairs={{0,8},{4,12},{8,0},{12,4},{16,24},{20,28},{24,16},{28,20},{1,9},{5... | collective-permute-start | bytes 921608 | tf_op jit(solution)/shard_map/ppermute | solution.py:582
  368.6 24.3 %collective-permute-start.55 = (bf16[1200,128]{1,0:T(8,128)(2,1)S(1)}, bf16[1200,128]{1,0:T(8,128)(2,1)S(1)}, u32[]{:S(2)}, u32[]{:S(2)}) collective-permute-start(bf16[1200,128]{1,0:T(8,128)(2,1)S(1)} %get-tuple-element.218), channel_id=1, source_target_pairs={{0,16},{4,20},{8,24},{12,28},{16,0},{20,4},{24,8},{28,12},{1,17},{... | collective-permute-start | bytes 921608 | tf_op jit(solution)/shard_map/ppermute | solution.py:582
  369.0 23.9 %collective-permute-start.56 = (bf16[1200,128]{1,0:T(8,128)(2,1)S(1)}, bf16[1200,128]{1,0:T(8,128)(2,1)S(1)}, u32[]{:S(2)}, u32[]{:S(2)}) collective-permute-start(bf16[1200,128]{1,0:T(8,128)(2,1)S(1)} %get-tuple-element.219), channel_id=1, source_target_pairs={{0,24},{4,28},{8,16},{12,20},{16,8},{20,12},{24,0},{28,4},{1,25},{... | collective-permute-start | bytes 921608 | tf_op jit(solution)/shard_map/ppermute | solution.py:582
  (120 other events, 865.9 us)
Sparse Core Ops, SparseCore 0:
  10.8 61.6 all-gather.5
  93.4 77.7 all-gather.3
  245.2 110.9 reduce-scatter.1

commit v7 on v6

--- a/solution.py
+++ b/solution.py
@@ -970,16 +970,20 @@
     hidden[...] = (normed * (1.0 + mod[4:5, :]) + mod[3:4, :]).astype(jnp.bfloat16)
 
 
-def row_call(kernel, name, outs, *operands, smem=0):
+def row_call(kernel, name, outs, *operands, smem=0, inside=None):
     return pl.pallas_call(
         kernel,
         out_shape=tuple(outs),
-        in_specs=smem_specs(smem) + vmem_specs(len(operands) - smem),
+        in_specs=smem_specs(smem) + (inside or vmem_specs)(len(operands) - smem),
         out_specs=vmem_specs(len(outs)),
-        compiler_params=pltpu.CompilerParams(vmem_limit_bytes=16 * 2**20),
+        compiler_params=pltpu.CompilerParams(vmem_limit_bytes=32 * 2**20 if inside else 16 * 2**20),
         cost_estimate=pl.CostEstimate(flops=10**9, bytes_accessed=4 * 10**6, transcendentals=0),
         name=name,
     )(*operands)
+
+
+def plain_specs(count):
+    return [pl.BlockSpec()] * count
 
 
 def frame_f32():
@@ -1932,6 +1936,7 @@
         mod_own,
         grad_three,
         attn_out,
+        inside=plain_specs,
     )
     back_list = spread_frames(grad_low)
     grad_attn_low = jnp.concatenate(back_list, axis=0)

time: 441 us -> 440 us (level)
  no operation moved by 1% of the time
where the time goes in v7:
time: 440 us; the launch traced here: 433 us
  waiting for transfers between devices  196 us (45%)
  Pallas kernels  114 us (26%)
  starting transfers between devices  63.1 us (14%)
  local copies, waits for them, and re-layouts  29.9 us (7%)
  between operations  19 us (4%)
  other arithmetic  7.96 us (2%)
    ppermute x64, waiting for transfers between devices, swap(): return lax.ppermute(values, axis, [(i, i ^ bit) for i in range(size)])  187 us
    ppermute x64, starting transfers between devices, swap(): return lax.ppermute(values, axis, [(i, i ^ bit) for i in range(size)])  63 us
    pallas_call x1, Pallas kernels, call_attend_back(): pl.pallas_call(attend_back_kernel, out_shape=tuple((jax.ShapeDtypeStruct(...  30 us
    unnamed x160, local copies, waits for them, and re-layouts  28 us
    pallas_call x1, Pallas kernels, call_attend(): pl.pallas_call(attend_kernel, out_shape=tuple((jax.ShapeDtypeStruct((HD,...  22.6 us
    pallas_call x9, Pallas kernels, row_call(): pl.pallas_call(kernel, out_shape=tuple(outs), in_specs=smem_specs(smem) +...  12.5 us
    pallas_call x4, Pallas kernels, call_mlp(): pl.pallas_call(kernel, out_shape=(frame_f32(), frame_low()) + outs, in_sp...  11.4 us
    all_gather x1, waiting for transfers between devices, shards_halves(): front_pieces = lax.all_gather(front_shard, 'ctx', axis=0)  9.15 us
  transfers between devices with their start and end apart: 67, of which 43 were waited for; matrix products, arithmetic and copies ran while one was open for 3% of the time, Pallas kernels for 19%

profile of v7, /device:TPU:0, one launch (start us, length us, event | category | flops | bytes accessed | tf_op | source)
XLA Modules:
  0.0 433.3 jit_solution(2022387257126900707)
XLA Ops:
  28.9 6.4 %collective-permute-done.9.refs_3_ = bf16[512,128]{1,0:T(8,128)(2,1)S(1)} collective-permute-done((bf16[512,128]{1,0:T(8,128)(2,1)}, bf16[512,128]{1,0:T(8,128)(2,1)S(1)}, u32[]{:S(2)}, u32[]{:S(2)}) %collective-permute-start.9) | collective-permute-done | bytes 131104 | tf_op jit(solution)/shard_map/ppermute | solution.py:582
  63.3 9.2 %all-gather.6.cloned.1.call-done = bf16[10368,128]{1,0:T(8,128)(2,1)} async-done(((bf16[1296,128]{1,0:T(8,128)(2,1)}), bf16[10368,128]{1,0:T(8,128)(2,1)}) %all-gather.6.cloned.1.call-update) | async-done | bytes 2654224 | tf_op jit(solution)/shard_map/all_gather | solution.py:1792
  73.3 8.4 %front.1 = (bf16[912,1024]{1,0:T(8,128)(2,1)}, bf16[1024,384]{1,0:T(8,128)(2,1)}, bf16[4,256,1024]{2,1,0:T(8,128)(2,1)}, f32[256,1024]{1,0:T(8,128)}, bf16[192,1...) custom-call(s32[24]{0:T(128)S(1)} %copy-done.39, ...), custom_call_target="tpu_custom_call" | custom-call | flops 2000000000 | bytes 10000000 | tf_op jit(solution)/shard_map/front/pallas_call | solution.py:925
  86.1 6.7 %collective-permute-done.15.refs_1_ = bf16[192,1024]{1,0:T(8,128)(2,1)S(1)} collective-permute-done((bf16[192,1024]{1,0:T(8,128)(2,1)S(1)}, bf16[192,1024]{1,0:T(8,128)(2,1)S(1)}, u32[]{:S(2)}, u32[]{:S(2)}) %collective-permute-start.15) | collective-permute-done | bytes 393248 | tf_op jit(solution)/shard_map/ppermute | solution.py:582
  95.8 6.8 %collective-permute-done.17.refs_3_ = bf16[192,1024]{1,0:T(8,128)(2,1)S(1)} collective-permute-done((bf16[192,1024]{1,0:T(8,128)(2,1)S(1)}, bf16[192,1024]{1,0:T(8,128)(2,1)S(1)}, u32[]{:S(2)}, u32[]{:S(2)}) %collective-permute-start.17) | collective-permute-done | bytes 393248 | tf_op jit(solution)/shard_map/ppermute | solution.py:582
  102.7 22.6 %attend.1 = (bf16[64,1024]{1,0:T(8,128)(2,1)S(1)}, bf16[64,1024]{1,0:T(8,128)(2,1)S(1)}, bf16[64,1024]{1,0:T(8,128)(2,1)S(1)}, bf16[64,1024]{1,0:T(8,128)(2,1)S(...) custom-call(s32[18]{0:T(128)S(1)} %copy-done.56, bf16[192,1024]{1,0:T(8,128)(2,1)S(1)} %copy-done.64, ...), custom_call_target="tpu_custom_call" | custom-call | flops 8999999488 | bytes 5000000 | tf_op jit(solution)/shard_map/attend/pallas_call | solution.py:1625
  134.1 5.3 %collective-permute-done.19 = bf16[64,1024]{1,0:T(8,128)(2,1)S(1)} collective-permute-done((bf16[64,1024]{1,0:T(8,128)(2,1)S(1)}, bf16[64,1024]{1,0:T(8,128)(2,1)S(1)}, u32[]{:S(2)}, u32[]{:S(2)}) %collective-permute-start.19) | collective-permute-done | bytes 131104 | tf_op jit(solution)/shard_map/ppermute | solution.py:582
  144.3 12.1 %collective-permute-done.23.across = bf16[256,1024]{1,0:T(8,128)(2,1)S(1)} collective-permute-done((bf16[256,1024]{1,0:T(8,128)(2,1)S(1)}, bf16[256,1024]{1,0:T(8,128)(2,1)S(1)}, u32[]{:S(2)}, u32[]{:S(2)}) %collective-permute-start.23) | collective-permute-done | bytes 524320 | tf_op jit(solution)/shard_map/ppermute | solution.py:582
  160.2 11.6 %collective-permute-done.24.first.refs_2_ = bf16[256,1024]{1,0:T(8,128)(2,1)S(1)} collective-permute-done((bf16[256,1024]{1,0:T(8,128)(2,1)S(1)}, bf16[256,1024]{1,0:T(8,128)(2,1)S(1)}, u32[]{:S(2)}, u32[]{:S(2)}) %collective-permute-start.24) | collective-permute-done | bytes 524320 | tf_op jit(solution)/shard_map/ppermute | solution.py:582
  188.5 9.4 %collective-permute-done.29.across = bf16[256,1024]{1,0:T(8,128)(2,1)S(1)} collective-permute-done((bf16[256,1024]{1,0:T(8,128)(2,1)S(1)}, bf16[256,1024]{1,0:T(8,128)(2,1)S(1)}, u32[]{:S(2)}, u32[]{:S(2)}) %collective-permute-start.29) | collective-permute-done | bytes 524320 | tf_op jit(solution)/shard_map/ppermute | solution.py:582
  207.6 8.3 %collective-permute-done.32.first.refs_6_ = bf16[256,1024]{1,0:T(8,128)(2,1)S(1)} collective-permute-done((bf16[256,1024]{1,0:T(8,128)(2,1)S(1)}, bf16[256,1024]{1,0:T(8,128)(2,1)S(1)}, u32[]{:S(2)}, u32[]{:S(2)}) %collective-permute-start.32) | collective-permute-done | bytes 524320 | tf_op jit(solution)/shard_map/ppermute | solution.py:582
  224.9 5.6 %weight_grad.1 = bf16[1024,2048]{1,0:T(8,128)(2,1)S(1)} custom-call(bf16[256,1024]{1,0:T(8,128)(2,1)S(1)} %copy-done.43, bf16[256,1024]{1,0:T(8,128)(2,1)S(1)} %collective-permute-done.27.second.refs_1_, bf16[256,1024]{1,0:T(8,128)(2,1)S(1)} %copy-done.46, bf16[256,1024]{1,0:T(8,128)(2,1)S(1)} %copy-done.49, ...), custom_call_target="tpu_custom_call" | custom-call | flops 5000000000 | bytes 20000000 | tf_op jit(solution)/shard_map/weight_grad/pallas_call | solution.py:1265
  232.5 5.1 %collective-permute-done.35.across = bf16[256,1024]{1,0:T(8,128)(2,1)} collective-permute-done((bf16[256,1024]{1,0:T(8,128)(2,1)}, bf16[256,1024]{1,0:T(8,128)(2,1)}, u32[]{:S(2)}, u32[]{:S(2)}) %collective-permute-start.35) | collective-permute-done | bytes 524320 | tf_op jit(solution)/shard_map/ppermute | solution.py:582
  247.7 11.5 %collective-permute-done.37 = bf16[256,1024]{1,0:T(8,128)(2,1)S(1)} collective-permute-done((bf16[256,1024]{1,0:T(8,128)(2,1)S(1)}, bf16[256,1024]{1,0:T(8,128)(2,1)S(1)}, u32[]{:S(2)}, u32[]{:S(2)}) %collective-permute-start.37) | collective-permute-done | bytes 524320 | tf_op jit(solution)/shard_map/ppermute | solution.py:582
  267.2 6.2 %collective-permute-done.41.refs_7_ = bf16[64,1024]{1,0:T(8,128)(2,1)S(1)} collective-permute-done((bf16[64,1024]{1,0:T(8,128)(2,1)S(1)}, bf16[64,1024]{1,0:T(8,128)(2,1)S(1)}, u32[]{:S(2)}, u32[]{:S(2)}) %collective-permute-start.41) | collective-permute-done | bytes 131104 | tf_op jit(solution)/shard_map/ppermute | solution.py:582
  273.4 5.6 %collective-permute-done.40.refs_6_ = bf16[64,1024]{1,0:T(8,128)(2,1)S(1)} collective-permute-done((bf16[64,1024]{1,0:T(8,128)(2,1)S(1)}, bf16[64,1024]{1,0:T(8,128)(2,1)S(1)}, u32[]{:S(2)}, u32[]{:S(2)}) %collective-permute-start.40) | collective-permute-done | bytes 131104 | tf_op jit(solution)/shard_map/ppermute | solution.py:582
  279.1 30.0 %attend_back.1 = (bf16[192,1024]{1,0:T(8,128)(2,1)S(1)}, bf16[192,1024]{1,0:T(8,128)(2,1)S(1)}, bf16[192,1024]{1,0:T(8,128)(2,1)S(1)}, bf16[192,1024]{1,0:T(8,128)(2,1)S(1)}) custom-call(s32[18]{0:T(128)S(1)} %copy-done.56, bf16[192,1024]{1,0:T(8,128)(2,1)S(1)} %copy-done.65, bf16[192,1024]{1,0:T(8,128)(2,1)S(1)} %copy-done.51, ...), custom_call_target="tpu_custom_call" | custom-call | flops 30000001024 | bytes 10000000 | tf_op jit(solution)/shard_map/attend_back/pallas_call | solution.py:1733
  312.7 7.6 %collective-permute-done.42.refs_1_ = bf16[192,1024]{1,0:T(8,128)(2,1)S(1)} collective-permute-done((bf16[192,1024]{1,0:T(8,128)(2,1)S(1)}, bf16[192,1024]{1,0:T(8,128)(2,1)S(1)}, u32[]{:S(2)}, u32[]{:S(2)}) %collective-permute-start.42) | collective-permute-done | bytes 393248 | tf_op jit(solution)/shard_map/ppermute | solution.py:582
  322.3 7.6 %collective-permute-done.44.refs_3_ = bf16[192,1024]{1,0:T(8,128)(2,1)S(1)} collective-permute-done((bf16[192,1024]{1,0:T(8,128)(2,1)S(1)}, bf16[192,1024]{1,0:T(8,128)(2,1)S(1)}, u32[]{:S(2)}, u32[]{:S(2)}) %collective-permute-start.44) | collective-permute-done | bytes 393248 | tf_op jit(solution)/shard_map/ppermute | solution.py:582
  339.7 8.9 %collective-permute-done.49.across = bf16[256,1024]{1,0:T(8,128)(2,1)S(1)} collective-permute-done((bf16[256,1024]{1,0:T(8,128)(2,1)S(1)}, bf16[256,1024]{1,0:T(8,128)(2,1)S(1)}, u32[]{:S(2)}, u32[]{:S(2)}) %collective-permute-start.49) | collective-permute-done | bytes 524320 | tf_op jit(solution)/shard_map/ppermute | solution.py:582
  373.9 7.5 %collective-permute-done.54.refs_3_ = bf16[1200,128]{1,0:T(8,128)(2,1)S(1)} collective-permute-done((bf16[1200,128]{1,0:T(8,128)(2,1)}, bf16[1200,128]{1,0:T(8,128)(2,1)S(1)}, u32[]{:S(2)}, u32[]{:S(2)}) %collective-permute-start.54) | collective-permute-done | bytes 307232 | tf_op jit(solution)/shard_map/ppermute | solution.py:582
  381.4 11.5 %collective-permute-done.55.refs_4_ = bf16[1200,128]{1,0:T(8,128)(2,1)S(1)} collective-permute-done((bf16[1200,128]{1,0:T(8,128)(2,1)S(1)}, bf16[1200,128]{1,0:T(8,128)(2,1)S(1)}, u32[]{:S(2)}, u32[]{:S(2)}) %collective-permute-start.55) | collective-permute-done | bytes 307232 | tf_op jit(solution)/shard_map/ppermute | solution.py:582
  406.2 5.1 %collective-permute-start.62 = (f32[1,128]{1,0:T(1,128)S(1)}, f32[1,128]{1,0:T(1,128)S(1)}, u32[]{:S(2)}, u32[]{:S(2)}) collective-permute-start(f32[1,128]{1,0:T(1,128)S(1)} %add.127.refs_3_.refs_1_), channel_id=1, source_target_pairs={{0,16},{4,20},{8,24},{12,28},{16,0},{20,4},{24,8},{28,12},{1,17},{... | collective-permute-start | bytes 1544 | tf_op jit(solution)/shard_map/ppermute | solution.py:582
  415.5 8.6 %adam.1 = (f32[4,128,256]{2,1,0:T(8,128)}, f32[4,128,256]{2,1,0:T(8,128)}, f32[4,128,256]{2,1,0:T(8,128)}, bf16[4,128,256]{2,1,0:T(8,128)(2,1)}, f32[2,128,1024]...) custom-call(f32[2]{0:T(128)S(1)} %get-tuple-element.285.refs_0_, ...), custom_call_target="tpu_custom_call" | custom-call | flops 10000000 | bytes 20000000 | tf_op jit(solution)/shard_map/adam/pallas_call | solution.py:1487
  (358 shorter events, 186.4 us)
Async XLA Ops:
  7.2 65.2 %all-gather.6.cloned.1.call-start = ((), (), s32[]{:S(2)}) async-start(), calls=%async_computation.3 | async-start | bytes 2985984 | tf_op jit(solution)/shard_map/all_gather | solution.py:1792
  9.2 165.4 %all-gather.4.cloned.1.call-start = ((), (), s32[]{:S(2)}) async-start(), calls=%async_computation.1 | async-start | bytes 4718592 | tf_op jit(solution)/shard_map/all_gather | solution.py:1860
  11.6 17.3 %collective-permute-start.10 = (bf16[512,128]{1,0:T(8,128)(2,1)}, bf16[512,128]{1,0:T(8,128)(2,1)S(1)}, u32[]{:S(2)}, u32[]{:S(2)}) collective-permute-start(bf16[512,128]{1,0:T(8,128)(2,1)} %tokens.1.refs_0_), channel_id=1, source_target_pairs={{0,24},{4,28},{8,16},{12,20},{16,8},{20,12},{24,0},{28,4},{1,25},{... | collective-permute-start | bytes 393224 | tf_op jit(solution)/shard_map/ppermute | solution.py:582
  16.6 18.7 %collective-permute-start.9 = (bf16[512,128]{1,0:T(8,128)(2,1)}, bf16[512,128]{1,0:T(8,128)(2,1)S(1)}, u32[]{:S(2)}, u32[]{:S(2)}) collective-permute-start(bf16[512,128]{1,0:T(8,128)(2,1)} %tokens.1.refs_0_), channel_id=1, source_target_pairs={{0,16},{4,20},{8,24},{12,28},{16,0},{20,4},{24,8},{28,12},{1,17},{... | collective-permute-start | bytes 393224 | tf_op jit(solution)/shard_map/ppermute | solution.py:582
  16.6 18.7 %collective-permute-start.8 = (bf16[512,128]{1,0:T(8,128)(2,1)}, bf16[512,128]{1,0:T(8,128)(2,1)S(1)}, u32[]{:S(2)}, u32[]{:S(2)}) collective-permute-start(bf16[512,128]{1,0:T(8,128)(2,1)} %tokens.1.refs_0_), channel_id=1, source_target_pairs={{0,8},{4,12},{8,0},{12,4},{16,24},{20,28},{24,16},{28,20},{1,9},{5... | collective-permute-start | bytes 393224 | tf_op jit(solution)/shard_map/ppermute | solution.py:582
  27.1 12.0 %collective-permute-start.1 = (f32[4,4,1536]{2,1,0:T(4,128)S(1)}, f32[4,4,1536]{2,1,0:T(4,128)S(1)}, u32[]{:S(2)}, u32[]{:S(2)}) collective-permute-start(f32[4,4,1536]{2,1,0:T(4,128)S(1)} %select_bitcast_fusion), channel_id=1, source_target_pairs={{0,4},{4,0},{8,12},{12,8},{16,20},{20,16},{24,28},{28,24},{1,5},{5... | collective-permute-start | bytes 294920 | tf_op jit(solution)/shard_map/ppermute | solution.py:582
  35.3 17.8 %collective-permute-start.11 = (bf16[1536,128]{1,0:T(8,128)(2,1)S(1)}, bf16[1536,128]{1,0:T(8,128)(2,1)S(1)}, u32[]{:S(2)}, u32[]{:S(2)}) collective-permute-start(bf16[1536,128]{1,0:T(8,128)(2,1)S(1)} %pad_maximum_fusion.3), channel_id=1, source_target_pairs={{0,4},{4,0},{8,12},{12,8},{16,20},{20,16},{24,28},{28,24},{1,5},{5... | collective-permute-start | bytes 1179656 | tf_op jit(solution)/shard_map/ppermute | solution.py:582
  93.2 279.5 %reduce-scatter.2.cloned.1.call-start = ((), (), s32[]{:S(2)}) async-start(), calls=%async_computation.2 | async-start | bytes 4718592 | tf_op jit(solution)/shard_map/reduce_scatter | solution.py:1951
  142.2 14.2 %collective-permute-start.23 = (bf16[256,1024]{1,0:T(8,128)(2,1)S(1)}, bf16[256,1024]{1,0:T(8,128)(2,1)S(1)}, u32[]{:S(2)}, u32[]{:S(2)}) collective-permute-start(bf16[256,1024]{1,0:T(8,128)(2,1)S(1)} %fusion), channel_id=1, source_target_pairs={{0,2},{1,3},{2,0},{3,1},{4,6},{5,7},{6,4},{7,5},{8,10},{9,11},{10,... | collective-permute-start | bytes 1572872 | tf_op jit(solution)/shard_map/ppermute | solution.py:582
  158.5 13.4 %collective-permute-start.24 = (bf16[256,1024]{1,0:T(8,128)(2,1)S(1)}, bf16[256,1024]{1,0:T(8,128)(2,1)S(1)}, u32[]{:S(2)}, u32[]{:S(2)}) collective-permute-start(bf16[256,1024]{1,0:T(8,128)(2,1)S(1)} %get-tuple-element.159.first.refs_0_), channel_id=1, source_target_pairs={{0,2},{1,3},{2,0},{3,1},{4,6},{5,7},{6,4},{7,5},{8,10},{9,11},{10,... | collective-permute-start | bytes 1572872 | tf_op jit(solution)/shard_map/ppermute | solution.py:582
  183.9 14.0 %collective-permute-start.29 = (bf16[256,1024]{1,0:T(8,128)(2,1)S(1)}, bf16[256,1024]{1,0:T(8,128)(2,1)S(1)}, u32[]{:S(2)}, u32[]{:S(2)}) collective-permute-start(bf16[256,1024]{1,0:T(8,128)(2,1)S(1)} %add_convert_fusion.2), channel_id=1, source_target_pairs={{0,2},{1,3},{2,0},{3,1},{4,6},{5,7},{6,4},{7,5},{8,10},{9,11},{10,... | collective-permute-start | bytes 1572872 | tf_op jit(solution)/shard_map/ppermute | solution.py:582
  201.6 14.3 %collective-permute-start.32 = (bf16[256,1024]{1,0:T(8,128)(2,1)S(1)}, bf16[256,1024]{1,0:T(8,128)(2,1)S(1)}, u32[]{:S(2)}, u32[]{:S(2)}) collective-permute-start(bf16[256,1024]{1,0:T(8,128)(2,1)S(1)} %get-tuple-element.164.first.refs_4_), channel_id=1, source_target_pairs={{0,2},{1,3},{2,0},{3,1},{4,6},{5,7},{6,4},{7,5},{8,10},{9,11},{10,... | collective-permute-start | bytes 1572872 | tf_op jit(solution)/shard_map/ppermute | solution.py:582
  220.6 11.9 %collective-permute-start.31 = (bf16[256,1024]{1,0:T(8,128)(2,1)}, bf16[256,1024]{1,0:T(8,128)(2,1)}, u32[]{:S(2)}, u32[]{:S(2)}) collective-permute-start(bf16[256,1024]{1,0:T(8,128)(2,1)} %get-tuple-element.167), channel_id=1, source_target_pairs={{0,1},{1,0},{2,3},{3,2},{4,5},{5,4},{6,7},{7,6},{8,9},{9,8},{10,11... | collective-permute-start | bytes 1572872 | tf_op jit(solution)/shard_map/ppermute | solution.py:582
  223.3 14.3 %collective-permute-start.35 = (bf16[256,1024]{1,0:T(8,128)(2,1)}, bf16[256,1024]{1,0:T(8,128)(2,1)}, u32[]{:S(2)}, u32[]{:S(2)}) collective-permute-start(bf16[256,1024]{1,0:T(8,128)(2,1)} %add_convert_fusion.1), channel_id=1, source_target_pairs={{0,2},{1,3},{2,0},{3,1},{4,6},{5,7},{6,4},{7,5},{8,10},{9,11},{10,... | collective-permute-start | bytes 1572872 | tf_op jit(solution)/shard_map/ppermute | solution.py:582
  246.1 13.1 %collective-permute-start.37 = (bf16[256,1024]{1,0:T(8,128)(2,1)S(1)}, bf16[256,1024]{1,0:T(8,128)(2,1)S(1)}, u32[]{:S(2)}, u32[]{:S(2)}) collective-permute-start(bf16[256,1024]{1,0:T(8,128)(2,1)S(1)} %copy-done.29), channel_id=1, source_target_pairs={{0,2},{1,3},{2,0},{3,1},{4,6},{5,7},{6,4},{7,5},{8,10},{9,11},{10,... | collective-permute-start | bytes 1572872 | tf_op jit(solution)/shard_map/ppermute | solution.py:582
  247.7 11.6 %collective-permute-start.36 = (bf16[256,1024]{1,0:T(8,128)(2,1)S(1)}, bf16[256,1024]{1,0:T(8,128)(2,1)S(1)}, u32[]{:S(2)}, u32[]{:S(2)}) collective-permute-start(bf16[256,1024]{1,0:T(8,128)(2,1)S(1)} %copy-done.29), channel_id=1, source_target_pairs={{0,1},{1,0},{2,3},{3,2},{4,5},{5,4},{6,7},{7,6},{8,9},{9,8},{10,11... | collective-permute-start | bytes 1572872 | tf_op jit(solution)/shard_map/ppermute | solution.py:582
  264.7 14.3 %collective-permute-start.40 = (bf16[64,1024]{1,0:T(8,128)(2,1)S(1)}, bf16[64,1024]{1,0:T(8,128)(2,1)S(1)}, u32[]{:S(2)}, u32[]{:S(2)}) collective-permute-start(bf16[64,1024]{1,0:T(8,128)(2,1)S(1)} %get-tuple-element.260), channel_id=1, source_target_pairs={{0,8},{4,12},{8,0},{12,4},{16,24},{20,28},{24,16},{28,20},{1,9},{5... | collective-permute-start | bytes 393224 | tf_op jit(solution)/shard_map/ppermute | solution.py:582
  310.2 12.1 %collective-permute-start.43 = (bf16[192,1024]{1,0:T(8,128)(2,1)S(1)}, bf16[192,1024]{1,0:T(8,128)(2,1)S(1)}, u32[]{:S(2)}, u32[]{:S(2)}) collective-permute-start(bf16[192,1024]{1,0:T(8,128)(2,1)S(1)} %get-tuple-element.188), channel_id=1, source_target_pairs={{0,8},{4,12},{8,0},{12,4},{16,24},{20,28},{24,16},{28,20},{1,9},{5... | collective-permute-start | bytes 1179656 | tf_op jit(solution)/shard_map/ppermute | solution.py:582
  310.2 19.7 %collective-permute-start.44 = (bf16[192,1024]{1,0:T(8,128)(2,1)S(1)}, bf16[192,1024]{1,0:T(8,128)(2,1)S(1)}, u32[]{:S(2)}, u32[]{:S(2)}) collective-permute-start(bf16[192,1024]{1,0:T(8,128)(2,1)S(1)} %get-tuple-element.189), channel_id=1, source_target_pairs={{0,12},{4,8},{8,4},{12,0},{16,28},{20,24},{24,20},{28,16},{1,13},{... | collective-permute-start | bytes 1179656 | tf_op jit(solution)/shard_map/ppermute | solution.py:582
  334.5 14.0 %collective-permute-start.49 = (bf16[256,1024]{1,0:T(8,128)(2,1)S(1)}, bf16[256,1024]{1,0:T(8,128)(2,1)S(1)}, u32[]{:S(2)}, u32[]{:S(2)}) collective-permute-start(bf16[256,1024]{1,0:T(8,128)(2,1)S(1)} %add_convert_fusion), channel_id=1, source_target_pairs={{0,2},{1,3},{2,0},{3,1},{4,6},{5,7},{6,4},{7,5},{8,10},{9,11},{10,... | collective-permute-start | bytes 1572872 | tf_op jit(solution)/shard_map/ppermute | solution.py:582
  339.1 26.0 %collective-permute-start.46 = (bf16[4,768,128]{2,1,0:T(8,128)(2,1)S(1)}, bf16[4,768,128]{2,1,0:T(8,128)(2,1)S(1)}, u32[]{:S(2)}, u32[]{:S(2)}) collective-permute-start(bf16[4,768,128]{2,1,0:T(8,128)(2,1)S(1)} %get-tuple-element.197), channel_id=1, source_target_pairs={{0,4},{4,0},{8,12},{12,8},{16,20},{20,16},{24,28},{28,24},{1,5},{5... | collective-permute-start | bytes 2359304 | tf_op jit(solution)/shard_map/ppermute | solution.py:582
  368.4 13.0 %collective-permute-start.54 = (bf16[1200,128]{1,0:T(8,128)(2,1)}, bf16[1200,128]{1,0:T(8,128)(2,1)S(1)}, u32[]{:S(2)}, u32[]{:S(2)}) collective-permute-start(bf16[1200,128]{1,0:T(8,128)(2,1)} %get-tuple-element.217), channel_id=1, source_target_pairs={{0,8},{4,12},{8,0},{12,4},{16,24},{20,28},{24,16},{28,20},{1,9},{5... | collective-permute-start | bytes 921608 | tf_op jit(solution)/shard_map/ppermute | solution.py:582
  368.6 24.3 %collective-permute-start.55 = (bf16[1200,128]{1,0:T(8,128)(2,1)S(1)}, bf16[1200,128]{1,0:T(8,128)(2,1)S(1)}, u32[]{:S(2)}, u32[]{:S(2)}) collective-permute-start(bf16[1200,128]{1,0:T(8,128)(2,1)S(1)} %get-tuple-element.218), channel_id=1, source_target_pairs={{0,16},{4,20},{8,24},{12,28},{16,0},{20,4},{24,8},{28,12},{1,17},{... | collective-permute-start | bytes 921608 | tf_op jit(solution)/shard_map/ppermute | solution.py:582
  369.0 23.9 %collective-permute-start.56 = (bf16[1200,128]{1,0:T(8,128)(2,1)S(1)}, bf16[1200,128]{1,0:T(8,128)(2,1)S(1)}, u32[]{:S(2)}, u32[]{:S(2)}) collective-permute-start(bf16[1200,128]{1,0:T(8,128)(2,1)S(1)} %get-tuple-element.219), channel_id=1, source_target_pairs={{0,24},{4,28},{8,16},{12,20},{16,8},{20,12},{24,0},{28,4},{1,25},{... | collective-permute-start | bytes 921608 | tf_op jit(solution)/shard_map/ppermute | solution.py:582
  (120 other events, 865.9 us)
Sparse Core Ops, SparseCore 0:
  10.8 61.6 all-gather.5
  93.4 77.7 all-gather.3
  245.2 110.9 reduce-scatter.1
